TPU v7x, 32 devices: a whole 2x2x4 slice. The times are simulated.
32 devices in a mesh: seq: 8 (over z, y), rows: 4 (over x, core).
Axes of the slice: x: 2, y: 2, z: 4, core: 2. Of those that a mesh axis runs over, the one named last changes fastest.
Arguments:
- inputs: bfloat16 [8, 1024, 2048], P('rows', 'seq'), may hold values from -6 to 6
- segment_ids: int32 [8, 1024], P('rows', 'seq'), may hold values from 0 to 1, as said below
- mix_gain: float32 [2048], replicated, may hold values from 0.25 to 1.75
- in_weight: bfloat16 [2048, 2, 2560], P(None, None, 'seq'), may hold values from -0.125 to 0.125
- conv_weight: float32 [4, 2560], replicated, may hold values from -3 to 3
- conv_bias: float32 [2560], replicated, may hold values from -3 to 3
- gate_weight: bfloat16 [160, 2, 2560], replicated, may hold values from -0.5 to 0.5
- gate_bias: float32 [2, 2560], replicated, may hold values from -3 to 3
- decay_param: float32 [2560], replicated, may hold values from 2 to 9
- out_weight: bfloat16 [2048, 2560], P(None, 'seq'), may hold values from -0.3125 to 0.3125
- mlp_gain: float32 [2048], replicated, may hold values from 0.25 to 1.75
- mlp_in: bfloat16 [2048, 2, 6144], P(None, None, 'seq'), may hold values from -0.125 to 0.125
- down_weight: bfloat16 [2048, 6144], P(None, 'seq'), may hold values from -0.109375 to 0.109375
- cotangent: bfloat16 [8, 1024, 2048], P('rows', 'seq'), may hold values from -6 to 6
Outputs:
- outputs: bfloat16 [8, 1024, 2048], P('rows', 'seq')
- grad_inputs: float32 [8, 1024, 2048], P('rows', 'seq')
- grad_mix_gain: float32 [2048], P(('seq', 'rows'))
- grad_in_weight: float32 [2048, 2, 2560], P(('seq', 'rows'))
- grad_conv_weight: float32 [4, 2560], P(None, ('seq', 'rows'))
- grad_conv_bias: float32 [2560], P(('seq', 'rows'))
- grad_gate_weight: float32 [160, 2, 2560], P(None, None, ('seq', 'rows'))
- grad_gate_bias: float32 [2, 2560], P(None, ('seq', 'rows'))
- grad_decay_param: float32 [2560], P(('seq', 'rows'))
- grad_out_weight: float32 [2048, 2560], P(('seq', 'rows'))
- grad_mlp_gain: float32 [2048], P(('seq', 'rows'))
- grad_mlp_in: float32 [2048, 2, 6144], P(('seq', 'rows'))
- grad_down_weight: float32 [2048, 6144], P(('seq', 'rows'))
Inputs may be any that keep to these rules, and one draw needn't show every extreme that they name: `segment_ids`: in each row the ids start at 0 and rise by 0 or 1 from one position to the next; in each aligned group of 2 rows one row holds a single document and another reaches the largest id.
All inputs are finite; a program needn't handle non-finite values.
Results may differ from a plain program's by a relative error of at most 0.011.
Values may be sent and summed in bfloat16 or wider, within the bound.
A program may use at most 896 MiB of HBM per device.

v0:
```python
import jax
import jax.numpy as jnp
from jax import lax
from jax.sharding import PartitionSpec as P

EPS = 1e-06


def from_behind(block, axis, distance):
    devices = range(lax.axis_size(axis))
    route = [(i - distance, i) for i in devices if i - distance in devices]
    return lax.ppermute(block, axis, route)


def rms_norm(values, scale_vec):
    return values * lax.rsqrt(jnp.mean(values * values, axis=-1, keepdims=True) + EPS) * scale_vec


def gelu(values):
    return jax.nn.gelu(values, approximate=True)


def gated_product(values):
    return gelu(values[:, 0]) * values[:, 1]


def gated_mix(left_side, right_side):
    return gelu(left_side) * right_side


def pair_combine(earlier, later_pair):
    return (earlier[0] * later_pair[0], later_pair[0] * earlier[1] + later_pair[1])


def recurrence_inputs(conv_vals, gate_logits, decay_param, reset_flags):
    recur_gate = jax.nn.sigmoid(gate_logits[..., 0, :])
    input_gate = jax.nn.sigmoid(gate_logits[..., 1, :])
    log_decay = -8.0 * jax.nn.softplus(-decay_param) * recur_gate
    carry_mask = 1.0 - reset_flags
    decays = jnp.exp(log_decay) * carry_mask
    normalizer = reset_flags + carry_mask * jnp.sqrt(-jnp.expm1(2.0 * log_decay))
    return (decays, normalizer * input_gate * conv_vals)


def scan_pairs(decays, driven, scan_axis):
    return lax.associative_scan(pair_combine, (decays, driven), axis=scan_axis)


def reverse_pairs(decays, driven, scan_axis):
    result = scan_pairs(jnp.flip(decays, scan_axis), jnp.flip(driven, scan_axis), scan_axis)
    return (jnp.flip(result[0], scan_axis), jnp.flip(result[1], scan_axis))


def state_grads(products, passed, grad_states, states, start_state, incoming):
    passed = passed + products * incoming[:, None, :]
    following = jnp.concatenate([passed[:, 1:], incoming[:, None, :]], axis=1)
    summed = grad_states + following
    before = jnp.concatenate([start_state[:, None, :], states[:, :-1]], axis=1)
    return (summed * before, summed)


def fold_weight(weight, step_fn, start_value):
    return step_fn(start_value, lax.all_gather(weight, "seq", axis=1, tiled=True), jnp.int32(0))


def map_weight(weight, piece_fn):
    return piece_fn(lax.all_gather(weight, "seq", axis=1, tiled=True), jnp.int32(0))


def per_device(
    inputs,
    segment_ids,
    mix_gain,
    in_weight,
    conv_weight,
    conv_bias,
    gate_weight,
    gate_bias,
    decay_param,
    out_weight,
    mlp_gain,
    mlp_in,
    down_weight,
    cotangent,
):
    micro_count, tokens_mb, model_width = inputs.shape
    token_count = micro_count * tokens_mb
    recur_width = conv_weight.shape[1]
    conv_lag = conv_weight.shape[0] - 1
    block_width = gate_weight.shape[0]
    block_count = recur_width // block_width
    mixer_shape = (micro_count, tokens_mb, recur_width)
    f32 = jnp.float32
    bf16 = jnp.bfloat16
    in_cols = in_weight.reshape(2 * model_width, in_weight.shape[2])
    mlp_cols = mlp_in.reshape(2 * model_width, mlp_in.shape[2])
    flat_in = inputs.reshape(token_count, model_width).astype(f32)
    normed = rms_norm(flat_in, mix_gain).astype(bf16)

    def in_piece(weight_cols, offset):
        return jnp.einsum(
            "td,dkr->tkr",
            normed,
            weight_cols.reshape(model_width, 2, -1),
            preferred_element_type=f32,
        )

    branches = map_weight(in_cols, in_piece)
    gate_branch = branches[:, 0].reshape(mixer_shape)
    recur_low = branches[:, 1].astype(bf16).reshape(mixer_shape)
    recur_vals = lax.optimization_barrier(recur_low).astype(f32)
    seg_plus = (segment_ids + 1).astype(f32)
    tail_in = (
        from_behind(recur_vals[:, tokens_mb - conv_lag :].astype(jnp.bfloat16), "seq", 1).astype(
            jnp.float32
        ),
        from_behind(seg_plus[:, tokens_mb - conv_lag :].astype(jnp.bfloat16), "seq", 1).astype(
            jnp.float32
        ),
    )
    recur_ext = jnp.concatenate([tail_in[0], recur_vals], axis=1)
    seg_ext = jnp.concatenate([tail_in[1], seg_plus], axis=1)
    same_masks = [
        (seg_ext[:, conv_lag - k : conv_lag - k + tokens_mb] == seg_plus).astype(f32)[..., None]
        for k in range(conv_lag + 1)
    ]
    lagged = [recur_ext[:, conv_lag - k : conv_lag - k + tokens_mb] for k in range(conv_lag + 1)]
    conv_out = conv_bias
    for k in range(conv_lag + 1):
        conv_out = conv_out + conv_weight[k] * lagged[k] * same_masks[k]
    reset_flags = (seg_ext[:, conv_lag - 1 : conv_lag - 1 + tokens_mb] != seg_plus).astype(f32)
    conv_low = conv_out.astype(bf16)
    conv_vals = lax.optimization_barrier(conv_low).astype(f32)
    conv_blocks = conv_low.reshape(micro_count, tokens_mb, block_count, block_width)
    gate_blocks = gate_weight.reshape(block_width, 2, block_count, block_width)
    gate_logits = jnp.einsum(
        "mtnj,jknc->mtknc", conv_blocks, gate_blocks, preferred_element_type=f32
    )
    gate_logits = gate_logits.reshape(micro_count, tokens_mb, 2, recur_width) + gate_bias
    reset_col = reset_flags[..., None]
    decays, driven = recurrence_inputs(conv_vals, gate_logits, decay_param, reset_col)
    kept_states = []
    rounded = []
    for m in range(micro_count):
        channel_in = (
            lax.all_to_all(decays[m], "seq", split_axis=1, concat_axis=0, tiled=True),
            lax.all_to_all(driven[m], "seq", split_axis=1, concat_axis=0, tiled=True),
        )
        channel_states = scan_pairs(channel_in[0], channel_in[1], 0)[1]
        kept_states.append((channel_in[0], channel_states))
        rounded.append(
            lax.all_to_all(
                channel_states.astype(bf16), "seq", split_axis=0, concat_axis=1, tiled=True
            )
        )
    states_low = jnp.stack(rounded)
    states_vals = lax.optimization_barrier(states_low).astype(f32)
    mixed = (gelu(gate_branch) * states_vals).astype(bf16).reshape(token_count, recur_width)

    def out_step(running, weight_cols, offset):
        return jnp.einsum("tr,dr->td", mixed, weight_cols, preferred_element_type=f32)

    middle = flat_in + fold_weight(out_weight, out_step, jnp.zeros((token_count, model_width), f32))
    normed_two = rms_norm(middle, mlp_gain).astype(bf16)

    def mlp_piece(weight_cols, offset):
        return jnp.einsum(
            "td,dkf->tkf",
            normed_two,
            weight_cols.reshape(model_width, 2, -1),
            preferred_element_type=f32,
        )

    gate_up = map_weight(mlp_cols, mlp_piece)
    hidden = gated_product(gate_up).astype(bf16)

    def down_step(running, weight_cols, offset):
        return jnp.einsum("tf,df->td", hidden, weight_cols, preferred_element_type=f32)

    down_out = fold_weight(down_weight, down_step, jnp.zeros((token_count, model_width), f32))
    outputs = (middle + down_out).astype(bf16).reshape(inputs.shape)
    cot_low = cotangent.reshape(token_count, model_width)

    def down_back(weight_cols, offset):
        return jnp.dot(cot_low, weight_cols, preferred_element_type=f32)[:, None, :]

    grad_hidden = map_weight(down_weight, down_back)[:, 0]
    grad_gate_up = jax.vjp(gated_product, gate_up)[1](grad_hidden)[0].astype(bf16)

    def mlp_back(running, weight_cols, offset):
        return jnp.einsum(
            "tkf,dkf->td",
            grad_gate_up,
            weight_cols.reshape(model_width, 2, -1),
            preferred_element_type=f32,
        )

    grad_normed_two = fold_weight(mlp_cols, mlp_back, jnp.zeros((token_count, model_width), f32))
    grad_mid_norm, grad_mlp_gain = jax.vjp(rms_norm, middle, mlp_gain)[1](grad_normed_two)
    grad_middle = cot_low.astype(f32) + grad_mid_norm
    grad_mid_low = grad_middle.astype(bf16)

    def out_back(weight_cols, offset):
        return jnp.dot(grad_mid_low, weight_cols, preferred_element_type=f32)[:, None, :]

    grad_mixed = map_weight(out_weight, out_back)[:, 0].reshape(mixer_shape)
    grad_gate_branch, grad_states = jax.vjp(gated_mix, gate_branch, states_vals)[1](grad_mixed)
    grad_low = grad_states.astype(bf16)
    back_decays = []
    back_driven = []
    for m in range(micro_count):
        channel_decays, channel_states = kept_states[m]
        grad_channel = lax.all_to_all(
            grad_low[m], "seq", split_axis=1, concat_axis=0, tiled=True
        ).astype(f32)
        products, passed = reverse_pairs(
            channel_decays[None], (channel_decays * grad_channel)[None], 1
        )
        zero_state = jnp.zeros((1, channel_decays.shape[1]), f32)
        part_decays, part_driven = state_grads(
            products, passed, grad_channel[None], channel_states[None], zero_state, zero_state
        )
        returned = (
            lax.all_to_all(
                part_decays[0].astype(jnp.bfloat16), "seq", split_axis=0, concat_axis=1, tiled=True
            ).astype(jnp.float32),
            lax.all_to_all(
                part_driven[0].astype(jnp.bfloat16), "seq", split_axis=0, concat_axis=1, tiled=True
            ).astype(jnp.float32),
        )
        back_decays.append(returned[0])
        back_driven.append(returned[1])
    grad_decays = jnp.stack(back_decays)
    grad_driven = jnp.stack(back_driven)

    def gate_math(conv_in, logits_in, decay_in):
        return recurrence_inputs(conv_in, logits_in, decay_in, reset_col)

    grad_conv_direct, grad_logits, grad_decay = jax.vjp(
        gate_math, conv_vals, gate_logits, decay_param
    )[1]((grad_decays, grad_driven))
    grad_logits_low = grad_logits.astype(bf16).reshape(
        micro_count, tokens_mb, 2, block_count, block_width
    )
    grad_conv = grad_conv_direct + jnp.einsum(
        "mtknc,jknc->mtnj", grad_logits_low, gate_blocks, preferred_element_type=f32
    ).reshape(mixer_shape)
    grad_gate_weight = jnp.einsum(
        "mtnj,mtknc->jknc", conv_blocks, grad_logits_low, preferred_element_type=f32
    ).reshape(block_width, 2, recur_width)
    grad_gate_bias = jnp.sum(grad_logits, axis=(0, 1))
    next_head = (
        from_behind(grad_conv[:, :conv_lag].astype(jnp.bfloat16), "seq", -1).astype(jnp.float32),
        from_behind(seg_plus[:, :conv_lag].astype(jnp.bfloat16), "seq", -1).astype(jnp.float32),
    )
    grad_ext = jnp.concatenate([grad_conv, next_head[0]], axis=1)
    seg_next = jnp.concatenate([seg_plus, next_head[1]], axis=1)
    grad_recur = conv_weight[0] * grad_conv
    for k in range(1, conv_lag + 1):
        next_mask = (seg_next[:, k : k + tokens_mb] == seg_plus).astype(f32)[..., None]
        grad_recur = grad_recur + conv_weight[k] * grad_ext[:, k : k + tokens_mb] * next_mask
    grad_conv_weight = jnp.stack(
        [jnp.sum(grad_conv * lagged[k] * same_masks[k], axis=(0, 1)) for k in range(conv_lag + 1)]
    )
    grad_conv_bias = jnp.sum(grad_conv, axis=(0, 1))
    grad_branches = jnp.stack([grad_gate_branch.astype(bf16), grad_recur.astype(bf16)], axis=2)
    grad_branches = grad_branches.reshape(token_count, 2, recur_width)

    def in_back(running, weight_cols, offset):
        return jnp.einsum(
            "tkr,dkr->td",
            grad_branches,
            weight_cols.reshape(model_width, 2, -1),
            preferred_element_type=f32,
        )

    grad_normed = fold_weight(in_cols, in_back, jnp.zeros((token_count, model_width), f32))
    grad_in_norm, grad_mix_gain = jax.vjp(rms_norm, flat_in, mix_gain)[1](grad_normed)
    grad_inputs = (grad_middle + grad_in_norm).reshape(inputs.shape)
    ffn_width = grad_gate_up.shape[2]
    branch_flat = grad_branches.reshape(token_count, 2 * recur_width)
    gate_up_flat = grad_gate_up.reshape(token_count, 2 * ffn_width)

    def outer_rows(left_side, right_side):
        return jnp.einsum("tc,tx->cx", left_side, right_side, preferred_element_type=f32)

    grad_block = lax.psum_scatter(
        jnp.concatenate(
            [
                outer_rows(normed, branch_flat),
                outer_rows(normed_two, gate_up_flat),
                outer_rows(grad_mid_low, mixed),
                outer_rows(cot_low, hidden),
            ],
            axis=1,
        ),
        ("seq", "rows"),
        scatter_dimension=0,
        tiled=True,
    )
    own_rows = grad_block.shape[0]
    first_edge = 2 * recur_width
    second_edge = first_edge + 2 * ffn_width
    third_edge = second_edge + recur_width
    grad_in_weight = grad_block[:, :first_edge].reshape(own_rows, 2, recur_width)
    grad_mlp_in = grad_block[:, first_edge:second_edge].reshape(own_rows, 2, ffn_width)
    grad_out_weight = grad_block[:, second_edge:third_edge]
    grad_down_weight = grad_block[:, third_edge:]
    small_grads = (
        lax.psum_scatter(grad_mix_gain, ("seq", "rows"), scatter_dimension=0, tiled=True),
        lax.psum_scatter(grad_conv_weight, ("seq", "rows"), scatter_dimension=1, tiled=True),
        lax.psum_scatter(grad_conv_bias, ("seq", "rows"), scatter_dimension=0, tiled=True),
        lax.psum_scatter(grad_gate_weight, ("seq", "rows"), scatter_dimension=2, tiled=True),
        lax.psum_scatter(grad_gate_bias, ("seq", "rows"), scatter_dimension=1, tiled=True),
        lax.psum_scatter(grad_decay, ("seq", "rows"), scatter_dimension=0, tiled=True),
        lax.psum_scatter(grad_mlp_gain, ("seq", "rows"), scatter_dimension=0, tiled=True),
    )
    return (
        outputs,
        grad_inputs,
        small_grads[0],
        grad_in_weight,
        small_grads[1],
        small_grads[2],
        small_grads[3],
        small_grads[4],
        small_grads[5],
        grad_out_weight,
        small_grads[6],
        grad_mlp_in,
        grad_down_weight,
    )


def solution(mesh):
    return jax.shard_map(
        per_device,
        mesh=mesh,
        in_specs=(
            P("rows", "seq", None),
            P("rows", "seq"),
            P(),
            P(None, None, "seq"),
            P(),
            P(),
            P(),
            P(),
            P(),
            P(None, "seq"),
            P(),
            P(None, None, "seq"),
            P(None, "seq"),
            P("rows", "seq", None),
        ),
        out_specs=(
            P("rows", "seq", None),
            P("rows", "seq", None),
            P(("seq", "rows")),
            P(("seq", "rows"), None, None),
            P(None, ("seq", "rows")),
            P(("seq", "rows")),
            P(None, None, ("seq", "rows")),
            P(None, ("seq", "rows")),
            P(("seq", "rows")),
            P(("seq", "rows"), None),
            P(("seq", "rows")),
            P(("seq", "rows"), None, None),
            P(("seq", "rows"), None),
        ),
        check_vma=False,
    )
```

profile of v0, /device:TPU:0, one launch (start us, length us, event | category | flops | bytes accessed | tf_op | source)
XLA Modules:
  0.0 5436.1 jit_solution(2763106443084791379)
XLA Ops:
  67.4 362.3 %all-gather.5.cloned.1.call-done = bf16[4096,2560]{0,1:T(8,128)(2,1)} async-done(((bf16[4096,320]{0,1:T(8,128)(2,1)}), bf16[4096,2560]{0,1:T(8,128)(2,1)}) %all-gather.5.cloned.1.call-update) | async-done | bytes 20971536 | tf_op jit(solution)/shard_map/all_gather | solution.py:67
  429.7 26.1 copy.295
  455.8 41.0 reshape.361
  536.5 67.4 %all_to_all.174 = f32[128,8,320]{0,2,1:T(8,128)} all-to-all(f32[128,8,320]{0,2,1:T(8,128)S(1)} %bitcast.386), channel_id=1, replica_groups=mesh['seq'=8,'rows'=4] {'seq'}, dimensions={1} | all-to-all | bytes 2621440 | tf_op jit(solution)/shard_map/all_to_all | solution.py:147
  603.9 103.6 %all_to_all.175 = f32[128,8,320]{0,2,1:T(8,128)} all-to-all(f32[128,8,320]{0,2,1:T(8,128)S(1)} %bitcast.385), channel_id=1, replica_groups=mesh['seq'=8,'rows'=4] {'seq'}, dimensions={1} | all-to-all | bytes 2621440 | tf_op jit(solution)/shard_map/all_to_all | solution.py:147
  1352.9 26.4 pad.401
  1599.6 24.5 slice.1377
  1648.6 24.7 slice.1370
  1680.6 24.5 slice.1476
  1812.0 92.4 %reshape.367 = bf16[2048,2,6144]{2,1,0:T(2,128)(2,1)} reshape(bf16[4096,6144]{1,0:T(8,128)(2,1)} %all-gather.9.cloned.1.call-done) | data formatting | bytes 100663296 | tf_op jit(solution)/shard_map/reshape | solution.py:170
  1904.4 60.8 %fusion.2 = f32[256,2,6144]{2,0,1:T(8,128)} fusion(bf16[2048,2,6144]{2,1,0:T(2,128)(2,1)} %reshape.367, f32[256,2048]{1,0:T(8,128)} %get-tuple-element.256, f32[2048]{0:T(1024)S(1)} %copy-done.127, f32[256]{0:T(256)S(1)} %fusion.168), kind=kOutput, calls=%fused_computation.3 | convolution fusion | flops 12886474752 | bytes 65020928 | tf_op jit(solution)/shard_map/td,dkf->tkf/dot_general | solution.py:167
  1965.3 128.3 %all-gather.11.cloned.1.call-done = bf16[2048,6144]{1,0:T(8,128)(2,1)} async-done(((bf16[2048,768]{1,0:T(8,128)(2,1)}), bf16[2048,6144]{1,0:T(8,128)(2,1)}) %all-gather.11.cloned.1.call-update) | async-done | bytes 25165840 | tf_op jit(solution)/shard_map/all_gather | solution.py:63
  2122.6 59.9 %multiply_reduce_fusion.4 = (f32[2048]{0:T(1024)}, f32[256]{0:T(256)S(1)}, f32[256,2048]{1,0:T(8,128)}) fusion(f32[256,2048]{1,0:T(8,128)} %get-tuple-element.256, f32[256]{0:T(256)S(1)} %fusion.168, f32[2048]{0:T(1024)S(1)} %copy-done.127, bf16[256,2,6144]{2,0,1:T(8,128)(2,1)} %add_convert_fusion, bf16[2048,2,6144]{2,1,0:T(2,128)(2,1)} %reshape.367), kind=kOutput, calls=%fused_computation.169 | convolution fusion | flops 12888045568 | bytes 60835840 | tf_op jit(solution)/shard_map/tkf,dkf->td/dot_general | solution.py:191
  2216.9 35.5 fusion.180
  2834.6 26.8 pad.443
  2878.5 24.6 pad.462
  2903.1 25.0 pad.463
  3169.7 26.7 pad.483
  3212.6 24.7 pad.502
  3237.2 24.7 pad.503
  3431.7 160.7 %pad_maximum_fusion = f32[2048,26112]{1,0:T(8,128)} fusion(f32[2048,6144]{1,0:T(8,128)} %convolution_bitcast_fusion, f32[2048,2560]{1,0:T(8,128)} %fusion.133, f32[2048,12288]{1,0:T(8,128)} %fusion.180, f32[2048,5120]{1,0:T(8,128)} %fusion.199), kind=kLoop, calls=%fused_computation | loop fusion | flops 160432128 | bytes 427819008 | tf_op jit(solution)/shard_map/concatenate | solution.py:288
  3629.8 41.9 all-reduce.132
  3680.3 42.9 reduce-scatter.15.cloned.1.call-done
  3725.1 1690.0 %reduce-scatter.11.cloned.1.call-done = f32[64,26112]{1,0:T(8,128)} async-done(((f32[2048,26112]{1,0:T(8,128)}), f32[64,26112]{1,0:T(8,128)}) %reduce-scatter.11.cloned.1.call-update) | async-done | bytes 6684688 | tf_op jit(solution)/shard_map/reduce_scatter | solution.py:287
  (1207 shorter events, 2251.2 us)
Async XLA Ops:
  7.2 422.5 %all-gather.5.cloned.1.call-start = ((), (), s32[]{:S(2)}) async-start(), calls=%async_computation.16 | async-start | bytes 23592960 | tf_op jit(solution)/shard_map/all_gather | solution.py:67
  25.0 1778.1 %all-gather.7.cloned.1.call-start = ((), (), s32[]{:S(2)}) async-start(), calls=%async_computation.17 | async-start | bytes 11796480 | tf_op jit(solution)/shard_map/all_gather | solution.py:63
  25.8 1786.2 %all-gather.9.cloned.1.call-start = ((), (), s32[]{:S(2)}) async-start(), calls=%async_computation.18 | async-start | bytes 56623104 | tf_op jit(solution)/shard_map/all_gather | solution.py:67
  39.7 2053.8 %all-gather.11.cloned.1.call-start = ((), (), s32[]{:S(2)}) async-start(), calls=%async_computation.19 | async-start | bytes 28311552 | tf_op jit(solution)/shard_map/all_gather | solution.py:63
  40.5 26.3 collective-permute-start.3
  41.9 24.9 collective-permute-start
  51.7 465.7 %copy-start.179 = (f32[2560]{0:T(1024)}, f32[2560]{0:T(1024)S(1)}, u32[]{:S(2)}) copy-start(f32[2560]{0:T(1024)S(1)} %get-tuple-element.73) | copy-start | bytes 30724
  52.1 1529.0 %copy-start.177 = (f32[2560]{0:T(1024)}, f32[2560]{0:T(1024)S(1)}, u32[]{:S(2)}) copy-start(f32[2560]{0:T(1024)S(1)} %fusion.163) | copy-start | bytes 30724
  511.5 5.4 collective-permute-start.1
  707.5 125.6 %all-to-all-start.1 = ((f32[128,8,320]{0,2,1:T(8,128)}), f32[128,8,320]{0,2,1:T(8,128)S(1)}, u32[]{:S(2)}, u32[]{:S(2)}) async-start(f32[128,8,320]{0,2,1:T(8,128)} %bitcast.14), calls=%async_computation.1 | async-start | bytes 2621440 | tf_op jit(solution)/shard_map/all_to_all | solution.py:146
  833.1 238.0 %all-to-all-start.4 = ((f32[128,8,320]{0,2,1:T(8,128)}), f32[128,8,320]{0,2,1:T(8,128)S(1)}, u32[]{:S(2)}, u32[]{:S(2)}) async-start(f32[128,8,320]{0,2,1:T(8,128)} %bitcast.384), calls=%async_computation.4 | async-start | bytes 2621440 | tf_op jit(solution)/shard_map/all_to_all | solution.py:146
  1382.9 191.7 %all-to-all-start.2 = ((bf16[8,128,320]{1,2,0:T(8,128)(2,1)}), bf16[8,128,320]{1,2,0:T(8,128)(2,1)}, u32[]{:S(2)}, u32[]{:S(2)}) async-start(bf16[8,128,320]{1,2,0:T(8,128)(2,1)} %bitcast.315), calls=%async_computation.2 | async-start | bytes 1310720 | tf_op jit(solution)/shard_map/all_to_all | solution.py:152
  1574.6 221.7 %all-to-all-start.5 = ((bf16[8,128,320]{1,2,0:T(8,128)(2,1)}), bf16[8,128,320]{1,2,0:T(8,128)(2,1)S(1)}, u32[]{:S(2)}, u32[]{:S(2)}) async-start(bf16[8,128,320]{1,2,0:T(8,128)(2,1)} %bitcast.314), calls=%async_computation.5 | async-start | bytes 1310720 | tf_op jit(solution)/shard_map/all_to_all | solution.py:152
  2212.3 40.1 all-to-all-start.6
  2252.4 242.2 %all-to-all-start.8 = ((bf16[128,8,320]{0,2,1:T(8,128)(2,1)}), bf16[128,8,320]{0,2,1:T(8,128)(2,1)}, u32[]{:S(2)}, u32[]{:S(2)}) async-start(bf16[128,8,320]{0,2,1:T(8,128)(2,1)} %bitcast.40), calls=%async_computation.8 | async-start | bytes 1310720 | tf_op jit(solution)/shard_map/all_to_all | solution.py:213
  2952.9 186.9 %all-to-all-start.7 = ((bf16[8,128,320]{1,2,0:T(8,128)(2,1)}), bf16[8,128,320]{1,2,0:T(8,128)(2,1)S(1)}, u32[]{:S(2)}, u32[]{:S(2)}) async-start(bf16[8,128,320]{1,2,0:T(8,128)(2,1)} %copy.361), calls=%async_computation.7 | async-start | bytes 1310720 | tf_op jit(solution)/shard_map/all_to_all | solution.py:227
  3139.7 146.2 %all-to-all-start.10 = ((bf16[8,128,320]{1,2,0:T(8,128)(2,1)}), bf16[8,128,320]{1,2,0:T(8,128)(2,1)}, u32[]{:S(2)}, u32[]{:S(2)}) async-start(bf16[8,128,320]{1,2,0:T(8,128)(2,1)} %copy.378), calls=%async_computation.10 | async-start | bytes 1310720 | tf_op jit(solution)/shard_map/all_to_all | solution.py:224
  3286.0 29.0 all-to-all-start.9
  3315.0 20.9 all-to-all-start.11
  3321.0 356.5 %reduce-scatter.17.cloned.1.call-start = ((), (), s32[]{:S(2)}) async-start(), calls=%async_computation.23 | async-start | bytes 1351680
  3350.2 328.7 %reduce-scatter.13.cloned.1.call-start = ((), (), s32[]{:S(2)}) async-start(), calls=%async_computation.21 | async-start | bytes 1351680
  3377.2 18.2 collective-permute-start.2
  3378.5 344.7 %reduce-scatter.15.cloned.1.call-start = ((), (), s32[]{:S(2)}) async-start(), calls=%async_computation.22 | async-start | bytes 4055040
  3395.1 2020.0 %reduce-scatter.11.cloned.1.call-start = ((), (), s32[]{:S(2)}) async-start(), calls=%async_computation.20 | async-start | bytes 220594176 | tf_op jit(solution)/shard_map/reduce_scatter | solution.py:287
  (220 other events, 6958.7 us)
Sparse Core Ops, SparseCore 0:
  25.1 404.4 all-gather.4
  431.9 176.4 all-gather.6
  609.9 1001.9 all-gather.8
  1613.3 480.1 all-gather.10
  3350.3 134.1 reduce-scatter.16
  3486.7 131.1 reduce-scatter.12
  3623.3 99.9 reduce-scatter.14
  3729.7 1685.4 reduce-scatter.10
where the time goes:
time: 5460 us; the launch traced here: 5440 us
  waiting for transfers between devices  2240 us (41%)
  local copies, waits for them, and re-layouts  2230 us (41%)
  other arithmetic  356 us (7%)
  matrix products  309 us (6%)
  blocking collectives  213 us (4%)
  starting transfers between devices  69.9 us (1%)
    reduce_scatter x1, waiting for transfers between devices, per_device(): lax.psum_scatter(jnp.concatenate([outer_rows(normed, branch_flat), outer_...  1690 us
    slice x236, local copies, waits for them, and re-layouts, scan_pairs(): return lax.associative_scan(pair_combine, (decays, driven), axis=scan_axis)  1240 us
    pad x108, local copies, waits for them, and re-layouts, scan_pairs(): return lax.associative_scan(pair_combine, (decays, driven), axis=scan_axis)  588 us
    all_gather x2, waiting for transfers between devices, map_weight(): lax.all_gather(weight, 'seq', axis=1, tiled=True)  362 us
    all_to_all x2, blocking collectives, per_device(): lax.all_to_all(driven[m], 'seq', split_axis=1, concat_axis=0, tiled=True)  171 us
    concatenate x1, other arithmetic, per_device(): jnp.concatenate([outer_rows(normed, branch_flat), outer_rows(normed_two,...  161 us
    all_gather x2, waiting for transfers between devices, fold_weight(): lax.all_gather(weight, 'seq', axis=1, tiled=True)  128 us
  transfers between devices with their start and end apart: 22, of which 6 were waited for; matrix products, arithmetic and copies ran while one was open for 42% of the time, Pallas kernels for 0%

commit v1 on v0

v1 whole, which is shorter than its diff:
```python
import functools

import jax
import jax.numpy as jnp
from jax import lax
from jax.experimental import pallas as pl
from jax.experimental.pallas import tpu as pltpu
from jax.sharding import Mesh
from jax.sharding import PartitionSpec as P

EPS = 1e-06
MESH = pl.DeviceIdType.MESH
PLANE = ("i", "g", "c")
EVERY = ("t", "i", "g", "c")
F32 = jnp.float32
BF16 = jnp.bfloat16
GELU_A = 0.7978845608028654
GELU_B = 0.044715
HALO = 8
LANES = 128


def gelu_parts(x):
    square = x * x
    th = jnp.tanh(GELU_A * x * (1.0 + GELU_B * square))
    half = 0.5 * (1.0 + th)
    slope = half + 0.5 * x * (1.0 - th * th) * (GELU_A * (1.0 + 3.0 * GELU_B * square))
    return x * half, slope


def one_minus_exp(y):
    series = 1.0 + y * (-1.0 / 2 + y * (1.0 / 6 + y * (-1.0 / 24 + y * (1.0 / 120 + y * (-1.0 / 720 + y * (1.0 / 5040))))))
    return jnp.where(y < 0.35, y * series, 1.0 - jnp.exp(-y))


def sigmoid(x):
    return 1.0 / (1.0 + jnp.exp(-x))


def gate_values(conv_low, wg0, wg1, vec):
    logits0 = jnp.dot(conv_low, wg0, preferred_element_type=F32) + vec[5:6]
    logits1 = jnp.dot(conv_low, wg1, preferred_element_type=F32) + vec[6:7]
    recur_gate = sigmoid(logits0)
    input_gate = sigmoid(logits1)
    log_decay = -vec[7:8] * recur_gate
    return recur_gate, input_gate, log_decay


def greet(count):
    me = lax.axis_index("t")
    barrier = pltpu.get_barrier_semaphore()
    for step in range(1, count):
        pl.semaphore_signal(barrier, inc=1, device_id={"t": lax.rem(me + step, count)}, device_id_type=MESH)
    pl.semaphore_wait(barrier, count - 1)
    return me


def put_tiles(ref, at, values):
    tiles, lanes = ref.shape[0], ref.shape[2]
    short = tiles * lanes - values.shape[1]
    if short:
        values = jnp.concatenate([values, jnp.zeros((values.shape[0], short), values.dtype)], axis=1)
    for j in range(tiles):
        ref[j, at, :] = values[:, j * lanes : (j + 1) * lanes]


def get_tiles(ref, at, width):
    joined = jnp.concatenate([ref[j, at, :] for j in range(ref.shape[0])], axis=1)
    return joined[:, :width]


def join_tiles(parts, width):
    return jnp.concatenate(parts, axis=1)[:, :width]


def exchange(count, me, send, slots, send_sem, recv_sem):
    for step in range(1, count):
        pltpu.make_async_remote_copy(
            src_ref=send,
            dst_ref=slots.at[me],
            send_sem=send_sem.at[step],
            recv_sem=recv_sem.at[step],
            device_id={"t": lax.rem(me + step, count)},
            device_id_type=MESH,
        ).start()
    for step in range(1, count):
        other = lax.rem(me + count - step, count)
        pltpu.make_async_remote_copy(
            src_ref=send,
            dst_ref=slots.at[other],
            send_sem=send_sem.at[step],
            recv_sem=recv_sem.at[step],
            device_id={"t": other},
            device_id_type=MESH,
        ).wait()


def mixer_forward_kernel(
    count, seg, recur, gate, mask, wg0, wg1, vec_ref, conv_out, decay_out, states_out, mixed_out, halo_out, cin_out,
    drive, h_ref, a_ref, ext, halo_send, halo_recv, summary, slots, send_sem, recv_sem, halo_sems,
):
    me = greet(count)
    rows = 8
    for r in range(rows):
        halo_send[r * HALO : (r + 1) * HALO, :] = recur[
            (rows + r) * seg + seg - 16 : (rows + r) * seg + seg, :
        ].astype(F32)[16 - HALO :]
    halo_copy = pltpu.make_async_remote_copy(
        src_ref=halo_send,
        dst_ref=halo_recv,
        send_sem=halo_sems.at[0],
        recv_sem=halo_sems.at[1],
        device_id={"t": lax.rem(me + 1, count)},
        device_id_type=MESH,
    )
    halo_copy.start()
    halo_copy.wait()
    for r in range(rows):
        halo_out[r * HALO : (r + 1) * HALO, :] = halo_recv[r * HALO : (r + 1) * HALO, :]
        halo_out[(rows + r) * HALO : (rows + r + 1) * HALO, :] = recur[r * seg + seg - 16 : r * seg + seg, :].astype(F32)[
            16 - HALO :
        ]
    vec = vec_ref[...]

    def local(s, none):
        at = pl.ds(pl.multiple_of(s * seg, seg), seg)
        x = recur[at, :].astype(F32)
        ext[0:HALO, :] = halo_out[pl.ds(pl.multiple_of(s * HALO, HALO), HALO), :]
        ext[HALO : HALO + seg, :] = x
        m = mask[at, :]
        conv = vec[4:5] + vec[0:1] * x
        for k in range(1, 4):
            conv = conv + vec[k : k + 1] * ext[HALO - k : HALO - k + seg, :] * m[:, k - 1 : k]
        conv_low = conv.astype(BF16)
        conv_out[at, :] = conv_low
        recur_gate, input_gate, log_decay = gate_values(conv_low, wg0[...], wg1[...], vec)
        keep = m[:, 0:1]
        put_tiles(decay_out, at, jnp.exp(log_decay) * keep)
        scale = (1.0 - keep) + keep * jnp.sqrt(one_minus_exp(-2.0 * log_decay))
        put_tiles(drive, at, scale * input_gate * conv_low.astype(F32))
        return none

    lax.fori_loop(0, 2 * rows, local, 0)

    tiles, lanes = drive.shape[0], drive.shape[2]

    def scan(k, carried):
        at = pl.ds(k, 2 * rows, stride=seg)
        after = []
        for j in range(tiles):
            h, a = carried[j]
            d = decay_out[j, at, :]
            h = d * h + drive[j, at, :]
            a = a * d
            h_ref[j, at, :] = h
            a_ref[j, at, :] = a
            after.append((h, a))
        return tuple(after)

    width = recur.shape[1]
    start = (jnp.zeros((2 * rows, lanes), F32), jnp.ones((2 * rows, lanes), F32))
    last = lax.fori_loop(0, seg, scan, (start,) * tiles, unroll=4)
    last_h = join_tiles([part[0] for part in last], width)
    last_a = join_tiles([part[1] for part in last], width)
    summary[0:rows, :] = last_a[rows:] * last_a[:rows]
    summary[rows : 2 * rows, :] = last_a[rows:] * last_h[:rows] + last_h[rows:]
    exchange(count, me, summary, slots, send_sem, recv_sem)
    carry = jnp.zeros((rows, width), F32)
    for z in range(count - 1):
        carry = jnp.where(z < me, slots[z, 0:rows, :] * carry + slots[z, rows : 2 * rows, :], carry)
    cin_out[0:rows, :] = carry
    cin_out[rows : 2 * rows, :] = last_a[:rows] * carry + last_h[:rows]

    def finish(s, none):
        at = pl.ds(pl.multiple_of(s * seg, seg), seg)
        states = get_tiles(h_ref, at, width) + get_tiles(a_ref, at, width) * cin_out[pl.ds(s, 1), :]
        states_out[at, :] = states
        act, _ = gelu_parts(gate[at, :])
        mixed_out[at, :] = (act * states.astype(BF16).astype(F32)).astype(BF16)
        return none

    lax.fori_loop(0, 2 * rows, finish, 0)


def mixer_backward_kernel(
    count, seg, grad_mixed, gate, states, decay, conv_low_ref, recur, halo, cin, mask, wg0, wg1, wg0t, wg1t, vec_ref,
    grad_gate_out, grad_recur_out, gw0_out, gw1_out, small_out,
    tot, prod, gc, ext, halo_send, halo_recv, summary, slots, uin, send_sem, recv_sem, halo_sems,
):
    me = greet(count)
    rows = 8
    width = recur.shape[1]
    vec = vec_ref[...]

    def local(s, none):
        at = pl.ds(pl.multiple_of(s * seg, seg), seg)
        act, slope = gelu_parts(gate[at, :])
        gm = grad_mixed[at, :].astype(F32)
        grad_gate_out[at, :] = (gm * states[at, :].astype(BF16).astype(F32) * slope).astype(BF16)
        put_tiles(tot, at, (gm * act).astype(BF16).astype(F32))
        return none

    lax.fori_loop(0, 2 * rows, local, 0)

    tiles, lanes = tot.shape[0], tot.shape[2]

    def scan(k, carried):
        at = pl.ds(seg - 1 - k, 2 * rows, stride=seg)
        after = []
        for j in range(tiles):
            u, p = carried[j]
            d = decay[j, at, :]
            total = tot[j, at, :] + u
            tot[j, at, :] = total
            prod[j, at, :] = p
            after.append((d * total, d * p))
        return tuple(after)

    start = (jnp.zeros((2 * rows, lanes), F32), jnp.ones((2 * rows, lanes), F32))
    last = lax.fori_loop(0, seg, scan, (start,) * tiles, unroll=4)
    u = join_tiles([part[0] for part in last], width)
    p = join_tiles([part[1] for part in last], width)
    summary[0:rows, :] = p[:rows] * p[rows:]
    summary[rows : 2 * rows, :] = p[:rows] * u[rows:] + u[:rows]
    exchange(count, me, summary, slots, send_sem, recv_sem)
    carry = jnp.zeros((rows, width), F32)
    for z in range(count - 1, 0, -1):
        carry = jnp.where(z > me, slots[z, 0:rows, :] * carry + slots[z, rows : 2 * rows, :], carry)
    uin[rows : 2 * rows, :] = carry
    uin[0:rows, :] = p[rows:] * carry + u[rows:]
    gw0_out[...] = jnp.zeros_like(gw0_out)
    gw1_out[...] = jnp.zeros_like(gw1_out)
    small_out[...] = jnp.zeros_like(small_out)

    def gates(s, none):
        at = pl.ds(pl.multiple_of(s * seg, seg), seg)
        total = get_tiles(tot, at, width) + get_tiles(prod, at, width) * uin[pl.ds(s, 1), :]
        ext[HALO - 1 : HALO, :] = cin[pl.ds(s, 1), :]
        ext[HALO : HALO + seg, :] = states[at, :]
        before = ext[HALO - 1 : HALO - 1 + seg, :]
        conv_low = conv_low_ref[at, :]
        conv_vals = conv_low.astype(F32)
        m = mask[at, :]
        keep = m[:, 0:1]
        recur_gate, input_gate, log_decay = gate_values(conv_low, wg0[...], wg1[...], vec)
        root = jnp.sqrt(one_minus_exp(-2.0 * log_decay))
        scale = (1.0 - keep) + keep * root
        driven_in = total * conv_vals
        grad_log = total * before * get_tiles(decay, at, width) - driven_in * input_gate * keep * (jnp.exp(2.0 * log_decay) / root)
        grad0 = grad_log * log_decay * (1.0 - recur_gate)
        grad1 = driven_in * scale * input_gate * (1.0 - input_gate)
        low0 = grad0.astype(BF16)
        low1 = grad1.astype(BF16)
        grad_conv = (
            total * scale * input_gate
            + jnp.dot(low0, wg0t[...], preferred_element_type=F32)
            + jnp.dot(low1, wg1t[...], preferred_element_type=F32)
        )
        gc[at, :] = grad_conv
        turned = (((0,), (0,)), ((), ()))
        gw0_out[...] += lax.dot_general(conv_low, low0, turned, preferred_element_type=F32)
        gw1_out[...] += lax.dot_general(conv_low, low1, turned, preferred_element_type=F32)
        x = recur[at, :].astype(F32)
        ext[0:HALO, :] = halo[pl.ds(pl.multiple_of(s * HALO, HALO), HALO), :]
        ext[HALO : HALO + seg, :] = x

        def add(row, values):
            small_out[row : row + 1, :] += jnp.sum(values, axis=0, keepdims=True)

        add(0, grad_conv * x)
        for k in range(1, 4):
            add(k, grad_conv * ext[HALO - k : HALO - k + seg, :] * m[:, k - 1 : k])
        add(4, grad_conv)
        add(5, grad0)
        add(6, grad1)
        add(7, grad_log * recur_gate)
        return none

    lax.fori_loop(0, 2 * rows, gates, 0)
    small_out[7:8, :] = small_out[7:8, :] * vec[8:9]
    for r in range(rows):
        halo_send[r * HALO : (r + 1) * HALO, :] = gc[r * seg : r * seg + HALO, :]
    halo_copy = pltpu.make_async_remote_copy(
        src_ref=halo_send,
        dst_ref=halo_recv,
        send_sem=halo_sems.at[0],
        recv_sem=halo_sems.at[1],
        device_id={"t": lax.rem(me + count - 1, count)},
        device_id_type=MESH,
    )
    halo_copy.start()
    halo_copy.wait()

    def back(s, none):
        at = pl.ds(pl.multiple_of(s * seg, seg), seg)
        m = mask[at, :]
        ext[0:seg, :] = gc[at, :]
        result = vec[0:1] * gc[at, :]

        @pl.when(s < rows)
        def _():
            ext[seg : seg + HALO, :] = gc[pl.ds(pl.multiple_of((s + rows) * seg, seg), HALO), :]

        @pl.when(s >= rows)
        def _():
            ext[seg : seg + HALO, :] = halo_recv[pl.ds(pl.multiple_of((s - rows) * HALO, HALO), HALO), :]

        for k in range(1, 4):
            result = result + vec[k : k + 1] * ext[k : k + seg, :] * m[:, 2 + k : 3 + k]
        grad_recur_out[at, :] = result.astype(BF16)
        return none

    lax.fori_loop(0, 2 * rows, back, 0)


def whole(count):
    return [pl.BlockSpec(memory_space=pltpu.VMEM)] * count


def mixer_params(number):
    return pltpu.CompilerParams(collective_id=number, has_side_effects=True, vmem_limit_bytes=60 * 1024 * 1024)


def mixer_forward(count, seg, recur, gate, mask, wg0, wg1, vec):
    n, width = recur.shape
    full = functools.partial(jax.ShapeDtypeStruct, (n, width))
    tiles = -(-width // LANES)
    tiled = jax.ShapeDtypeStruct((tiles, n, LANES), F32)
    return pl.pallas_call(
        functools.partial(mixer_forward_kernel, count, seg),
        name="mixer_forward",
        out_shape=(
            full(BF16), tiled, full(F32), full(BF16),
            jax.ShapeDtypeStruct((16 * HALO, width), F32), jax.ShapeDtypeStruct((16, width), F32),
        ),
        in_specs=whole(6),
        out_specs=tuple(whole(6)),
        scratch_shapes=[
            pltpu.VMEM((tiles, n, LANES), F32),
            pltpu.VMEM((tiles, n, LANES), F32),
            pltpu.VMEM((tiles, n, LANES), F32),
            pltpu.VMEM((seg + HALO, width), F32),
            pltpu.VMEM((8 * HALO, width), F32),
            pltpu.VMEM((8 * HALO, width), F32),
            pltpu.VMEM((16, width), F32),
            pltpu.VMEM((count, 16, width), F32),
            pltpu.SemaphoreType.DMA((count,)),
            pltpu.SemaphoreType.DMA((count,)),
            pltpu.SemaphoreType.DMA((2,)),
        ],
        compiler_params=mixer_params(1),
    )(recur, gate, mask, wg0, wg1, vec)


def mixer_backward(count, seg, grad_mixed, gate, states, decay, conv_low, recur, halo, cin, mask, wg0, wg1, wg0t, wg1t, vec):
    n, width = recur.shape
    full = functools.partial(jax.ShapeDtypeStruct, (n, width))
    tiles = -(-width // LANES)
    tiled = jax.ShapeDtypeStruct((tiles, n, LANES), F32)
    return pl.pallas_call(
        functools.partial(mixer_backward_kernel, count, seg),
        name="mixer_backward",
        out_shape=(
            full(BF16), full(BF16),
            jax.ShapeDtypeStruct((width, width), F32), jax.ShapeDtypeStruct((width, width), F32),
            jax.ShapeDtypeStruct((8, width), F32),
        ),
        in_specs=whole(14),
        out_specs=tuple(whole(5)),
        scratch_shapes=[
            pltpu.VMEM((tiles, n, LANES), F32),
            pltpu.VMEM((tiles, n, LANES), F32),
            pltpu.VMEM((n, width), F32),
            pltpu.VMEM((seg + HALO, width), F32),
            pltpu.VMEM((8 * HALO, width), F32),
            pltpu.VMEM((8 * HALO, width), F32),
            pltpu.VMEM((16, width), F32),
            pltpu.VMEM((count, 16, width), F32),
            pltpu.VMEM((16, width), F32),
            pltpu.SemaphoreType.DMA((count,)),
            pltpu.SemaphoreType.DMA((count,)),
            pltpu.SemaphoreType.DMA((2,)),
        ],
        compiler_params=mixer_params(2),
    )(grad_mixed, gate, states, decay, conv_low, recur, halo, cin, mask, wg0, wg1, wg0t, wg1t, vec)


def gather_tokens(block):
    return lax.all_gather(block, PLANE, axis=0, tiled=True)


def scatter_tokens(partial):
    return lax.psum_scatter(partial, PLANE, scatter_dimension=0, tiled=True)


def rms(values):
    return lax.rsqrt(jnp.mean(values * values, axis=-1, keepdims=True) + EPS)


def rms_back(values, scale, gain, grad):
    weighted = grad * gain
    inner = jnp.mean(values * weighted, axis=-1, keepdims=True)
    return scale * weighted - values * (scale * scale * scale * inner), jnp.sum(grad * values * scale, axis=0)


def nt(left, right, out):
    return lax.dot_general(left, right, (((1,), (1,)), ((), ())), preferred_element_type=F32).astype(out)


def tn(left, right, out):
    return lax.dot_general(left, right, (((0,), (0,)), ((), ())), preferred_element_type=F32).astype(out)


def nn(left, right, out):
    return jnp.dot(left, right, preferred_element_type=F32).astype(out)


def per_device(
    inputs, segment_ids, mix_gain, in_weight, conv_weight, conv_bias, gate_weight, gate_bias, decay_param, out_weight,
    mlp_gain, mlp_in, down_weight, cotangent,
):
    planes = lax.axis_size("t")
    rows_here, seg, width = inputs.shape
    row_groups = lax.axis_size("g") * lax.axis_size("c")
    own_tokens = rows_here * seg
    recur_width = conv_weight.shape[1]
    block_width = gate_weight.shape[0]
    members = 2 * row_groups
    channels = recur_width // members
    t, i = lax.axis_index("t"), lax.axis_index("i")
    r = lax.axis_index("g") * lax.axis_size("c") + lax.axis_index("c")
    member = 2 * r + i
    first = member * channels

    def member_columns(weight):
        if planes == row_groups:
            part = weight.shape[0] // row_groups
            quarter = lax.dynamic_slice_in_dim(weight, r * part, part, 0)
            quarters = lax.all_gather(quarter, "t", axis=0, tiled=False)
            return lax.all_to_all(quarters, ("g", "c"), 0, 0, tiled=True).reshape(weight.shape)
        every = lax.all_gather(weight, ("t", "i"), axis=1, tiled=True)
        return lax.dynamic_slice_in_dim(every, first, channels, 1)

    in_gate = in_weight[:, 0]
    in_recur = in_weight[:, 1]
    mixer_w = member_columns(jnp.concatenate([in_gate, in_recur, out_weight], axis=0))
    w_gate, w_recur, w_out = mixer_w[:width], mixer_w[width : 2 * width], mixer_w[2 * width :]
    hidden_part = mlp_in.shape[2] // row_groups

    def own_part(weight):
        return lax.dynamic_slice_in_dim(weight.T, r * hidden_part, hidden_part, 0)

    mlp_w = jnp.concatenate([own_part(mlp_in[:, 0]), own_part(mlp_in[:, 1]), own_part(down_weight)], axis=0)
    mlp_w = lax.all_gather(mlp_w, "t", axis=0, tiled=False)
    mlp_w = mlp_w.reshape(planes, 3, hidden_part, width)
    w_left = mlp_w[:, 0].reshape(-1, width)
    w_right = mlp_w[:, 1].reshape(-1, width)
    w_down = mlp_w[:, 2].reshape(-1, width)

    ids = lax.all_gather((segment_ids + 1).astype(F32), ("g", "c"), axis=0, tiled=True)
    ids = lax.all_gather(ids, ("t", "i"), axis=1, tiled=True)
    span = 2 * seg
    ids = jnp.pad(ids, ((0, 0), (HALO, HALO)))
    ids = lax.dynamic_slice_in_dim(ids, t * span, span + 2 * HALO, 1)
    here = ids[:, HALO : HALO + span]
    columns = [(ids[:, HALO - k : HALO - k + span] == here) for k in (1, 2, 3)]
    columns += [(ids[:, HALO + k : HALO + k + span] == here) for k in (1, 2, 3)]
    columns += [jnp.zeros_like(columns[0])] * 2
    mask = jnp.stack(columns, axis=-1).astype(F32)
    mask = mask.reshape(mask.shape[0], 2, seg, 8).transpose(1, 0, 2, 3).reshape(-1, 8)

    def own(values):
        return lax.dynamic_slice_in_dim(values, first, channels, values.ndim - 1)

    decay_own = own(decay_param)
    vec = jnp.concatenate(
        [
            own(conv_weight),
            own(conv_bias)[None],
            own(gate_bias),
            8.0 * jax.nn.softplus(-decay_own)[None],
            8.0 * jax.nn.sigmoid(-decay_own)[None],
            jnp.zeros((7, channels), F32),
        ]
    )
    blocks = channels // block_width
    gate_own = own(gate_weight).reshape(block_width, 2, blocks, block_width)
    spread = jnp.zeros((2, blocks, block_width, blocks, block_width), BF16)
    for n in range(blocks):
        spread = spread.at[:, n, :, n, :].set(gate_own[:, :, n, :].transpose(1, 0, 2))
    spread = spread.reshape(2, channels, channels)
    wg0, wg1 = spread[0], spread[1]

    flat_in = inputs.reshape(own_tokens, width).astype(F32)
    scale_in = rms(flat_in)
    normed = gather_tokens((flat_in * scale_in * mix_gain).astype(BF16))
    cot_own = cotangent.reshape(own_tokens, width)
    cot = gather_tokens(cot_own)
    gate_branch = nn(normed, w_gate, F32)
    recur = nn(normed, w_recur, BF16)
    conv_low, decay, states, mixed, halo, cin = mixer_forward(planes, seg, recur, gate_branch, mask, wg0, wg1, vec)
    middle = flat_in + scatter_tokens(nt(mixed, w_out, BF16)).astype(F32)
    scale_mid = rms(middle)
    normed_two = gather_tokens((middle * scale_mid * mlp_gain).astype(BF16))
    left = nt(normed_two, w_left, F32)
    right = nt(normed_two, w_right, F32)
    act, slope = gelu_parts(left)
    hidden = (act * right).astype(BF16)
    down = scatter_tokens(nn(hidden, w_down, BF16))
    outputs = (middle + down.astype(F32)).astype(BF16).reshape(inputs.shape)

    grad_hidden = nt(cot, w_down, F32)
    grad_left = (grad_hidden * right * slope).astype(BF16)
    grad_right = (grad_hidden * act).astype(BF16)
    partial = lax.dot(grad_left, w_left, preferred_element_type=F32) + lax.dot(
        grad_right, w_right, preferred_element_type=F32
    )
    grad_normed_two = scatter_tokens(partial.astype(BF16)).astype(F32)
    grad_mid_norm, grad_mlp_gain = rms_back(middle, scale_mid, mlp_gain, grad_normed_two)
    grad_middle = cot_own.astype(F32) + grad_mid_norm
    grad_mid = gather_tokens(grad_middle.astype(BF16))
    grad_mixed = nn(grad_mid, w_out, F32)
    grad_gate, grad_recur, gw0, gw1, small = mixer_backward(
        planes, seg, grad_mixed, gate_branch, states, decay, conv_low, recur, halo, cin, mask, wg0, wg1, wg0.T, wg1.T, vec
    )
    partial = lax.dot_general(grad_gate, w_gate, (((1,), (1,)), ((), ())), preferred_element_type=F32) + lax.dot_general(
        grad_recur, w_recur, (((1,), (1,)), ((), ())), preferred_element_type=F32
    )
    grad_normed = scatter_tokens(partial.astype(BF16)).astype(F32)
    grad_in_norm, grad_mix_gain = rms_back(flat_in, scale_in, mix_gain, grad_normed)
    grad_inputs = (grad_middle + grad_in_norm).reshape(inputs.shape)

    def to_owners(grad):
        reduced = lax.psum_scatter(grad, "t", scatter_dimension=0, tiled=True)
        return lax.all_to_all(reduced.reshape(members, -1, grad.shape[1]), PLANE, 0, 0, tiled=True)

    own_rows = width // (planes * members)
    mlp_grads = to_owners(
        jnp.concatenate([tn(normed_two, grad_left, BF16), tn(normed_two, grad_right, BF16), tn(cot, hidden, BF16)], axis=1)
    )
    mixer_grads = to_owners(
        jnp.concatenate([tn(normed, grad_gate, BF16), tn(normed, grad_recur, BF16), tn(grad_mid, mixed, BF16)], axis=1)
    )
    mlp_grads = mlp_grads.reshape(2, row_groups, own_rows, 3, planes, hidden_part).astype(F32)
    mlp_grads = mlp_grads.transpose(2, 3, 4, 0, 1, 5).reshape(own_rows, 3, -1)
    mixer_grads = mixer_grads.reshape(2, row_groups, own_rows, 3, channels).astype(F32)
    mixer_grads = mixer_grads.transpose(2, 3, 1, 0, 4).reshape(own_rows, 3, -1)

    column_block = lax.broadcasted_iota(jnp.int32, (block_width, channels), 1) // block_width

    def diagonal(gw):
        return sum(
            jnp.where(column_block == n, gw[n * block_width : (n + 1) * block_width], 0.0) for n in range(blocks)
        )

    gate_grads = jnp.concatenate([diagonal(gw0), diagonal(gw1), small], axis=0)
    if planes == row_groups:
        pieces = gate_grads.reshape(gate_grads.shape[0], row_groups, -1).transpose(1, 0, 2)
        pieces = lax.all_to_all(pieces, ("g", "c"), 0, 0, tiled=True)
        gate_grads = lax.psum_scatter(pieces, "t", scatter_dimension=0, tiled=False)
    else:
        placed = jnp.zeros((gate_grads.shape[0], recur_width), F32)
        placed = lax.dynamic_update_slice_in_dim(placed, gate_grads, first, 1)
        gate_grads = lax.psum_scatter(placed, EVERY, scatter_dimension=1, tiled=True)
    grad_gate_weight = jnp.stack([gate_grads[:block_width], gate_grads[block_width : 2 * block_width]], axis=1)
    small = gate_grads[2 * block_width :]
    return (
        outputs,
        grad_inputs,
        lax.psum_scatter(grad_mix_gain, EVERY, scatter_dimension=0, tiled=True),
        mixer_grads[:, :2],
        small[0:4],
        small[4],
        grad_gate_weight,
        small[5:7],
        small[7],
        mixer_grads[:, 2],
        lax.psum_scatter(grad_mlp_gain, EVERY, scatter_dimension=0, tiled=True),
        mlp_grads[:, :2],
        mlp_grads[:, 2],
    )


def solution(mesh):
    seq, rows = mesh.shape["seq"], mesh.shape["rows"]
    grid = Mesh(mesh.devices.reshape(seq // 2, 2, rows // 2, 2), EVERY)
    row_axes, seq_axes = ("g", "c"), ("t", "i")
    tokens = P(row_axes, seq_axes, None)
    return jax.shard_map(
        per_device,
        mesh=grid,
        in_specs=(
            tokens,
            P(row_axes, seq_axes),
            P(),
            P(None, None, seq_axes),
            P(),
            P(),
            P(),
            P(),
            P(),
            P(None, seq_axes),
            P(),
            P(None, None, seq_axes),
            P(None, seq_axes),
            tokens,
        ),
        out_specs=(
            tokens,
            tokens,
            P(EVERY),
            P(EVERY, None, None),
            P(None, EVERY),
            P(EVERY),
            P(None, None, EVERY),
            P(None, EVERY),
            P(EVERY),
            P(EVERY, None),
            P(EVERY),
            P(EVERY, None, None),
            P(EVERY, None),
        ),
        check_vma=False,
    )
```

time: 5460 us -> 1250 us (0.23)
  local copies, waits for them, and re-layouts: 2230 us -> 140 us
  waiting for transfers between devices: 2240 us -> 620 us
  other arithmetic: 356 us -> 34.7 us
  matrix products: 309 us -> 176 us
  Pallas kernels: 0 us -> 97.2 us
  blocking collectives: 213 us -> 149 us
    reduce_scatter x1 -> x7, waiting for transfers between devices: 1690 us -> 246 us  [the longest x4 188 us: scatter_tokens(): return lax.psum_scatter(partial, PLANE, scatter_dimension=0, tiled=True)]
    slice x251 -> x12, local copies, waits for them, and re-layouts: 1260 us -> 29.2 us  [the longest x1 12.6 us: per_device(): mlp_in[:, 0]]
    pad x108 -> x0, local copies, waits for them, and re-layouts: 588 us -> none  [scan_pairs(): return lax.associative_scan(pair_combine, (decays, driven), axis=scan_axis)]
    all_to_all x2 -> x0, blocking collectives: 171 us -> none  [per_device(): lax.all_to_all(driven[m], 'seq', split_axis=1, concat_axis=0, tiled=True)]
    concatenate x55 -> x5, other arithmetic: 179 us -> 12.5 us  [the longest x1 4.51 us: per_device(): jnp.concatenate([tn(normed_two, grad_left, BF16), tn(normed_two, grad_rig...]
    all_gather x4 -> x6, waiting for transfers between devices: 491 us -> 343 us  [the longest x1 163 us: per_device(): mlp_w = lax.all_gather(mlp_w, 't', axis=0, tiled=False)]
    dot_general x15 -> x18, matrix products: 309 us -> 176 us  [the longest x4 47.5 us: nt(): lax.dot_general(left, right, (((1,), (1,)), ((), ())), preferred_element_...]
    reshape x8 -> x9, local copies, waits for them, and re-layouts: 166 us -> 45 us  [the longest x3 25.5 us: per_device(): mlp_grads = mlp_grads.transpose(2, 3, 4, 0, 1, 5).reshape(own_rows, 3, -1)]
  transfers between devices with their start and end apart: 22 -> 17, of which waited for: 6 -> 13; matrix products, arithmetic and copies ran while one was open for 42% -> 21% of each run, Pallas kernels for 0% -> 5%
where the time goes in v1:
time: 1250 us
  waiting for transfers between devices  620 us (50%)
  matrix products  176 us (14%)
  blocking collectives  149 us (12%)
  local copies, waits for them, and re-layouts  140 us (11%)
  Pallas kernels  97.2 us (8%)
  other arithmetic  34.7 us (3%)
  starting transfers between devices  17.5 us (1%)
  between operations  14.8 us (1%)
    reduce_scatter x4, waiting for transfers between devices, scatter_tokens(): return lax.psum_scatter(partial, PLANE, scatter_dimension=0, tiled=True)  188 us
    all_gather x1, waiting for transfers between devices, per_device(): mlp_w = lax.all_gather(mlp_w, 't', axis=0, tiled=False)  163 us
    all_gather x4, waiting for transfers between devices, gather_tokens(): return lax.all_gather(block, PLANE, axis=0, tiled=True)  106 us
    all_gather x1, blocking collectives, per_device(): lax.all_gather((segment_ids + 1).astype(F32), ('g', 'c'), axis=0, tiled=T...  78.9 us
    all_gather x1, waiting for transfers between devices, member_columns(): quarters = lax.all_gather(quarter, 't', axis=0, tiled=False)  74 us
    pallas_call x1, Pallas kernels, mixer_backward(): pl.pallas_call(functools.partial(mixer_backward_kernel, count, seg), name...  59.7 us
    dot_general x4, matrix products, nt(): lax.dot_general(left, right, (((1,), (1,)), ((), ())), preferred_element_...  47.5 us
    dot_general x6, matrix products, tn(): lax.dot_general(left, right, (((0,), (0,)), ((), ())), preferred_element_...  44.1 us
  transfers between devices with their start and end apart: 17, of which 13 were waited for; matrix products, arithmetic and copies ran while one was open for 21% of the time, Pallas kernels for 5%

profile of v1, /device:TPU:0, one launch (start us, length us, event | category | flops | bytes accessed | tf_op | source)
XLA Modules:
  0.0 1249.5 jit_solution(2694998953006205498)
XLA Ops:
  18.9 74.0 %all-gather.18.cloned.1.call-done = bf16[6144,320]{0,1:T(8,128)(2,1)} async-done(((bf16[1536,320]{0,1:T(8,128)(2,1)}), bf16[6144,320]{0,1:T(8,128)(2,1)}) %all-gather.18.cloned.1.call-update) | async-done | bytes 3932176 | tf_op jit(solution)/shard_map/all_gather | solution.py:439
  102.4 78.9 %all-gather.2 = f32[4,2,128]{2,1,0:T(2,128)S(1)} all-gather(f32[1,2,128]{2,1,0:T(2,128)S(1)} %convert_bitcast_fusion.1), channel_id=1, replica_groups=mesh['t'=4,'i'=2,'g'=2,'c'=2] {'g','c'}, dimensions={0}, use_global_device_ids=true | all-gather | bytes 5120 | tf_op jit(solution)/shard_map/all_gather | solution.py:460
  181.2 30.6 %all_gather.34 = f32[8,1024]{1,0:T(8,128)S(1)} all-gather(f32[8,128]{1,0:T(8,128)S(1)} %bitcast.194), channel_id=1, replica_groups=mesh['t'=4,'i'=2,'g'=2,'c'=2] {'t','i'}, dimensions={1}, use_global_device_ids=true | all-gather | bytes 36864 | tf_op jit(solution)/shard_map/all_gather | solution.py:461
  252.7 37.6 %mixer_forward.1 = (bf16[2048,320]{1,0:T(8,128)(2,1)}, f32[3,2048,128]{2,1,0:T(8,128)}, f32[2048,320]{1,0:T(8,128)}, bf16[2048,320]{1,0:T(8,128)(2,1)}, f32[128,320]{1,0:T(8,128)}, /*index=5*/f32[16,320]{1,0:T(8,128)}) custom-call(bf16[2048,320]{1,0:T(8,128)(2,1)} %convolution_convert_fusion.5.recur, f32[2048,320]{1,0:T(8,128)} %fusion.27.gate, ...), custom_call_target="tpu_custom_call" | custom-call | tf_op jit(solution)/shard_map/mixer_forward/pallas_call | solution.py:329
  299.9 12.6 %fusion.59 = (bf16[2048,1,768]{2,1,0:T(2,128)(2,1)S(1)}, bf16[2048,1,768]{2,1,0:T(2,128)(2,1)S(1)}) fusion(bf16[2048,2,768]{2,1,0:T(2,128)(2,1)} %param.29), kind=kLoop, calls=%fused_computation.134 | loop fusion | bytes 12582912 | tf_op jit(solution)/shard_map/slice | solution.py:453
  338.4 32.5 %reduce-scatter.8.cloned.1.call-done = bf16[256,2048]{1,0:T(8,128)(2,1)} async-done(((bf16[2048,2048]{1,0:T(8,128)(2,1)}), bf16[256,2048]{1,0:T(8,128)(2,1)}) %reduce-scatter.8.cloned.1.call-update) | async-done | bytes 1048592 | tf_op jit(solution)/shard_map/reduce_scatter | solution.py:393
  375.8 163.4 %all-gather.20.cloned.1.call-done = bf16[2304,2048]{1,0:T(8,128)(2,1)} async-done(((bf16[576,2048]{1,0:T(8,128)(2,1)}), bf16[2304,2048]{1,0:T(8,128)(2,1)}) %all-gather.20.cloned.1.call-update) | async-done | bytes 9437200 | tf_op jit(solution)/shard_map/all_gather | solution.py:454
  546.3 48.0 %all-gather.12.cloned.1.call-done = bf16[2048,2048]{1,0:T(8,128)(2,1)} async-done(((bf16[256,2048]{1,0:T(8,128)(2,1)}), bf16[2048,2048]{1,0:T(8,128)(2,1)}) %all-gather.12.cloned.1.call-update) | async-done | bytes 8388624 | tf_op jit(solution)/shard_map/all_gather | solution.py:389
  594.2 11.9 fusion.63
  614.7 35.8 %all-gather.14.cloned.1.call-done = bf16[2048,2048]{1,0:T(8,128)(2,1)} async-done(((bf16[256,2048]{1,0:T(8,128)(2,1)}), bf16[2048,2048]{1,0:T(8,128)(2,1)}) %all-gather.14.cloned.1.call-update) | async-done | bytes 8388624 | tf_op jit(solution)/shard_map/all_gather | solution.py:389
  650.6 17.5 %fusion.2 = (bf16[2048,768]{1,0:T(8,128)(2,1)S(1)}, bf16[2048,768]{1,0:T(8,128)(2,1)S(1)}, bf16[2048,768]{1,0:T(8,128)(2,1)}) fusion(f32[2048,768]{1,0:T(8,128)} %fusion.62, f32[2048,768]{1,0:T(8,128)} %fusion.63, bf16[768,2048]{1,0:T(8,128)(2,1)} %bitcast.179, bf16[2048,2048]{1,0:T(8,128)(2,1)} %all-gather.14.cloned.1.call-done), kind=kOutput, calls=%fused_computation.9 | convolution fusion | flops 6480199680 | bytes 33554432 | tf_op jit(solution)/shard_map/dot_general | solution.py:407
  677.9 12.5 add_convert_fusion.1
  690.4 71.4 %reduce-scatter.12.cloned.1.call-done = bf16[256,2048]{1,0:T(8,128)(2,1)} async-done(((bf16[2048,2048]{1,0:T(8,128)(2,1)}), bf16[256,2048]{1,0:T(8,128)(2,1)}) %reduce-scatter.12.cloned.1.call-update) | async-done | bytes 1048592 | tf_op jit(solution)/shard_map/reduce_scatter | solution.py:393
  765.9 10.5 fusion.4
  798.1 22.3 %all-gather.16.cloned.1.call-done = bf16[2048,2048]{1,0:T(8,128)(2,1)} async-done(((bf16[256,2048]{1,0:T(8,128)(2,1)}), bf16[2048,2048]{1,0:T(8,128)(2,1)}) %all-gather.16.cloned.1.call-update) | async-done | bytes 8388624 | tf_op jit(solution)/shard_map/all_gather | solution.py:389
  830.4 59.7 %mixer_backward.1 = (bf16[2048,320]{1,0:T(8,128)(2,1)}, bf16[2048,320]{1,0:T(8,128)(2,1)}, f32[320,320]{1,0:T(8,128)}, f32[320,320]{1,0:T(8,128)}, f32[8,320]{1,0:T(8,128)}) custom-call(f32[2048,320]{1,0:T(8,128)} %fusion.22.grad_mixed, f32[2048,320]{1,0:T(8,128)} %fusion.27.gate, f32[2048,320]{1,0:T(8,128)} %get-tuple-element.49.states, ...), custom_call_target="tpu_custom_call" | custom-call | tf_op jit(solution)/shard_map/mixer_backward/pallas_call | solution.py:360
  926.2 14.6 %add_convert_fusion = bf16[2048,2048]{1,0:T(8,128)(2,1)} fusion(f32[2048,2048]{1,0:T(8,128)} %fusion.25, bf16[2048,320]{1,0:T(8,128)(2,1)} %get-tuple-element.55, bf16[6144,320]{0,1:T(8,128)(2,1)} %bitcast.172), kind=kOutput, calls=%fused_computation | convolution fusion | flops 2692743168 | bytes 28049408 | tf_op jit(solution)/shard_map/dot_general | solution.py:526
  940.9 11.3 convolution_convert_fusion
  952.2 35.6 %reduce-scatter.20.cloned.1.call-done = bf16[512,2304]{0,1:T(8,128)(2,1)} async-done(((bf16[2048,2304]{0,1:T(8,128)(2,1)}), bf16[512,2304]{0,1:T(8,128)(2,1)}) %reduce-scatter.20.cloned.1.call-update) | async-done | bytes 2359312 | tf_op jit(solution)/shard_map/reduce_scatter | solution.py:534
  996.6 29.5 %all-to-all-done.3 = bf16[8,64,2304]{2,1,0:T(8,128)(2,1)} async-done(((bf16[8,64,2304]{2,1,0:T(8,128)(2,1)}), bf16[8,64,2304]{2,1,0:T(8,128)(2,1)}, u32[]{:S(2)}, u32[]{:S(2)}) %all-to-all-start.3) | async-done | bytes 2359328 | tf_op jit(solution)/shard_map/all_to_all | solution.py:535
  1069.6 18.3 %reduce-scatter.18.cloned.1.call-done = f32[1,328,80]{1,2,0:T(8,128)} async-done(((f32[4,328,80]{1,2,0:T(8,128)}), f32[1,328,80]{1,2,0:T(8,128)}) %reduce-scatter.18.cloned.1.call-update) | async-done | bytes 104976 | tf_op jit(solution)/shard_map/reduce_scatter | solution.py:560
  1110.0 51.5 %reduce-scatter.14.cloned.1.call-done = bf16[256,2048]{1,0:T(8,128)(2,1)} async-done(((bf16[2048,2048]{1,0:T(8,128)(2,1)}), bf16[256,2048]{1,0:T(8,128)(2,1)}) %reduce-scatter.14.cloned.1.call-update) | async-done | bytes 1048592 | tf_op jit(solution)/shard_map/reduce_scatter | solution.py:393
  1163.3 39.8 %all-reduce.4 = (f32[2048]{0:T(1024)S(1)}, f32[2048]{0:T(1024)S(1)}) all-reduce(f32[2048]{0:T(1024)S(1)} %get-tuple-element.139, f32[2048]{0:T(1024)S(1)} %get-tuple-element.137), channel_id=8, replica_groups=mesh['t'=4,'i'=2,'g'=2,'c'=2] {'t','i','g','c'}, use_global_device_ids=true, to_apply=%region_9.10.clone | all-reduce | flops 4096 | bytes 32768
  1204.2 32.6 %reduce-scatter.10.cloned.1.call-done = bf16[256,2048]{1,0:T(8,128)(2,1)} async-done(((bf16[2048,2048]{1,0:T(8,128)(2,1)}), bf16[256,2048]{1,0:T(8,128)(2,1)}) %reduce-scatter.10.cloned.1.call-update) | async-done | bytes 1048592 | tf_op jit(solution)/shard_map/reduce_scatter | solution.py:393
  (209 shorter events, 282.7 us)
Async XLA Ops:
  7.2 325.0 %copy-start = (bf16[2048,768]{1,0:T(8,128)(2,1)S(1)}, bf16[2048,768]{1,0:T(8,128)(2,1)}, u32[]{:S(2)}) copy-start(bf16[2048,768]{1,0:T(8,128)(2,1)} %param.30) | copy-start | bytes 9437188
  7.2 85.7 %all-gather.18.cloned.1.call-start = ((), (), s32[]{:S(2)}) async-start(), calls=%async_computation.22 | async-start | bytes 4915200 | tf_op jit(solution)/shard_map/all_gather | solution.py:439
  13.7 222.1 %all-gather.10.cloned.1.call-start = ((), (), s32[]{:S(2)}) async-start(), calls=%async_computation.11 | async-start | bytes 9437184 | tf_op jit(solution)/shard_map/all_gather | solution.py:389
  97.3 133.9 %all-to-all-start = ((bf16[4,1536,320]{1,2,0:T(8,128)(2,1)}), bf16[4,1536,320]{1,2,0:T(8,128)(2,1)}, u32[]{:S(2)}, u32[]{:S(2)}) async-start(bf16[4,1536,320]{1,2,0:T(8,128)(2,1)} %bitcast.165), calls=%async_computation | async-start | bytes 7864320 | tf_op jit(solution)/shard_map/all_to_all | solution.py:440
  102.3 268.6 %reduce-scatter.8.cloned.1.call-start = ((), (), s32[]{:S(2)}) async-start(), calls=%async_computation.12 | async-start | bytes 9437184 | tf_op jit(solution)/shard_map/reduce_scatter | solution.py:393
  299.9 239.3 %all-gather.20.cloned.1.call-start = ((), (), s32[]{:S(2)}) async-start(), calls=%async_computation.23 | async-start | bytes 11796480 | tf_op jit(solution)/shard_map/all_gather | solution.py:454
  338.3 255.9 %all-gather.12.cloned.1.call-start = ((), (), s32[]{:S(2)}) async-start(), calls=%async_computation.13 | async-start | bytes 9437184 | tf_op jit(solution)/shard_map/all_gather | solution.py:389
  375.1 275.4 %all-gather.14.cloned.1.call-start = ((), (), s32[]{:S(2)}) async-start(), calls=%async_computation.15 | async-start | bytes 9437184 | tf_op jit(solution)/shard_map/all_gather | solution.py:389
  375.7 386.1 %reduce-scatter.12.cloned.1.call-start = ((), (), s32[]{:S(2)}) async-start(), calls=%async_computation.16 | async-start | bytes 9437184 | tf_op jit(solution)/shard_map/reduce_scatter | solution.py:393
  690.3 71.5 %copy-start.3 = (bf16[256,2048]{1,0:T(8,128)(2,1)S(1)}, bf16[256,2048]{1,0:T(8,128)(2,1)}, u32[]{:S(2)}) copy-start(bf16[256,2048]{1,0:T(8,128)(2,1)} %reduce-scatter.8.cloned.1.call-done) | copy-start | bytes 3145732
  690.4 73.5 %copy-start.5 = (bf16[2,128,2048]{2,1,0:T(8,128)(2,1)S(1)}, bf16[2,128,2048]{2,1,0:T(8,128)(2,1)}, u32[]{:S(2)}) copy-start(bf16[2,128,2048]{2,1,0:T(8,128)(2,1)} %param.31) | copy-start | bytes 3145732
  690.4 130.0 %all-gather.16.cloned.1.call-start = ((), (), s32[]{:S(2)}) async-start(), calls=%async_computation.17 | async-start | bytes 9437184 | tf_op jit(solution)/shard_map/all_gather | solution.py:389
  765.9 221.9 %reduce-scatter.20.cloned.1.call-start = ((), (), s32[]{:S(2)}) async-start(), calls=%async_computation.21 | async-start | bytes 11796480 | tf_op jit(solution)/shard_map/reduce_scatter | solution.py:534
  798.1 265.4 %reduce-scatter.16.cloned.1.call-start = ((), (), s32[]{:S(2)}) async-start(), calls=%async_computation.19 | async-start | bytes 4915200 | tf_op jit(solution)/shard_map/reduce_scatter | solution.py:534
  830.3 59.7 %copy-start.26 = (bf16[2048,320]{1,0:T(8,128)(2,1)S(1)}, bf16[2048,320]{1,0:T(8,128)(2,1)}, u32[]{:S(2)}) copy-start(bf16[2048,320]{1,0:T(8,128)(2,1)} %get-tuple-element.48) | copy-start | bytes 3932164
  912.1 13.2 %all-to-all-start.2 = ((f32[4,328,80]{1,2,0:T(8,128)}), f32[4,328,80]{1,2,0:T(8,128)S(1)}, u32[]{:S(2)}, u32[]{:S(2)}) async-start(f32[4,328,80]{1,2,0:T(8,128)} %bitcast.191), calls=%async_computation.7 | async-start | bytes 983040 | tf_op jit(solution)/shard_map/all_to_all | solution.py:559
  915.6 172.4 %reduce-scatter.18.cloned.1.call-start = ((), (), s32[]{:S(2)}) async-start(), calls=%async_computation.20 | async-start | bytes 614400 | tf_op jit(solution)/shard_map/reduce_scatter | solution.py:560
  926.1 235.3 %reduce-scatter.14.cloned.1.call-start = ((), (), s32[]{:S(2)}) async-start(), calls=%async_computation.18 | async-start | bytes 9437184 | tf_op jit(solution)/shard_map/reduce_scatter | solution.py:393
  940.8 296.0 %reduce-scatter.10.cloned.1.call-start = ((), (), s32[]{:S(2)}) async-start(), calls=%async_computation.14 | async-start | bytes 9437184 | tf_op jit(solution)/shard_map/reduce_scatter | solution.py:393
  992.0 34.1 %all-to-all-start.3 = ((bf16[8,64,2304]{2,1,0:T(8,128)(2,1)}), bf16[8,64,2304]{2,1,0:T(8,128)(2,1)}, u32[]{:S(2)}, u32[]{:S(2)}) async-start(bf16[8,64,2304]{2,1,0:T(8,128)(2,1)} %bitcast.175), calls=%async_computation.10 | async-start | bytes 4718592 | tf_op jit(solution)/shard_map/all_to_all | solution.py:535
  1065.7 28.7 %all-to-all-start.1 = ((bf16[8,64,960]{2,1,0:T(8,128)(2,1)}), bf16[8,64,960]{2,1,0:T(8,128)(2,1)S(1)}, u32[]{:S(2)}, u32[]{:S(2)}) async-start(bf16[8,64,960]{2,1,0:T(8,128)(2,1)} %bitcast.33), calls=%async_computation.6 | async-start | bytes 2097152 | tf_op jit(solution)/shard_map/all_to_all | solution.py:535
  1106.9 54.5 %copy-start.17 = (f32[2048]{0:T(1024)S(1)}, f32[2048]{0:T(1024)}, u32[]{:S(2)}) copy-start(f32[2048]{0:T(1024)} %param.20) | copy-start | bytes 24580
  1106.9 54.5 %copy-start.19 = (f32[256]{0:T(256)S(1)}, f32[256]{0:T(256)}, u32[]{:S(2)}) copy-start(f32[256]{0:T(256)} %copy-done.18) | copy-start | bytes 3076
  1107.0 97.2 %copy-start.22 = (f32[2,128]{1,0:T(2,128)S(1)}, f32[2,128]{1,0:T(2,128)}, u32[]{:S(2)}) copy-start(f32[2,128]{1,0:T(2,128)} %copy-done.21) | copy-start | bytes 3076
  (29 other events, 310.5 us)
Sparse Core Ops, SparseCore 0:
  13.8 79.0 all-gather.17
  95.4 86.0 all-gather.9
  300.0 70.8 reduce-scatter.7
  372.4 166.7 all-gather.19
  541.6 52.5 all-gather.11
  596.1 54.3 all-gather.13
  690.5 71.2 reduce-scatter.11
  766.0 54.3 all-gather.15
  822.7 164.9 reduce-scatter.19
  989.9 73.4 reduce-scatter.15
  1066.3 21.6 reduce-scatter.17
  1091.7 69.6 reduce-scatter.13
  1164.9 71.8 reduce-scatter.9

commit v2 on v1

--- a/solution.py
+++ b/solution.py
@@ -385,12 +385,430 @@
     )(grad_mixed, gate, states, decay, conv_low, recur, halo, cin, mask, wg0, wg1, wg0t, wg1t, vec)
 
 
-def gather_tokens(block):
-    return lax.all_gather(block, PLANE, axis=0, tiled=True)
-
-
-def scatter_tokens(partial):
-    return lax.psum_scatter(partial, PLANE, scatter_dimension=0, tiled=True)
+class Place:
+    def __init__(self):
+        self.i, self.g, self.c = lax.axis_index("i"), lax.axis_index("g"), lax.axis_index("c")
+        self.core, self.across, self.along = {"c": 1 - self.c}, {"g": 1 - self.g}, {"i": 1 - self.i}
+
+    def chunk(self, di, dg, dc):
+        i = 1 - self.i if di else self.i
+        g = 1 - self.g if dg else self.g
+        c = 1 - self.c if dc else self.c
+        return (i * 2 + g) * 2 + c
+
+    def greet(self):
+        barrier = pltpu.get_barrier_semaphore()
+        for peer in (self.core, self.across, self.along):
+            pl.semaphore_signal(barrier, inc=1, device_id=peer, device_id_type=MESH)
+        pl.semaphore_wait(barrier, 3)
+
+
+class Gather:
+    COPIES = 11
+
+    def __init__(self, place, block, out, send, recv):
+        self.place, self.block, self.out, self.send, self.recv = place, block, out, send, recv
+        self.tokens = block.shape[0]
+        self.half = self.tokens // 2
+
+    def rows(self, chunk, part):
+        start = chunk * self.tokens + (self.half if part == 1 else 0)
+        return self.out.at[pl.ds(pl.multiple_of(start, self.half), self.tokens if part == 2 else self.half)]
+
+    def mine(self, part):
+        if part == 2:
+            return self.block
+        return self.block.at[pl.ds(part * self.half, self.half)]
+
+    def copy(self, number, source, chunk, part, peer):
+        return pltpu.make_async_remote_copy(
+            src_ref=source,
+            dst_ref=self.rows(chunk, part),
+            send_sem=self.send.at[number],
+            recv_sem=self.recv.at[number],
+            device_id=peer,
+            device_id_type=MESH,
+        )
+
+    def begin(self, part):
+        place = self.place
+        own = place.chunk(0, 0, 0)
+        self.kept = getattr(self, "kept", [])
+        mine = self.mine(part)
+        order = ((0 + part, place.across), (2 + part, place.along))
+        for number, peer in order:
+            self.kept.append((self.copy(number, mine, own, part, peer), None))
+            self.kept[-1][0].start()
+        self.kept.append((self.copy(4 + part, mine, own, part, place.core), None))
+        self.kept[-1][0].start()
+        keep = pltpu.make_async_copy(mine, self.rows(own, part), self.send.at[self.COPIES + part])
+        keep.start()
+        self.local = getattr(self, "local", []) + [keep]
+
+    def arrived(self, number, chunk, part):
+        self.copy(number, self.rows(chunk, part), chunk, part, self.place.core).wait_recv()
+
+    def forward(self, number, chunk, part, peer):
+        moved = self.copy(number, self.rows(chunk, part), chunk, part, peer)
+        moved.start()
+        self.kept.append((moved, None))
+
+    def pass_on(self):
+        place = self.place
+        ax, al, dia = place.chunk(0, 1, 0), place.chunk(1, 0, 0), place.chunk(1, 1, 0)
+        self.arrived(0, ax, 0)
+        self.forward(6, ax, 0, place.along)
+        self.arrived(3, al, 1)
+        self.forward(7, al, 1, place.across)
+        self.arrived(1, ax, 1)
+        self.forward(8, ax, 2, place.core)
+        self.arrived(2, al, 0)
+        self.forward(9, al, 2, place.core)
+        self.arrived(6, dia, 0)
+        self.arrived(7, dia, 1)
+        self.forward(10, dia, 2, place.core)
+
+    def finish(self):
+        place = self.place
+        self.arrived(4, place.chunk(0, 0, 1), 0)
+        self.arrived(5, place.chunk(0, 0, 1), 1)
+        self.arrived(8, place.chunk(0, 1, 1), 2)
+        self.arrived(9, place.chunk(1, 0, 1), 2)
+        self.arrived(10, place.chunk(1, 1, 1), 2)
+        for moved, _ in self.kept:
+            moved.wait_send()
+        for keep in self.local:
+            keep.wait()
+
+
+GATHER_SEMS = Gather.COPIES + 2
+SLICE = 16
+
+
+def first_gather_kernel(planes, normed, cot, ids, normed_out, cot_out, ids_out, before_out, after_out, *sems):
+    place = Place()
+    place.greet()
+    me = lax.axis_index("t")
+    gathers = []
+    for number, (block, out) in enumerate(((normed, normed_out), (cot, cot_out))):
+        gather = Gather(place, block, out, sems[2 * number], sems[2 * number + 1])
+        gather.begin(0)
+        gather.begin(1)
+        gathers.append(gather)
+    for gather in gathers:
+        gather.pass_on()
+    for gather in gathers:
+        gather.finish()
+
+
+class Scatter:
+    def __init__(self, place, product, core_send, core_recv, held, acc, across_recv, along_recv, second, second_recv, send, recv):
+        self.place, self.product = place, product
+        self.core_send, self.core_recv, self.held, self.acc = core_send, core_recv, held, acc
+        self.across_recv, self.along_recv, self.second, self.second_recv = across_recv, along_recv, second, second_recv
+        self.send, self.recv = send, recv
+        self.kept = []
+
+    def copy(self, number, source, target, peer):
+        return pltpu.make_async_remote_copy(
+            src_ref=source,
+            dst_ref=target,
+            send_sem=self.send.at[number],
+            recv_sem=self.recv.at[number],
+            device_id=peer,
+            device_id_type=MESH,
+        )
+
+    def start(self, *parts):
+        moved = self.copy(*parts)
+        moved.start()
+        self.kept.append(moved)
+
+    def run(self):
+        place = self.place
+        order = ((1, 1), (0, 1), (1, 0), (0, 0))
+        tile = 256
+        per_half = self.held.shape[3] // tile
+        for di, dg in order:
+            q = 2 * di + dg
+            chunk = place.chunk(di, dg, 1)
+
+            def send_tile(n, none):
+                at = pl.ds(pl.multiple_of(n % per_half * tile, tile), tile)
+                self.core_send[q, n // per_half, :, at] = self.product(chunk, n).astype(BF16)
+                return none
+
+            lax.fori_loop(0, 2 * per_half, send_tile, 0)
+            self.start(q, self.core_send.at[q], self.core_recv.at[q], place.core)
+        for di, dg in order:
+            q = 2 * di + dg
+            chunk = place.chunk(di, dg, 0)
+            self.copy(q, self.core_send.at[q], self.core_recv.at[q], place.core).wait_recv()
+
+            def sum_tile(n, none):
+                at = pl.ds(pl.multiple_of(n % per_half * tile, tile), tile)
+                value = self.product(chunk, n) + self.core_recv[q, n // per_half, :, at].astype(F32)
+                if q:
+                    self.held[q - 1, n // per_half, :, at] = value.astype(BF16)
+                else:
+                    self.acc[n // per_half, :, at] = value
+                return none
+
+            lax.fori_loop(0, 2 * per_half, sum_tile, 0)
+            if dg:
+                self.start(4 + di, self.held.at[q - 1, 0], self.across_recv.at[di], place.across)
+            if di:
+                self.start(6 + dg, self.held.at[q - 1, 1], self.along_recv.at[dg], place.along)
+        for half, number, buffer, mine, peer, out in (
+            (0, 5, self.across_recv, 2, place.along, 8),
+            (1, 7, self.along_recv, 1, place.across, 9),
+        ):
+            self.copy(number, buffer.at[1], buffer.at[1], place.core).wait_recv()
+
+            def add_rows(n, none):
+                at = pl.ds(pl.multiple_of(n * SLICE, SLICE), SLICE)
+                total = self.held[mine - 1, half, at, :].astype(F32) + buffer[1, at, :].astype(F32)
+                self.second[half, at, :] = total.astype(BF16)
+                return none
+
+            lax.fori_loop(0, self.held.shape[2] // SLICE, add_rows, 0)
+            self.start(out, self.second.at[half], self.second_recv.at[half], peer)
+        for number, buffer in ((4, self.across_recv), (6, self.along_recv)):
+            self.copy(number, buffer.at[0], buffer.at[0], place.core).wait_recv()
+        for number, half in ((8, 0), (9, 1)):
+            self.copy(number, self.second.at[half], self.second_recv.at[half], place.core).wait_recv()
+
+    def rows(self, at):
+        first = self.acc[0, at, :] + self.across_recv[0, at, :].astype(F32) + self.second_recv[0, at, :].astype(F32)
+        last = self.acc[1, at, :] + self.along_recv[0, at, :].astype(F32) + self.second_recv[1, at, :].astype(F32)
+        return jnp.concatenate([first, last], axis=1)
+
+    def finish(self):
+        for moved in self.kept:
+            moved.wait_send()
+
+    @staticmethod
+    def scratch(tokens, width):
+        half = width // 2
+        return [
+            pltpu.VMEM((4, 2, tokens, half), BF16),
+            pltpu.VMEM((4, 2, tokens, half), BF16),
+            pltpu.VMEM((3, 2, tokens, half), BF16),
+            pltpu.VMEM((2, tokens, half), F32),
+            pltpu.VMEM((2, tokens, half), BF16),
+            pltpu.VMEM((2, tokens, half), BF16),
+            pltpu.VMEM((2, tokens, half), BF16),
+            pltpu.VMEM((2, tokens, half), BF16),
+            pltpu.SemaphoreType.DMA((10,)),
+            pltpu.SemaphoreType.DMA((10,)),
+        ]
+
+
+SCATTER_BUFFERS = 10
+
+
+def pair_product(lefts, rights, tokens):
+    def product(chunk, n):
+        at = pl.ds(pl.multiple_of(chunk * tokens, tokens), tokens)
+        cols = pl.ds(pl.multiple_of(n * 256, 256), 256)
+        total = None
+        for left, right in zip(lefts, rights):
+            term = jnp.dot(left[at, :], right[:, cols], preferred_element_type=F32)
+            total = term if total is None else total + term
+        return total
+
+    return product
+
+
+def for_slices(start, stop, body):
+    def step(n, none):
+        body(pl.ds(pl.multiple_of(n * SLICE, SLICE), SLICE))
+        return none
+
+    lax.fori_loop(start // SLICE, stop // SLICE, step, 0)
+
+
+def middle_kernel(left, right, own_in, gain, middle_out, gathered, *scratch):
+    buffers, (block, send, recv) = scratch[:SCATTER_BUFFERS], scratch[SCATTER_BUFFERS:]
+    tokens = own_in.shape[0]
+    place = Place()
+    place.greet()
+    scatter = Scatter(place, pair_product([left], [right], tokens), *buffers)
+    scatter.run()
+
+    def body(at):
+        middle = own_in[at, :].astype(F32) + scatter.rows(at)
+        middle_out[at, :] = middle
+        block[at, :] = (middle * rms(middle) * gain[...]).astype(BF16)
+
+    gather = Gather(place, block, gathered, send, recv)
+    for part in (0, 1):
+        for_slices(part * tokens // 2, (part + 1) * tokens // 2, body)
+        gather.begin(part)
+    gather.pass_on()
+    scatter.finish()
+    gather.finish()
+
+
+def turn_kernel(left0, left1, right0, right1, middle, gain, cot, grad_middle_out, gain_out, gathered, *scratch):
+    buffers, (block, send, recv) = scratch[:SCATTER_BUFFERS], scratch[SCATTER_BUFFERS:]
+    tokens = cot.shape[0]
+    place = Place()
+    place.greet()
+    scatter = Scatter(place, pair_product([left0, left1], [right0, right1], tokens), *buffers)
+    scatter.run()
+    gain_out[...] = jnp.zeros_like(gain_out)
+
+    def body(at):
+        values = middle[at, :]
+        grad = scatter.rows(at)
+        scale = rms(values)
+        weighted = grad * gain[...]
+        inner = jnp.mean(values * weighted, axis=-1, keepdims=True)
+        total = cot[at, :].astype(F32) + scale * weighted - values * (scale * scale * scale * inner)
+        grad_middle_out[at, :] = total
+        block[at, :] = total.astype(BF16)
+        term = grad * values * scale
+        gain_out[...] += term[0:8] + term[8:16]
+
+    gather = Gather(place, block, gathered, send, recv)
+    for part in (0, 1):
+        for_slices(part * tokens // 2, (part + 1) * tokens // 2, body)
+        gather.begin(part)
+    gather.pass_on()
+    scatter.finish()
+    gather.finish()
+
+
+def scatter_kernel(count, *refs):
+    lefts, rights, out, buffers = refs[:count], refs[count : 2 * count], refs[2 * count], refs[2 * count + 1 :]
+    tokens = out.shape[0]
+    place = Place()
+    place.greet()
+    scatter = Scatter(place, pair_product(lefts, rights, tokens), *buffers)
+    scatter.run()
+
+    def body(at):
+        out[at, :] = scatter.rows(at).astype(out.dtype)
+
+    for_slices(0, tokens, body)
+    scatter.finish()
+
+
+ANYWHERE = pl.BlockSpec(memory_space=pl.ANY)
+GATHER_SCRATCH = [pltpu.SemaphoreType.DMA((GATHER_SEMS,))] * 2
+
+
+def first_gather(planes, normed, cot):
+    tokens, width = normed.shape
+    full = jax.ShapeDtypeStruct((8 * tokens, width), BF16)
+
+    def kernel(normed_ref, cot_ref, normed_out, cot_out, *sems):
+        first_gather_kernel(planes, normed_ref, cot_ref, None, normed_out, cot_out, None, None, None, *sems)
+
+    return pl.pallas_call(
+        kernel,
+        name="first_gather",
+        out_shape=(full, full),
+        in_specs=[ANYWHERE] * 2,
+        out_specs=(ANYWHERE,) * 2,
+        scratch_shapes=GATHER_SCRATCH * 2,
+        compiler_params=mixer_params(3),
+    )(normed, cot)
+
+
+def middle_step(mixed, w_out, own_in, gain):
+    tokens, width = own_in.shape
+    return pl.pallas_call(
+        middle_kernel,
+        name="middle_step",
+        out_shape=(jax.ShapeDtypeStruct((tokens, width), F32), jax.ShapeDtypeStruct((8 * tokens, width), BF16)),
+        in_specs=whole(4),
+        out_specs=(pl.BlockSpec(memory_space=pltpu.VMEM), ANYWHERE),
+        scratch_shapes=Scatter.scratch(tokens, width) + [pltpu.VMEM((tokens, width), BF16)] + GATHER_SCRATCH,
+        compiler_params=mixer_params(4),
+    )(mixed, w_out, own_in, gain[None])
+
+
+def turn_step(left0, left1, right0, right1, middle, gain, cot):
+    tokens, width = cot.shape
+    return pl.pallas_call(
+        turn_kernel,
+        name="turn_step",
+        out_shape=(
+            jax.ShapeDtypeStruct((tokens, width), F32),
+            jax.ShapeDtypeStruct((8, width), F32),
+            jax.ShapeDtypeStruct((8 * tokens, width), BF16),
+        ),
+        in_specs=whole(7),
+        out_specs=(*whole(2), ANYWHERE),
+        scratch_shapes=Scatter.scratch(tokens, width) + [pltpu.VMEM((tokens, width), BF16)] + GATHER_SCRATCH,
+        compiler_params=mixer_params(5),
+    )(left0, left1, right0, right1, middle, gain[None], cot)
+
+
+def scatter_step(number, lefts, rights):
+    tokens, width = lefts[0].shape[0] // 8, rights[0].shape[1]
+    return pl.pallas_call(
+        functools.partial(scatter_kernel, len(lefts)),
+        name="scatter_step",
+        out_shape=jax.ShapeDtypeStruct((tokens, width), F32),
+        in_specs=whole(2 * len(lefts)),
+        out_specs=pl.BlockSpec(memory_space=pltpu.VMEM),
+        scratch_shapes=Scatter.scratch(tokens, width),
+        compiler_params=mixer_params(number),
+    )(*lefts, *rights)
+
+
+def swap_kernel(groups, quarters, out, send, recv):
+    g, c = lax.axis_index("g"), lax.axis_index("c")
+    me = g * 2 + c
+    barrier = pltpu.get_barrier_semaphore()
+    for step in range(1, groups):
+        other = lax.rem(me + step, groups)
+        pl.semaphore_signal(barrier, inc=1, device_id={"g": other // 2, "c": other % 2}, device_id_type=MESH)
+    pl.semaphore_wait(barrier, groups - 1)
+    keep = pltpu.make_async_copy(quarters.at[me], out.at[:, me], send.at[0])
+    keep.start()
+    moved = []
+    for step in range(1, groups):
+        other = lax.rem(me + step, groups)
+        copy = pltpu.make_async_remote_copy(
+            src_ref=quarters.at[other],
+            dst_ref=out.at[:, me],
+            send_sem=send.at[step],
+            recv_sem=recv.at[step],
+            device_id={"g": other // 2, "c": other % 2},
+            device_id_type=MESH,
+        )
+        copy.start()
+        moved.append(copy)
+    for step in range(1, groups):
+        other = lax.rem(me + groups - step, groups)
+        pltpu.make_async_remote_copy(
+            src_ref=quarters.at[other],
+            dst_ref=out.at[:, other],
+            send_sem=send.at[step],
+            recv_sem=recv.at[step],
+            device_id={"g": other // 2, "c": other % 2},
+            device_id_type=MESH,
+        ).wait_recv()
+    for copy in moved:
+        copy.wait_send()
+    keep.wait()
+
+
+def swap(quarters):
+    groups, kinds, part, width = quarters.shape
+    return pl.pallas_call(
+        functools.partial(swap_kernel, groups),
+        name="swap",
+        out_shape=jax.ShapeDtypeStruct((kinds, groups, part, width), quarters.dtype),
+        in_specs=[ANYWHERE],
+        out_specs=ANYWHERE,
+        scratch_shapes=[pltpu.SemaphoreType.DMA((groups,)), pltpu.SemaphoreType.DMA((groups,))],
+        compiler_params=mixer_params(6),
+    )(quarters)
 
 
 def rms(values):
@@ -432,19 +850,16 @@
     member = 2 * r + i
     first = member * channels
 
-    def member_columns(weight):
-        if planes == row_groups:
-            part = weight.shape[0] // row_groups
-            quarter = lax.dynamic_slice_in_dim(weight, r * part, part, 0)
-            quarters = lax.all_gather(quarter, "t", axis=0, tiled=False)
-            return lax.all_to_all(quarters, ("g", "c"), 0, 0, tiled=True).reshape(weight.shape)
-        every = lax.all_gather(weight, ("t", "i"), axis=1, tiled=True)
-        return lax.dynamic_slice_in_dim(every, first, channels, 1)
-
-    in_gate = in_weight[:, 0]
-    in_recur = in_weight[:, 1]
-    mixer_w = member_columns(jnp.concatenate([in_gate, in_recur, out_weight], axis=0))
-    w_gate, w_recur, w_out = mixer_w[:width], mixer_w[width : 2 * width], mixer_w[2 * width :]
+    mixer_own = jnp.stack([in_weight[:, 0].T, in_weight[:, 1].T, out_weight.T])
+    if planes == row_groups:
+        part = channels // row_groups
+        quarter = lax.dynamic_slice_in_dim(mixer_own, r * part, part, 1)
+        mixer_w = swap(lax.all_gather(quarter, "t", axis=0, tiled=False))
+    else:
+        every = lax.all_gather(mixer_own, ("t", "i"), axis=1, tiled=True)
+        mixer_w = lax.dynamic_slice_in_dim(every, first, channels, 1)
+    mixer_w = mixer_w.reshape(3, channels, width)
+    w_gate, w_recur, w_out = mixer_w[0], mixer_w[1], mixer_w[2]
     hidden_part = mlp_in.shape[2] // row_groups
 
     def own_part(weight):
@@ -491,44 +906,34 @@
     spread = spread.reshape(2, channels, channels)
     wg0, wg1 = spread[0], spread[1]
 
-    flat_in = inputs.reshape(own_tokens, width).astype(F32)
+    own_in = inputs.reshape(own_tokens, width)
+    flat_in = own_in.astype(F32)
     scale_in = rms(flat_in)
-    normed = gather_tokens((flat_in * scale_in * mix_gain).astype(BF16))
     cot_own = cotangent.reshape(own_tokens, width)
-    cot = gather_tokens(cot_own)
-    gate_branch = nn(normed, w_gate, F32)
-    recur = nn(normed, w_recur, BF16)
+    normed, cot = first_gather(planes, (flat_in * scale_in * mix_gain).astype(BF16), cot_own)
+    gate_branch = nt(normed, w_gate, F32)
+    recur = nt(normed, w_recur, BF16)
     conv_low, decay, states, mixed, halo, cin = mixer_forward(planes, seg, recur, gate_branch, mask, wg0, wg1, vec)
-    middle = flat_in + scatter_tokens(nt(mixed, w_out, BF16)).astype(F32)
-    scale_mid = rms(middle)
-    normed_two = gather_tokens((middle * scale_mid * mlp_gain).astype(BF16))
+    middle, normed_two = middle_step(mixed, w_out, own_in, mlp_gain)
     left = nt(normed_two, w_left, F32)
     right = nt(normed_two, w_right, F32)
     act, slope = gelu_parts(left)
     hidden = (act * right).astype(BF16)
-    down = scatter_tokens(nn(hidden, w_down, BF16))
-    outputs = (middle + down.astype(F32)).astype(BF16).reshape(inputs.shape)
 
     grad_hidden = nt(cot, w_down, F32)
     grad_left = (grad_hidden * right * slope).astype(BF16)
     grad_right = (grad_hidden * act).astype(BF16)
-    partial = lax.dot(grad_left, w_left, preferred_element_type=F32) + lax.dot(
-        grad_right, w_right, preferred_element_type=F32
-    )
-    grad_normed_two = scatter_tokens(partial.astype(BF16)).astype(F32)
-    grad_mid_norm, grad_mlp_gain = rms_back(middle, scale_mid, mlp_gain, grad_normed_two)
-    grad_middle = cot_own.astype(F32) + grad_mid_norm
-    grad_mid = gather_tokens(grad_middle.astype(BF16))
-    grad_mixed = nn(grad_mid, w_out, F32)
+    grad_middle, grad_mlp_gain, grad_mid = turn_step(grad_left, grad_right, w_left, w_right, middle, mlp_gain, cot_own)
+    grad_mlp_gain = jnp.sum(grad_mlp_gain, axis=0)
+    grad_mixed = nt(grad_mid, w_out, F32)
     grad_gate, grad_recur, gw0, gw1, small = mixer_backward(
         planes, seg, grad_mixed, gate_branch, states, decay, conv_low, recur, halo, cin, mask, wg0, wg1, wg0.T, wg1.T, vec
     )
-    partial = lax.dot_general(grad_gate, w_gate, (((1,), (1,)), ((), ())), preferred_element_type=F32) + lax.dot_general(
-        grad_recur, w_recur, (((1,), (1,)), ((), ())), preferred_element_type=F32
-    )
-    grad_normed = scatter_tokens(partial.astype(BF16)).astype(F32)
+    grad_normed = scatter_step(7, [grad_gate, grad_recur], [w_gate, w_recur])
     grad_in_norm, grad_mix_gain = rms_back(flat_in, scale_in, mix_gain, grad_normed)
     grad_inputs = (grad_middle + grad_in_norm).reshape(inputs.shape)
+    down = scatter_step(8, [hidden], [w_down])
+    outputs = (middle + down).astype(BF16).reshape(inputs.shape)
 
     def to_owners(grad):
         reduced = lax.psum_scatter(grad, "t", scatter_dimension=0, tiled=True)

time: 1250 us -> 923 us (0.74)
  waiting for transfers between devices: 620 us -> 46.5 us
  Pallas kernels: 97.2 us -> 512 us
  matrix products: 176 us -> 103 us
  blocking collectives: 149 us -> 80.8 us
  local copies, waits for them, and re-layouts: 140 us -> 122 us
    pallas_call x0 -> x6, Pallas kernels: none -> 416 us  [the longest x2 108 us: scatter_step(): pl.pallas_call(functools.partial(scatter_kernel, len(lefts)), name='scatt...]
    reduce_scatter x4 -> x0, waiting for transfers between devices: 188 us -> none  [scatter_tokens(): return lax.psum_scatter(partial, PLANE, scatter_dimension=0, tiled=True)]
    all_gather x5 -> x1, waiting for transfers between devices: 180 us -> 0.01 us  [per_device(): mixer_w = swap(lax.all_gather(quarter, 't', axis=0, tiled=False))]
    all_gather x1, waiting for transfers between devices: 163 us -> 0.02 us  [per_device(): mlp_w = lax.all_gather(mlp_w, 't', axis=0, tiled=False)]
    dot_general x8 -> x0, matrix products: 84.8 us -> none  [the longest x4 38.2 us: nn(): return jnp.dot(left, right, preferred_element_type=F32).astype(out)]
    all_gather x1, blocking collectives: 78.9 us -> 5.76 us  [per_device(): lax.all_gather((segment_ids + 1).astype(F32), ('g', 'c'), axis=0, tiled=T...]
    all_to_all x2, waiting for transfers between devices: 29.5 us -> 0.01 us  [to_owners(): lax.all_to_all(reduced.reshape(members, -1, grad.shape[1]), PLANE, 0, 0,...]
    dot_general x4 -> x6, matrix products: 47.5 us -> 58 us  [nt(): lax.dot_general(left, right, (((1,), (1,)), ((), ())), preferred_element_...]
  transfers between devices with their start and end apart: 17 -> 8, of which waited for: 13 -> 2; matrix products, arithmetic and copies ran while one was open for 21% -> 15% of each run, Pallas kernels for 5% -> 39%
where the time goes in v2:
time: 923 us; the launch traced here: 916 us
  Pallas kernels  512 us (55%)
  local copies, waits for them, and re-layouts  122 us (13%)
  matrix products  103 us (11%)
  blocking collectives  80.8 us (9%)
  waiting for transfers between devices  46.5 us (5%)
  other arithmetic  23.3 us (3%)
  between operations  14.9 us (2%)
  starting transfers between devices  13.5 us (1%)
    pallas_call x2, Pallas kernels, scatter_step(): pl.pallas_call(functools.partial(scatter_kernel, len(lefts)), name='scatt...  108 us
    pallas_call x1, Pallas kernels, turn_step(): pl.pallas_call(turn_kernel, name='turn_step', out_shape=(jax.ShapeDtypeSt...  100 us
    pallas_call x1, Pallas kernels, middle_step(): pl.pallas_call(middle_kernel, name='middle_step', out_shape=(jax.ShapeDty...  89.5 us
    pallas_call x1, Pallas kernels, first_gather(): pl.pallas_call(kernel, name='first_gather', out_shape=(full, full), in_sp...  75.2 us
    dot_general x6, matrix products, nt(): lax.dot_general(left, right, (((1,), (1,)), ((), ())), preferred_element_...  58 us
    pallas_call x1, Pallas kernels, mixer_backward(): pl.pallas_call(functools.partial(mixer_backward_kernel, count, seg), name...  50.7 us
    pallas_call x1, Pallas kernels, mixer_forward(): pl.pallas_call(functools.partial(mixer_forward_kernel, count, seg), name=...  45.5 us
    dot_general x6, matrix products, tn(): lax.dot_general(left, right, (((0,), (0,)), ((), ())), preferred_element_...  45 us
  transfers between devices with their start and end apart: 8, of which 2 were waited for; matrix products, arithmetic and copies ran while one was open for 15% of the time, Pallas kernels for 39%

profile of v2, /device:TPU:0, one launch (start us, length us, event | category | flops | bytes accessed | tf_op | source)
XLA Modules:
  0.0 916.1 jit_solution(6564353239106824091)
XLA Ops:
  16.1 12.8 %fusion.34 = (bf16[2048,1,768]{2,1,0:T(2,128)(2,1)S(1)}, bf16[2048,1,768]{2,1,0:T(2,128)(2,1)S(1)}) fusion(bf16[2048,2,768]{2,1,0:T(2,128)(2,1)} %param.29), kind=kLoop, calls=%fused_computation.97 | loop fusion | bytes 12582912 | tf_op jit(solution)/shard_map/slice | solution.py:868
  28.8 7.8 constant_dynamic-slice_fusion.1
  54.7 32.1 %all_gather.21 = f32[8,1024]{1,0:T(8,128)S(1)} all-gather(f32[8,128]{1,0:T(8,128)S(1)} %bitcast.162), channel_id=1, replica_groups=mesh['t'=4,'i'=2,'g'=2,'c'=2] {'t','i'}, dimensions={1}, use_global_device_ids=true | all-gather | bytes 36864 | tf_op jit(solution)/shard_map/all_gather | solution.py:876
  97.2 75.2 %first_gather.1 = (bf16[2048,2048]{1,0:T(8,128)(2,1)}, bf16[2048,2048]{1,0:T(8,128)(2,1)}) custom-call(bf16[256,2048]{1,0:T(8,128)(2,1)} %fusion.2.normed_ref, bf16[256,2048]{1,0:T(8,128)(2,1)} %bitcast.147), custom_call_target="tpu_custom_call" | custom-call | tf_op jit(solution)/shard_map/first_gather/pallas_call | solution.py:709
  175.2 43.4 %swap.1 = bf16[3,4,80,2048]{3,2,1,0:T(8,128)(2,1)} custom-call(bf16[4,3,80,2048]{3,2,1,0:T(8,128)(2,1)} %bitcast.150), custom_call_target="tpu_custom_call" | custom-call | tf_op jit(solution)/shard_map/swap/pallas_call | solution.py:803
  222.5 10.1 %convolution_convert_fusion.3.recur = bf16[2048,320]{1,0:T(8,128)(2,1)} fusion(bf16[2048,2048]{1,0:T(8,128)(2,1)} %get-tuple-element.55, bf16[320,2048]{1,0:T(8,128)(2,1)S(1)} %bitcast.145), kind=kOutput, calls=%fused_computation.18 | convolution fusion | flops 2685009920 | bytes 11010048 | tf_op jit(solution)/shard_map/dot_general | solution.py:825
  239.0 45.5 %mixer_forward.1 = (bf16[2048,320]{1,0:T(8,128)(2,1)}, f32[3,2048,128]{2,1,0:T(8,128)}, f32[2048,320]{1,0:T(8,128)}, bf16[2048,320]{1,0:T(8,128)(2,1)}, f32[128,320]{1,0:T(8,128)}, /*index=5*/f32[16,320]{1,0:T(8,128)}) custom-call(bf16[2048,320]{1,0:T(8,128)(2,1)} %convolution_convert_fusion.3.recur, f32[2048,320]{1,0:T(8,128)} %fusion.38.gate, ...), custom_call_target="tpu_custom_call" | custom-call | tf_op jit(solution)/shard_map/mixer_forward/pallas_call | solution.py:329
  284.4 89.5 %middle_step.1 = (f32[256,2048]{1,0:T(8,128)}, bf16[2048,2048]{1,0:T(8,128)(2,1)}) custom-call(bf16[2048,320]{1,0:T(8,128)(2,1)} %get-tuple-element.56.left, bf16[320,2048]{1,0:T(8,128)(2,1)} %bitcast.141, bf16[256,2048]{1,0:T(8,128)(2,1)} %bitcast.129, f32[1,2048]{1,0:T(1,128)} %bitcast.160), custom_call_target="tpu_custom_call" | custom-call | tf_op jit(solution)/shard_map/middle_step/pallas_call | solution.py:722
  388.6 8.6 fusion.40
  397.1 17.3 %multiply_convert_fusion = (bf16[2048,768]{1,0:T(8,128)(2,1)}, bf16[2048,768]{1,0:T(8,128)(2,1)}, bf16[2048,768]{1,0:T(8,128)(2,1)}) fusion(f32[2048,768]{1,0:T(8,128)S(1)} %fusion.39, f32[2048,768]{1,0:T(8,128)} %fusion.40, bf16[2048,2048]{1,0:T(8,128)(2,1)} %get-tuple-element.59, bf16[768,2048]{1,0:T(8,128)(2,1)S(1)} %bitcast.135), kind=kOutput, calls=%fused_computation.1 | convolution fusion | flops 6480199680 | bytes 33554432 | tf_op jit(solution)/shard_map/dot_general | solution.py:825
  414.5 100.3 %turn_step.1 = (f32[256,2048]{1,0:T(8,128)}, f32[8,2048]{1,0:T(8,128)}, bf16[2048,2048]{1,0:T(8,128)(2,1)}) custom-call(bf16[2048,768]{1,0:T(8,128)(2,1)} %get-tuple-element.145.left0, bf16[2048,768]{1,0:T(8,128)(2,1)} %get-tuple-element.144.left1, bf16[768,2048]{1,0:T(8,128)(2,1)} %bitcast.134, bf16[768,2048]{1,0:T(8,128)(2,1)} %bitcast.132, ...), custom_call_target="tpu_custom_call" | custom-call | tf_op jit(solution)/shard_map/turn_step/pallas_call | solution.py:735
  514.8 8.8 fusion.41.grad_mixed
  527.7 50.7 %mixer_backward.1 = (bf16[2048,320]{1,0:T(8,128)(2,1)}, bf16[2048,320]{1,0:T(8,128)(2,1)}, f32[320,320]{1,0:T(8,128)}, f32[320,320]{1,0:T(8,128)}, f32[8,320]{1,0:T(8,128)}) custom-call(f32[2048,320]{1,0:T(8,128)} %fusion.41.grad_mixed, f32[2048,320]{1,0:T(8,128)} %fusion.38.gate, f32[2048,320]{1,0:T(8,128)} %get-tuple-element.62.states, ...), custom_call_target="tpu_custom_call" | custom-call | tf_op jit(solution)/shard_map/mixer_backward/pallas_call | solution.py:360
  594.1 10.8 %convolution_convert_fusion.1 = bf16[2048,768]{0,1:T(8,128)(2,1)S(1)} fusion(bf16[2048,2048]{1,0:T(8,128)(2,1)} %get-tuple-element.58, bf16[2048,768]{1,0:T(8,128)(2,1)} %get-tuple-element.144.left1), kind=kOutput, calls=%fused_computation.16 | convolution fusion | flops 6444023808 | bytes 14680064 | tf_op jit(solution)/shard_map/dot_general | solution.py:829
  604.9 9.3 %convolution_convert_fusion.2 = bf16[2048,768]{0,1:T(8,128)(2,1)S(1)} fusion(bf16[2048,2048]{1,0:T(8,128)(2,1)} %get-tuple-element.58, bf16[2048,768]{1,0:T(8,128)(2,1)S(1)} %copy-done.13), kind=kOutput, calls=%fused_computation.17 | convolution fusion | flops 6444023808 | bytes 14680064 | tf_op jit(solution)/shard_map/dot_general | solution.py:829
  614.2 7.5 convolution_convert_fusion
  633.0 54.0 %scatter_step.3 = f32[256,2048]{1,0:T(8,128)} custom-call(bf16[2048,320]{1,0:T(8,128)(2,1)} %get-tuple-element.67.refs_0_, bf16[2048,320]{1,0:T(8,128)(2,1)} %get-tuple-element.68.refs_1_, bf16[320,2048]{1,0:T(8,128)(2,1)} %bitcast.144, bf16[320,2048]{1,0:T(8,128)(2,1)} %bitcast.146), custom_call_target="tpu_custom_call" | custom-call | tf_op jit(solution)/shard_map/scatter_step/pallas_call | solution.py:752
  700.0 53.8 %scatter_step.2 = f32[256,2048]{1,0:T(8,128)} custom-call(bf16[2048,768]{1,0:T(8,128)(2,1)} %get-tuple-element.146.refs_0_, bf16[768,2048]{1,0:T(8,128)(2,1)} %bitcast.136), custom_call_target="tpu_custom_call" | custom-call | tf_op jit(solution)/shard_map/scatter_step/pallas_call | solution.py:752
  753.8 42.9 %all-reduce.4 = (f32[2048]{0:T(1024)S(1)}, f32[2048]{0:T(1024)S(1)}) all-reduce(f32[2048]{0:T(1024)S(1)} %get-tuple-element.138, f32[2048]{0:T(1024)S(1)} %reduce_sum.39), channel_id=4, replica_groups=mesh['t'=4,'i'=2,'g'=2,'c'=2] {'t','i','g','c'}, use_global_device_ids=true, to_apply=%region_3.4.clone | all-reduce | flops 4096 | bytes 32768
  797.9 33.5 %reduce-scatter.8.cloned.1.call-done = bf16[512,2304]{0,1:T(8,128)(2,1)} async-done(((bf16[2048,2304]{0,1:T(8,128)(2,1)}), bf16[512,2304]{0,1:T(8,128)(2,1)}) %reduce-scatter.8.cloned.1.call-update) | async-done | bytes 2359312 | tf_op jit(solution)/shard_map/reduce_scatter | solution.py:939
  843.3 12.4 %reduce-scatter.6.cloned.1.call-done = f32[1,328,80]{1,2,0:T(8,128)} async-done(((f32[4,328,80]{1,2,0:T(8,128)}), f32[1,328,80]{1,2,0:T(8,128)}) %reduce-scatter.6.cloned.1.call-update) | async-done | bytes 104976 | tf_op jit(solution)/shard_map/reduce_scatter | solution.py:965
  874.9 7.7 reshape.272
  882.6 9.4 %copy.159 = f32[64,3,4,2,4,192]{5,4,3,2,0,1:T(4,128)} copy(f32[64,3,4,2,4,192]{5,2,1,0,4,3:T(4,128)} %bitcast.130) | data formatting | bytes 9437184 | tf_op jit(solution)/shard_map/reshape | solution.py:950
  892.0 8.4 reshape.265
  (182 shorter events, 149.4 us)
Async XLA Ops:
  7.2 168.0 %all-gather.6.cloned.1.call-start = ((), (), s32[]{:S(2)}) async-start(), calls=%async_computation.9 | async-start | bytes 4915200 | tf_op jit(solution)/shard_map/all_gather | solution.py:857
  13.2 360.7 %all-gather.8.cloned.1.call-start = ((), (), s32[]{:S(2)}) async-start(), calls=%async_computation.10 | async-start | bytes 11796480 | tf_op jit(solution)/shard_map/all_gather | solution.py:869
  48.9 640.5 %reduce-scatter.4.cloned.1.call-start = ((), (), s32[]{:S(2)}) async-start(), calls=%async_computation.6 | async-start | bytes 4915200 | tf_op jit(solution)/shard_map/reduce_scatter | solution.py:939
  91.7 80.7 %copy-start.15 = (bf16[320,320]{0,1:T(8,128)(2,1)}, bf16[320,320]{0,1:T(8,128)(2,1)S(1)}, u32[]{:S(2)}) copy-start(bf16[320,320]{0,1:T(8,128)(2,1)S(1)} %squeeze.47) | copy-start | bytes 614404
  93.2 82.0 %copy-start.16 = (bf16[320,320]{0,1:T(8,128)(2,1)}, bf16[320,320]{0,1:T(8,128)(2,1)S(1)}, u32[]{:S(2)}) copy-start(bf16[320,320]{0,1:T(8,128)(2,1)S(1)} %squeeze.48) | copy-start | bytes 614404
  96.0 79.3 %copy-start.25 = (f32[256]{0:T(256)}, f32[256]{0:T(256)S(1)}, u32[]{:S(2)}) copy-start(f32[256]{0:T(256)S(1)} %rsqrt_bitcast_fusion) | copy-start | bytes 3076
  218.7 13.9 %slice-start.3 = ((s8[8388608]{0:T(1024)(128)(4,1)}), s8[4194304]{0:T(1024)(128)(4,1)S(1)}, s32[]{:S(2)}) async-start(s8[8388608]{0:T(1024)(128)(4,1)} %bitcast.165), calls=%async_computation.14 | async-start | bytes 8388608
  222.5 10.1 %copy-start.11 = (bf16[1,4,80,2048]{3,2,1,0:T(8,128)(2,1)}, bf16[1,4,80,2048]{3,2,1,0:T(8,128)(2,1)S(1)}, u32[]{:S(2)}) copy-start(bf16[1,4,80,2048]{3,2,1,0:T(8,128)(2,1)S(1)} %get-tuple-element.153) | copy-start | bytes 3932164
  222.5 10.1 %slice-start.4 = ((s8[8388608]{0:T(1024)(128)(4,1)}), s8[4194304]{0:T(1024)(128)(4,1)S(1)}, s32[]{:S(2)}) async-start(s8[8388608]{0:T(1024)(128)(4,1)} %bitcast.165), calls=%async_computation.15 | async-start | bytes 8388608
  378.5 10.1 %copy-start.7 = (bf16[4,1,192,2048]{3,2,1,0:T(8,128)(2,1)}, bf16[4,1,192,2048]{3,2,1,0:T(8,128)(2,1)S(1)}, u32[]{:S(2)}) copy-start(bf16[4,1,192,2048]{3,2,1,0:T(8,128)(2,1)S(1)} %get-tuple-element.149) | copy-start | bytes 9437188
  378.5 10.1 %copy-start.6 = (bf16[4,1,192,2048]{3,2,1,0:T(8,128)(2,1)}, bf16[4,1,192,2048]{3,2,1,0:T(8,128)(2,1)S(1)}, u32[]{:S(2)}) copy-start(bf16[4,1,192,2048]{3,2,1,0:T(8,128)(2,1)S(1)} %get-tuple-element.148) | copy-start | bytes 9437188
  378.5 18.7 %copy-start.8 = (bf16[4,1,192,2048]{3,2,1,0:T(8,128)(2,1)}, bf16[4,1,192,2048]{3,2,1,0:T(8,128)(2,1)S(1)}, u32[]{:S(2)}) copy-start(bf16[4,1,192,2048]{3,2,1,0:T(8,128)(2,1)S(1)} %get-tuple-element.147) | copy-start | bytes 9437188
  414.5 100.3 %copy-start.10 = (bf16[1,4,80,2048]{3,2,1,0:T(8,128)(2,1)S(1)}, bf16[1,4,80,2048]{3,2,1,0:T(8,128)(2,1)}, u32[]{:S(2)}) copy-start(bf16[1,4,80,2048]{3,2,1,0:T(8,128)(2,1)} %get-tuple-element.152) | copy-start | bytes 3932164
  594.0 10.9 %copy-start.13 = (bf16[2048,768]{1,0:T(8,128)(2,1)S(1)}, bf16[2048,768]{1,0:T(8,128)(2,1)}, u32[]{:S(2)}) copy-start(bf16[2048,768]{1,0:T(8,128)(2,1)} %get-tuple-element.145.left0) | copy-start | bytes 9437188
  594.0 237.4 %reduce-scatter.8.cloned.1.call-start = ((), (), s32[]{:S(2)}) async-start(), calls=%async_computation.8 | async-start | bytes 11796480 | tf_op jit(solution)/shard_map/reduce_scatter | solution.py:939
  594.0 20.2 %slice-start.1 = ((s8[8388608]{0:T(1024)(128)(4,1)}), s8[4194304]{0:T(1024)(128)(4,1)S(1)}, s32[]{:S(2)}) async-start(s8[8388608]{0:T(1024)(128)(4,1)} %bitcast.163), calls=%async_computation.12 | async-start | bytes 8388608
  628.7 63.0 %all-to-all-start.1 = ((f32[4,328,80]{1,2,0:T(8,128)}), f32[4,328,80]{1,2,0:T(8,128)}, u32[]{:S(2)}, u32[]{:S(2)}) async-start(f32[4,328,80]{1,2,0:T(8,128)} %bitcast.46), calls=%async_computation.2 | async-start | bytes 983040 | tf_op jit(solution)/shard_map/all_to_all | solution.py:964
  633.0 54.1 %copy-start.3 = (bf16[2,128,2048]{2,1,0:T(8,128)(2,1)S(1)}, bf16[2,128,2048]{2,1,0:T(8,128)(2,1)}, u32[]{:S(2)}) copy-start(bf16[2,128,2048]{2,1,0:T(8,128)(2,1)} %param.18) | copy-start | bytes 3145732
  633.0 54.1 %copy-start.23 = (f32[2048]{0:T(1024)S(1)}, f32[2048]{0:T(1024)}, u32[]{:S(2)}) copy-start(f32[2048]{0:T(1024)} %param.20) | copy-start | bytes 24580
  633.0 54.1 %copy-start.26 = (f32[256]{0:T(256)S(1)}, f32[256]{0:T(256)}, u32[]{:S(2)}) copy-start(f32[256]{0:T(256)} %copy-done.25) | copy-start | bytes 3076
  691.7 144.1 %all-to-all-start = ((bf16[8,64,960]{2,1,0:T(8,128)(2,1)}), bf16[8,64,960]{2,1,0:T(8,128)(2,1)}, u32[]{:S(2)}, u32[]{:S(2)}) async-start(bf16[8,64,960]{2,1,0:T(8,128)(2,1)} %bitcast.149), calls=%async_computation.1 | async-start | bytes 2097152 | tf_op jit(solution)/shard_map/all_to_all | solution.py:940
  695.9 159.8 %reduce-scatter.6.cloned.1.call-start = ((), (), s32[]{:S(2)}) async-start(), calls=%async_computation.7 | async-start | bytes 614400 | tf_op jit(solution)/shard_map/reduce_scatter | solution.py:965
  700.0 53.8 %copy-start.24 = (f32[8,2048]{1,0:T(8,128)S(1)}, f32[8,2048]{1,0:T(8,128)}, u32[]{:S(2)}) copy-start(f32[8,2048]{1,0:T(8,128)} %get-tuple-element.72) | copy-start | bytes 196612
  835.8 39.1 %all-to-all-start.2 = ((bf16[8,64,2304]{2,1,0:T(8,128)(2,1)}), bf16[8,64,2304]{2,1,0:T(8,128)(2,1)}, u32[]{:S(2)}, u32[]{:S(2)}) async-start(bf16[8,64,2304]{2,1,0:T(8,128)(2,1)} %bitcast.52), calls=%async_computation.5 | async-start | bytes 4718592 | tf_op jit(solution)/shard_map/all_to_all | solution.py:940
  (22 other events, 126.0 us)
Sparse Core Ops, SparseCore 0:
  13.3 79.3 all-gather.5
  94.2 167.5 all-gather.7
  594.1 72.4 reduce-scatter.3
  668.8 162.6 reduce-scatter.7
  833.6 22.0 reduce-scatter.5

commit v3 on v2

--- a/solution.py
+++ b/solution.py
@@ -18,6 +18,9 @@
 GELU_B = 0.044715
 HALO = 8
 LANES = 128
+SLICE = 16
+ANYWHERE = pl.BlockSpec(memory_space=pl.ANY)
+GATHER_SCRATCH = [pltpu.SemaphoreType.DMA((13,))] * 2
 
 
 def gelu_parts(x):
@@ -96,10 +99,16 @@
 
 
 def mixer_forward_kernel(
-    count, seg, recur, gate, mask, wg0, wg1, vec_ref, conv_out, decay_out, states_out, mixed_out, halo_out, cin_out,
+    count, seg, rows_here, recur, gate, ids, ids_before, ids_after, wg0, wg1, vec_ref, cot, quarters,
+    conv_out, decay_out, states_out, mixed_out, halo_out, cin_out, mask, cot_out, swapped,
     drive, h_ref, a_ref, ext, halo_send, halo_recv, summary, slots, send_sem, recv_sem, halo_sems,
+    gather_send, gather_recv, swap_send, swap_recv,
 ):
-    me = greet(count)
+    place = Place()
+    me = lax.axis_index("t")
+    place.greet([place.peer(0, 1, 1)] + [{"t": lax.rem(me + step, count)} for step in range(1, count)])
+    gather = Gather(place, cot, cot_out, gather_send, gather_recv)
+    move = Swap(quarters, swapped, swap_send, swap_recv)
     rows = 8
     for r in range(rows):
         halo_send[r * HALO : (r + 1) * HALO, :] = recur[
@@ -114,6 +123,9 @@
         device_id_type=MESH,
     )
     halo_copy.start()
+    gather.begin(0)
+    gather.begin(1)
+    move.begin()
     halo_copy.wait()
     for r in range(rows):
         halo_out[r * HALO : (r + 1) * HALO, :] = halo_recv[r * HALO : (r + 1) * HALO, :]
@@ -121,6 +133,20 @@
             16 - HALO :
         ]
     vec = vec_ref[...]
+
+    def ids_of(ref, s):
+        chunk = s // rows_here
+        return ref[chunk, s % rows_here : s % rows_here + 1, :]
+
+    nothing = jnp.zeros((1, LANES), F32)
+    for s in range(2 * rows):
+        here = ids_of(ids, s)
+        back = ids_of(ids, s - rows) if s >= rows else jnp.where(me > 0, ids_of(ids_before, s + rows), nothing)
+        ahead = ids_of(ids, s + rows) if s < rows else jnp.where(me < count - 1, ids_of(ids_after, s - rows), nothing)
+        lines = [jnp.concatenate([back[:, seg - k :], here[:, : seg - k]], axis=1) for k in (1, 2, 3)]
+        lines += [jnp.concatenate([here[:, k:], ahead[:, :k]], axis=1) for k in (1, 2, 3)]
+        lines = [jnp.where(line == here, 1.0, 0.0) for line in lines] + [nothing] * 2
+        mask[s * seg : (s + 1) * seg, :] = jnp.concatenate(lines, axis=0).T
 
     def local(s, none):
         at = pl.ds(pl.multiple_of(s * seg, seg), seg)
@@ -141,7 +167,7 @@
         return none
 
     lax.fori_loop(0, 2 * rows, local, 0)
-
+    gather.pass_first()
     tiles, lanes = drive.shape[0], drive.shape[2]
 
     def scan(k, carried):
@@ -164,6 +190,7 @@
     last_a = join_tiles([part[1] for part in last], width)
     summary[0:rows, :] = last_a[rows:] * last_a[:rows]
     summary[rows : 2 * rows, :] = last_a[rows:] * last_h[:rows] + last_h[rows:]
+    gather.pass_second()
     exchange(count, me, summary, slots, send_sem, recv_sem)
     carry = jnp.zeros((rows, width), F32)
     for z in range(count - 1):
@@ -180,6 +207,9 @@
         return none
 
     lax.fori_loop(0, 2 * rows, finish, 0)
+    gather.pass_third()
+    gather.finish()
+    move.finish()
 
 
 def mixer_backward_kernel(
@@ -321,20 +351,24 @@
     return pltpu.CompilerParams(collective_id=number, has_side_effects=True, vmem_limit_bytes=60 * 1024 * 1024)
 
 
-def mixer_forward(count, seg, recur, gate, mask, wg0, wg1, vec):
+def mixer_forward(count, seg, rows_here, recur, gate, ids, wg0, wg1, vec, cot, quarters):
     n, width = recur.shape
     full = functools.partial(jax.ShapeDtypeStruct, (n, width))
     tiles = -(-width // LANES)
     tiled = jax.ShapeDtypeStruct((tiles, n, LANES), F32)
+    groups, kinds, part, depth = quarters.shape
     return pl.pallas_call(
-        functools.partial(mixer_forward_kernel, count, seg),
+        functools.partial(mixer_forward_kernel, count, seg, rows_here),
         name="mixer_forward",
         out_shape=(
             full(BF16), tiled, full(F32), full(BF16),
             jax.ShapeDtypeStruct((16 * HALO, width), F32), jax.ShapeDtypeStruct((16, width), F32),
+            jax.ShapeDtypeStruct((n, 8), F32),
+            jax.ShapeDtypeStruct((8 * cot.shape[0], cot.shape[1]), BF16),
+            jax.ShapeDtypeStruct((kinds, groups, part, depth), BF16),
         ),
-        in_specs=whole(6),
-        out_specs=tuple(whole(6)),
+        in_specs=whole(8) + [ANYWHERE] * 2,
+        out_specs=(*whole(7), ANYWHERE, ANYWHERE),
         scratch_shapes=[
             pltpu.VMEM((tiles, n, LANES), F32),
             pltpu.VMEM((tiles, n, LANES), F32),
@@ -347,9 +381,11 @@
             pltpu.SemaphoreType.DMA((count,)),
             pltpu.SemaphoreType.DMA((count,)),
             pltpu.SemaphoreType.DMA((2,)),
+            *GATHER_SCRATCH,
+            *swap_scratch(groups),
         ],
         compiler_params=mixer_params(1),
-    )(recur, gate, mask, wg0, wg1, vec)
+    )(recur, gate, *ids, wg0, wg1, vec, cot, quarters)
 
 
 def mixer_backward(count, seg, grad_mixed, gate, states, decay, conv_low, recur, halo, cin, mask, wg0, wg1, wg0t, wg1t, vec):
@@ -396,11 +432,19 @@
         c = 1 - self.c if dc else self.c
         return (i * 2 + g) * 2 + c
 
-    def greet(self):
+    def peer(self, di, dg, dc):
+        return {
+            "i": 1 - self.i if di else self.i,
+            "g": 1 - self.g if dg else self.g,
+            "c": 1 - self.c if dc else self.c,
+        }
+
+    def greet(self, more=()):
         barrier = pltpu.get_barrier_semaphore()
-        for peer in (self.core, self.across, self.along):
+        peers = [self.core, self.across, self.along, *more]
+        for peer in peers:
             pl.semaphore_signal(barrier, inc=1, device_id=peer, device_id_type=MESH)
-        pl.semaphore_wait(barrier, 3)
+        pl.semaphore_wait(barrier, len(peers))
 
 
 class Gather:
@@ -453,20 +497,32 @@
         moved.start()
         self.kept.append((moved, None))
 
-    def pass_on(self):
+    def pass_first(self):
         place = self.place
-        ax, al, dia = place.chunk(0, 1, 0), place.chunk(1, 0, 0), place.chunk(1, 1, 0)
+        ax, al = place.chunk(0, 1, 0), place.chunk(1, 0, 0)
         self.arrived(0, ax, 0)
         self.forward(6, ax, 0, place.along)
         self.arrived(3, al, 1)
         self.forward(7, al, 1, place.across)
+
+    def pass_second(self):
+        place = self.place
+        ax, al = place.chunk(0, 1, 0), place.chunk(1, 0, 0)
         self.arrived(1, ax, 1)
         self.forward(8, ax, 2, place.core)
         self.arrived(2, al, 0)
         self.forward(9, al, 2, place.core)
+
+    def pass_third(self):
+        dia = self.place.chunk(1, 1, 0)
         self.arrived(6, dia, 0)
         self.arrived(7, dia, 1)
-        self.forward(10, dia, 2, place.core)
+        self.forward(10, dia, 2, self.place.core)
+
+    def pass_on(self):
+        self.pass_first()
+        self.pass_second()
+        self.pass_third()
 
     def finish(self):
         place = self.place
@@ -481,24 +537,56 @@
             keep.wait()
 
 
-GATHER_SEMS = Gather.COPIES + 2
-SLICE = 16
-
-
-def first_gather_kernel(planes, normed, cot, ids, normed_out, cot_out, ids_out, before_out, after_out, *sems):
+OTHERS = [(di, dg, dc) for di in (0, 1) for dg in (0, 1) for dc in (0, 1) if di or dg or dc]
+
+
+def first_gather_kernel(count, normed, ids, normed_out, ids_out, before_out, after_out, plane_ids, before, after, send, recv, ids_send, ids_recv):
     place = Place()
-    place.greet()
     me = lax.axis_index("t")
-    gathers = []
-    for number, (block, out) in enumerate(((normed, normed_out), (cot, cot_out))):
-        gather = Gather(place, block, out, sems[2 * number], sems[2 * number + 1])
-        gather.begin(0)
-        gather.begin(1)
-        gathers.append(gather)
-    for gather in gathers:
-        gather.pass_on()
-    for gather in gathers:
-        gather.finish()
+    up, down = {"t": lax.rem(me + 1, count)}, {"t": lax.rem(me + count - 1, count)}
+    place.greet([place.peer(*offset) for offset in OTHERS if sum(offset) > 1] + [up, down])
+    gather = Gather(place, normed, normed_out, send, recv)
+    gather.begin(0)
+    gather.begin(1)
+    own = place.chunk(0, 0, 0)
+    moved = []
+
+    def move(number, source, target, peer):
+        copy = pltpu.make_async_remote_copy(
+            src_ref=source,
+            dst_ref=target,
+            send_sem=ids_send.at[number],
+            recv_sem=ids_recv.at[number],
+            device_id=peer,
+            device_id_type=MESH,
+        )
+        copy.start()
+        moved.append(copy)
+
+    for number, offset in enumerate(OTHERS):
+        move(number, ids, plane_ids.at[own], place.peer(*offset))
+    plane_ids[own] = ids[...]
+    for number, offset in enumerate(OTHERS):
+        chunk = place.chunk(*offset)
+        pltpu.make_async_remote_copy(
+            src_ref=ids,
+            dst_ref=plane_ids.at[chunk],
+            send_sem=ids_send.at[number],
+            recv_sem=ids_recv.at[number],
+            device_id=place.peer(*offset),
+            device_id_type=MESH,
+        ).wait_recv()
+    move(7, plane_ids, before, up)
+    move(8, plane_ids, after, down)
+    gather.pass_on()
+    for copy in moved[7:]:
+        copy.wait_recv()
+    for copy in moved:
+        copy.wait_send()
+    ids_out[...] = plane_ids[...]
+    before_out[...] = before[...]
+    after_out[...] = after[...]
+    gather.finish()
 
 
 class Scatter:
@@ -529,7 +617,7 @@
         order = ((1, 1), (0, 1), (1, 0), (0, 0))
         tile = 256
         per_half = self.held.shape[3] // tile
-        for di, dg in order:
+        def give(di, dg):
             q = 2 * di + dg
             chunk = place.chunk(di, dg, 1)
 
@@ -540,7 +628,8 @@
 
             lax.fori_loop(0, 2 * per_half, send_tile, 0)
             self.start(q, self.core_send.at[q], self.core_recv.at[q], place.core)
-        for di, dg in order:
+
+        def take(di, dg):
             q = 2 * di + dg
             chunk = place.chunk(di, dg, 0)
             self.copy(q, self.core_send.at[q], self.core_recv.at[q], place.core).wait_recv()
@@ -559,6 +648,15 @@
                 self.start(4 + di, self.held.at[q - 1, 0], self.across_recv.at[di], place.across)
             if di:
                 self.start(6 + dg, self.held.at[q - 1, 1], self.along_recv.at[dg], place.along)
+
+        give(*order[0])
+        give(*order[1])
+        take(*order[0])
+        give(*order[2])
+        take(*order[1])
+        give(*order[3])
+        take(*order[2])
+        take(*order[3])
         for half, number, buffer, mine, peer, out in (
             (0, 5, self.across_recv, 2, place.along, 8),
             (1, 7, self.along_recv, 1, place.across, 9),
@@ -695,26 +793,18 @@
     scatter.finish()
 
 
-ANYWHERE = pl.BlockSpec(memory_space=pl.ANY)
-GATHER_SCRATCH = [pltpu.SemaphoreType.DMA((GATHER_SEMS,))] * 2
-
-
-def first_gather(planes, normed, cot):
+def first_gather(planes, normed, ids):
     tokens, width = normed.shape
-    full = jax.ShapeDtypeStruct((8 * tokens, width), BF16)
-
-    def kernel(normed_ref, cot_ref, normed_out, cot_out, *sems):
-        first_gather_kernel(planes, normed_ref, cot_ref, None, normed_out, cot_out, None, None, None, *sems)
-
+    every = (8, *ids.shape)
     return pl.pallas_call(
-        kernel,
+        functools.partial(first_gather_kernel, planes),
         name="first_gather",
-        out_shape=(full, full),
-        in_specs=[ANYWHERE] * 2,
-        out_specs=(ANYWHERE,) * 2,
-        scratch_shapes=GATHER_SCRATCH * 2,
+        out_shape=(jax.ShapeDtypeStruct((8 * tokens, width), BF16), *[jax.ShapeDtypeStruct(every, F32)] * 3),
+        in_specs=[ANYWHERE, *whole(1)],
+        out_specs=(ANYWHERE, *whole(3)),
+        scratch_shapes=[pltpu.VMEM(every, F32)] * 3 + GATHER_SCRATCH + [pltpu.SemaphoreType.DMA((9,))] * 2,
         compiler_params=mixer_params(3),
-    )(normed, cot)
+    )(normed, ids)
 
 
 def middle_step(mixed, w_out, own_in, gain):
@@ -760,55 +850,166 @@
     )(*lefts, *rights)
 
 
-def swap_kernel(groups, quarters, out, send, recv):
-    g, c = lax.axis_index("g"), lax.axis_index("c")
-    me = g * 2 + c
-    barrier = pltpu.get_barrier_semaphore()
-    for step in range(1, groups):
-        other = lax.rem(me + step, groups)
-        pl.semaphore_signal(barrier, inc=1, device_id={"g": other // 2, "c": other % 2}, device_id_type=MESH)
-    pl.semaphore_wait(barrier, groups - 1)
-    keep = pltpu.make_async_copy(quarters.at[me], out.at[:, me], send.at[0])
-    keep.start()
-    moved = []
-    for step in range(1, groups):
-        other = lax.rem(me + step, groups)
-        copy = pltpu.make_async_remote_copy(
-            src_ref=quarters.at[other],
-            dst_ref=out.at[:, me],
-            send_sem=send.at[step],
-            recv_sem=recv.at[step],
+class Swap:
+    def __init__(self, quarters, out, send, recv):
+        self.quarters, self.out, self.send, self.recv = quarters, out, send, recv
+        self.groups = quarters.shape[0]
+        self.me = lax.axis_index("g") * 2 + lax.axis_index("c")
+
+    def copy(self, step, other, slot):
+        return pltpu.make_async_remote_copy(
+            src_ref=self.quarters.at[other],
+            dst_ref=self.out.at[:, slot],
+            send_sem=self.send.at[step],
+            recv_sem=self.recv.at[step],
             device_id={"g": other // 2, "c": other % 2},
             device_id_type=MESH,
         )
-        copy.start()
-        moved.append(copy)
-    for step in range(1, groups):
-        other = lax.rem(me + groups - step, groups)
-        pltpu.make_async_remote_copy(
-            src_ref=quarters.at[other],
-            dst_ref=out.at[:, other],
-            send_sem=send.at[step],
-            recv_sem=recv.at[step],
-            device_id={"g": other // 2, "c": other % 2},
-            device_id_type=MESH,
-        ).wait_recv()
-    for copy in moved:
-        copy.wait_send()
-    keep.wait()
+
+    def peers(self):
+        others = [lax.rem(self.me + step, self.groups) for step in range(1, self.groups)]
+        return [{"g": other // 2, "c": other % 2} for other in others]
+
+    def begin(self):
+        self.keep = pltpu.make_async_copy(self.quarters.at[self.me], self.out.at[:, self.me], self.send.at[0])
+        self.keep.start()
+        self.moved = []
+        for step in range(1, self.groups):
+            self.moved.append(self.copy(step, lax.rem(self.me + step, self.groups), self.me))
+            self.moved[-1].start()
+
+    def finish(self):
+        for step in range(1, self.groups):
+            other = lax.rem(self.me + self.groups - step, self.groups)
+            self.copy(step, other, other).wait_recv()
+        for copy in self.moved:
+            copy.wait_send()
+        self.keep.wait()
+
+
+def swap_scratch(groups):
+    return [pltpu.SemaphoreType.DMA((groups,)), pltpu.SemaphoreType.DMA((groups,))]
+
+
+def swap_kernel(quarters, out, send, recv):
+    move = Swap(quarters, out, send, recv)
+    barrier = pltpu.get_barrier_semaphore()
+    for peer in move.peers():
+        pl.semaphore_signal(barrier, inc=1, device_id=peer, device_id_type=MESH)
+    pl.semaphore_wait(barrier, move.groups - 1)
+    move.begin()
+    move.finish()
 
 
 def swap(quarters):
     groups, kinds, part, width = quarters.shape
     return pl.pallas_call(
-        functools.partial(swap_kernel, groups),
+        swap_kernel,
         name="swap",
         out_shape=jax.ShapeDtypeStruct((kinds, groups, part, width), quarters.dtype),
         in_specs=[ANYWHERE],
         out_specs=ANYWHERE,
-        scratch_shapes=[pltpu.SemaphoreType.DMA((groups,)), pltpu.SemaphoreType.DMA((groups,))],
+        scratch_shapes=swap_scratch(groups),
         compiler_params=mixer_params(6),
     )(quarters)
+
+
+def small_kernel(count, with_gates, pieces, gains, gates_out, gains_out, rows_recv, gains_recv, gains_sum, gates_all, gains_all, send, recv):
+    place = Place()
+    me = lax.axis_index("t")
+    place.greet(
+        [place.peer(*offset) for offset in OTHERS if sum(offset) > 1]
+        + [{"t": lax.rem(me + step, count)} for step in range(1, count)]
+    )
+    own = place.chunk(0, 0, 0)
+    rank = place.g * 2 + place.c
+    moved = []
+
+    def move(number, source, target, peer):
+        copy = pltpu.make_async_remote_copy(
+            src_ref=source,
+            dst_ref=target,
+            send_sem=send.at[number],
+            recv_sem=recv.at[number],
+            device_id=peer,
+            device_id_type=MESH,
+        )
+        return copy
+
+    def start(*parts):
+        copy = move(*parts)
+        copy.start()
+        moved.append(copy)
+
+    for number, offset in enumerate(OTHERS):
+        peer, chunk = place.peer(*offset), place.chunk(*offset)
+        start(number, gains.at[chunk], gains_recv.at[own], peer)
+        if with_gates and not offset[0]:
+            start(7 + number, pieces.at[lax.rem(chunk, 4)], rows_recv.at[rank], peer)
+    gains_recv[own] = gains[own]
+    if with_gates:
+        rows_recv[rank] = pieces[rank]
+    for number, offset in enumerate(OTHERS):
+        peer, chunk = place.peer(*offset), place.chunk(*offset)
+        move(number, gains.at[chunk], gains_recv.at[chunk], peer).wait_recv()
+        if with_gates and not offset[0]:
+            other = lax.rem(chunk, 4)
+            move(7 + number, pieces.at[other], rows_recv.at[other], peer).wait_recv()
+    total = gains_recv[0]
+    for n in range(1, 8):
+        total = total + gains_recv[n]
+    gains_sum[...] = total
+    for step in range(1, count):
+        to = lax.rem(me + step, count)
+        start(10 + 2 * step, gains_sum, gains_all.at[me], {"t": to})
+        if with_gates:
+            start(11 + 2 * step, rows_recv.at[to], gates_all.at[me], {"t": to})
+    gains_all[me] = total
+    if with_gates:
+        gates_all[me] = rows_recv[me]
+    for step in range(1, count):
+        other = lax.rem(me + count - step, count)
+        move(10 + 2 * step, gains_sum, gains_all.at[other], {"t": other}).wait_recv()
+        if with_gates:
+            move(11 + 2 * step, rows_recv.at[other], gates_all.at[other], {"t": other}).wait_recv()
+    row = gains_all[0, pl.ds(me, 1), :]
+    for z in range(1, count):
+        row = row + gains_all[z, pl.ds(me, 1), :]
+    gains_out[...] = jnp.broadcast_to(row, gains_out.shape)
+    if with_gates:
+        gates = gates_all[0].astype(F32)
+        for z in range(1, count):
+            gates = gates + gates_all[z].astype(F32)
+        gates_out[...] = gates
+    else:
+        gates_out[...] = jnp.zeros_like(gates_out)
+    for copy in moved:
+        copy.wait_send()
+
+
+def small_step(planes, pieces, gains):
+    with_gates = pieces.shape[0] == planes
+    slots = max(planes, 4) if with_gates else 1
+    block = pieces.shape[1:] if with_gates else (16, LANES)
+    pieces = pieces if with_gates else jnp.zeros((1, *block), BF16)
+    sems = 12 + 2 * planes
+    return pl.pallas_call(
+        functools.partial(small_kernel, planes, with_gates),
+        name="small_step",
+        out_shape=(jax.ShapeDtypeStruct(block, F32), jax.ShapeDtypeStruct((8, LANES), F32)),
+        in_specs=whole(2),
+        out_specs=tuple(whole(2)),
+        scratch_shapes=[
+            pltpu.VMEM((slots, *block), BF16),
+            pltpu.VMEM(gains.shape, F32),
+            pltpu.VMEM(gains.shape[1:], F32),
+            pltpu.VMEM((slots, *block), BF16),
+            pltpu.VMEM((planes, *gains.shape[1:]), F32),
+            pltpu.SemaphoreType.DMA((sems,)),
+            pltpu.SemaphoreType.DMA((sems,)),
+        ],
+        compiler_params=mixer_params(9),
+    )(pieces, gains)
 
 
 def rms(values):
@@ -850,39 +1051,42 @@
     member = 2 * r + i
     first = member * channels
 
-    mixer_own = jnp.stack([in_weight[:, 0].T, in_weight[:, 1].T, out_weight.T])
-    if planes == row_groups:
-        part = channels // row_groups
-        quarter = lax.dynamic_slice_in_dim(mixer_own, r * part, part, 1)
-        mixer_w = swap(lax.all_gather(quarter, "t", axis=0, tiled=False))
+    own_in = inputs.reshape(own_tokens, width)
+    flat_in = own_in.astype(F32)
+    scale_in = rms(flat_in)
+    cot_own = cotangent.reshape(own_tokens, width)
+    own_ids = jnp.pad((segment_ids + 1).astype(F32), ((0, 8 - rows_here), (0, 0)))
+
+    normed, *ids = first_gather(planes, (flat_in * scale_in * mix_gain).astype(BF16), own_ids)
+    mlp_in, down_weight, normed = lax.optimization_barrier((mlp_in, down_weight, normed))
+
+    direct = planes == row_groups
+    in_own = in_weight.transpose(1, 2, 0)
+    out_own = out_weight.T[None]
+    part = channels // row_groups if direct else 0
+
+    def quarter(weight, part):
+        return lax.dynamic_slice_in_dim(weight, r * part, part, weight.ndim - 1)
+
+    def spread_units(weight):
+        return lax.all_gather(weight, "t", axis=0, tiled=False)
+
+    def whole_units(weight):
+        every = lax.all_gather(weight, ("t", "i"), axis=1, tiled=True)
+        return lax.dynamic_slice_in_dim(every, first, channels, 1)
+
+    if direct:
+        in_w = swap(spread_units(quarter(in_weight, part).transpose(1, 2, 0)))
+        out_quarters = spread_units(quarter(out_weight, part).T[None])
     else:
-        every = lax.all_gather(mixer_own, ("t", "i"), axis=1, tiled=True)
-        mixer_w = lax.dynamic_slice_in_dim(every, first, channels, 1)
-    mixer_w = mixer_w.reshape(3, channels, width)
-    w_gate, w_recur, w_out = mixer_w[0], mixer_w[1], mixer_w[2]
+        in_w = whole_units(in_own)
+        out_quarters = jnp.zeros((row_groups, 1, 16, width), BF16)
+    w_gate, w_recur = in_w.reshape(2, channels, width)
     hidden_part = mlp_in.shape[2] // row_groups
-
-    def own_part(weight):
-        return lax.dynamic_slice_in_dim(weight.T, r * hidden_part, hidden_part, 0)
-
-    mlp_w = jnp.concatenate([own_part(mlp_in[:, 0]), own_part(mlp_in[:, 1]), own_part(down_weight)], axis=0)
-    mlp_w = lax.all_gather(mlp_w, "t", axis=0, tiled=False)
-    mlp_w = mlp_w.reshape(planes, 3, hidden_part, width)
+    mlp_w = spread_units(quarter(mlp_in, hidden_part).transpose(1, 2, 0))
     w_left = mlp_w[:, 0].reshape(-1, width)
     w_right = mlp_w[:, 1].reshape(-1, width)
-    w_down = mlp_w[:, 2].reshape(-1, width)
-
-    ids = lax.all_gather((segment_ids + 1).astype(F32), ("g", "c"), axis=0, tiled=True)
-    ids = lax.all_gather(ids, ("t", "i"), axis=1, tiled=True)
-    span = 2 * seg
-    ids = jnp.pad(ids, ((0, 0), (HALO, HALO)))
-    ids = lax.dynamic_slice_in_dim(ids, t * span, span + 2 * HALO, 1)
-    here = ids[:, HALO : HALO + span]
-    columns = [(ids[:, HALO - k : HALO - k + span] == here) for k in (1, 2, 3)]
-    columns += [(ids[:, HALO + k : HALO + k + span] == here) for k in (1, 2, 3)]
-    columns += [jnp.zeros_like(columns[0])] * 2
-    mask = jnp.stack(columns, axis=-1).astype(F32)
-    mask = mask.reshape(mask.shape[0], 2, seg, 8).transpose(1, 0, 2, 3).reshape(-1, 8)
+    w_down = spread_units(quarter(down_weight, hidden_part).T).reshape(-1, width)
 
     def own(values):
         return lax.dynamic_slice_in_dim(values, first, channels, values.ndim - 1)
@@ -906,50 +1110,63 @@
     spread = spread.reshape(2, channels, channels)
     wg0, wg1 = spread[0], spread[1]
 
-    own_in = inputs.reshape(own_tokens, width)
-    flat_in = own_in.astype(F32)
-    scale_in = rms(flat_in)
-    cot_own = cotangent.reshape(own_tokens, width)
-    normed, cot = first_gather(planes, (flat_in * scale_in * mix_gain).astype(BF16), cot_own)
     gate_branch = nt(normed, w_gate, F32)
     recur = nt(normed, w_recur, BF16)
-    conv_low, decay, states, mixed, halo, cin = mixer_forward(planes, seg, recur, gate_branch, mask, wg0, wg1, vec)
+    conv_low, decay, states, mixed, halo, cin, mask, cot, w_out = mixer_forward(
+        planes, seg, rows_here, recur, gate_branch, ids, wg0, wg1, vec, cot_own, out_quarters
+    )
+    w_out = (w_out if direct else whole_units(out_own)).reshape(channels, width)
     middle, normed_two = middle_step(mixed, w_out, own_in, mlp_gain)
     left = nt(normed_two, w_left, F32)
     right = nt(normed_two, w_right, F32)
     act, slope = gelu_parts(left)
     hidden = (act * right).astype(BF16)
 
+    def over_planes(grad):
+        return lax.psum_scatter(grad, "t", scatter_dimension=0, tiled=True)
+
+    def to_owners(reduced):
+        return lax.all_to_all(reduced.reshape(members, -1, reduced.shape[1]), PLANE, 0, 0, tiled=True)
+
+    grad_down = tn(cot, hidden, BF16)
+    grad_down, hidden, w_down = lax.optimization_barrier((grad_down, hidden, w_down))
+    grad_down = over_planes(grad_down)
     grad_hidden = nt(cot, w_down, F32)
     grad_left = (grad_hidden * right * slope).astype(BF16)
     grad_right = (grad_hidden * act).astype(BF16)
+    grad_mlp_in = jnp.concatenate([tn(normed_two, grad_left, BF16), tn(normed_two, grad_right, BF16)], axis=1)
+    grad_mlp_in, grad_left, grad_right = lax.optimization_barrier((grad_mlp_in, grad_left, grad_right))
+    grad_mlp_in = over_planes(grad_mlp_in)
     grad_middle, grad_mlp_gain, grad_mid = turn_step(grad_left, grad_right, w_left, w_right, middle, mlp_gain, cot_own)
+    grad_down, grad_mid = lax.optimization_barrier((grad_down, grad_mid))
     grad_mlp_gain = jnp.sum(grad_mlp_gain, axis=0)
+    grad_out = tn(grad_mid, mixed, BF16)
     grad_mixed = nt(grad_mid, w_out, F32)
+    grad_out, grad_mixed = lax.optimization_barrier((grad_out, grad_mixed))
+    grad_out = over_planes(grad_out)
     grad_gate, grad_recur, gw0, gw1, small = mixer_backward(
         planes, seg, grad_mixed, gate_branch, states, decay, conv_low, recur, halo, cin, mask, wg0, wg1, wg0.T, wg1.T, vec
     )
+    grad_mlp_in, grad_gate, grad_recur = lax.optimization_barrier((grad_mlp_in, grad_gate, grad_recur))
+    grad_in = jnp.concatenate([tn(normed, grad_gate, BF16), tn(normed, grad_recur, BF16)], axis=1)
+    grad_in, grad_gate, grad_recur = lax.optimization_barrier((grad_in, grad_gate, grad_recur))
+    grad_in = over_planes(grad_in)
     grad_normed = scatter_step(7, [grad_gate, grad_recur], [w_gate, w_recur])
     grad_in_norm, grad_mix_gain = rms_back(flat_in, scale_in, mix_gain, grad_normed)
     grad_inputs = (grad_middle + grad_in_norm).reshape(inputs.shape)
+    grad_out, hidden, grad_normed = lax.optimization_barrier((grad_out, hidden, grad_normed))
     down = scatter_step(8, [hidden], [w_down])
     outputs = (middle + down).astype(BF16).reshape(inputs.shape)
 
-    def to_owners(grad):
-        reduced = lax.psum_scatter(grad, "t", scatter_dimension=0, tiled=True)
-        return lax.all_to_all(reduced.reshape(members, -1, grad.shape[1]), PLANE, 0, 0, tiled=True)
-
     own_rows = width // (planes * members)
-    mlp_grads = to_owners(
-        jnp.concatenate([tn(normed_two, grad_left, BF16), tn(normed_two, grad_right, BF16), tn(cot, hidden, BF16)], axis=1)
-    )
-    mixer_grads = to_owners(
-        jnp.concatenate([tn(normed, grad_gate, BF16), tn(normed, grad_recur, BF16), tn(grad_mid, mixed, BF16)], axis=1)
-    )
-    mlp_grads = mlp_grads.reshape(2, row_groups, own_rows, 3, planes, hidden_part).astype(F32)
-    mlp_grads = mlp_grads.transpose(2, 3, 4, 0, 1, 5).reshape(own_rows, 3, -1)
-    mixer_grads = mixer_grads.reshape(2, row_groups, own_rows, 3, channels).astype(F32)
-    mixer_grads = mixer_grads.transpose(2, 3, 1, 0, 4).reshape(own_rows, 3, -1)
+
+    def hidden_order(reduced, kinds):
+        grad = to_owners(reduced).reshape(2, row_groups, own_rows, kinds, planes, hidden_part).astype(F32)
+        return grad.transpose(2, 3, 4, 0, 1, 5).reshape(own_rows, kinds, -1)
+
+    def channel_order(reduced, kinds):
+        grad = to_owners(reduced).reshape(2, row_groups, own_rows, kinds, channels).astype(F32)
+        return grad.transpose(2, 3, 1, 0, 4).reshape(own_rows, kinds, -1)
 
     column_block = lax.broadcasted_iota(jnp.int32, (block_width, channels), 1) // block_width
 
@@ -959,30 +1176,38 @@
         )
 
     gate_grads = jnp.concatenate([diagonal(gw0), diagonal(gw1), small], axis=0)
-    if planes == row_groups:
+    pieces = jnp.zeros((0, 8, LANES), F32)
+    if direct:
         pieces = gate_grads.reshape(gate_grads.shape[0], row_groups, -1).transpose(1, 0, 2)
-        pieces = lax.all_to_all(pieces, ("g", "c"), 0, 0, tiled=True)
-        gate_grads = lax.psum_scatter(pieces, "t", scatter_dimension=0, tiled=False)
+        pieces = jnp.pad(pieces.astype(BF16), ((0, 0), (0, -pieces.shape[1] % 16), (0, LANES - part)))
+    gains = jnp.stack([grad_mlp_gain, grad_mix_gain]).reshape(2, planes, members, own_rows)
+    gains = gains.transpose(2, 1, 0, 3).reshape(members, planes, 2 * own_rows)
+    short = LANES - 2 * own_rows
+    gains = jnp.pad(gains, ((0, 0), (0, -planes % 8), (0, short)))
+    gate_sums, gains = small_step(planes, pieces, gains)
+    if direct:
+        gate_grads = gate_sums[:, :part]
     else:
         placed = jnp.zeros((gate_grads.shape[0], recur_width), F32)
         placed = lax.dynamic_update_slice_in_dim(placed, gate_grads, first, 1)
         gate_grads = lax.psum_scatter(placed, EVERY, scatter_dimension=1, tiled=True)
     grad_gate_weight = jnp.stack([gate_grads[:block_width], gate_grads[block_width : 2 * block_width]], axis=1)
-    small = gate_grads[2 * block_width :]
+    small = gate_grads[2 * block_width : 2 * block_width + 8]
+    mlp_in_grads = hidden_order(grad_mlp_in, 2)
     return (
         outputs,
         grad_inputs,
-        lax.psum_scatter(grad_mix_gain, EVERY, scatter_dimension=0, tiled=True),
-        mixer_grads[:, :2],
+        gains[0, own_rows : 2 * own_rows],
+        channel_order(grad_in, 2),
         small[0:4],
         small[4],
         grad_gate_weight,
         small[5:7],
         small[7],
-        mixer_grads[:, 2],
-        lax.psum_scatter(grad_mlp_gain, EVERY, scatter_dimension=0, tiled=True),
-        mlp_grads[:, :2],
-        mlp_grads[:, 2],
+        channel_order(grad_out, 1)[:, 0],
+        gains[0, :own_rows],
+        mlp_in_grads,
+        hidden_order(grad_down, 1)[:, 0],
     )
 
 

time: 923 us -> 792 us (0.86)
  blocking collectives: 80.8 us -> 0 us
  waiting for transfers between devices: 46.5 us -> 24.5 us
  local copies, waits for them, and re-layouts: 122 us -> 107 us
  Pallas kernels: 512 us -> 498 us
    reduce_scatter x3 -> x4, waiting for transfers between devices: 45.9 us -> 0.06 us  [over_planes(): return lax.psum_scatter(grad, 't', scatter_dimension=0, tiled=True)]
    unnamed x1 -> x0, blocking collectives: 42.9 us -> none
    all_gather x2 -> x0, blocking collectives: 37.9 us -> none  [the longest x1 32.1 us: per_device(): ids = lax.all_gather(ids, ('t', 'i'), axis=1, tiled=True)]
    optimization_barrier x0 -> x5, local copies, waits for them, and re-layouts: none -> 25.9 us  [the longest x2 20.9 us: per_device(): lax.optimization_barrier((mlp_in, down_weight, normed))]
    all_to_all x3 -> x4, waiting for transfers between devices: 0.01 us -> 24.2 us  [to_owners(): lax.all_to_all(reduced.reshape(members, -1, reduced.shape[1]), PLANE, 0,...]
    slice x7 -> x1, local copies, waits for them, and re-layouts: 24 us -> 3.59 us  [per_device(): w_left = mlp_w[:, 0].reshape(-1, width)]
    unnamed x85 -> x74, local copies, waits for them, and re-layouts: 26.7 us -> 8.24 us
    pallas_call x2, Pallas kernels: 108 us -> 97.2 us  [scatter_step(): pl.pallas_call(functools.partial(scatter_kernel, len(lefts)), name='scatt...]
  transfers between devices with their start and end apart: 8 -> 12, of which waited for: 2 -> 2; matrix products, arithmetic and copies ran while one was open for 15% -> 27% of each run, Pallas kernels for 39% -> 63%
where the time goes in v3:
time: 792 us; the launch traced here: 787 us
  Pallas kernels  498 us (63%)
  matrix products  109 us (14%)
  local copies, waits for them, and re-layouts  107 us (14%)
  waiting for transfers between devices  24.5 us (3%)
  other arithmetic  17.3 us (2%)
  starting transfers between devices  15.7 us (2%)
  between operations  15.4 us (2%)
    pallas_call x2, Pallas kernels, scatter_step(): pl.pallas_call(functools.partial(scatter_kernel, len(lefts)), name='scatt...  97.2 us
    pallas_call x1, Pallas kernels, turn_step(): pl.pallas_call(turn_kernel, name='turn_step', out_shape=(jax.ShapeDtypeSt...  95.8 us
    pallas_call x1, Pallas kernels, middle_step(): pl.pallas_call(middle_kernel, name='middle_step', out_shape=(jax.ShapeDty...  88 us
    pallas_call x1, Pallas kernels, mixer_forward(): pl.pallas_call(functools.partial(mixer_forward_kernel, count, seg, rows_h...  62 us
    dot_general x6, matrix products, nt(): lax.dot_general(left, right, (((1,), (1,)), ((), ())), preferred_element_...  62 us
    pallas_call x1, Pallas kernels, mixer_backward(): pl.pallas_call(functools.partial(mixer_backward_kernel, count, seg), name...  55.5 us
    pallas_call x1, Pallas kernels, first_gather(): pl.pallas_call(functools.partial(first_gather_kernel, planes), name='firs...  48.4 us
    dot_general x6, matrix products, tn(): lax.dot_general(left, right, (((0,), (0,)), ((), ())), preferred_element_...  46.8 us
  transfers between devices with their start and end apart: 12, of which 2 were waited for; matrix products, arithmetic and copies ran while one was open for 27% of the time, Pallas kernels for 63%

profile of v3, /device:TPU:0, one launch (start us, length us, event | category | flops | bytes accessed | tf_op | source)
XLA Modules:
  0.0 786.7 jit_solution(221103009781626998)
XLA Ops:
  15.9 48.4 %first_gather.1 = (bf16[2048,2048]{1,0:T(8,128)(2,1)}, f32[8,8,128]{2,1,0:T(8,128)}, f32[8,8,128]{2,1,0:T(8,128)}, f32[8,8,128]{2,1,0:T(8,128)}) custom-call(bf16[256,2048]{1,0:T(8,128)(2,1)} %fusion.2.normed, f32[8,128]{1,0:T(8,128)} %pad.21.ids), custom_call_target="tpu_custom_call" | custom-call | tf_op jit(solution)/shard_map/first_gather/pallas_call | solution.py:799
  64.3 16.2 %copy.99 = bf16[2048,2,768]{0,2,1:T(8,128)(2,1)} copy(bf16[2048,2,768]{2,1,0:T(2,128)(2,1)} %param.29) | data formatting | bytes 12582912 | tf_op jit(solution)/shard_map/optimization_barrier | solution.py:1061
  100.2 30.5 %swap.1 = bf16[2,4,80,2048]{3,2,1,0:T(8,128)(2,1)} custom-call(bf16[4,2,80,2048]{3,2,1,0:T(8,128)(2,1)} %bitcast.122), custom_call_target="tpu_custom_call" | custom-call | tf_op jit(solution)/shard_map/swap/pallas_call | solution.py:906
  133.0 10.1 %convolution_convert_fusion.3.recur = bf16[2048,320]{1,0:T(8,128)(2,1)} fusion(bf16[2048,2048]{1,0:T(8,128)(2,1)} %get-tuple-element.84, bf16[320,2048]{1,0:T(8,128)(2,1)S(1)} %bitcast.118), kind=kOutput, calls=%fused_computation.14 | convolution fusion | flops 2685009920 | bytes 11010048 | tf_op jit(solution)/shard_map/dot_general | solution.py:1026
  143.2 6.3 fusion.25.gate
  149.5 62.0 %mixer_forward.1 = (bf16[2048,320]{1,0:T(8,128)(2,1)}, f32[3,2048,128]{2,1,0:T(8,128)}, f32[2048,320]{1,0:T(8,128)}, bf16[2048,320]{1,0:T(8,128)(2,1)}, f32[128,...) custom-call(bf16[2048,320]{1,0:T(8,128)(2,1)} %convolution_convert_f, ...), custom_call_target="tpu_custom_call" | custom-call | tf_op jit(solution)/shard_map/mixer_forward/pallas_call | solution.py:360
  211.5 88.0 %middle_step.1 = (f32[256,2048]{1,0:T(8,128)}, bf16[2048,2048]{1,0:T(8,128)(2,1)}) custom-call(bf16[2048,320]{1,0:T(8,128)(2,1)} %get-tuple-element.88.left, bf16[320,2048]{1,0:T(8,128)(2,1)} %bitcast.129, bf16[256,2048]{1,0:T(8,128)(2,1)} %bitcast.107, f32[1,2048]{1,0:T(1,128)} %bitcast.134), custom_call_target="tpu_custom_call" | custom-call | tf_op jit(solution)/shard_map/middle_step/pallas_call | solution.py:812
  306.4 8.5 %fusion.26 = f32[2048,768]{1,0:T(8,128)} fusion(bf16[2048,2048]{1,0:T(8,128)(2,1)S(1)} %copy-done.30, bf16[768,2048]{1,0:T(8,128)(2,1)S(1)} %bitcast.109), kind=kOutput, calls=%fused_computation.77 | convolution fusion | flops 6442450944 | bytes 17825792 | tf_op jit(solution)/shard_map/dot_general | solution.py:1026
  314.9 14.4 %multiply_convert_fusion.2 = (bf16[2048,768]{1,0:T(8,128)(2,1)S(1)}, f32[2048,768]{1,0:T(8,128)}) fusion(f32[2048,768]{1,0:T(8,128)} %fusion.26, bf16[2048,2048]{1,0:T(8,128)(2,1)} %get-tuple-element.92, bf16[768,2048]{1,0:T(8,128)(2,1)S(1)} %bitcast.111), kind=kOutput, calls=%fused_computation.3 | convolution fusion | flops 6458179584 | bytes 27262976 | tf_op jit(solution)/shard_map/dot_general | solution.py:1026
  331.0 8.5 %convolution_convert_fusion.2 = bf16[2048,768]{1,0:T(8,128)(2,1)} fusion(bf16[2048,2048]{1,0:T(8,128)(2,1)S(1)} %bitcast.139, bf16[2048,768]{1,0:T(8,128)(2,1)S(1)} %get-tuple-element.117.refs_0_), kind=kOutput, calls=%fused_computation.13 | convolution fusion | flops 6444023808 | bytes 14680064 | tf_op jit(solution)/shard_map/dot_general | solution.py:1030
  339.6 16.7 %multiply_convert_fusion.1 = (bf16[2048,768]{1,0:T(8,128)(2,1)S(1)}, bf16[2048,768]{1,0:T(8,128)(2,1)S(1)}) fusion(f32[2048,768]{1,0:T(8,128)} %fusion.26, f32[2048,768]{1,0:T(8,128)} %get-tuple-element.204, bf16[2048,2048]{1,0:T(8,128)(2,1)} %get-tuple-element.91, bf16[768,2048]{1,0:T(8,128)(2,1)} %all-gather.15.cloned.1.call-done.refs_1_), kind=kOutput, calls=%fused_computation.2 | convolution fusion | flops 6477053952 | bytes 30408704 | tf_op jit(solution)/shard_map/dot_general | solution.py:1026
  356.3 11.6 %convolution_convert_fusion = bf16[2048,768]{0,1:T(8,128)(2,1)S(1)} fusion(bf16[2048,2048]{1,0:T(8,128)(2,1)} %get-tuple-element.92, bf16[2048,768]{1,0:T(8,128)(2,1)S(1)} %get-tuple-element.98.left1), kind=kOutput, calls=%fused_computation.11 | convolution fusion | flops 6444023808 | bytes 14680064 | tf_op jit(solution)/shard_map/dot_general | solution.py:1030
  367.9 9.3 %convolution_convert_fusion.1 = bf16[2048,768]{0,1:T(8,128)(2,1)S(1)} fusion(bf16[2048,2048]{1,0:T(8,128)(2,1)} %get-tuple-element.92, bf16[2048,768]{1,0:T(8,128)(2,1)S(1)} %get-tuple-element.97.left0), kind=kOutput, calls=%fused_computation.12 | convolution fusion | flops 6444023808 | bytes 14680064 | tf_op jit(solution)/shard_map/dot_general | solution.py:1030
  380.7 95.8 %turn_step.1 = (f32[256,2048]{1,0:T(8,128)}, f32[8,2048]{1,0:T(8,128)}, bf16[2048,2048]{1,0:T(8,128)(2,1)}) custom-call(bf16[2048,768]{1,0:T(8,128)(2,1)} %copy-done.9, bf16[2048,768]{1,0:T(8,128)(2,1)} %copy-done.10, bf16[768,2048]{1,0:T(8,128)(2,1)} %bitcast.110, bf16[768,2048]{1,0:T(8,128)(2,1)} %bitcast.112, f32[256,2048]{1,0:T(8,128)} %get-tuple-element.90.middle, ...), custom_call_target="tpu_custom_call" | custom-call | tf_op jit(solution)/shard_map/turn_step/pallas_call | solution.py:825
  490.0 55.5 %mixer_backward.1 = (bf16[2048,320]{1,0:T(8,128)(2,1)}, bf16[2048,320]{1,0:T(8,128)(2,1)}, f32[320,320]{1,0:T(8,128)}, f32[320,320]{1,0:T(8,128)}, f32[8,320]{1,0:T(8,128)}) custom-call(f32[2048,320]{1,0:T(8,128)} %copy.101.grad_mixed, f32[2048,320]{1,0:T(8,128)} %fusion.25.gate, f32[2048,320]{1,0:T(8,128)} %get-tuple-element.105.states, ...), custom_call_target="tpu_custom_call" | custom-call | tf_op jit(solution)/shard_map/mixer_backward/pallas_call | solution.py:396
  545.5 6.9 convolution_convert_fusion.4
  552.4 6.3 convolution_convert_fusion.5
  565.9 11.0 %all-to-all-done.3 = bf16[8,64,768]{2,1,0:T(8,128)(2,1)S(1)} async-done(((bf16[8,64,768]{2,1,0:T(8,128)(2,1)}), bf16[8,64,768]{2,1,0:T(8,128)(2,1)S(1)}, u32[]{:S(2)}, u32[]{:S(2)}) %all-to-all-start.3) | async-done | bytes 786464 | tf_op jit(solution)/shard_map/all_to_all | solution.py:1129
  585.6 48.5 %scatter_step.2 = f32[256,2048]{1,0:T(8,128)} custom-call(bf16[2048,320]{1,0:T(8,128)(2,1)} %get-tuple-element.115.refs_0_, bf16[2048,320]{1,0:T(8,128)(2,1)} %get-tuple-element.116.refs_1_, bf16[320,2048]{1,0:T(8,128)(2,1)} %bitcast.117, bf16[320,2048]{1,0:T(8,128)(2,1)} %bitcast.119), custom_call_target="tpu_custom_call" | custom-call | tf_op jit(solution)/shard_map/scatter_step/pallas_call | solution.py:842
  641.6 20.6 %small_step.1 = (f32[336,128]{1,0:T(8,128)}, f32[8,128]{1,0:T(8,128)}) custom-call(bf16[4,336,128]{2,1,0:T(8,128)(2,1)} %pad.22.pieces, f32[8,8,128]{2,1,0:T(8,128)} %pad.23.gains), custom_call_target="tpu_custom_call" | custom-call | tf_op jit(solution)/shard_map/small_step/pallas_call | solution.py:996
  666.0 48.7 %scatter_step.3 = f32[256,2048]{1,0:T(8,128)} custom-call(bf16[2048,768]{1,0:T(8,128)(2,1)} %copy-done.11, bf16[768,2048]{1,0:T(8,128)(2,1)} %all-gather.15.cloned.1.call-done.refs_1_), custom_call_target="tpu_custom_call" | custom-call | tf_op jit(solution)/shard_map/scatter_step/pallas_call | solution.py:842
  727.9 13.2 %all-to-all-done.2 = bf16[8,64,1536]{2,1,0:T(8,128)(2,1)S(1)} async-done(((bf16[8,64,1536]{2,1,0:T(8,128)(2,1)}), bf16[8,64,1536]{2,1,0:T(8,128)(2,1)S(1)}, u32[]{:S(2)}, u32[]{:S(2)}) %all-to-all-start.2) | async-done | bytes 1572896 | tf_op jit(solution)/shard_map/all_to_all | solution.py:1129
  754.4 6.9 copy.113
  761.3 6.9 reshape.271
  (183 shorter events, 120.2 us)
Async XLA Ops:
  7.2 93.0 %all-gather.9.cloned.1.call-start = ((), (), s32[]{:S(2)}) async-start(), calls=%async_computation.12 | async-start | bytes 3276800 | tf_op jit(solution)/shard_map/all_gather | solution.py:1072
  9.8 139.7 %all-gather.11.cloned.1.call-start = ((), (), s32[]{:S(2)}) async-start(), calls=%async_computation.13 | async-start | bytes 1638400 | tf_op jit(solution)/shard_map/all_gather | solution.py:1072
  11.7 287.9 %all-gather.13.cloned.1.call-start = ((), (), s32[]{:S(2)}) async-start(), calls=%async_computation.14 | async-start | bytes 7864320 | tf_op jit(solution)/shard_map/all_gather | solution.py:1072
  14.6 66.0 %copy-start.28 = (f32[2,128]{1,0:T(2,128)}, f32[2,128]{1,0:T(2,128)S(1)}, u32[]{:S(2)}) copy-start(f32[2,128]{1,0:T(2,128)S(1)} %multiply_reduce_fusion) | copy-start | bytes 3076
  14.6 66.0 %copy-start.25 = (f32[256]{0:T(256)}, f32[256]{0:T(256)S(1)}, u32[]{:S(2)}) copy-start(f32[256]{0:T(256)S(1)} %rsqrt_bitcast_fusion) | copy-start | bytes 3076
  83.3 256.2 %all-gather.15.cloned.1.call-start = ((), (), s32[]{:S(2)}) async-start(), calls=%async_computation.15 | async-start | bytes 3932160 | tf_op jit(solution)/shard_map/all_gather | solution.py:1072
  90.2 386.4 %reduce-scatter.5.cloned.1.call-start = ((), (), s32[]{:S(2)}) async-start(), calls=%async_computation.8 | async-start | bytes 3932160 | tf_op jit(solution)/shard_map/reduce_scatter | solution.py:1126
  93.5 37.2 %copy-start.12 = (bf16[320,320]{0,1:T(8,128)(2,1)}, bf16[320,320]{0,1:T(8,128)(2,1)S(1)}, u32[]{:S(2)}) copy-start(bf16[320,320]{0,1:T(8,128)(2,1)S(1)} %squeeze.26) | copy-start | bytes 614404
  95.0 38.0 %copy-start.13 = (bf16[320,320]{0,1:T(8,128)(2,1)}, bf16[320,320]{0,1:T(8,128)(2,1)S(1)}, u32[]{:S(2)}) copy-start(bf16[320,320]{0,1:T(8,128)(2,1)S(1)} %squeeze.27) | copy-start | bytes 614404
  130.8 12.4 %slice-start = ((s8[8388608]{0:T(1024)(128)(4,1)}), s8[4194304]{0:T(1024)(128)(4,1)S(1)}, s32[]{:S(2)}) async-start(s8[8388608]{0:T(1024)(128)(4,1)} %bitcast.136), calls=%async_computation.16 | async-start | bytes 8388608
  303.2 11.7 %copy-start.5 = (bf16[4,1,192,2048]{3,2,1,0:T(8,128)(2,1)}, bf16[4,1,192,2048]{3,2,1,0:T(8,128)(2,1)S(1)}, u32[]{:S(2)}) copy-start(bf16[4,1,192,2048]{3,2,1,0:T(8,128)(2,1)S(1)} %get-tuple-element.185) | copy-start | bytes 9437188
  306.4 24.6 %slice-start.2 = ((s8[8388608]{0:T(1024)(128)(4,1)}), s8[4194304]{0:T(1024)(128)(4,1)S(1)}, s32[]{:S(2)}) async-start(s8[8388608]{0:T(1024)(128)(4,1)} %bitcast.138), calls=%async_computation.18 | async-start | bytes 8388608
  314.9 16.1 %slice-start.3 = ((s8[8388608]{0:T(1024)(128)(4,1)}), s8[4194304]{0:T(1024)(128)(4,1)S(1)}, s32[]{:S(2)}) async-start(s8[8388608]{0:T(1024)(128)(4,1)} %bitcast.138), calls=%async_computation.19 | async-start | bytes 8388608
  339.6 205.9 %reduce-scatter.9.cloned.1.call-start = ((), (), s32[]{:S(2)}) async-start(), calls=%async_computation.10 | async-start | bytes 7864320 | tf_op jit(solution)/shard_map/reduce_scatter | solution.py:1126
  380.7 253.5 %reduce-scatter.7.cloned.1.call-start = ((), (), s32[]{:S(2)}) async-start(), calls=%async_computation.9 | async-start | bytes 1638400 | tf_op jit(solution)/shard_map/reduce_scatter | solution.py:1126
  487.5 238.3 %reduce-scatter.11.cloned.1.call-start = ((), (), s32[]{:S(2)}) async-start(), calls=%async_computation.11 | async-start | bytes 3276800 | tf_op jit(solution)/shard_map/reduce_scatter | solution.py:1126
  560.4 16.4 %all-to-all-start.3 = ((bf16[8,64,768]{2,1,0:T(8,128)(2,1)}), bf16[8,64,768]{2,1,0:T(8,128)(2,1)S(1)}, u32[]{:S(2)}, u32[]{:S(2)}) async-start(bf16[8,64,768]{2,1,0:T(8,128)(2,1)} %bitcast.40), calls=%async_computation.7 | async-start | bytes 1572864 | tf_op jit(solution)/shard_map/all_to_all | solution.py:1129
  585.6 48.5 %copy-start.3 = (bf16[2,128,2048]{2,1,0:T(8,128)(2,1)S(1)}, bf16[2,128,2048]{2,1,0:T(8,128)(2,1)}, u32[]{:S(2)}) copy-start(bf16[2,128,2048]{2,1,0:T(8,128)(2,1)} %param.18) | copy-start | bytes 3145732
  585.6 48.6 %copy-start.23 = (f32[2048]{0:T(1024)S(1)}, f32[2048]{0:T(1024)}, u32[]{:S(2)}) copy-start(f32[2048]{0:T(1024)} %param.20) | copy-start | bytes 24580
  585.6 48.6 %copy-start.26 = (f32[256]{0:T(256)S(1)}, f32[256]{0:T(256)}, u32[]{:S(2)}) copy-start(f32[256]{0:T(256)} %copy-done.25) | copy-start | bytes 3076
  638.2 78.2 %all-to-all-start.1 = ((bf16[8,64,320]{2,1,0:T(8,128)(2,1)}), bf16[8,64,320]{2,1,0:T(8,128)(2,1)S(1)}, u32[]{:S(2)}, u32[]{:S(2)}) async-start(bf16[8,64,320]{2,1,0:T(8,128)(2,1)} %bitcast.34), calls=%async_computation.5 | async-start | bytes 786432 | tf_op jit(solution)/shard_map/all_to_all | solution.py:1129
  666.0 48.7 %copy-start.15 = (bf16[512,1536]{0,1:T(8,128)(2,1)S(1)}, bf16[512,1536]{0,1:T(8,128)(2,1)}, u32[]{:S(2)}) copy-start(bf16[512,1536]{0,1:T(8,128)(2,1)} %reduce-scatter.9.cloned.1.call-done) | copy-start | bytes 4718596
  716.3 24.8 %all-to-all-start.2 = ((bf16[8,64,1536]{2,1,0:T(8,128)(2,1)}), bf16[8,64,1536]{2,1,0:T(8,128)(2,1)S(1)}, u32[]{:S(2)}, u32[]{:S(2)}) async-start(bf16[8,64,1536]{2,1,0:T(8,128)(2,1)} %bitcast.38), calls=%async_computation.6 | async-start | bytes 3145728 | tf_op jit(solution)/shard_map/all_to_all | solution.py:1129
  741.1 27.1 %all-to-all-start = ((bf16[8,64,640]{2,1,0:T(8,128)(2,1)}), bf16[8,64,640]{2,1,0:T(8,128)(2,1)}, u32[]{:S(2)}, u32[]{:S(2)}) async-start(bf16[8,64,640]{2,1,0:T(8,128)(2,1)} %bitcast.28), calls=%async_computation.4 | async-start | bytes 1310720 | tf_op jit(solution)/shard_map/all_to_all | solution.py:1129
  (24 other events, 152.0 us)
Sparse Core Ops, SparseCore 0:
  10.2 58.8 all-gather.8
  70.6 31.4 all-gather.10
  104.3 118.5 all-gather.12
  224.9 61.6 all-gather.14
  339.7 59.0 reduce-scatter.4
  401.0 110.7 reduce-scatter.8
  514.1 33.8 reduce-scatter.6
  560.6 49.8 reduce-scatter.10

commit v4 on v3

--- a/solution.py
+++ b/solution.py
@@ -214,10 +214,14 @@
 
 def mixer_backward_kernel(
     count, seg, grad_mixed, gate, states, decay, conv_low_ref, recur, halo, cin, mask, wg0, wg1, wg0t, wg1t, vec_ref,
-    grad_gate_out, grad_recur_out, gw0_out, gw1_out, small_out,
-    tot, prod, gc, ext, halo_send, halo_recv, summary, slots, uin, send_sem, recv_sem, halo_sems,
+    hidden, w_down, grad_gate_out, grad_recur_out, gw0_out, gw1_out, small_out, down_out,
+    tot, prod, ext, halo_send, halo_recv, summary, slots, uin, send_sem, recv_sem, halo_sems, *buffers,
 ):
-    me = greet(count)
+    place = Place()
+    me = lax.axis_index("t")
+    place.greet([{"t": lax.rem(me + step, count)} for step in range(1, count)])
+    scatter = Scatter(place, pair_product([hidden], [w_down], down_out.shape[0]), *buffers)
+    scatter.run_first()
     rows = 8
     width = recur.shape[1]
     vec = vec_ref[...]
@@ -250,6 +254,7 @@
     last = lax.fori_loop(0, seg, scan, (start,) * tiles, unroll=4)
     u = join_tiles([part[0] for part in last], width)
     p = join_tiles([part[1] for part in last], width)
+    scatter.run_second()
     summary[0:rows, :] = p[:rows] * p[rows:]
     summary[rows : 2 * rows, :] = p[:rows] * u[rows:] + u[:rows]
     exchange(count, me, summary, slots, send_sem, recv_sem)
@@ -286,7 +291,7 @@
             + jnp.dot(low0, wg0t[...], preferred_element_type=F32)
             + jnp.dot(low1, wg1t[...], preferred_element_type=F32)
         )
-        gc[at, :] = grad_conv
+        put_tiles(tot, at, grad_conv)
         turned = (((0,), (0,)), ((), ()))
         gw0_out[...] += lax.dot_general(conv_low, low0, turned, preferred_element_type=F32)
         gw1_out[...] += lax.dot_general(conv_low, low1, turned, preferred_element_type=F32)
@@ -309,7 +314,7 @@
     lax.fori_loop(0, 2 * rows, gates, 0)
     small_out[7:8, :] = small_out[7:8, :] * vec[8:9]
     for r in range(rows):
-        halo_send[r * HALO : (r + 1) * HALO, :] = gc[r * seg : r * seg + HALO, :]
+        halo_send[r * HALO : (r + 1) * HALO, :] = get_tiles(tot, pl.ds(r * seg, HALO), width)
     halo_copy = pltpu.make_async_remote_copy(
         src_ref=halo_send,
         dst_ref=halo_recv,
@@ -324,12 +329,13 @@
     def back(s, none):
         at = pl.ds(pl.multiple_of(s * seg, seg), seg)
         m = mask[at, :]
-        ext[0:seg, :] = gc[at, :]
-        result = vec[0:1] * gc[at, :]
+        grad_conv = get_tiles(tot, at, width)
+        ext[0:seg, :] = grad_conv
+        result = vec[0:1] * grad_conv
 
         @pl.when(s < rows)
         def _():
-            ext[seg : seg + HALO, :] = gc[pl.ds(pl.multiple_of((s + rows) * seg, seg), HALO), :]
+            ext[seg : seg + HALO, :] = get_tiles(tot, pl.ds(pl.multiple_of((s + rows) * seg, seg), HALO), width)
 
         @pl.when(s >= rows)
         def _():
@@ -341,6 +347,13 @@
         return none
 
     lax.fori_loop(0, 2 * rows, back, 0)
+    scatter.run_third()
+
+    def body(at):
+        down_out[at, :] = scatter.rows(at)
+
+    for_slices(0, down_out.shape[0], body)
+    scatter.finish()
 
 
 def whole(count):
@@ -388,8 +401,9 @@
     )(recur, gate, *ids, wg0, wg1, vec, cot, quarters)
 
 
-def mixer_backward(count, seg, grad_mixed, gate, states, decay, conv_low, recur, halo, cin, mask, wg0, wg1, wg0t, wg1t, vec):
+def mixer_backward(count, seg, grad_mixed, gate, states, decay, conv_low, recur, halo, cin, mask, wg0, wg1, wg0t, wg1t, vec, hidden, w_down):
     n, width = recur.shape
+    tokens, depth = n // 8, w_down.shape[1]
     full = functools.partial(jax.ShapeDtypeStruct, (n, width))
     tiles = -(-width // LANES)
     tiled = jax.ShapeDtypeStruct((tiles, n, LANES), F32)
@@ -399,14 +413,13 @@
         out_shape=(
             full(BF16), full(BF16),
             jax.ShapeDtypeStruct((width, width), F32), jax.ShapeDtypeStruct((width, width), F32),
-            jax.ShapeDtypeStruct((8, width), F32),
+            jax.ShapeDtypeStruct((8, width), F32), jax.ShapeDtypeStruct((tokens, depth), F32),
         ),
-        in_specs=whole(14),
-        out_specs=tuple(whole(5)),
+        in_specs=whole(16),
+        out_specs=tuple(whole(6)),
         scratch_shapes=[
             pltpu.VMEM((tiles, n, LANES), F32),
             pltpu.VMEM((tiles, n, LANES), F32),
-            pltpu.VMEM((n, width), F32),
             pltpu.VMEM((seg + HALO, width), F32),
             pltpu.VMEM((8 * HALO, width), F32),
             pltpu.VMEM((8 * HALO, width), F32),
@@ -416,9 +429,10 @@
             pltpu.SemaphoreType.DMA((count,)),
             pltpu.SemaphoreType.DMA((count,)),
             pltpu.SemaphoreType.DMA((2,)),
+            *Scatter.scratch(tokens, depth),
         ],
         compiler_params=mixer_params(2),
-    )(grad_mixed, gate, states, decay, conv_low, recur, halo, cin, mask, wg0, wg1, wg0t, wg1t, vec)
+    )(grad_mixed, gate, states, decay, conv_low, recur, halo, cin, mask, wg0, wg1, wg0t, wg1t, vec, hidden, w_down)
 
 
 class Place:
@@ -613,6 +627,11 @@
         self.kept.append(moved)
 
     def run(self):
+        self.run_first()
+        self.run_second()
+        self.run_third()
+
+    def run_first(self):
         place = self.place
         order = ((1, 1), (0, 1), (1, 0), (0, 0))
         tile = 256
@@ -657,6 +676,9 @@
         give(*order[3])
         take(*order[2])
         take(*order[3])
+
+    def run_second(self):
+        place = self.place
         for half, number, buffer, mine, peer, out in (
             (0, 5, self.across_recv, 2, place.along, 8),
             (1, 7, self.along_recv, 1, place.across, 9),
@@ -671,6 +693,9 @@
 
             lax.fori_loop(0, self.held.shape[2] // SLICE, add_rows, 0)
             self.start(out, self.second.at[half], self.second_recv.at[half], peer)
+
+    def run_third(self):
+        place = self.place
         for number, buffer in ((4, self.across_recv), (6, self.along_recv)):
             self.copy(number, buffer.at[0], buffer.at[0], place.core).wait_recv()
         for number, half in ((8, 0), (9, 1)):
@@ -778,19 +803,261 @@
     gather.finish()
 
 
-def scatter_kernel(count, *refs):
-    lefts, rights, out, buffers = refs[:count], refs[count : 2 * count], refs[2 * count], refs[2 * count + 1 :]
-    tokens = out.shape[0]
+class Owners:
+    def __init__(self, place, reduced, out, send, recv):
+        self.place, self.reduced, self.out, self.send, self.recv = place, reduced, out, send, recv
+        self.own = place.chunk(0, 0, 0)
+
+    def copy(self, number, offset, slot):
+        return pltpu.make_async_remote_copy(
+            src_ref=self.reduced.at[self.place.chunk(*offset)],
+            dst_ref=self.out.at[slot],
+            send_sem=self.send.at[number],
+            recv_sem=self.recv.at[number],
+            device_id=self.place.peer(*offset),
+            device_id_type=MESH,
+        )
+
+    def begin(self):
+        self.keep = pltpu.make_async_copy(self.reduced.at[self.own], self.out.at[self.own], self.send.at[7])
+        self.keep.start()
+        self.moved = [self.copy(number, offset, self.own) for number, offset in enumerate(OTHERS)]
+        for copy in self.moved:
+            copy.start()
+
+    def finish(self):
+        for number, offset in enumerate(OTHERS):
+            self.copy(number, offset, self.place.chunk(*offset)).wait_recv()
+        for copy in self.moved:
+            copy.wait_send()
+        self.keep.wait()
+
+
+OWNERS_SCRATCH = [pltpu.SemaphoreType.DMA((8,))] * 2
+BEYOND = [offset for offset in OTHERS if sum(offset) > 1]
+
+
+class GateSums:
+    def __init__(self, place, count, pieces, rows_recv, gates_all, send, recv):
+        self.place, self.count, self.pieces = place, count, pieces
+        self.rows_recv, self.gates_all, self.send, self.recv = rows_recv, gates_all, send, recv
+        self.me = lax.axis_index("t")
+        self.rank = place.g * 2 + place.c
+        self.near = [offset for offset in OTHERS if not offset[0]]
+        self.moved = []
+
+    def copy(self, number, source, target, peer):
+        return pltpu.make_async_remote_copy(
+            src_ref=source,
+            dst_ref=target,
+            send_sem=self.send.at[number],
+            recv_sem=self.recv.at[number],
+            device_id=peer,
+            device_id_type=MESH,
+        )
+
+    def begin(self):
+        for number, offset in enumerate(self.near):
+            other = lax.rem(self.place.chunk(*offset), 4)
+            self.moved.append(self.copy(number, self.pieces.at[other], self.rows_recv.at[self.rank], self.place.peer(*offset)))
+            self.moved[-1].start()
+        self.rows_recv[self.rank] = self.pieces[self.rank]
+
+    def pass_on(self):
+        for number, offset in enumerate(self.near):
+            other = lax.rem(self.place.chunk(*offset), 4)
+            self.copy(number, self.pieces.at[other], self.rows_recv.at[other], self.place.peer(*offset)).wait_recv()
+        for step in range(1, self.count):
+            to = lax.rem(self.me + step, self.count)
+            self.moved.append(self.copy(2 + step, self.rows_recv.at[to], self.gates_all.at[self.me], {"t": to}))
+            self.moved[-1].start()
+        self.gates_all[self.me] = self.rows_recv[self.me]
+
+    def finish(self, out):
+        for step in range(1, self.count):
+            other = lax.rem(self.me + self.count - step, self.count)
+            self.copy(2 + step, self.rows_recv.at[other], self.gates_all.at[other], {"t": other}).wait_recv()
+        total = self.gates_all[0].astype(F32)
+        for z in range(1, self.count):
+            total = total + self.gates_all[z].astype(F32)
+        out[...] = total
+        for copy in self.moved:
+            copy.wait_send()
+
+
+def sum_everywhere(place, count, values, inbox, plane_box, send, recv):
+    me = lax.axis_index("t")
+    moved = []
+
+    def copy(number, target, peer):
+        return pltpu.make_async_remote_copy(
+            src_ref=values.at[min(number, 3)],
+            dst_ref=target,
+            send_sem=send.at[number],
+            recv_sem=recv.at[number],
+            device_id=peer,
+            device_id_type=MESH,
+        )
+
+    for number, peer in enumerate((place.core, place.across, place.along)):
+        moved.append(copy(number, inbox.at[number], peer))
+        moved[-1].start()
+        copy(number, inbox.at[number], peer).wait_recv()
+        values[number + 1] = values[number] + inbox[number]
+    for step in range(1, count):
+        moved.append(copy(2 + step, plane_box.at[me], {"t": lax.rem(me + step, count)}))
+        moved[-1].start()
+    plane_box[me] = values[3]
+    for step in range(1, count):
+        other = lax.rem(me + count - step, count)
+        copy(2 + step, plane_box.at[other], {"t": other}).wait_recv()
+    total = plane_box[0]
+    for z in range(1, count):
+        total = total + plane_box[z]
+    for sent in moved:
+        sent.wait_send()
+    return total
+
+
+def final_kernel(
+    count, with_gates, left0, left1, right0, right1, own_in, gain, mlp_gains, pieces, reduced0, reduced1,
+    grad_out, gains_out, gates_out, owned0, owned1,
+    gain_sum, values, inbox, plane_box, sum_send, sum_recv, rows_recv, gates_all, gates_send, gates_recv,
+    send0, recv0, send1, recv1, *buffers,
+):
+    tokens, width = own_in.shape
     place = Place()
-    place.greet()
-    scatter = Scatter(place, pair_product(lefts, rights, tokens), *buffers)
-    scatter.run()
+    me = lax.axis_index("t")
+    place.greet([place.peer(*offset) for offset in BEYOND] + [{"t": lax.rem(me + step, count)} for step in range(1, count)])
+    scatter = Scatter(place, pair_product([left0, left1], [right0, right1], tokens), *buffers)
+    owners = [Owners(place, reduced0, owned0, send0, recv0), Owners(place, reduced1, owned1, send1, recv1)]
+    gates = GateSums(place, count, pieces, rows_recv, gates_all, gates_send, gates_recv)
+    scatter.run_first()
+    if with_gates:
+        gates.begin()
+    owners[0].begin()
+    owners[1].begin()
+    scatter.run_second()
+    if with_gates:
+        gates.pass_on()
+    scatter.run_third()
+    gain_sum[...] = jnp.zeros_like(gain_sum)
 
     def body(at):
-        out[at, :] = scatter.rows(at).astype(out.dtype)
+        x = own_in[at, :].astype(F32)
+        grad = scatter.rows(at)
+        scale = rms(x)
+        weighted = grad * gain[...]
+        inner = jnp.mean(x * weighted, axis=-1, keepdims=True)
+        grad_out[at, :] = scale * weighted - x * (scale * scale * scale * inner)
+        term = grad * x * scale
+        gain_sum[...] += term[0:8] + term[8:16]
 
     for_slices(0, tokens, body)
+    lines = width // LANES
+    for base, row in ((0, jnp.sum(mlp_gains[...], axis=0, keepdims=True)), (lines, jnp.sum(gain_sum[...], axis=0, keepdims=True))):
+        for n in range(lines):
+            values[0, base + n : base + n + 1, :] = row[:, n * LANES : (n + 1) * LANES]
+    gains_out[...] = sum_everywhere(place, count, values, inbox, plane_box, sum_send, sum_recv)
+    if with_gates:
+        gates.finish(gates_out)
+    else:
+        gates_out[...] = jnp.zeros_like(gates_out)
+    owners[0].finish()
+    owners[1].finish()
     scatter.finish()
+
+
+def final_step(planes, lefts, rights, own_in, gain, mlp_gains, pieces, reduced):
+    tokens, width = own_in.shape
+    with_gates = pieces.shape[0] == planes
+    block = pieces.shape[1:] if with_gates else (16, LANES)
+    slots = planes if with_gates else 1
+    pieces = pieces if with_gates else jnp.zeros((1, *block), BF16)
+    sums = (2 * width // LANES, LANES)
+    return pl.pallas_call(
+        functools.partial(final_kernel, planes, with_gates),
+        name="final_step",
+        out_shape=(
+            jax.ShapeDtypeStruct((tokens, width), F32),
+            jax.ShapeDtypeStruct(sums, F32),
+            jax.ShapeDtypeStruct(block, F32),
+            *[jax.ShapeDtypeStruct(part.shape, part.dtype) for part in reduced],
+        ),
+        in_specs=whole(8) + [ANYWHERE] * 2,
+        out_specs=(*whole(3), ANYWHERE, ANYWHERE),
+        scratch_shapes=[
+            pltpu.VMEM((8, width), F32),
+            pltpu.VMEM((4, *sums), F32),
+            pltpu.VMEM((3, *sums), F32),
+            pltpu.VMEM((planes, *sums), F32),
+            pltpu.SemaphoreType.DMA((planes + 2,)),
+            pltpu.SemaphoreType.DMA((planes + 2,)),
+            pltpu.VMEM((slots, *block), BF16),
+            pltpu.VMEM((slots, *block), BF16),
+            pltpu.SemaphoreType.DMA((planes + 2,)),
+            pltpu.SemaphoreType.DMA((planes + 2,)),
+            *OWNERS_SCRATCH,
+            *OWNERS_SCRATCH,
+            *Scatter.scratch(tokens, width),
+        ],
+        compiler_params=mixer_params(7),
+    )(*lefts, *rights, own_in, gain[None], mlp_gains, pieces, *reduced)
+
+
+def owners_kernel(reduced0, reduced1, out0, out1, send0, recv0, send1, recv1):
+    place = Place()
+    place.greet([place.peer(*offset) for offset in BEYOND])
+    owners = [Owners(place, reduced0, out0, send0, recv0), Owners(place, reduced1, out1, send1, recv1)]
+    for part in owners:
+        part.begin()
+    for part in owners:
+        part.finish()
+
+
+def owners_step(reduced):
+    return pl.pallas_call(
+        owners_kernel,
+        name="owners_step",
+        out_shape=tuple(jax.ShapeDtypeStruct(part.shape, part.dtype) for part in reduced),
+        in_specs=[ANYWHERE] * 2,
+        out_specs=(ANYWHERE,) * 2,
+        scratch_shapes=[*OWNERS_SCRATCH, *OWNERS_SCRATCH],
+        compiler_params=mixer_params(8),
+    )(*reduced)
+
+
+def place_kernel(planes, hidden, pairs, sources, out):
+    piece = sources.shape[2] // (len(pairs) * (planes if hidden else 1))
+    for k in pairs:
+        if hidden:
+            groups = [
+                ((t * 2 + i) * 4 * piece, [(i * 4 + r, (k * planes + t) * piece) for r in range(4)])
+                for t in range(planes)
+                for i in range(2)
+            ]
+        else:
+            groups = [(r * 2 * piece, [(i * 4 + r, k * piece) for i in range(2)]) for r in range(4)]
+        for start, parts in groups:
+            row = jnp.concatenate([sources[p, :, at : at + piece].astype(F32) for p, at in parts], axis=1)
+            if len(pairs) > 1:
+                out[:, k, start : start + row.shape[1]] = row
+            else:
+                out[:, start : start + row.shape[1]] = row
+
+
+def place_columns(planes, hidden, kinds, owned):
+    members, own_rows, columns = owned.shape
+    total = columns * members // kinds
+    shape = (own_rows, kinds, total) if kinds > 1 else (own_rows, total)
+    return pl.pallas_call(
+        functools.partial(place_kernel, planes, hidden, tuple(range(kinds))),
+        name="place_columns",
+        out_shape=jax.ShapeDtypeStruct(shape, F32),
+        in_specs=whole(1),
+        out_specs=pl.BlockSpec(memory_space=pltpu.VMEM),
+        compiler_params=pltpu.CompilerParams(vmem_limit_bytes=60 * 1024 * 1024),
+    )(owned)
 
 
 def first_gather(planes, normed, ids):
@@ -837,19 +1104,6 @@
     )(left0, left1, right0, right1, middle, gain[None], cot)
 
 
-def scatter_step(number, lefts, rights):
-    tokens, width = lefts[0].shape[0] // 8, rights[0].shape[1]
-    return pl.pallas_call(
-        functools.partial(scatter_kernel, len(lefts)),
-        name="scatter_step",
-        out_shape=jax.ShapeDtypeStruct((tokens, width), F32),
-        in_specs=whole(2 * len(lefts)),
-        out_specs=pl.BlockSpec(memory_space=pltpu.VMEM),
-        scratch_shapes=Scatter.scratch(tokens, width),
-        compiler_params=mixer_params(number),
-    )(*lefts, *rights)
-
-
 class Swap:
     def __init__(self, quarters, out, send, recv):
         self.quarters, self.out, self.send, self.recv = quarters, out, send, recv
@@ -914,112 +1168,8 @@
     )(quarters)
 
 
-def small_kernel(count, with_gates, pieces, gains, gates_out, gains_out, rows_recv, gains_recv, gains_sum, gates_all, gains_all, send, recv):
-    place = Place()
-    me = lax.axis_index("t")
-    place.greet(
-        [place.peer(*offset) for offset in OTHERS if sum(offset) > 1]
-        + [{"t": lax.rem(me + step, count)} for step in range(1, count)]
-    )
-    own = place.chunk(0, 0, 0)
-    rank = place.g * 2 + place.c
-    moved = []
-
-    def move(number, source, target, peer):
-        copy = pltpu.make_async_remote_copy(
-            src_ref=source,
-            dst_ref=target,
-            send_sem=send.at[number],
-            recv_sem=recv.at[number],
-            device_id=peer,
-            device_id_type=MESH,
-        )
-        return copy
-
-    def start(*parts):
-        copy = move(*parts)
-        copy.start()
-        moved.append(copy)
-
-    for number, offset in enumerate(OTHERS):
-        peer, chunk = place.peer(*offset), place.chunk(*offset)
-        start(number, gains.at[chunk], gains_recv.at[own], peer)
-        if with_gates and not offset[0]:
-            start(7 + number, pieces.at[lax.rem(chunk, 4)], rows_recv.at[rank], peer)
-    gains_recv[own] = gains[own]
-    if with_gates:
-        rows_recv[rank] = pieces[rank]
-    for number, offset in enumerate(OTHERS):
-        peer, chunk = place.peer(*offset), place.chunk(*offset)
-        move(number, gains.at[chunk], gains_recv.at[chunk], peer).wait_recv()
-        if with_gates and not offset[0]:
-            other = lax.rem(chunk, 4)
-            move(7 + number, pieces.at[other], rows_recv.at[other], peer).wait_recv()
-    total = gains_recv[0]
-    for n in range(1, 8):
-        total = total + gains_recv[n]
-    gains_sum[...] = total
-    for step in range(1, count):
-        to = lax.rem(me + step, count)
-        start(10 + 2 * step, gains_sum, gains_all.at[me], {"t": to})
-        if with_gates:
-            start(11 + 2 * step, rows_recv.at[to], gates_all.at[me], {"t": to})
-    gains_all[me] = total
-    if with_gates:
-        gates_all[me] = rows_recv[me]
-    for step in range(1, count):
-        other = lax.rem(me + count - step, count)
-        move(10 + 2 * step, gains_sum, gains_all.at[other], {"t": other}).wait_recv()
-        if with_gates:
-            move(11 + 2 * step, rows_recv.at[other], gates_all.at[other], {"t": other}).wait_recv()
-    row = gains_all[0, pl.ds(me, 1), :]
-    for z in range(1, count):
-        row = row + gains_all[z, pl.ds(me, 1), :]
-    gains_out[...] = jnp.broadcast_to(row, gains_out.shape)
-    if with_gates:
-        gates = gates_all[0].astype(F32)
-        for z in range(1, count):
-            gates = gates + gates_all[z].astype(F32)
-        gates_out[...] = gates
-    else:
-        gates_out[...] = jnp.zeros_like(gates_out)
-    for copy in moved:
-        copy.wait_send()
-
-
-def small_step(planes, pieces, gains):
-    with_gates = pieces.shape[0] == planes
-    slots = max(planes, 4) if with_gates else 1
-    block = pieces.shape[1:] if with_gates else (16, LANES)
-    pieces = pieces if with_gates else jnp.zeros((1, *block), BF16)
-    sems = 12 + 2 * planes
-    return pl.pallas_call(
-        functools.partial(small_kernel, planes, with_gates),
-        name="small_step",
-        out_shape=(jax.ShapeDtypeStruct(block, F32), jax.ShapeDtypeStruct((8, LANES), F32)),
-        in_specs=whole(2),
-        out_specs=tuple(whole(2)),
-        scratch_shapes=[
-            pltpu.VMEM((slots, *block), BF16),
-            pltpu.VMEM(gains.shape, F32),
-            pltpu.VMEM(gains.shape[1:], F32),
-            pltpu.VMEM((slots, *block), BF16),
-            pltpu.VMEM((planes, *gains.shape[1:]), F32),
-            pltpu.SemaphoreType.DMA((sems,)),
-            pltpu.SemaphoreType.DMA((sems,)),
-        ],
-        compiler_params=mixer_params(9),
-    )(pieces, gains)
-
-
 def rms(values):
     return lax.rsqrt(jnp.mean(values * values, axis=-1, keepdims=True) + EPS)
-
-
-def rms_back(values, scale, gain, grad):
-    weighted = grad * gain
-    inner = jnp.mean(values * weighted, axis=-1, keepdims=True)
-    return scale * weighted - values * (scale * scale * scale * inner), jnp.sum(grad * values * scale, axis=0)
 
 
 def nt(left, right, out):
@@ -1058,15 +1208,15 @@
     own_ids = jnp.pad((segment_ids + 1).astype(F32), ((0, 8 - rows_here), (0, 0)))
 
     normed, *ids = first_gather(planes, (flat_in * scale_in * mix_gain).astype(BF16), own_ids)
-    mlp_in, down_weight, normed = lax.optimization_barrier((mlp_in, down_weight, normed))
+    late_r, ids[0] = lax.optimization_barrier((r, ids[0]))
 
     direct = planes == row_groups
     in_own = in_weight.transpose(1, 2, 0)
     out_own = out_weight.T[None]
     part = channels // row_groups if direct else 0
 
-    def quarter(weight, part):
-        return lax.dynamic_slice_in_dim(weight, r * part, part, weight.ndim - 1)
+    def quarter(weight, part, rank=r):
+        return lax.dynamic_slice_in_dim(weight, rank * part, part, weight.ndim - 1)
 
     def spread_units(weight):
         return lax.all_gather(weight, "t", axis=0, tiled=False)
@@ -1083,10 +1233,10 @@
         out_quarters = jnp.zeros((row_groups, 1, 16, width), BF16)
     w_gate, w_recur = in_w.reshape(2, channels, width)
     hidden_part = mlp_in.shape[2] // row_groups
-    mlp_w = spread_units(quarter(mlp_in, hidden_part).transpose(1, 2, 0))
+    mlp_w = spread_units(quarter(mlp_in, hidden_part, late_r).transpose(1, 2, 0))
     w_left = mlp_w[:, 0].reshape(-1, width)
     w_right = mlp_w[:, 1].reshape(-1, width)
-    w_down = spread_units(quarter(down_weight, hidden_part).T).reshape(-1, width)
+    w_down = spread_units(quarter(down_weight, hidden_part, late_r).T).reshape(-1, width)
 
     def own(values):
         return lax.dynamic_slice_in_dim(values, first, channels, values.ndim - 1)
@@ -1125,9 +1275,6 @@
     def over_planes(grad):
         return lax.psum_scatter(grad, "t", scatter_dimension=0, tiled=True)
 
-    def to_owners(reduced):
-        return lax.all_to_all(reduced.reshape(members, -1, reduced.shape[1]), PLANE, 0, 0, tiled=True)
-
     grad_down = tn(cot, hidden, BF16)
     grad_down, hidden, w_down = lax.optimization_barrier((grad_down, hidden, w_down))
     grad_down = over_planes(grad_down)
@@ -1139,34 +1286,20 @@
     grad_mlp_in = over_planes(grad_mlp_in)
     grad_middle, grad_mlp_gain, grad_mid = turn_step(grad_left, grad_right, w_left, w_right, middle, mlp_gain, cot_own)
     grad_down, grad_mid = lax.optimization_barrier((grad_down, grad_mid))
-    grad_mlp_gain = jnp.sum(grad_mlp_gain, axis=0)
     grad_out = tn(grad_mid, mixed, BF16)
     grad_mixed = nt(grad_mid, w_out, F32)
     grad_out, grad_mixed = lax.optimization_barrier((grad_out, grad_mixed))
     grad_out = over_planes(grad_out)
-    grad_gate, grad_recur, gw0, gw1, small = mixer_backward(
-        planes, seg, grad_mixed, gate_branch, states, decay, conv_low, recur, halo, cin, mask, wg0, wg1, wg0.T, wg1.T, vec
+    grad_gate, grad_recur, gw0, gw1, small, down = mixer_backward(
+        planes, seg, grad_mixed, gate_branch, states, decay, conv_low, recur, halo, cin, mask, wg0, wg1, wg0.T, wg1.T, vec,
+        hidden, w_down,
     )
     grad_mlp_in, grad_gate, grad_recur = lax.optimization_barrier((grad_mlp_in, grad_gate, grad_recur))
     grad_in = jnp.concatenate([tn(normed, grad_gate, BF16), tn(normed, grad_recur, BF16)], axis=1)
     grad_in, grad_gate, grad_recur = lax.optimization_barrier((grad_in, grad_gate, grad_recur))
     grad_in = over_planes(grad_in)
-    grad_normed = scatter_step(7, [grad_gate, grad_recur], [w_gate, w_recur])
-    grad_in_norm, grad_mix_gain = rms_back(flat_in, scale_in, mix_gain, grad_normed)
-    grad_inputs = (grad_middle + grad_in_norm).reshape(inputs.shape)
-    grad_out, hidden, grad_normed = lax.optimization_barrier((grad_out, hidden, grad_normed))
-    down = scatter_step(8, [hidden], [w_down])
     outputs = (middle + down).astype(BF16).reshape(inputs.shape)
-
     own_rows = width // (planes * members)
-
-    def hidden_order(reduced, kinds):
-        grad = to_owners(reduced).reshape(2, row_groups, own_rows, kinds, planes, hidden_part).astype(F32)
-        return grad.transpose(2, 3, 4, 0, 1, 5).reshape(own_rows, kinds, -1)
-
-    def channel_order(reduced, kinds):
-        grad = to_owners(reduced).reshape(2, row_groups, own_rows, kinds, channels).astype(F32)
-        return grad.transpose(2, 3, 1, 0, 4).reshape(own_rows, kinds, -1)
 
     column_block = lax.broadcasted_iota(jnp.int32, (block_width, channels), 1) // block_width
 
@@ -1180,11 +1313,23 @@
     if direct:
         pieces = gate_grads.reshape(gate_grads.shape[0], row_groups, -1).transpose(1, 0, 2)
         pieces = jnp.pad(pieces.astype(BF16), ((0, 0), (0, -pieces.shape[1] % 16), (0, LANES - part)))
-    gains = jnp.stack([grad_mlp_gain, grad_mix_gain]).reshape(2, planes, members, own_rows)
-    gains = gains.transpose(2, 1, 0, 3).reshape(members, planes, 2 * own_rows)
-    short = LANES - 2 * own_rows
-    gains = jnp.pad(gains, ((0, 0), (0, -planes % 8), (0, short)))
-    gate_sums, gains = small_step(planes, pieces, gains)
+    reduced = [part.reshape(members, own_rows, -1) for part in (grad_mlp_in, grad_down)]
+    grad_in_norm, gains, gate_sums, owned_mlp_in, owned_down = final_step(
+        planes, [grad_gate, grad_recur], [w_gate, w_recur], own_in, mix_gain, grad_mlp_gain, pieces, reduced
+    )
+    grad_inputs = (grad_middle + grad_in_norm).reshape(inputs.shape)
+    index = ((t * 2 + i) * row_groups + r) * own_rows
+    gains = lax.dynamic_slice_in_dim(gains.reshape(2, width), index, own_rows, 1)
+    owned_in, owned_out = owners_step([part.reshape(members, own_rows, -1) for part in (grad_in, grad_out)])
+
+    def columns(owned, kinds, hidden):
+        if direct:
+            return place_columns(planes, hidden, kinds, owned)
+        owned = owned.reshape(2, row_groups, own_rows, kinds, planes if hidden else 1, -1).astype(F32)
+        order = (2, 3, 4, 0, 1, 5) if hidden else (2, 3, 1, 0, 4, 5)
+        owned = owned.transpose(order).reshape(own_rows, kinds, -1)
+        return owned if kinds > 1 else owned[:, 0]
+
     if direct:
         gate_grads = gate_sums[:, :part]
     else:
@@ -1193,21 +1338,20 @@
         gate_grads = lax.psum_scatter(placed, EVERY, scatter_dimension=1, tiled=True)
     grad_gate_weight = jnp.stack([gate_grads[:block_width], gate_grads[block_width : 2 * block_width]], axis=1)
     small = gate_grads[2 * block_width : 2 * block_width + 8]
-    mlp_in_grads = hidden_order(grad_mlp_in, 2)
     return (
         outputs,
         grad_inputs,
-        gains[0, own_rows : 2 * own_rows],
-        channel_order(grad_in, 2),
+        gains[1],
+        columns(owned_in, 2, False),
         small[0:4],
         small[4],
         grad_gate_weight,
         small[5:7],
         small[7],
-        channel_order(grad_out, 1)[:, 0],
-        gains[0, :own_rows],
-        mlp_in_grads,
-        hidden_order(grad_down, 1)[:, 0],
+        columns(owned_out, 1, False),
+        gains[0],
+        columns(owned_mlp_in, 2, True),
+        columns(owned_down, 1, True),
     )
 
 

time: 792 us -> 724 us (0.914)
  local copies, waits for them, and re-layouts: 107 us -> 56.8 us
  waiting for transfers between devices: 24.5 us -> 0.2 us
  Pallas kernels: 498 us -> 519 us
  starting transfers between devices: 15.7 us -> 0.33 us
    reshape x7 -> x1, local copies, waits for them, and re-layouts: 29.7 us -> 0.73 us  [per_device(): gains.reshape(2, width)]
    all_to_all x4 -> x0, waiting for transfers between devices: 24.2 us -> none  [to_owners(): lax.all_to_all(reduced.reshape(members, -1, reduced.shape[1]), PLANE, 0,...]
    optimization_barrier x3 -> x0, local copies, waits for them, and re-layouts: 21.8 us -> none  [the longest x2 20.9 us: per_device(): lax.optimization_barrier((mlp_in, down_weight, normed))]
    pallas_call x1, Pallas kernels: 55.5 us -> 76.2 us  [mixer_backward(): pl.pallas_call(functools.partial(mixer_backward_kernel, count, seg), name...]
    all_to_all x4 -> x0, starting transfers between devices: 15.4 us -> none  [to_owners(): lax.all_to_all(reduced.reshape(members, -1, reduced.shape[1]), PLANE, 0,...]
    another operation x7 -> x0, local copies, waits for them, and re-layouts: 11.1 us -> none  [the longest x3 8.76 us: per_device(): hidden_order(grad_down, 1)[:, 0]]
    pallas_call x3 -> x6, Pallas kernels: 118 us -> 118 us  [the longest x1 91.4 us: final_step(): pl.pallas_call(functools.partial(final_kernel, planes, with_gates), name=...]
  transfers between devices with their start and end apart: 12 -> 8, of which waited for: 2 -> 0; matrix products, arithmetic and copies ran while one was open for 27% -> 24% of each run, Pallas kernels for 63% -> 69%
where the time goes in v4:
time: 724 us; the launch traced here: 719 us
  Pallas kernels  519 us (72%)
  matrix products  108 us (15%)
  local copies, waits for them, and re-layouts  56.8 us (8%)
  other arithmetic  19.5 us (3%)
  between operations  15.2 us (2%)
    pallas_call x1, Pallas kernels, turn_step(): pl.pallas_call(turn_kernel, name='turn_step', out_shape=(jax.ShapeDtypeSt...  95.7 us
    pallas_call x1, Pallas kernels, final_step(): pl.pallas_call(functools.partial(final_kernel, planes, with_gates), name=...  91.4 us
    pallas_call x1, Pallas kernels, middle_step(): pl.pallas_call(middle_kernel, name='middle_step', out_shape=(jax.ShapeDty...  87.9 us
    pallas_call x1, Pallas kernels, mixer_backward(): pl.pallas_call(functools.partial(mixer_backward_kernel, count, seg), name...  76.2 us
    pallas_call x1, Pallas kernels, mixer_forward(): pl.pallas_call(functools.partial(mixer_forward_kernel, count, seg, rows_h...  62.2 us
    dot_general x6, matrix products, nt(): lax.dot_general(left, right, (((1,), (1,)), ((), ())), preferred_element_...  61.7 us
    pallas_call x1, Pallas kernels, first_gather(): pl.pallas_call(functools.partial(first_gather_kernel, planes), name='firs...  48.5 us
    dot_general x6, matrix products, tn(): lax.dot_general(left, right, (((0,), (0,)), ((), ())), preferred_element_...  46.6 us
  transfers between devices with their start and end apart: 8, of which 0 were waited for; matrix products, arithmetic and copies ran while one was open for 24% of the time, Pallas kernels for 69%

profile of v4, /device:TPU:0, one launch (start us, length us, event | category | flops | bytes accessed | tf_op | source)
XLA Modules:
  0.0 719.2 jit_solution(8122874869840667122)
XLA Ops:
  16.6 48.5 %first_gather.1 = (bf16[2048,2048]{1,0:T(8,128)(2,1)}, f32[8,8,128]{2,1,0:T(8,128)}, f32[8,8,128]{2,1,0:T(8,128)}, f32[8,8,128]{2,1,0:T(8,128)}) custom-call(bf16[256,2048]{1,0:T(8,128)(2,1)} %multiply_convert_fusion.3.normed, f32[8,128]{1,0:T(8,128)} %pad.17.ids), custom_call_target="tpu_custom_call" | custom-call | tf_op jit(solution)/shard_map/first_gather/pallas_call | solution.py:1066
  65.1 5.8 constant_dynamic-slice_fusion.2
  70.9 6.1 copy.104
  90.5 30.5 %swap.1 = bf16[2,4,80,2048]{3,2,1,0:T(8,128)(2,1)} custom-call(bf16[4,2,80,2048]{3,2,1,0:T(8,128)(2,1)} %bitcast.102), custom_call_target="tpu_custom_call" | custom-call | tf_op jit(solution)/shard_map/swap/pallas_call | solution.py:1160
  123.2 10.1 %convolution_convert_fusion.3.recur = bf16[2048,320]{1,0:T(8,128)(2,1)} fusion(bf16[2048,2048]{1,0:T(8,128)(2,1)} %get-tuple-element.86, bf16[320,2048]{1,0:T(8,128)(2,1)S(1)} %bitcast.97), kind=kOutput, calls=%fused_computation.10 | convolution fusion | flops 2685009920 | bytes 11010048 | tf_op jit(solution)/shard_map/dot_general | solution.py:1176
  133.4 6.3 fusion.17.gate
  139.7 62.2 %mixer_forward.1 = (bf16[2048,320]{1,0:T(8,128)(2,1)}, f32[3,2048,128]{2,1,0:T(8,128)}, f32[2048,320]{1,0:T(8,128)}, bf16[2048,320]{1,0:T(8,128)(2,1)}, f32[128,...) custom-call(bf16[2048,320]{1,0:T(8,128)(2,1)} %convolution_convert_f, ...), custom_call_target="tpu_custom_call" | custom-call | tf_op jit(solution)/shard_map/mixer_forward/pallas_call | solution.py:373
  201.9 87.9 %middle_step.1 = (f32[256,2048]{1,0:T(8,128)}, bf16[2048,2048]{1,0:T(8,128)(2,1)}) custom-call(bf16[2048,320]{1,0:T(8,128)(2,1)} %get-tuple-element.91.left, bf16[320,2048]{1,0:T(8,128)(2,1)} %bitcast.110, bf16[256,2048]{1,0:T(8,128)(2,1)} %bitcast.86, f32[1,2048]{1,0:T(1,128)} %bitcast.116), custom_call_target="tpu_custom_call" | custom-call | tf_op jit(solution)/shard_map/middle_step/pallas_call | solution.py:1079
  296.0 8.6 %fusion.18 = f32[2048,768]{1,0:T(8,128)} fusion(bf16[2048,2048]{1,0:T(8,128)(2,1)S(1)} %copy-done.16, bf16[768,2048]{1,0:T(8,128)(2,1)S(1)} %bitcast.88), kind=kOutput, calls=%fused_computation.63 | convolution fusion | flops 6442450944 | bytes 17825792 | tf_op jit(solution)/shard_map/dot_general | solution.py:1176
  304.6 14.2 %multiply_convert_fusion.2 = (bf16[2048,768]{1,0:T(8,128)(2,1)S(1)}, f32[2048,768]{1,0:T(8,128)}) fusion(f32[2048,768]{1,0:T(8,128)} %fusion.18, bf16[2048,2048]{1,0:T(8,128)(2,1)} %get-tuple-element.95, bf16[768,2048]{1,0:T(8,128)(2,1)S(1)} %bitcast.90), kind=kOutput, calls=%fused_computation.3 | convolution fusion | flops 6458179584 | bytes 27262976 | tf_op jit(solution)/shard_map/dot_general | solution.py:1176
  320.4 8.5 %convolution_convert_fusion.2 = bf16[2048,768]{1,0:T(8,128)(2,1)} fusion(bf16[2048,2048]{1,0:T(8,128)(2,1)S(1)} %bitcast.122, bf16[2048,768]{1,0:T(8,128)(2,1)S(1)} %get-tuple-element.110.hidden), kind=kOutput, calls=%fused_computation.9 | convolution fusion | flops 6444023808 | bytes 14680064 | tf_op jit(solution)/shard_map/dot_general | solution.py:1180
  329.0 16.6 %multiply_convert_fusion.1 = (bf16[2048,768]{1,0:T(8,128)(2,1)S(1)}, bf16[2048,768]{1,0:T(8,128)(2,1)S(1)}) fusion(f32[2048,768]{1,0:T(8,128)} %fusion.18, f32[2048,768]{1,0:T(8,128)} %get-tuple-element.208, bf16[2048,2048]{1,0:T(8,128)(2,1)} %get-tuple-element.94, bf16[768,2048]{1,0:T(8,128)(2,1)} %all-gather.15.cloned.1.call-done.w_down), kind=kOutput, calls=%fused_computation.2 | convolution fusion | flops 6477053952 | bytes 30408704 | tf_op jit(solution)/shard_map/dot_general | solution.py:1176
  345.7 11.6 %convolution_convert_fusion = bf16[2048,768]{0,1:T(8,128)(2,1)S(1)} fusion(bf16[2048,2048]{1,0:T(8,128)(2,1)} %get-tuple-element.95, bf16[2048,768]{1,0:T(8,128)(2,1)S(1)} %get-tuple-element.100.left1), kind=kOutput, calls=%fused_computation.7 | convolution fusion | flops 6444023808 | bytes 14680064 | tf_op jit(solution)/shard_map/dot_general | solution.py:1180
  357.3 9.2 %convolution_convert_fusion.1 = bf16[2048,768]{0,1:T(8,128)(2,1)S(1)} fusion(bf16[2048,2048]{1,0:T(8,128)(2,1)} %get-tuple-element.95, bf16[2048,768]{1,0:T(8,128)(2,1)S(1)} %get-tuple-element.99.left0), kind=kOutput, calls=%fused_computation.8 | convolution fusion | flops 6444023808 | bytes 14680064 | tf_op jit(solution)/shard_map/dot_general | solution.py:1180
  370.3 95.7 %turn_step.1 = (f32[256,2048]{1,0:T(8,128)}, f32[8,2048]{1,0:T(8,128)}, bf16[2048,2048]{1,0:T(8,128)(2,1)}) custom-call(bf16[2048,768]{1,0:T(8,128)(2,1)} %copy-done.7, bf16[2048,768]{1,0:T(8,128)(2,1)} %copy-done.8, bf16[768,2048]{1,0:T(8,128)(2,1)} %bitcast.89, bf16[768,2048]{1,0:T(8,128)(2,1)} %bitcast.91, f32[256,2048]{1,0:T(8,128)} %get-tuple-element.93.middle, ...), custom_call_target="tpu_custom_call" | custom-call | tf_op jit(solution)/shard_map/turn_step/pallas_call | solution.py:1092
  466.1 5.9 fusion.19
  472.7 4.2 convolution_convert_fusion.6
  479.5 76.2 %mixer_backward.1 = (bf16[2048,320]{1,0:T(8,128)(2,1)}, bf16[2048,320]{1,0:T(8,128)(2,1)}, f32[320,320]{1,0:T(8,128)}, f32[320,320]{1,0:T(8,128)}, f32[8,320]{1,0:T(8,128)}, /*index=5*/f32[256,2048]{1,0:T(8,128)}) custom-call(f32[2048,320]{1,0:T(8,128)} %copy.90.grad_mixed, f32[2048,320]{1,0:T(8,128)} %fusion.17.gate, ...), custom_call_target="tpu_custom_call" | custom-call | tf_op jit(solution)/shard_map/mixer_backward/pallas_call | solution.py:410
  555.8 6.8 convolution_convert_fusion.4
  562.6 6.3 convolution_convert_fusion.5
  580.9 91.4 %final_step.1 = (f32[256,2048]{1,0:T(8,128)}, f32[32,128]{1,0:T(8,128)}, f32[336,128]{1,0:T(8,128)}, bf16[8,64,1536]{2,1,0:T(8,128)(2,1)}, bf16[8,64,768]{2,1,0:T(8,128)(2,1)}) custom-call(bf16[2048,320]{1,0:T(8,128)(2,1)} %get-tuple-element.118.left0, bf16[2048,320]{1,0:T(8,128)(2,1)} %get-tuple-element.119.left1, bf16[320,2048]{1,0:T(8,128)(2,1)} %bitcast.96, ...), custom_call_target="tpu_custom_call" | custom-call | tf_op jit(solution)/shard_map/final_step/pallas_call | solution.py:978
  677.3 4.1 place_columns.6
  683.9 4.0 add.117
  692.0 15.3 %owners_step.1 = (bf16[8,64,640]{2,1,0:T(8,128)(2,1)}, bf16[8,64,320]{2,1,0:T(8,128)(2,1)}) custom-call(bf16[8,64,640]{2,1,0:T(8,128)(2,1)} %bitcast.103, bf16[8,64,320]{2,1,0:T(8,128)(2,1)} %bitcast.107), custom_call_target="tpu_custom_call" | custom-call | tf_op jit(solution)/shard_map/owners_step/pallas_call | solution.py:1019
  (131 shorter events, 68.0 us)
Async XLA Ops:
  7.2 69.8 %copy-start = (bf16[2048,768]{1,0:T(8,128)(2,1)S(1)}, bf16[2048,768]{1,0:T(8,128)(2,1)}, u32[]{:S(2)}) copy-start(bf16[2048,768]{1,0:T(8,128)(2,1)} %param.30) | copy-start | bytes 9437188
  7.2 6.9 copy-start.14
  7.2 83.3 %all-gather.9.cloned.1.call-start = ((), (), s32[]{:S(2)}) async-start(), calls=%async_computation.8 | async-start | bytes 3276800 | tf_op jit(solution)/shard_map/all_gather | solution.py:1222
  9.4 130.3 %all-gather.11.cloned.1.call-start = ((), (), s32[]{:S(2)}) async-start(), calls=%async_computation.9 | async-start | bytes 1638400 | tf_op jit(solution)/shard_map/all_gather | solution.py:1222
  11.2 278.6 %all-gather.13.cloned.1.call-start = ((), (), s32[]{:S(2)}) async-start(), calls=%async_computation.10 | async-start | bytes 7864320 | tf_op jit(solution)/shard_map/all_gather | solution.py:1222
  77.0 252.0 %all-gather.15.cloned.1.call-start = ((), (), s32[]{:S(2)}) async-start(), calls=%async_computation.11 | async-start | bytes 3932160 | tf_op jit(solution)/shard_map/all_gather | solution.py:1222
  80.7 385.4 %reduce-scatter.5.cloned.1.call-start = ((), (), s32[]{:S(2)}) async-start(), calls=%async_computation.4 | async-start | bytes 3932160 | tf_op jit(solution)/shard_map/reduce_scatter | solution.py:1276
  83.8 37.2 %copy-start.10 = (bf16[320,320]{0,1:T(8,128)(2,1)}, bf16[320,320]{0,1:T(8,128)(2,1)S(1)}, u32[]{:S(2)}) copy-start(bf16[320,320]{0,1:T(8,128)(2,1)S(1)} %squeeze.26) | copy-start | bytes 614404
  121.0 12.3 %slice-start = ((s8[8388608]{0:T(1024)(128)(4,1)}), s8[4194304]{0:T(1024)(128)(4,1)S(1)}, s32[]{:S(2)}) async-start(s8[8388608]{0:T(1024)(128)(4,1)} %bitcast.119), calls=%async_computation.12 | async-start | bytes 8388608
  123.2 10.1 %copy-start.6 = (bf16[1,4,80,2048]{3,2,1,0:T(8,128)(2,1)}, bf16[1,4,80,2048]{3,2,1,0:T(8,128)(2,1)S(1)}, u32[]{:S(2)}) copy-start(bf16[1,4,80,2048]{3,2,1,0:T(8,128)(2,1)S(1)} %get-tuple-element.192) | copy-start | bytes 3932164
  123.2 10.1 %copy-start.5 = (bf16[1,4,80,2048]{3,2,1,0:T(8,128)(2,1)}, bf16[1,4,80,2048]{3,2,1,0:T(8,128)(2,1)S(1)}, u32[]{:S(2)}) copy-start(bf16[1,4,80,2048]{3,2,1,0:T(8,128)(2,1)S(1)} %get-tuple-element.191) | copy-start | bytes 3932164
  123.2 10.1 %slice-start.1 = ((s8[8388608]{0:T(1024)(128)(4,1)}), s8[4194304]{0:T(1024)(128)(4,1)S(1)}, s32[]{:S(2)}) async-start(s8[8388608]{0:T(1024)(128)(4,1)} %bitcast.119), calls=%async_computation.13 | async-start | bytes 8388608
  293.7 10.9 %copy-start.2 = (bf16[4,1,192,2048]{3,2,1,0:T(8,128)(2,1)}, bf16[4,1,192,2048]{3,2,1,0:T(8,128)(2,1)S(1)}, u32[]{:S(2)}) copy-start(bf16[4,1,192,2048]{3,2,1,0:T(8,128)(2,1)S(1)} %get-tuple-element.189) | copy-start | bytes 9437188
  293.7 10.8 %copy-start.3 = (bf16[4,1,192,2048]{3,2,1,0:T(8,128)(2,1)}, bf16[4,1,192,2048]{3,2,1,0:T(8,128)(2,1)S(1)}, u32[]{:S(2)}) copy-start(bf16[4,1,192,2048]{3,2,1,0:T(8,128)(2,1)S(1)} %get-tuple-element.190) | copy-start | bytes 9437188
  296.0 24.4 %slice-start.2 = ((s8[8388608]{0:T(1024)(128)(4,1)}), s8[4194304]{0:T(1024)(128)(4,1)S(1)}, s32[]{:S(2)}) async-start(s8[8388608]{0:T(1024)(128)(4,1)} %bitcast.121), calls=%async_computation.14 | async-start | bytes 8388608
  304.6 15.9 %slice-start.3 = ((s8[8388608]{0:T(1024)(128)(4,1)}), s8[4194304]{0:T(1024)(128)(4,1)S(1)}, s32[]{:S(2)}) async-start(s8[8388608]{0:T(1024)(128)(4,1)} %bitcast.121), calls=%async_computation.15 | async-start | bytes 8388608
  329.0 226.8 %reduce-scatter.7.cloned.1.call-start = ((), (), s32[]{:S(2)}) async-start(), calls=%async_computation.5 | async-start | bytes 7864320 | tf_op jit(solution)/shard_map/reduce_scatter | solution.py:1276
  345.7 11.6 %copy-start.8 = (bf16[2048,768]{1,0:T(8,128)(2,1)}, bf16[2048,768]{1,0:T(8,128)(2,1)S(1)}, u32[]{:S(2)}) copy-start(bf16[2048,768]{1,0:T(8,128)(2,1)S(1)} %get-tuple-element.100.left1) | copy-start | bytes 9437188
  345.7 11.6 %copy-start.7 = (bf16[2048,768]{1,0:T(8,128)(2,1)}, bf16[2048,768]{1,0:T(8,128)(2,1)S(1)}, u32[]{:S(2)}) copy-start(bf16[2048,768]{1,0:T(8,128)(2,1)S(1)} %get-tuple-element.99.left0) | copy-start | bytes 9437188
  370.3 206.2 %reduce-scatter.11.cloned.1.call-start = ((), (), s32[]{:S(2)}) async-start(), calls=%async_computation.7 | async-start | bytes 1638400 | tf_op jit(solution)/shard_map/reduce_scatter | solution.py:1276
  466.0 6.7 copy-start.17
  476.9 212.9 %reduce-scatter.9.cloned.1.call-start = ((), (), s32[]{:S(2)}) async-start(), calls=%async_computation.6 | async-start | bytes 3276800 | tf_op jit(solution)/shard_map/reduce_scatter | solution.py:1276
  555.8 6.9 copy-start.13
  683.9 27.9 %copy-start.1 = (bf16[2048,768]{1,0:T(8,128)(2,1)S(1)}, bf16[2048,768]{1,0:T(8,128)(2,1)}, u32[]{:S(2)}) copy-start(bf16[2048,768]{1,0:T(8,128)(2,1)} %param.30) | copy-start | bytes 9437188
  (6 other events, 23.6 us)
Sparse Core Ops, SparseCore 0:
  10.2 58.8 all-gather.8
  70.6 31.5 all-gather.10
  103.8 118.5 all-gather.12
  223.7 61.6 all-gather.14
  329.1 59.2 reduce-scatter.4
  390.5 110.8 reduce-scatter.6
  503.7 33.3 reduce-scatter.10
  570.9 50.4 reduce-scatter.8

commit v5 on v4

--- a/solution.py
+++ b/solution.py
@@ -49,15 +49,6 @@
     return recur_gate, input_gate, log_decay
 
 
-def greet(count):
-    me = lax.axis_index("t")
-    barrier = pltpu.get_barrier_semaphore()
-    for step in range(1, count):
-        pl.semaphore_signal(barrier, inc=1, device_id={"t": lax.rem(me + step, count)}, device_id_type=MESH)
-    pl.semaphore_wait(barrier, count - 1)
-    return me
-
-
 def put_tiles(ref, at, values):
     tiles, lanes = ref.shape[0], ref.shape[2]
     short = tiles * lanes - values.shape[1]
@@ -76,30 +67,30 @@
     return jnp.concatenate(parts, axis=1)[:, :width]
 
 
-def exchange(count, me, send, slots, send_sem, recv_sem):
+def exchange_copy(step, send, target, other, send_sem, recv_sem):
+    return pltpu.make_async_remote_copy(
+        src_ref=send,
+        dst_ref=target,
+        send_sem=send_sem.at[step],
+        recv_sem=recv_sem.at[step],
+        device_id={"t": other},
+        device_id_type=MESH,
+    )
+
+
+def exchange_start(count, me, send, slots, send_sem, recv_sem):
     for step in range(1, count):
-        pltpu.make_async_remote_copy(
-            src_ref=send,
-            dst_ref=slots.at[me],
-            send_sem=send_sem.at[step],
-            recv_sem=recv_sem.at[step],
-            device_id={"t": lax.rem(me + step, count)},
-            device_id_type=MESH,
-        ).start()
+        exchange_copy(step, send, slots.at[me], lax.rem(me + step, count), send_sem, recv_sem).start()
+
+
+def exchange_wait(count, me, send, slots, send_sem, recv_sem):
     for step in range(1, count):
         other = lax.rem(me + count - step, count)
-        pltpu.make_async_remote_copy(
-            src_ref=send,
-            dst_ref=slots.at[other],
-            send_sem=send_sem.at[step],
-            recv_sem=recv_sem.at[step],
-            device_id={"t": other},
-            device_id_type=MESH,
-        ).wait()
+        exchange_copy(step, send, slots.at[other], other, send_sem, recv_sem).wait()
 
 
 def mixer_forward_kernel(
-    count, seg, rows_here, recur, gate, ids, ids_before, ids_after, wg0, wg1, vec_ref, cot, quarters,
+    count, seg, rows_here, branches, ids, ids_before, ids_after, wg0, wg1, vec_ref, cot, quarters,
     conv_out, decay_out, states_out, mixed_out, halo_out, cin_out, mask, cot_out, swapped,
     drive, h_ref, a_ref, ext, halo_send, halo_recv, summary, slots, send_sem, recv_sem, halo_sems,
     gather_send, gather_recv, swap_send, swap_recv,
@@ -110,10 +101,13 @@
     gather = Gather(place, cot, cot_out, gather_send, gather_recv)
     move = Swap(quarters, swapped, swap_send, swap_recv)
     rows = 8
+    width = branches.shape[1] // 2
+
+    def recur_at(at):
+        return branches[at, width:].astype(BF16).astype(F32)
+
     for r in range(rows):
-        halo_send[r * HALO : (r + 1) * HALO, :] = recur[
-            (rows + r) * seg + seg - 16 : (rows + r) * seg + seg, :
-        ].astype(F32)[16 - HALO :]
+        halo_send[r * HALO : (r + 1) * HALO, :] = recur_at(pl.ds((rows + r + 1) * seg - HALO, HALO))
     halo_copy = pltpu.make_async_remote_copy(
         src_ref=halo_send,
         dst_ref=halo_recv,
@@ -126,12 +120,8 @@
     gather.begin(0)
     gather.begin(1)
     move.begin()
-    halo_copy.wait()
     for r in range(rows):
-        halo_out[r * HALO : (r + 1) * HALO, :] = halo_recv[r * HALO : (r + 1) * HALO, :]
-        halo_out[(rows + r) * HALO : (rows + r + 1) * HALO, :] = recur[r * seg + seg - 16 : r * seg + seg, :].astype(F32)[
-            16 - HALO :
-        ]
+        halo_out[(rows + r) * HALO : (rows + r + 1) * HALO, :] = recur_at(pl.ds((r + 1) * seg - HALO, HALO))
     vec = vec_ref[...]
 
     def ids_of(ref, s):
@@ -150,7 +140,7 @@
 
     def local(s, none):
         at = pl.ds(pl.multiple_of(s * seg, seg), seg)
-        x = recur[at, :].astype(F32)
+        x = recur_at(at)
         ext[0:HALO, :] = halo_out[pl.ds(pl.multiple_of(s * HALO, HALO), HALO), :]
         ext[HALO : HALO + seg, :] = x
         m = mask[at, :]
@@ -166,8 +156,12 @@
         put_tiles(drive, at, scale * input_gate * conv_low.astype(F32))
         return none
 
-    lax.fori_loop(0, 2 * rows, local, 0)
+    lax.fori_loop(rows, 2 * rows, local, 0)
+    halo_copy.wait()
+    for r in range(rows):
+        halo_out[r * HALO : (r + 1) * HALO, :] = halo_recv[r * HALO : (r + 1) * HALO, :]
     gather.pass_first()
+    lax.fori_loop(0, rows, local, 0)
     tiles, lanes = drive.shape[0], drive.shape[2]
 
     def scan(k, carried):
@@ -183,15 +177,23 @@
             after.append((h, a))
         return tuple(after)
 
-    width = recur.shape[1]
     start = (jnp.zeros((2 * rows, lanes), F32), jnp.ones((2 * rows, lanes), F32))
     last = lax.fori_loop(0, seg, scan, (start,) * tiles, unroll=4)
     last_h = join_tiles([part[0] for part in last], width)
     last_a = join_tiles([part[1] for part in last], width)
     summary[0:rows, :] = last_a[rows:] * last_a[:rows]
     summary[rows : 2 * rows, :] = last_a[rows:] * last_h[:rows] + last_h[rows:]
+    exchange_start(count, me, summary, slots, send_sem, recv_sem)
     gather.pass_second()
-    exchange(count, me, summary, slots, send_sem, recv_sem)
+
+    def activate(s, none):
+        at = pl.ds(pl.multiple_of(s * seg, seg), seg)
+        act, _ = gelu_parts(branches[at, :width])
+        states_out[at, :] = act
+        return none
+
+    lax.fori_loop(0, 2 * rows, activate, 0)
+    exchange_wait(count, me, summary, slots, send_sem, recv_sem)
     carry = jnp.zeros((rows, width), F32)
     for z in range(count - 1):
         carry = jnp.where(z < me, slots[z, 0:rows, :] * carry + slots[z, rows : 2 * rows, :], carry)
@@ -201,8 +203,8 @@
     def finish(s, none):
         at = pl.ds(pl.multiple_of(s * seg, seg), seg)
         states = get_tiles(h_ref, at, width) + get_tiles(a_ref, at, width) * cin_out[pl.ds(s, 1), :]
+        act = states_out[at, :]
         states_out[at, :] = states
-        act, _ = gelu_parts(gate[at, :])
         mixed_out[at, :] = (act * states.astype(BF16).astype(F32)).astype(BF16)
         return none
 
@@ -213,8 +215,8 @@
 
 
 def mixer_backward_kernel(
-    count, seg, grad_mixed, gate, states, decay, conv_low_ref, recur, halo, cin, mask, wg0, wg1, wg0t, wg1t, vec_ref,
-    hidden, w_down, grad_gate_out, grad_recur_out, gw0_out, gw1_out, small_out, down_out,
+    count, seg, grad_mixed, branches, states, decay, conv_low_ref, halo, cin, mask, wg0, wg1, wg0t, wg1t, vec_ref,
+    hidden, w_down, grad_out, gw0_out, gw1_out, small_out, down_out,
     tot, prod, ext, halo_send, halo_recv, summary, slots, uin, send_sem, recv_sem, halo_sems, *buffers,
 ):
     place = Place()
@@ -223,14 +225,14 @@
     scatter = Scatter(place, pair_product([hidden], [w_down], down_out.shape[0]), *buffers)
     scatter.run_first()
     rows = 8
-    width = recur.shape[1]
+    width = branches.shape[1] // 2
     vec = vec_ref[...]
 
     def local(s, none):
         at = pl.ds(pl.multiple_of(s * seg, seg), seg)
-        act, slope = gelu_parts(gate[at, :])
+        act, slope = gelu_parts(branches[at, :width])
         gm = grad_mixed[at, :].astype(F32)
-        grad_gate_out[at, :] = (gm * states[at, :].astype(BF16).astype(F32) * slope).astype(BF16)
+        grad_out[at, :width] = (gm * states[at, :].astype(BF16).astype(F32) * slope).astype(BF16)
         put_tiles(tot, at, (gm * act).astype(BF16).astype(F32))
         return none
 
@@ -254,10 +256,11 @@
     last = lax.fori_loop(0, seg, scan, (start,) * tiles, unroll=4)
     u = join_tiles([part[0] for part in last], width)
     p = join_tiles([part[1] for part in last], width)
-    scatter.run_second()
     summary[0:rows, :] = p[:rows] * p[rows:]
     summary[rows : 2 * rows, :] = p[:rows] * u[rows:] + u[:rows]
-    exchange(count, me, summary, slots, send_sem, recv_sem)
+    exchange_start(count, me, summary, slots, send_sem, recv_sem)
+    scatter.run_second()
+    exchange_wait(count, me, summary, slots, send_sem, recv_sem)
     carry = jnp.zeros((rows, width), F32)
     for z in range(count - 1, 0, -1):
         carry = jnp.where(z > me, slots[z, 0:rows, :] * carry + slots[z, rows : 2 * rows, :], carry)
@@ -295,7 +298,7 @@
         turned = (((0,), (0,)), ((), ()))
         gw0_out[...] += lax.dot_general(conv_low, low0, turned, preferred_element_type=F32)
         gw1_out[...] += lax.dot_general(conv_low, low1, turned, preferred_element_type=F32)
-        x = recur[at, :].astype(F32)
+        x = branches[at, width:].astype(BF16).astype(F32)
         ext[0:HALO, :] = halo[pl.ds(pl.multiple_of(s * HALO, HALO), HALO), :]
         ext[HALO : HALO + seg, :] = x
 
@@ -324,7 +327,6 @@
         device_id_type=MESH,
     )
     halo_copy.start()
-    halo_copy.wait()
 
     def back(s, none):
         at = pl.ds(pl.multiple_of(s * seg, seg), seg)
@@ -343,10 +345,12 @@
 
         for k in range(1, 4):
             result = result + vec[k : k + 1] * ext[k : k + seg, :] * m[:, 2 + k : 3 + k]
-        grad_recur_out[at, :] = result.astype(BF16)
+        grad_out[at, width:] = result.astype(BF16)
         return none
 
-    lax.fori_loop(0, 2 * rows, back, 0)
+    lax.fori_loop(0, rows, back, 0)
+    halo_copy.wait()
+    lax.fori_loop(rows, 2 * rows, back, 0)
     scatter.run_third()
 
     def body(at):
@@ -364,8 +368,8 @@
     return pltpu.CompilerParams(collective_id=number, has_side_effects=True, vmem_limit_bytes=60 * 1024 * 1024)
 
 
-def mixer_forward(count, seg, rows_here, recur, gate, ids, wg0, wg1, vec, cot, quarters):
-    n, width = recur.shape
+def mixer_forward(count, seg, rows_here, branches, ids, wg0, wg1, vec, cot, quarters):
+    n, width = branches.shape[0], branches.shape[1] // 2
     full = functools.partial(jax.ShapeDtypeStruct, (n, width))
     tiles = -(-width // LANES)
     tiled = jax.ShapeDtypeStruct((tiles, n, LANES), F32)
@@ -380,7 +384,7 @@
             jax.ShapeDtypeStruct((8 * cot.shape[0], cot.shape[1]), BF16),
             jax.ShapeDtypeStruct((kinds, groups, part, depth), BF16),
         ),
-        in_specs=whole(8) + [ANYWHERE] * 2,
+        in_specs=whole(7) + [ANYWHERE] * 2,
         out_specs=(*whole(7), ANYWHERE, ANYWHERE),
         scratch_shapes=[
             pltpu.VMEM((tiles, n, LANES), F32),
@@ -398,11 +402,11 @@
             *swap_scratch(groups),
         ],
         compiler_params=mixer_params(1),
-    )(recur, gate, *ids, wg0, wg1, vec, cot, quarters)
-
-
-def mixer_backward(count, seg, grad_mixed, gate, states, decay, conv_low, recur, halo, cin, mask, wg0, wg1, wg0t, wg1t, vec, hidden, w_down):
-    n, width = recur.shape
+    )(branches, *ids, wg0, wg1, vec, cot, quarters)
+
+
+def mixer_backward(count, seg, grad_mixed, branches, states, decay, conv_low, halo, cin, mask, wg0, wg1, wg0t, wg1t, vec, hidden, w_down):
+    n, width = branches.shape[0], branches.shape[1] // 2
     tokens, depth = n // 8, w_down.shape[1]
     full = functools.partial(jax.ShapeDtypeStruct, (n, width))
     tiles = -(-width // LANES)
@@ -411,12 +415,12 @@
         functools.partial(mixer_backward_kernel, count, seg),
         name="mixer_backward",
         out_shape=(
-            full(BF16), full(BF16),
+            jax.ShapeDtypeStruct((n, 2 * width), BF16),
             jax.ShapeDtypeStruct((width, width), F32), jax.ShapeDtypeStruct((width, width), F32),
             jax.ShapeDtypeStruct((8, width), F32), jax.ShapeDtypeStruct((tokens, depth), F32),
         ),
-        in_specs=whole(16),
-        out_specs=tuple(whole(6)),
+        in_specs=whole(15),
+        out_specs=tuple(whole(5)),
         scratch_shapes=[
             pltpu.VMEM((tiles, n, LANES), F32),
             pltpu.VMEM((tiles, n, LANES), F32),
@@ -432,7 +436,7 @@
             *Scatter.scratch(tokens, depth),
         ],
         compiler_params=mixer_params(2),
-    )(grad_mixed, gate, states, decay, conv_low, recur, halo, cin, mask, wg0, wg1, wg0t, wg1t, vec, hidden, w_down)
+    )(grad_mixed, branches, states, decay, conv_low, halo, cin, mask, wg0, wg1, wg0t, wg1t, vec, hidden, w_down)
 
 
 class Place:
@@ -560,8 +564,6 @@
     up, down = {"t": lax.rem(me + 1, count)}, {"t": lax.rem(me + count - 1, count)}
     place.greet([place.peer(*offset) for offset in OTHERS if sum(offset) > 1] + [up, down])
     gather = Gather(place, normed, normed_out, send, recv)
-    gather.begin(0)
-    gather.begin(1)
     own = place.chunk(0, 0, 0)
     moved = []
 
@@ -579,6 +581,8 @@
 
     for number, offset in enumerate(OTHERS):
         move(number, ids, plane_ids.at[own], place.peer(*offset))
+    gather.begin(0)
+    gather.begin(1)
     plane_ids[own] = ids[...]
     for number, offset in enumerate(OTHERS):
         chunk = place.chunk(*offset)
@@ -773,13 +777,30 @@
     gather.finish()
 
 
-def turn_kernel(left0, left1, right0, right1, middle, gain, cot, grad_middle_out, gain_out, gathered, *scratch):
+def turn_kernel(left0, left1, right0, right1, middle, gain, cot, normed, grad_middle_out, gain_out, grads_out, gathered, *scratch):
     buffers, (block, send, recv) = scratch[:SCATTER_BUFFERS], scratch[SCATTER_BUFFERS:]
     tokens = cot.shape[0]
     place = Place()
     place.greet()
     scatter = Scatter(place, pair_product([left0, left1], [right0, right1], tokens), *buffers)
-    scatter.run()
+    hidden = left0.shape[1]
+
+    def weight_grads(start, stop):
+        def step(n, none):
+            at = pl.ds(pl.multiple_of(n * 256, 256), 256)
+            for k, part in enumerate((left0, left1)):
+                value = lax.dot_general(normed[:, at], part[...], (((0,), (0,)), ((), ())), preferred_element_type=F32)
+                grads_out[at, k * hidden : (k + 1) * hidden] = value.astype(BF16)
+            return none
+
+        lax.fori_loop(start, stop, step, 0)
+
+    steps = normed.shape[1] // 256
+    scatter.run_first()
+    weight_grads(0, steps // 4)
+    scatter.run_second()
+    weight_grads(steps // 4, steps // 2)
+    scatter.run_third()
     gain_out[...] = jnp.zeros_like(gain_out)
 
     def body(at):
@@ -798,7 +819,11 @@
     for part in (0, 1):
         for_slices(part * tokens // 2, (part + 1) * tokens // 2, body)
         gather.begin(part)
-    gather.pass_on()
+    weight_grads(steps // 2, 3 * steps // 4)
+    gather.pass_first()
+    weight_grads(3 * steps // 4, steps)
+    gather.pass_second()
+    gather.pass_third()
     scatter.finish()
     gather.finish()
 
@@ -920,23 +945,19 @@
 
 
 def final_kernel(
-    count, with_gates, left0, left1, right0, right1, own_in, gain, mlp_gains, pieces, reduced0, reduced1,
-    grad_out, gains_out, gates_out, owned0, owned1,
+    count, with_gates, left, right, own_in, gain, mlp_gains, pieces, grad_out, gains_out, gates_out,
     gain_sum, values, inbox, plane_box, sum_send, sum_recv, rows_recv, gates_all, gates_send, gates_recv,
-    send0, recv0, send1, recv1, *buffers,
+    *buffers,
 ):
     tokens, width = own_in.shape
     place = Place()
     me = lax.axis_index("t")
     place.greet([place.peer(*offset) for offset in BEYOND] + [{"t": lax.rem(me + step, count)} for step in range(1, count)])
-    scatter = Scatter(place, pair_product([left0, left1], [right0, right1], tokens), *buffers)
-    owners = [Owners(place, reduced0, owned0, send0, recv0), Owners(place, reduced1, owned1, send1, recv1)]
+    scatter = Scatter(place, pair_product([left], [right], tokens), *buffers)
     gates = GateSums(place, count, pieces, rows_recv, gates_all, gates_send, gates_recv)
     scatter.run_first()
     if with_gates:
         gates.begin()
-    owners[0].begin()
-    owners[1].begin()
     scatter.run_second()
     if with_gates:
         gates.pass_on()
@@ -963,12 +984,10 @@
         gates.finish(gates_out)
     else:
         gates_out[...] = jnp.zeros_like(gates_out)
-    owners[0].finish()
-    owners[1].finish()
     scatter.finish()
 
 
-def final_step(planes, lefts, rights, own_in, gain, mlp_gains, pieces, reduced):
+def final_step(planes, left, right, own_in, gain, mlp_gains, pieces):
     tokens, width = own_in.shape
     with_gates = pieces.shape[0] == planes
     block = pieces.shape[1:] if with_gates else (16, LANES)
@@ -982,10 +1001,9 @@
             jax.ShapeDtypeStruct((tokens, width), F32),
             jax.ShapeDtypeStruct(sums, F32),
             jax.ShapeDtypeStruct(block, F32),
-            *[jax.ShapeDtypeStruct(part.shape, part.dtype) for part in reduced],
         ),
-        in_specs=whole(8) + [ANYWHERE] * 2,
-        out_specs=(*whole(3), ANYWHERE, ANYWHERE),
+        in_specs=whole(6),
+        out_specs=tuple(whole(3)),
         scratch_shapes=[
             pltpu.VMEM((8, width), F32),
             pltpu.VMEM((4, *sums), F32),
@@ -997,12 +1015,10 @@
             pltpu.VMEM((slots, *block), BF16),
             pltpu.SemaphoreType.DMA((planes + 2,)),
             pltpu.SemaphoreType.DMA((planes + 2,)),
-            *OWNERS_SCRATCH,
-            *OWNERS_SCRATCH,
             *Scatter.scratch(tokens, width),
         ],
         compiler_params=mixer_params(7),
-    )(*lefts, *rights, own_in, gain[None], mlp_gains, pieces, *reduced)
+    )(left, right, own_in, gain[None], mlp_gains, pieces)
 
 
 def owners_kernel(reduced0, reduced1, out0, out1, send0, recv0, send1, recv1):
@@ -1015,7 +1031,7 @@
         part.finish()
 
 
-def owners_step(reduced):
+def owners_step(number, reduced):
     return pl.pallas_call(
         owners_kernel,
         name="owners_step",
@@ -1023,7 +1039,7 @@
         in_specs=[ANYWHERE] * 2,
         out_specs=(ANYWHERE,) * 2,
         scratch_shapes=[*OWNERS_SCRATCH, *OWNERS_SCRATCH],
-        compiler_params=mixer_params(8),
+        compiler_params=mixer_params(number),
     )(*reduced)
 
 
@@ -1087,7 +1103,7 @@
     )(mixed, w_out, own_in, gain[None])
 
 
-def turn_step(left0, left1, right0, right1, middle, gain, cot):
+def turn_step(left0, left1, right0, right1, middle, gain, cot, normed):
     tokens, width = cot.shape
     return pl.pallas_call(
         turn_kernel,
@@ -1095,13 +1111,14 @@
         out_shape=(
             jax.ShapeDtypeStruct((tokens, width), F32),
             jax.ShapeDtypeStruct((8, width), F32),
+            jax.ShapeDtypeStruct((width, 2 * left0.shape[1]), BF16),
             jax.ShapeDtypeStruct((8 * tokens, width), BF16),
         ),
-        in_specs=whole(7),
-        out_specs=(*whole(2), ANYWHERE),
+        in_specs=whole(8),
+        out_specs=(*whole(3), ANYWHERE),
         scratch_shapes=Scatter.scratch(tokens, width) + [pltpu.VMEM((tokens, width), BF16)] + GATHER_SCRATCH,
         compiler_params=mixer_params(5),
-    )(left0, left1, right0, right1, middle, gain[None], cot)
+    )(left0, left1, right0, right1, middle, gain[None], cot, normed)
 
 
 class Swap:
@@ -1231,12 +1248,12 @@
     else:
         in_w = whole_units(in_own)
         out_quarters = jnp.zeros((row_groups, 1, 16, width), BF16)
-    w_gate, w_recur = in_w.reshape(2, channels, width)
+    in_w = in_w.reshape(2 * channels, width)
     hidden_part = mlp_in.shape[2] // row_groups
-    mlp_w = spread_units(quarter(mlp_in, hidden_part, late_r).transpose(1, 2, 0))
-    w_left = mlp_w[:, 0].reshape(-1, width)
-    w_right = mlp_w[:, 1].reshape(-1, width)
-    w_down = spread_units(quarter(down_weight, hidden_part, late_r).T).reshape(-1, width)
+    w_left, w_right, w_down = [
+        spread_units(quarter(weight, hidden_part, late_r).T).reshape(-1, width)
+        for weight in (mlp_in[:, 0], mlp_in[:, 1], down_weight)
+    ]
 
     def own(values):
         return lax.dynamic_slice_in_dim(values, first, channels, values.ndim - 1)
@@ -1260,10 +1277,9 @@
     spread = spread.reshape(2, channels, channels)
     wg0, wg1 = spread[0], spread[1]
 
-    gate_branch = nt(normed, w_gate, F32)
-    recur = nt(normed, w_recur, BF16)
+    branches = nt(normed, in_w, F32)
     conv_low, decay, states, mixed, halo, cin, mask, cot, w_out = mixer_forward(
-        planes, seg, rows_here, recur, gate_branch, ids, wg0, wg1, vec, cot_own, out_quarters
+        planes, seg, rows_here, branches, ids, wg0, wg1, vec, cot_own, out_quarters
     )
     w_out = (w_out if direct else whole_units(out_own)).reshape(channels, width)
     middle, normed_two = middle_step(mixed, w_out, own_in, mlp_gain)
@@ -1281,22 +1297,21 @@
     grad_hidden = nt(cot, w_down, F32)
     grad_left = (grad_hidden * right * slope).astype(BF16)
     grad_right = (grad_hidden * act).astype(BF16)
-    grad_mlp_in = jnp.concatenate([tn(normed_two, grad_left, BF16), tn(normed_two, grad_right, BF16)], axis=1)
-    grad_mlp_in, grad_left, grad_right = lax.optimization_barrier((grad_mlp_in, grad_left, grad_right))
+    grad_middle, grad_mlp_gain, grad_mlp_in, grad_mid = turn_step(
+        grad_left, grad_right, w_left, w_right, middle, mlp_gain, cot_own, normed_two
+    )
     grad_mlp_in = over_planes(grad_mlp_in)
-    grad_middle, grad_mlp_gain, grad_mid = turn_step(grad_left, grad_right, w_left, w_right, middle, mlp_gain, cot_own)
     grad_down, grad_mid = lax.optimization_barrier((grad_down, grad_mid))
     grad_out = tn(grad_mid, mixed, BF16)
     grad_mixed = nt(grad_mid, w_out, F32)
     grad_out, grad_mixed = lax.optimization_barrier((grad_out, grad_mixed))
     grad_out = over_planes(grad_out)
-    grad_gate, grad_recur, gw0, gw1, small, down = mixer_backward(
-        planes, seg, grad_mixed, gate_branch, states, decay, conv_low, recur, halo, cin, mask, wg0, wg1, wg0.T, wg1.T, vec,
+    grad_branches, gw0, gw1, small, down = mixer_backward(
+        planes, seg, grad_mixed, branches, states, decay, conv_low, halo, cin, mask, wg0, wg1, wg0.T, wg1.T, vec,
         hidden, w_down,
     )
-    grad_mlp_in, grad_gate, grad_recur = lax.optimization_barrier((grad_mlp_in, grad_gate, grad_recur))
-    grad_in = jnp.concatenate([tn(normed, grad_gate, BF16), tn(normed, grad_recur, BF16)], axis=1)
-    grad_in, grad_gate, grad_recur = lax.optimization_barrier((grad_in, grad_gate, grad_recur))
+    grad_in = tn(normed, grad_branches, BF16)
+    grad_mlp_in, grad_in, grad_branches = lax.optimization_barrier((grad_mlp_in, grad_in, grad_branches))
     grad_in = over_planes(grad_in)
     outputs = (middle + down).astype(BF16).reshape(inputs.shape)
     own_rows = width // (planes * members)
@@ -1313,14 +1328,17 @@
     if direct:
         pieces = gate_grads.reshape(gate_grads.shape[0], row_groups, -1).transpose(1, 0, 2)
         pieces = jnp.pad(pieces.astype(BF16), ((0, 0), (0, -pieces.shape[1] % 16), (0, LANES - part)))
-    reduced = [part.reshape(members, own_rows, -1) for part in (grad_mlp_in, grad_down)]
-    grad_in_norm, gains, gate_sums, owned_mlp_in, owned_down = final_step(
-        planes, [grad_gate, grad_recur], [w_gate, w_recur], own_in, mix_gain, grad_mlp_gain, pieces, reduced
-    )
+    grad_in_norm, gains, gate_sums = final_step(planes, grad_branches, in_w, own_in, mix_gain, grad_mlp_gain, pieces)
     grad_inputs = (grad_middle + grad_in_norm).reshape(inputs.shape)
     index = ((t * 2 + i) * row_groups + r) * own_rows
     gains = lax.dynamic_slice_in_dim(gains.reshape(2, width), index, own_rows, 1)
-    owned_in, owned_out = owners_step([part.reshape(members, own_rows, -1) for part in (grad_in, grad_out)])
+
+
+    def exchanged(number, *grads):
+        return owners_step(number, [grad.reshape(members, own_rows, -1) for grad in grads])
+
+    owned_mlp_in, owned_down = exchanged(8, grad_mlp_in, grad_down)
+    owned_in, owned_out = exchanged(9, grad_in, grad_out)
 
     def columns(owned, kinds, hidden):
         if direct:

time: 724 us -> 750 us (1.036)
  waiting for transfers between devices: 0.2 us -> 32.9 us
  matrix products: 108 us -> 88.2 us
  Pallas kernels: 519 us -> 534 us
    reduce_scatter x4, waiting for transfers between devices: 0.05 us -> 32.7 us  [over_planes(): return lax.psum_scatter(grad, 't', scatter_dimension=0, tiled=True)]
    pallas_call x1 -> x2, Pallas kernels: 15.3 us -> 44.7 us  [owners_step(): pl.pallas_call(owners_kernel, name='owners_step', out_shape=tuple((jax.Sh...]
    pallas_call x1, Pallas kernels: 91.4 us -> 65.6 us  [final_step(): pl.pallas_call(functools.partial(final_kernel, planes, with_gates), name=...]
    dot_general x6 -> x3, matrix products: 46.6 us -> 26.8 us  [tn(): lax.dot_general(left, right, (((0,), (0,)), ((), ())), preferred_element_...]
    dynamic_slice x2 -> x4, local copies, waits for them, and re-layouts: 7.23 us -> 20.9 us  [quarter(): return lax.dynamic_slice_in_dim(weight, rank * part, part, weight.ndim - 1)]
    unnamed x48 -> x25, local copies, waits for them, and re-layouts: 13.9 us -> 4.97 us
    slice x1, local copies, waits for them, and re-layouts: 3.84 us -> 12.7 us  [per_device(): mlp_in[:, 0]]
    pallas_call x1, Pallas kernels: 76.2 us -> 84.1 us  [mixer_backward(): pl.pallas_call(functools.partial(mixer_backward_kernel, count, seg), name...]
  transfers between devices with their start and end apart: 8 -> 9, of which waited for: 0 -> 2; matrix products, arithmetic and copies ran while one was open for 24% -> 21% of each run, Pallas kernels for 69% -> 69%
where the time goes in v5:
time: 750 us; the launch traced here: 745 us
  Pallas kernels  534 us (71%)
  matrix products  88.2 us (12%)
  local copies, waits for them, and re-layouts  63.1 us (8%)
  waiting for transfers between devices  32.9 us (4%)
  between operations  14.5 us (2%)
  other arithmetic  12.4 us (2%)
    pallas_call x1, Pallas kernels, turn_step(): pl.pallas_call(turn_kernel, name='turn_step', out_shape=(jax.ShapeDtypeSt...  99.5 us
    pallas_call x1, Pallas kernels, middle_step(): pl.pallas_call(middle_kernel, name='middle_step', out_shape=(jax.ShapeDty...  88 us
    pallas_call x1, Pallas kernels, mixer_backward(): pl.pallas_call(functools.partial(mixer_backward_kernel, count, seg), name...  84.1 us
    pallas_call x1, Pallas kernels, final_step(): pl.pallas_call(functools.partial(final_kernel, planes, with_gates), name=...  65.6 us
    pallas_call x1, Pallas kernels, mixer_forward(): pl.pallas_call(functools.partial(mixer_forward_kernel, count, seg, rows_h...  63.5 us
    dot_general x5, matrix products, nt(): lax.dot_general(left, right, (((1,), (1,)), ((), ())), preferred_element_...  61.4 us
    pallas_call x1, Pallas kernels, first_gather(): pl.pallas_call(functools.partial(first_gather_kernel, planes), name='firs...  47.3 us
    pallas_call x2, Pallas kernels, owners_step(): pl.pallas_call(owners_kernel, name='owners_step', out_shape=tuple((jax.Sh...  44.7 us
  transfers between devices with their start and end apart: 9, of which 2 were waited for; matrix products, arithmetic and copies ran while one was open for 21% of the time, Pallas kernels for 69%

profile of v5, /device:TPU:0, one launch (start us, length us, event | category | flops | bytes accessed | tf_op | source)
XLA Modules:
  0.0 745.2 jit_solution(7880855105158020960)
XLA Ops:
  16.6 47.3 %first_gather.1 = (bf16[2048,2048]{1,0:T(8,128)(2,1)}, f32[8,8,128]{2,1,0:T(8,128)}, f32[8,8,128]{2,1,0:T(8,128)}, f32[8,8,128]{2,1,0:T(8,128)}) custom-call(bf16[256,2048]{1,0:T(8,128)(2,1)} %multiply_convert_fusion.3.normed, f32[8,128]{1,0:T(8,128)} %pad.17.ids), custom_call_target="tpu_custom_call" | custom-call | tf_op jit(solution)/shard_map/first_gather/pallas_call | solution.py:1082
  63.9 12.7 %fusion.13 = (bf16[2048,1,768]{2,1,0:T(2,128)(2,1)S(1)}, bf16[2048,1,768]{2,1,0:T(2,128)(2,1)S(1)}) fusion(bf16[2048,2,768]{2,1,0:T(2,128)(2,1)} %param.29), kind=kLoop, calls=%fused_computation.53 | loop fusion | bytes 12582912 | tf_op jit(solution)/shard_map/slice | solution.py:1255
  76.6 8.0 %constant_dynamic-slice_fusion.2 = (bf16[2048,1,192]{2,1,0:T(2,128)(2,1)}, bf16[2048,1,192]{2,1,0:T(2,128)(2,1)}) fusion(bf16[2048,1,768]{2,1,0:T(2,128)(2,1)S(1)} %get-tuple-element.178, s32[]{:T(128)S(6)} %select_n.50, bf16[2048,1,768]{2,1,0:T(2,128)(2,1)S(1)} %get-tuple-element.177), kind=kLoop, calls=%fused_computation.36 | loop fusion | bytes 3145732 | tf_op jit(solution)/shard_map/dynamic_slice | solution.py:1236
  84.6 5.7 copy.73
  90.5 5.7 copy.74
  109.7 29.4 %swap.1 = bf16[2,4,80,2048]{3,2,1,0:T(8,128)(2,1)} custom-call(bf16[4,2,80,2048]{3,2,1,0:T(8,128)(2,1)} %bitcast.88), custom_call_target="tpu_custom_call" | custom-call | tf_op jit(solution)/shard_map/swap/pallas_call | solution.py:1177
  139.1 11.4 %fusion.16.branches = f32[2048,640]{1,0:T(8,128)} fusion(bf16[2048,2048]{1,0:T(8,128)(2,1)} %get-tuple-element.80, bf16[640,2048]{1,0:T(8,128)(2,1)} %bitcast.81), kind=kOutput, calls=%fused_computation.56 | convolution fusion | flops 5368709120 | bytes 16252928 | tf_op jit(solution)/shard_map/dot_general | solution.py:1193
  150.6 63.5 %mixer_forward.1 = (bf16[2048,320]{1,0:T(8,128)(2,1)}, f32[3,2048,128]{2,1,0:T(8,128)}, f32[2048,320]{1,0:T(8,128)}, bf16[2048,320]{1,0:T(8,128)(2,1)}, f32[128,...) custom-call(f32[2048,640]{1,0:T(8,128)} %fusion.16.branches, ...), custom_call_target="tpu_custom_call" | custom-call | tf_op jit(solution)/shard_map/mixer_forward/pallas_call | solution.py:377
  214.1 88.0 %middle_step.1 = (f32[256,2048]{1,0:T(8,128)}, bf16[2048,2048]{1,0:T(8,128)(2,1)}) custom-call(bf16[2048,320]{1,0:T(8,128)(2,1)} %get-tuple-element.85.left, bf16[320,2048]{1,0:T(8,128)(2,1)} %bitcast.96, bf16[256,2048]{1,0:T(8,128)(2,1)} %bitcast.79, f32[1,2048]{1,0:T(1,128)} %bitcast.103), custom_call_target="tpu_custom_call" | custom-call | tf_op jit(solution)/shard_map/middle_step/pallas_call | solution.py:1095
  302.1 11.8 %fusion.17 = f32[2048,768]{1,0:T(8,128)} fusion(bf16[2048,2048]{1,0:T(8,128)(2,1)} %get-tuple-element.89.normed, bf16[768,2048]{1,0:T(8,128)(2,1)} %all-gather.15.cloned.1.call-done.right0), kind=kOutput, calls=%fused_computation.57 | convolution fusion | flops 6442450944 | bytes 17825792 | tf_op jit(solution)/shard_map/dot_general | solution.py:1193
  313.9 13.7 %multiply_convert_fusion.2 = (bf16[2048,768]{1,0:T(8,128)(2,1)S(1)}, f32[2048,768]{1,0:T(8,128)}) fusion(f32[2048,768]{1,0:T(8,128)} %fusion.17, bf16[2048,2048]{1,0:T(8,128)(2,1)} %get-tuple-element.89.normed, bf16[768,2048]{1,0:T(8,128)(2,1)} %all-gather.17.cloned.1.call-done.right1), kind=kOutput, calls=%fused_computation.2 | convolution fusion | flops 6458179584 | bytes 27262976 | tf_op jit(solution)/shard_map/dot_general | solution.py:1193
  327.6 11.5 %convolution_convert_fusion = bf16[2048,768]{1,0:T(8,128)(2,1)} fusion(bf16[2048,2048]{1,0:T(8,128)(2,1)} %get-tuple-element.88, bf16[2048,768]{1,0:T(8,128)(2,1)S(1)} %get-tuple-element.102.hidden), kind=kOutput, calls=%fused_computation.6 | convolution fusion | flops 6444023808 | bytes 14680064 | tf_op jit(solution)/shard_map/dot_general | solution.py:1197
  339.2 18.6 %multiply_convert_fusion = (bf16[2048,768]{1,0:T(8,128)(2,1)}, bf16[2048,768]{1,0:T(8,128)(2,1)}) fusion(f32[2048,768]{1,0:T(8,128)} %fusion.17, f32[2048,768]{1,0:T(8,128)} %get-tuple-element.194, bf16[2048,2048]{1,0:T(8,128)(2,1)} %get-tuple-element.88, bf16[768,2048]{1,0:T(8,128)(2,1)} %all-gather.19.cloned.1.call-done.w_down), kind=kOutput, calls=%fused_computation | convolution fusion | flops 6477053952 | bytes 30408704 | tf_op jit(solution)/shard_map/dot_general | solution.py:1193
  357.8 99.5 %turn_step.1 = (f32[256,2048]{1,0:T(8,128)}, f32[8,2048]{1,0:T(8,128)}, bf16[2048,1536]{1,0:T(8,128)(2,1)}, bf16[2048,2048]{1,0:T(8,128)(2,1)}) custom-call(bf16[2048,768]{1,0:T(8,128)(2,1)} %get-tuple-element.176.left0, bf16[2048,768]{1,0:T(8,128)(2,1)} %get-tuple-element.175.left1, bf16[768,2048]{1,0:T(8,128)(2,1)} %all-gather.15.cloned.1.call-done.right0, ...), custom_call_target="tpu_custom_call" | custom-call | tf_op jit(solution)/shard_map/turn_step/pallas_call | solution.py:1108
  457.5 5.9 fusion.18
  465.3 4.1 convolution_convert_fusion.2
  471.9 84.1 %mixer_backward.1 = (bf16[2048,640]{1,0:T(8,128)(2,1)}, f32[320,320]{1,0:T(8,128)}, f32[320,320]{1,0:T(8,128)}, f32[8,320]{1,0:T(8,128)}, f32[256,2048]{1,0:T(8,128)}) custom-call(f32[2048,320]{1,0:T(8,128)} %copy.76.grad_mixed, f32[2048,640]{1,0:T(8,128)} %fusion.16.branches, f32[2048,320]{1,0:T(8,128)} %get-tuple-element.96.states, ...), custom_call_target="tpu_custom_call" | custom-call | tf_op jit(solution)/shard_map/mixer_backward/pallas_call | solution.py:414
  556.0 11.1 %convolution_convert_fusion.1 = bf16[2048,640]{1,0:T(8,128)(2,1)} fusion(bf16[2048,2048]{1,0:T(8,128)(2,1)} %get-tuple-element.80, bf16[2048,640]{1,0:T(8,128)(2,1)} %get-tuple-element.107.left), kind=kOutput, calls=%fused_computation.7 | convolution fusion | flops 5370019840 | bytes 13631488 | tf_op jit(solution)/shard_map/dot_general | solution.py:1197
  573.9 30.3 %reduce-scatter.11.cloned.1.call-done = bf16[512,320]{0,1:T(8,128)(2,1)} async-done(((bf16[2048,320]{0,1:T(8,128)(2,1)}), bf16[512,320]{0,1:T(8,128)(2,1)}) %reduce-scatter.11.cloned.1.call-update) | async-done | bytes 327696 | tf_op jit(solution)/shard_map/reduce_scatter | solution.py:1292
  606.1 65.6 %final_step.1 = (f32[256,2048]{1,0:T(8,128)}, f32[32,128]{1,0:T(8,128)}, f32[336,128]{1,0:T(8,128)}) custom-call(bf16[2048,640]{1,0:T(8,128)(2,1)} %get-tuple-element.107.left, bf16[640,2048]{1,0:T(8,128)(2,1)} %bitcast.82, bf16[256,2048]{1,0:T(8,128)(2,1)} %bitcast.80, f32[1,2048]{1,0:T(1,128)} %bitcast.105, f32[8,2048]{1,0:T(8,128)} %get-tuple-element.108.mlp_gains, ...), custom_call_target="tpu_custom_call" | custom-call | tf_op jit(solution)/shard_map/final_step/pallas_call | solution.py:997
  676.6 29.4 %owners_step.3 = (bf16[8,64,1536]{2,1,0:T(8,128)(2,1)}, bf16[8,64,768]{2,1,0:T(8,128)(2,1)}) custom-call(bf16[8,64,1536]{2,1,0:T(8,128)(2,1)} %bitcast.92, bf16[8,64,768]{2,1,0:T(8,128)(2,1)} %bitcast.100), custom_call_target="tpu_custom_call" | custom-call | tf_op jit(solution)/shard_map/owners_step/pallas_call | solution.py:1035
  706.1 4.2 place_columns.6
  712.8 3.9 add.118
  718.6 15.3 %owners_step.2 = (bf16[8,64,640]{2,1,0:T(8,128)(2,1)}, bf16[8,64,320]{2,1,0:T(8,128)(2,1)}) custom-call(bf16[8,64,640]{2,1,0:T(8,128)(2,1)} %bitcast.101, bf16[8,64,320]{2,1,0:T(8,128)(2,1)} %bitcast.93), custom_call_target="tpu_custom_call" | custom-call | tf_op jit(solution)/shard_map/owners_step/pallas_call | solution.py:1035
  (103 shorter events, 49.7 us)
Async XLA Ops:
  7.2 89.1 %copy-start = (bf16[2048,768]{1,0:T(8,128)(2,1)S(1)}, bf16[2048,768]{1,0:T(8,128)(2,1)}, u32[]{:S(2)}) copy-start(bf16[2048,768]{1,0:T(8,128)(2,1)} %param.30) | copy-start | bytes 9437188
  7.2 102.5 %all-gather.11.cloned.1.call-start = ((), (), s32[]{:S(2)}) async-start(), calls=%async_computation.8 | async-start | bytes 3276800 | tf_op jit(solution)/shard_map/all_gather | solution.py:1239
  9.4 141.2 %all-gather.13.cloned.1.call-start = ((), (), s32[]{:S(2)}) async-start(), calls=%async_computation.9 | async-start | bytes 1638400 | tf_op jit(solution)/shard_map/all_gather | solution.py:1239
  11.2 290.9 %all-gather.15.cloned.1.call-start = ((), (), s32[]{:S(2)}) async-start(), calls=%async_computation.10 | async-start | bytes 3932160 | tf_op jit(solution)/shard_map/all_gather | solution.py:1239
  90.4 223.5 %all-gather.17.cloned.1.call-start = ((), (), s32[]{:S(2)}) async-start(), calls=%async_computation.11 | async-start | bytes 3932160 | tf_op jit(solution)/shard_map/all_gather | solution.py:1239
  96.2 242.9 %all-gather.19.cloned.1.call-start = ((), (), s32[]{:S(2)}) async-start(), calls=%async_computation.12 | async-start | bytes 3932160 | tf_op jit(solution)/shard_map/all_gather | solution.py:1239
  99.9 357.5 %reduce-scatter.5.cloned.1.call-start = ((), (), s32[]{:S(2)}) async-start(), calls=%async_computation.4 | async-start | bytes 3932160 | tf_op jit(solution)/shard_map/reduce_scatter | solution.py:1292
  103.0 47.6 %copy-start.4 = (bf16[320,320]{0,1:T(8,128)(2,1)}, bf16[320,320]{0,1:T(8,128)(2,1)S(1)}, u32[]{:S(2)}) copy-start(bf16[320,320]{0,1:T(8,128)(2,1)S(1)} %squeeze.28) | copy-start | bytes 614404
  104.4 46.2 %copy-start.5 = (bf16[320,320]{0,1:T(8,128)(2,1)}, bf16[320,320]{0,1:T(8,128)(2,1)S(1)}, u32[]{:S(2)}) copy-start(bf16[320,320]{0,1:T(8,128)(2,1)S(1)} %squeeze.29) | copy-start | bytes 614404
  327.6 11.5 %copy-start.3 = (bf16[2048,768]{1,0:T(8,128)(2,1)}, bf16[2048,768]{1,0:T(8,128)(2,1)S(1)}, u32[]{:S(2)}) copy-start(bf16[2048,768]{1,0:T(8,128)(2,1)S(1)} %get-tuple-element.102.hidden) | copy-start | bytes 9437188
  339.2 230.4 %reduce-scatter.7.cloned.1.call-start = ((), (), s32[]{:S(2)}) async-start(), calls=%async_computation.5 | async-start | bytes 7864320 | tf_op jit(solution)/shard_map/reduce_scatter | solution.py:1292
  457.4 146.8 %reduce-scatter.11.cloned.1.call-start = ((), (), s32[]{:S(2)}) async-start(), calls=%async_computation.7 | async-start | bytes 1638400 | tf_op jit(solution)/shard_map/reduce_scatter | solution.py:1292
  457.4 6.0 copy-start.6
  457.4 7.9 %copy-start.10 = (bf16[2048,2048]{1,0:T(8,128)(2,1)S(1)}, bf16[2048,2048]{1,0:T(8,128)(2,1)}, u32[]{:S(2)}) copy-start(bf16[2048,2048]{1,0:T(8,128)(2,1)} %get-tuple-element.94) | copy-start | bytes 25165828
  469.5 249.1 %reduce-scatter.9.cloned.1.call-start = ((), (), s32[]{:S(2)}) async-start(), calls=%async_computation.6 | async-start | bytes 3276800 | tf_op jit(solution)/shard_map/reduce_scatter | solution.py:1292
  556.0 13.7 %copy-start.9 = (f32[8,320]{1,0:T(8,128)S(1)}, f32[8,320]{1,0:T(8,128)}, u32[]{:S(2)}) copy-start(f32[8,320]{1,0:T(8,128)} %get-tuple-element.111) | copy-start | bytes 30724
  556.0 13.7 %copy-start.7 = (f32[320,320]{1,0:T(8,128)S(1)}, f32[320,320]{1,0:T(8,128)}, u32[]{:S(2)}) copy-start(f32[320,320]{1,0:T(8,128)} %get-tuple-element.109) | copy-start | bytes 1228804
  556.0 13.7 %copy-start.8 = (f32[320,320]{1,0:T(8,128)S(1)}, f32[320,320]{1,0:T(8,128)}, u32[]{:S(2)}) copy-start(f32[320,320]{1,0:T(8,128)} %get-tuple-element.110) | copy-start | bytes 1228804
  567.2 3.9 copy-start.2
  710.2 28.2 %copy-start.1 = (bf16[2048,768]{1,0:T(8,128)(2,1)S(1)}, bf16[2048,768]{1,0:T(8,128)(2,1)}, u32[]{:S(2)}) copy-start(bf16[2048,768]{1,0:T(8,128)(2,1)} %param.30) | copy-start | bytes 9437188
Sparse Core Ops, SparseCore 0:
  10.2 58.8 all-gather.10
  70.6 31.4 all-gather.12
  104.3 64.5 all-gather.14
  170.9 64.1 all-gather.16
  237.1 62.0 all-gather.18
  339.3 58.5 reduce-scatter.4
  457.5 112.0 reduce-scatter.6
  572.5 31.6 reduce-scatter.10
  606.5 56.3 reduce-scatter.8

commit v6 on v5

--- a/solution.py
+++ b/solution.py
@@ -20,7 +20,7 @@
 LANES = 128
 SLICE = 16
 ANYWHERE = pl.BlockSpec(memory_space=pl.ANY)
-GATHER_SCRATCH = [pltpu.SemaphoreType.DMA((13,))] * 2
+GATHER_SCRATCH = [pltpu.SemaphoreType.DMA((14,))] * 2
 
 
 def gelu_parts(x):
@@ -47,6 +47,15 @@
     input_gate = sigmoid(logits1)
     log_decay = -vec[7:8] * recur_gate
     return recur_gate, input_gate, log_decay
+
+
+def spread_blocks(gates, out):
+    size, width = gates.shape[1], gates.shape[2]
+    column = lax.broadcasted_iota(jnp.int32, (size, width), 1) // size
+    for k in range(2):
+        block = gates[k].astype(F32)
+        for n in range(width // size):
+            out[k, n * size : (n + 1) * size, :] = jnp.where(column == n, block, 0.0).astype(BF16)
 
 
 def put_tiles(ref, at, values):
@@ -90,18 +99,24 @@
 
 
 def mixer_forward_kernel(
-    count, seg, rows_here, branches, ids, ids_before, ids_after, wg0, wg1, vec_ref, cot, quarters,
+    count, seg, rows_here, branches_far, ids, ids_before, ids_after, gate_blocks, vec_ref, cot, quarters,
     conv_out, decay_out, states_out, mixed_out, halo_out, cin_out, mask, cot_out, swapped,
     drive, h_ref, a_ref, ext, halo_send, halo_recv, summary, slots, send_sem, recv_sem, halo_sems,
-    gather_send, gather_recv, swap_send, swap_recv,
+    gather_send, gather_recv, swap_send, swap_recv, branches, wg, load,
 ):
     place = Place()
     me = lax.axis_index("t")
+    loaded = pltpu.make_async_copy(branches_far, branches, load.at[0])
+    loaded.start()
     place.greet([place.peer(0, 1, 1)] + [{"t": lax.rem(me + step, count)} for step in range(1, count)])
     gather = Gather(place, cot, cot_out, gather_send, gather_recv)
     move = Swap(quarters, swapped, swap_send, swap_recv)
+    gather.begin_whole()
+    move.begin()
+    spread_blocks(gate_blocks, wg)
     rows = 8
     width = branches.shape[1] // 2
+    loaded.wait()
 
     def recur_at(at):
         return branches[at, width:].astype(BF16).astype(F32)
@@ -117,9 +132,6 @@
         device_id_type=MESH,
     )
     halo_copy.start()
-    gather.begin(0)
-    gather.begin(1)
-    move.begin()
     for r in range(rows):
         halo_out[(rows + r) * HALO : (rows + r + 1) * HALO, :] = recur_at(pl.ds((r + 1) * seg - HALO, HALO))
     vec = vec_ref[...]
@@ -149,7 +161,7 @@
             conv = conv + vec[k : k + 1] * ext[HALO - k : HALO - k + seg, :] * m[:, k - 1 : k]
         conv_low = conv.astype(BF16)
         conv_out[at, :] = conv_low
-        recur_gate, input_gate, log_decay = gate_values(conv_low, wg0[...], wg1[...], vec)
+        recur_gate, input_gate, log_decay = gate_values(conv_low, wg[0], wg[1], vec)
         keep = m[:, 0:1]
         put_tiles(decay_out, at, jnp.exp(log_decay) * keep)
         scale = (1.0 - keep) + keep * jnp.sqrt(one_minus_exp(-2.0 * log_decay))
@@ -215,15 +227,31 @@
 
 
 def mixer_backward_kernel(
-    count, seg, grad_mixed, branches, states, decay, conv_low_ref, halo, cin, mask, wg0, wg1, wg0t, wg1t, vec_ref,
-    hidden, w_down, grad_out, gw0_out, gw1_out, small_out, down_out,
-    tot, prod, ext, halo_send, halo_recv, summary, slots, uin, send_sem, recv_sem, halo_sems, *buffers,
+    count, seg, grad_mixed_far, branches_far, states_far, decay_far, conv_far, mask_far, halo, cin, gate_blocks, vec_ref,
+    hidden, w_down, middle_far, grad_out, gw0_out, gw1_out, small_out, outputs,
+    tot, prod, ext, halo_send, halo_recv, summary, slots, uin, send_sem, recv_sem, halo_sems,
+    grad_mixed, branches, states, decay, conv_low_ref, mask, middle, wg, load, *buffers,
 ):
     place = Place()
+    pairs = (
+        (grad_mixed_far, grad_mixed),
+        (branches_far, branches),
+        (states_far, states),
+        (decay_far, decay),
+        (conv_far, conv_low_ref),
+        (mask_far, mask),
+        (middle_far, middle),
+    )
+    loads = [pltpu.make_async_copy(far, near, load.at[n]) for n, (far, near) in enumerate(pairs)]
+    for part in loads:
+        part.start()
     me = lax.axis_index("t")
     place.greet([{"t": lax.rem(me + step, count)} for step in range(1, count)])
-    scatter = Scatter(place, pair_product([hidden], [w_down], down_out.shape[0]), *buffers)
+    scatter = Scatter(place, pair_product([hidden], [w_down], outputs.shape[0]), *buffers)
+    spread_blocks(gate_blocks, wg)
     scatter.run_first()
+    for part in loads:
+        part.wait()
     rows = 8
     width = branches.shape[1] // 2
     vec = vec_ref[...]
@@ -280,7 +308,7 @@
         conv_vals = conv_low.astype(F32)
         m = mask[at, :]
         keep = m[:, 0:1]
-        recur_gate, input_gate, log_decay = gate_values(conv_low, wg0[...], wg1[...], vec)
+        recur_gate, input_gate, log_decay = gate_values(conv_low, wg[0], wg[1], vec)
         root = jnp.sqrt(one_minus_exp(-2.0 * log_decay))
         scale = (1.0 - keep) + keep * root
         driven_in = total * conv_vals
@@ -289,10 +317,11 @@
         grad1 = driven_in * scale * input_gate * (1.0 - input_gate)
         low0 = grad0.astype(BF16)
         low1 = grad1.astype(BF16)
+        inputs_of = (((1,), (1,)), ((), ()))
         grad_conv = (
             total * scale * input_gate
-            + jnp.dot(low0, wg0t[...], preferred_element_type=F32)
-            + jnp.dot(low1, wg1t[...], preferred_element_type=F32)
+            + lax.dot_general(low0, wg[0], inputs_of, preferred_element_type=F32)
+            + lax.dot_general(low1, wg[1], inputs_of, preferred_element_type=F32)
         )
         put_tiles(tot, at, grad_conv)
         turned = (((0,), (0,)), ((), ()))
@@ -351,12 +380,13 @@
     lax.fori_loop(0, rows, back, 0)
     halo_copy.wait()
     lax.fori_loop(rows, 2 * rows, back, 0)
-    scatter.run_third()
+    scatter.run_third(0)
+    scatter.run_third(1)
 
     def body(at):
-        down_out[at, :] = scatter.rows(at)
-
-    for_slices(0, down_out.shape[0], body)
+        outputs[at, :] = (middle[at, :] + scatter.rows(at)).astype(BF16)
+
+    for_slices(0, outputs.shape[0], body)
     scatter.finish()
 
 
@@ -368,7 +398,7 @@
     return pltpu.CompilerParams(collective_id=number, has_side_effects=True, vmem_limit_bytes=60 * 1024 * 1024)
 
 
-def mixer_forward(count, seg, rows_here, branches, ids, wg0, wg1, vec, cot, quarters):
+def mixer_forward(count, seg, rows_here, branches, ids, gate_blocks, vec, cot, quarters):
     n, width = branches.shape[0], branches.shape[1] // 2
     full = functools.partial(jax.ShapeDtypeStruct, (n, width))
     tiles = -(-width // LANES)
@@ -384,7 +414,7 @@
             jax.ShapeDtypeStruct((8 * cot.shape[0], cot.shape[1]), BF16),
             jax.ShapeDtypeStruct((kinds, groups, part, depth), BF16),
         ),
-        in_specs=whole(7) + [ANYWHERE] * 2,
+        in_specs=[ANYWHERE, *whole(5), ANYWHERE, ANYWHERE],
         out_specs=(*whole(7), ANYWHERE, ANYWHERE),
         scratch_shapes=[
             pltpu.VMEM((tiles, n, LANES), F32),
@@ -400,12 +430,15 @@
             pltpu.SemaphoreType.DMA((2,)),
             *GATHER_SCRATCH,
             *swap_scratch(groups),
+            pltpu.VMEM(branches.shape, F32),
+            pltpu.VMEM((2, width, width), BF16),
+            pltpu.SemaphoreType.DMA((1,)),
         ],
         compiler_params=mixer_params(1),
-    )(branches, *ids, wg0, wg1, vec, cot, quarters)
-
-
-def mixer_backward(count, seg, grad_mixed, branches, states, decay, conv_low, halo, cin, mask, wg0, wg1, wg0t, wg1t, vec, hidden, w_down):
+    )(branches, *ids, gate_blocks, vec, cot, quarters)
+
+
+def mixer_backward(count, seg, grad_mixed, branches, states, decay, conv_low, mask, halo, cin, gate_blocks, vec, hidden, w_down, middle):
     n, width = branches.shape[0], branches.shape[1] // 2
     tokens, depth = n // 8, w_down.shape[1]
     full = functools.partial(jax.ShapeDtypeStruct, (n, width))
@@ -417,9 +450,9 @@
         out_shape=(
             jax.ShapeDtypeStruct((n, 2 * width), BF16),
             jax.ShapeDtypeStruct((width, width), F32), jax.ShapeDtypeStruct((width, width), F32),
-            jax.ShapeDtypeStruct((8, width), F32), jax.ShapeDtypeStruct((tokens, depth), F32),
+            jax.ShapeDtypeStruct((8, width), F32), jax.ShapeDtypeStruct((tokens, depth), BF16),
         ),
-        in_specs=whole(15),
+        in_specs=[*[ANYWHERE] * 6, *whole(6), ANYWHERE],
         out_specs=tuple(whole(5)),
         scratch_shapes=[
             pltpu.VMEM((tiles, n, LANES), F32),
@@ -433,10 +466,13 @@
             pltpu.SemaphoreType.DMA((count,)),
             pltpu.SemaphoreType.DMA((count,)),
             pltpu.SemaphoreType.DMA((2,)),
+            *[pltpu.VMEM(part.shape, part.dtype) for part in (grad_mixed, branches, states, decay, conv_low, mask, middle)],
+            pltpu.VMEM((2, width, width), BF16),
+            pltpu.SemaphoreType.DMA((7,)),
             *Scatter.scratch(tokens, depth),
         ],
         compiler_params=mixer_params(2),
-    )(grad_mixed, branches, states, decay, conv_low, halo, cin, mask, wg0, wg1, wg0t, wg1t, vec, hidden, w_down)
+    )(grad_mixed, branches, states, decay, conv_low, mask, halo, cin, gate_blocks, vec, hidden, w_down, middle)
 
 
 class Place:
@@ -466,7 +502,7 @@
 
 
 class Gather:
-    COPIES = 11
+    COPIES = 12
 
     def __init__(self, place, block, out, send, recv):
         self.place, self.block, self.out, self.send, self.recv = place, block, out, send, recv
@@ -492,20 +528,25 @@
             device_id_type=MESH,
         )
 
-    def begin(self, part):
+    def begin(self, part, whole=False):
         place = self.place
         own = place.chunk(0, 0, 0)
-        self.kept = getattr(self, "kept", [])
-        mine = self.mine(part)
-        order = ((0 + part, place.across), (2 + part, place.along))
-        for number, peer in order:
-            self.kept.append((self.copy(number, mine, own, part, peer), None))
-            self.kept[-1][0].start()
-        self.kept.append((self.copy(4 + part, mine, own, part, place.core), None))
-        self.kept[-1][0].start()
-        keep = pltpu.make_async_copy(mine, self.rows(own, part), self.send.at[self.COPIES + part])
+        other = 1 - part if whole else part
+        self.give(0 + part, own, part, place.across)
+        self.give(2 + other, own, other, place.along)
+        self.give(4 + part, own, part, place.core)
+        keep = pltpu.make_async_copy(self.mine(part), self.rows(own, part), self.send.at[self.COPIES + part])
         keep.start()
         self.local = getattr(self, "local", []) + [keep]
+
+    def begin_whole(self):
+        self.begin(0, True)
+        self.begin(1, True)
+
+    def give(self, number, chunk, part, peer):
+        moved = self.copy(number, self.mine(part), chunk, part, peer)
+        moved.start()
+        self.kept = getattr(self, "kept", []) + [moved]
 
     def arrived(self, number, chunk, part):
         self.copy(number, self.rows(chunk, part), chunk, part, self.place.core).wait_recv()
@@ -513,7 +554,7 @@
     def forward(self, number, chunk, part, peer):
         moved = self.copy(number, self.rows(chunk, part), chunk, part, peer)
         moved.start()
-        self.kept.append((moved, None))
+        self.kept.append(moved)
 
     def pass_first(self):
         place = self.place
@@ -534,8 +575,9 @@
     def pass_third(self):
         dia = self.place.chunk(1, 1, 0)
         self.arrived(6, dia, 0)
+        self.forward(10, dia, 0, self.place.core)
         self.arrived(7, dia, 1)
-        self.forward(10, dia, 2, self.place.core)
+        self.forward(11, dia, 1, self.place.core)
 
     def pass_on(self):
         self.pass_first()
@@ -548,8 +590,9 @@
         self.arrived(5, place.chunk(0, 0, 1), 1)
         self.arrived(8, place.chunk(0, 1, 1), 2)
         self.arrived(9, place.chunk(1, 0, 1), 2)
-        self.arrived(10, place.chunk(1, 1, 1), 2)
-        for moved, _ in self.kept:
+        self.arrived(10, place.chunk(1, 1, 1), 0)
+        self.arrived(11, place.chunk(1, 1, 1), 1)
+        for moved in self.kept:
             moved.wait_send()
         for keep in self.local:
             keep.wait()
@@ -581,8 +624,7 @@
 
     for number, offset in enumerate(OTHERS):
         move(number, ids, plane_ids.at[own], place.peer(*offset))
-    gather.begin(0)
-    gather.begin(1)
+    gather.begin_whole()
     plane_ids[own] = ids[...]
     for number, offset in enumerate(OTHERS):
         chunk = place.chunk(*offset)
@@ -630,11 +672,6 @@
         moved.start()
         self.kept.append(moved)
 
-    def run(self):
-        self.run_first()
-        self.run_second()
-        self.run_third()
-
     def run_first(self):
         place = self.place
         order = ((1, 1), (0, 1), (1, 0), (0, 0))
@@ -681,29 +718,34 @@
         take(*order[2])
         take(*order[3])
 
+    def second_copy(self, half, part):
+        tokens = self.second.shape[1] // 2
+        at = pl.ds(part * tokens, tokens)
+        peer = self.place.across if half else self.place.along
+        return 8 + 2 * part + half, self.second.at[half, at], self.second_recv.at[half, at], peer
+
     def run_second(self):
         place = self.place
-        for half, number, buffer, mine, peer, out in (
-            (0, 5, self.across_recv, 2, place.along, 8),
-            (1, 7, self.along_recv, 1, place.across, 9),
-        ):
-            self.copy(number, buffer.at[1], buffer.at[1], place.core).wait_recv()
-
-            def add_rows(n, none):
-                at = pl.ds(pl.multiple_of(n * SLICE, SLICE), SLICE)
-                total = self.held[mine - 1, half, at, :].astype(F32) + buffer[1, at, :].astype(F32)
-                self.second[half, at, :] = total.astype(BF16)
-                return none
-
-            lax.fori_loop(0, self.held.shape[2] // SLICE, add_rows, 0)
-            self.start(out, self.second.at[half], self.second_recv.at[half], peer)
-
-    def run_third(self):
+        tokens = self.second.shape[1] // 2
+        for part in (0, 1):
+            for half, number, buffer, mine in ((0, 5, self.across_recv, 2), (1, 7, self.along_recv, 1)):
+                if part == 0:
+                    self.copy(number, buffer.at[1], buffer.at[1], place.core).wait_recv()
+
+                def add_rows(at):
+                    total = self.held[mine - 1, half, at, :].astype(F32) + buffer[1, at, :].astype(F32)
+                    self.second[half, at, :] = total.astype(BF16)
+
+                for_slices(part * tokens, (part + 1) * tokens, add_rows)
+                self.start(*self.second_copy(half, part))
+
+    def run_third(self, part):
         place = self.place
-        for number, buffer in ((4, self.across_recv), (6, self.along_recv)):
-            self.copy(number, buffer.at[0], buffer.at[0], place.core).wait_recv()
-        for number, half in ((8, 0), (9, 1)):
-            self.copy(number, self.second.at[half], self.second_recv.at[half], place.core).wait_recv()
+        if part == 0:
+            for number, buffer in ((4, self.across_recv), (6, self.along_recv)):
+                self.copy(number, buffer.at[0], buffer.at[0], place.core).wait_recv()
+        for half in (0, 1):
+            self.copy(*self.second_copy(half, part)).wait_recv()
 
     def rows(self, at):
         first = self.acc[0, at, :] + self.across_recv[0, at, :].astype(F32) + self.second_recv[0, at, :].astype(F32)
@@ -726,8 +768,8 @@
             pltpu.VMEM((2, tokens, half), BF16),
             pltpu.VMEM((2, tokens, half), BF16),
             pltpu.VMEM((2, tokens, half), BF16),
-            pltpu.SemaphoreType.DMA((10,)),
-            pltpu.SemaphoreType.DMA((10,)),
+            pltpu.SemaphoreType.DMA((12,)),
+            pltpu.SemaphoreType.DMA((12,)),
         ]
 
 
@@ -761,7 +803,8 @@
     place = Place()
     place.greet()
     scatter = Scatter(place, pair_product([left], [right], tokens), *buffers)
-    scatter.run()
+    scatter.run_first()
+    scatter.run_second()
 
     def body(at):
         middle = own_in[at, :].astype(F32) + scatter.rows(at)
@@ -770,6 +813,7 @@
 
     gather = Gather(place, block, gathered, send, recv)
     for part in (0, 1):
+        scatter.run_third(part)
         for_slices(part * tokens // 2, (part + 1) * tokens // 2, body)
         gather.begin(part)
     gather.pass_on()
@@ -777,8 +821,10 @@
     gather.finish()
 
 
-def turn_kernel(left0, left1, right0, right1, middle, gain, cot, normed, grad_middle_out, gain_out, grads_out, gathered, *scratch):
-    buffers, (block, send, recv) = scratch[:SCATTER_BUFFERS], scratch[SCATTER_BUFFERS:]
+def turn_kernel(left0, left1, right0, right1, middle, gain, cot, normed_far, grad_middle_out, gain_out, grads_out, gathered, *scratch):
+    buffers, (block, send, recv, normed, load) = scratch[:SCATTER_BUFFERS], scratch[SCATTER_BUFFERS:]
+    loaded = pltpu.make_async_copy(normed_far, normed, load.at[0])
+    loaded.start()
     tokens = cot.shape[0]
     place = Place()
     place.greet()
@@ -797,10 +843,10 @@
 
     steps = normed.shape[1] // 256
     scatter.run_first()
+    loaded.wait()
     weight_grads(0, steps // 4)
     scatter.run_second()
     weight_grads(steps // 4, steps // 2)
-    scatter.run_third()
     gain_out[...] = jnp.zeros_like(gain_out)
 
     def body(at):
@@ -817,6 +863,7 @@
 
     gather = Gather(place, block, gathered, send, recv)
     for part in (0, 1):
+        scatter.run_third(part)
         for_slices(part * tokens // 2, (part + 1) * tokens // 2, body)
         gather.begin(part)
     weight_grads(steps // 2, 3 * steps // 4)
@@ -945,7 +992,7 @@
 
 
 def final_kernel(
-    count, with_gates, left, right, own_in, gain, mlp_gains, pieces, grad_out, gains_out, gates_out,
+    count, with_gates, left, right, own_in, gain, mlp_gains, pieces, grad_middle, grad_out, gains_out, gates_out,
     gain_sum, values, inbox, plane_box, sum_send, sum_recv, rows_recv, gates_all, gates_send, gates_recv,
     *buffers,
 ):
@@ -961,7 +1008,8 @@
     scatter.run_second()
     if with_gates:
         gates.pass_on()
-    scatter.run_third()
+    scatter.run_third(0)
+    scatter.run_third(1)
     gain_sum[...] = jnp.zeros_like(gain_sum)
 
     def body(at):
@@ -970,7 +1018,7 @@
         scale = rms(x)
         weighted = grad * gain[...]
         inner = jnp.mean(x * weighted, axis=-1, keepdims=True)
-        grad_out[at, :] = scale * weighted - x * (scale * scale * scale * inner)
+        grad_out[at, :] = grad_middle[at, :] + scale * weighted - x * (scale * scale * scale * inner)
         term = grad * x * scale
         gain_sum[...] += term[0:8] + term[8:16]
 
@@ -987,7 +1035,7 @@
     scatter.finish()
 
 
-def final_step(planes, left, right, own_in, gain, mlp_gains, pieces):
+def final_step(planes, left, right, own_in, gain, mlp_gains, pieces, grad_middle):
     tokens, width = own_in.shape
     with_gates = pieces.shape[0] == planes
     block = pieces.shape[1:] if with_gates else (16, LANES)
@@ -1002,7 +1050,7 @@
             jax.ShapeDtypeStruct(sums, F32),
             jax.ShapeDtypeStruct(block, F32),
         ),
-        in_specs=whole(6),
+        in_specs=whole(7),
         out_specs=tuple(whole(3)),
         scratch_shapes=[
             pltpu.VMEM((8, width), F32),
@@ -1018,7 +1066,7 @@
             *Scatter.scratch(tokens, width),
         ],
         compiler_params=mixer_params(7),
-    )(left, right, own_in, gain[None], mlp_gains, pieces)
+    )(left, right, own_in, gain[None], mlp_gains, pieces, grad_middle)
 
 
 def owners_kernel(reduced0, reduced1, out0, out1, send0, recv0, send1, recv1):
@@ -1114,9 +1162,12 @@
             jax.ShapeDtypeStruct((width, 2 * left0.shape[1]), BF16),
             jax.ShapeDtypeStruct((8 * tokens, width), BF16),
         ),
-        in_specs=whole(8),
+        in_specs=[*whole(7), ANYWHERE],
         out_specs=(*whole(3), ANYWHERE),
-        scratch_shapes=Scatter.scratch(tokens, width) + [pltpu.VMEM((tokens, width), BF16)] + GATHER_SCRATCH,
+        scratch_shapes=Scatter.scratch(tokens, width)
+        + [pltpu.VMEM((tokens, width), BF16)]
+        + GATHER_SCRATCH
+        + [pltpu.VMEM(normed.shape, BF16), pltpu.SemaphoreType.DMA((1,))],
         compiler_params=mixer_params(5),
     )(left0, left1, right0, right1, middle, gain[None], cot, normed)
 
@@ -1250,36 +1301,33 @@
         out_quarters = jnp.zeros((row_groups, 1, 16, width), BF16)
     in_w = in_w.reshape(2 * channels, width)
     hidden_part = mlp_in.shape[2] // row_groups
+    gated = quarter(mlp_in, hidden_part, late_r).transpose(1, 2, 0)
     w_left, w_right, w_down = [
-        spread_units(quarter(weight, hidden_part, late_r).T).reshape(-1, width)
-        for weight in (mlp_in[:, 0], mlp_in[:, 1], down_weight)
+        spread_units(part).reshape(-1, width)
+        for part in (gated[0], gated[1], quarter(down_weight, hidden_part, late_r).T)
     ]
 
     def own(values):
         return lax.dynamic_slice_in_dim(values, first, channels, values.ndim - 1)
 
-    decay_own = own(decay_param)
-    vec = jnp.concatenate(
-        [
-            own(conv_weight),
-            own(conv_bias)[None],
-            own(gate_bias),
-            8.0 * jax.nn.softplus(-decay_own)[None],
-            8.0 * jax.nn.sigmoid(-decay_own)[None],
-            jnp.zeros((7, channels), F32),
-        ]
+    vec = own(
+        jnp.concatenate(
+            [
+                conv_weight,
+                conv_bias[None],
+                gate_bias,
+                8.0 * jax.nn.softplus(-decay_param)[None],
+                8.0 * jax.nn.sigmoid(-decay_param)[None],
+                jnp.zeros((7, recur_width), F32),
+            ]
+        )
     )
+    gate_blocks = own(gate_weight).transpose(1, 0, 2)
     blocks = channels // block_width
-    gate_own = own(gate_weight).reshape(block_width, 2, blocks, block_width)
-    spread = jnp.zeros((2, blocks, block_width, blocks, block_width), BF16)
-    for n in range(blocks):
-        spread = spread.at[:, n, :, n, :].set(gate_own[:, :, n, :].transpose(1, 0, 2))
-    spread = spread.reshape(2, channels, channels)
-    wg0, wg1 = spread[0], spread[1]
 
     branches = nt(normed, in_w, F32)
     conv_low, decay, states, mixed, halo, cin, mask, cot, w_out = mixer_forward(
-        planes, seg, rows_here, branches, ids, wg0, wg1, vec, cot_own, out_quarters
+        planes, seg, rows_here, branches, ids, gate_blocks, vec, cot_own, out_quarters
     )
     w_out = (w_out if direct else whole_units(out_own)).reshape(channels, width)
     middle, normed_two = middle_step(mixed, w_out, own_in, mlp_gain)
@@ -1304,16 +1352,13 @@
     grad_down, grad_mid = lax.optimization_barrier((grad_down, grad_mid))
     grad_out = tn(grad_mid, mixed, BF16)
     grad_mixed = nt(grad_mid, w_out, F32)
-    grad_out, grad_mixed = lax.optimization_barrier((grad_out, grad_mixed))
-    grad_out = over_planes(grad_out)
-    grad_branches, gw0, gw1, small, down = mixer_backward(
-        planes, seg, grad_mixed, branches, states, decay, conv_low, halo, cin, mask, wg0, wg1, wg0.T, wg1.T, vec,
-        hidden, w_down,
+    grad_branches, gw0, gw1, small, outputs = mixer_backward(
+        planes, seg, grad_mixed, branches, states, decay, conv_low, mask, halo, cin, gate_blocks, vec, hidden, w_down, middle
     )
-    grad_in = tn(normed, grad_branches, BF16)
+    grad_in = jnp.concatenate([tn(normed, grad_branches, BF16), grad_out], axis=1)
     grad_mlp_in, grad_in, grad_branches = lax.optimization_barrier((grad_mlp_in, grad_in, grad_branches))
     grad_in = over_planes(grad_in)
-    outputs = (middle + down).astype(BF16).reshape(inputs.shape)
+    outputs = outputs.reshape(inputs.shape)
     own_rows = width // (planes * members)
 
     column_block = lax.broadcasted_iota(jnp.int32, (block_width, channels), 1) // block_width
@@ -1328,8 +1373,10 @@
     if direct:
         pieces = gate_grads.reshape(gate_grads.shape[0], row_groups, -1).transpose(1, 0, 2)
         pieces = jnp.pad(pieces.astype(BF16), ((0, 0), (0, -pieces.shape[1] % 16), (0, LANES - part)))
-    grad_in_norm, gains, gate_sums = final_step(planes, grad_branches, in_w, own_in, mix_gain, grad_mlp_gain, pieces)
-    grad_inputs = (grad_middle + grad_in_norm).reshape(inputs.shape)
+    grad_inputs, gains, gate_sums = final_step(
+        planes, grad_branches, in_w, own_in, mix_gain, grad_mlp_gain, pieces, grad_middle
+    )
+    grad_inputs = grad_inputs.reshape(inputs.shape)
     index = ((t * 2 + i) * row_groups + r) * own_rows
     gains = lax.dynamic_slice_in_dim(gains.reshape(2, width), index, own_rows, 1)
 
@@ -1338,7 +1385,8 @@
         return owners_step(number, [grad.reshape(members, own_rows, -1) for grad in grads])
 
     owned_mlp_in, owned_down = exchanged(8, grad_mlp_in, grad_down)
-    owned_in, owned_out = exchanged(9, grad_in, grad_out)
+    split = 2 * channels
+    owned_in, owned_out = exchanged(9, grad_in[:, :split], grad_in[:, split:])
 
     def columns(owned, kinds, hidden):
         if direct:

time: 750 us -> 688 us (0.917)
  Pallas kernels: 534 us -> 513 us
  waiting for transfers between devices: 32.9 us -> 12.8 us
  local copies, waits for them, and re-layouts: 63.1 us -> 44.5 us
    reduce_scatter x4 -> x3, waiting for transfers between devices: 32.7 us -> 12.1 us  [over_planes(): return lax.psum_scatter(grad, 't', scatter_dimension=0, tiled=True)]
    dynamic_slice x4 -> x2, local copies, waits for them, and re-layouts: 20.9 us -> 7.23 us  [quarter(): return lax.dynamic_slice_in_dim(weight, rank * part, part, weight.ndim - 1)]
    unnamed x25 -> x30, local copies, waits for them, and re-layouts: 4.97 us -> 16.4 us
    pallas_call x1, Pallas kernels: 84.1 us -> 72.8 us  [mixer_backward(): pl.pallas_call(functools.partial(mixer_backward_kernel, count, seg), name...]
  transfers between devices with their start and end apart: 9 -> 8, of which waited for: 2 -> 1; matrix products, arithmetic and copies ran while one was open for 21% -> 19% of each run, Pallas kernels for 69% -> 72%
where the time goes in v6:
time: 688 us; the launch traced here: 684 us
  Pallas kernels  513 us (75%)
  matrix products  91.1 us (13%)
  local copies, waits for them, and re-layouts  44.5 us (6%)
  between operations  14.8 us (2%)
  waiting for transfers between devices  12.8 us (2%)
  other arithmetic  7.29 us (1%)
    pallas_call x1, Pallas kernels, turn_step(): pl.pallas_call(turn_kernel, name='turn_step', out_shape=(jax.ShapeDtypeSt...  93.6 us
    pallas_call x1, Pallas kernels, middle_step(): pl.pallas_call(middle_kernel, name='middle_step', out_shape=(jax.ShapeDty...  85.2 us
    pallas_call x1, Pallas kernels, mixer_backward(): pl.pallas_call(functools.partial(mixer_backward_kernel, count, seg), name...  72.8 us
    pallas_call x1, Pallas kernels, final_step(): pl.pallas_call(functools.partial(final_kernel, planes, with_gates), name=...  70.3 us
    dot_general x5, matrix products, nt(): lax.dot_general(left, right, (((1,), (1,)), ((), ())), preferred_element_...  64.4 us
    pallas_call x1, Pallas kernels, mixer_forward(): pl.pallas_call(functools.partial(mixer_forward_kernel, count, seg, rows_h...  59.6 us
    pallas_call x1, Pallas kernels, first_gather(): pl.pallas_call(functools.partial(first_gather_kernel, planes), name='firs...  45.6 us
    pallas_call x2, Pallas kernels, owners_step(): pl.pallas_call(owners_kernel, name='owners_step', out_shape=tuple((jax.Sh...  44.7 us
  transfers between devices with their start and end apart: 8, of which 1 were waited for; matrix products, arithmetic and copies ran while one was open for 19% of the time, Pallas kernels for 72%

profile of v6, /device:TPU:0, one launch (start us, length us, event | category | flops | bytes accessed | tf_op | source)
XLA Modules:
  0.0 684.4 jit_solution(12288819801632194080)
XLA Ops:
  16.6 45.6 %first_gather.1 = (bf16[2048,2048]{1,0:T(8,128)(2,1)}, f32[8,8,128]{2,1,0:T(8,128)}, f32[8,8,128]{2,1,0:T(8,128)}, f32[8,8,128]{2,1,0:T(8,128)}) custom-call(bf16[256,2048]{1,0:T(8,128)(2,1)} %multiply_convert_fusion.3.normed, f32[8,128]{1,0:T(8,128)} %pad.8.ids), custom_call_target="tpu_custom_call" | custom-call | tf_op jit(solution)/shard_map/first_gather/pallas_call | solution.py:1130
  62.2 5.8 constant_dynamic-slice_fusion.2
  68.0 6.0 copy.56
  74.1 2.7 fusion.13
  84.5 30.4 %swap.1 = bf16[2,4,80,2048]{3,2,1,0:T(8,128)(2,1)} custom-call(bf16[4,2,80,2048]{3,2,1,0:T(8,128)(2,1)} %bitcast.70), custom_call_target="tpu_custom_call" | custom-call | tf_op jit(solution)/shard_map/swap/pallas_call | solution.py:1228
  115.0 11.4 %fusion.14.branches_far = f32[2048,640]{1,0:T(8,128)} fusion(bf16[2048,2048]{1,0:T(8,128)(2,1)} %get-tuple-element.54, bf16[640,2048]{1,0:T(8,128)(2,1)} %bitcast.60), kind=kOutput, calls=%fused_computation.51 | convolution fusion | flops 5368709120 | bytes 16252928 | tf_op jit(solution)/shard_map/dot_general | solution.py:1244
  126.4 59.6 %mixer_forward.1 = (bf16[2048,320]{1,0:T(8,128)(2,1)}, f32[3,2048,128]{2,1,0:T(8,128)}, f32[2048,320]{1,0:T(8,128)}, bf16[2048,320]{1,0:T(8,128)(2,1)}, f32[128,...) custom-call(f32[2048,640]{1,0:T(8,128)} %fusion.14.branches_far, ...), custom_call_target="tpu_custom_call" | custom-call | tf_op jit(solution)/shard_map/mixer_forward/pallas_call | solution.py:407
  185.9 85.2 %middle_step.1 = (f32[256,2048]{1,0:T(8,128)}, bf16[2048,2048]{1,0:T(8,128)(2,1)}) custom-call(bf16[2048,320]{1,0:T(8,128)(2,1)} %get-tuple-element.60.left, bf16[320,2048]{1,0:T(8,128)(2,1)} %bitcast.79, bf16[256,2048]{1,0:T(8,128)(2,1)} %bitcast.58, f32[1,2048]{1,0:T(1,128)} %bitcast.84), custom_call_target="tpu_custom_call" | custom-call | tf_op jit(solution)/shard_map/middle_step/pallas_call | solution.py:1143
  271.1 11.8 %fusion.15 = f32[2048,768]{1,0:T(8,128)} fusion(bf16[2048,2048]{1,0:T(8,128)(2,1)} %get-tuple-element.62.normed_far, bf16[768,2048]{1,0:T(8,128)(2,1)} %bitcast.66), kind=kOutput, calls=%fused_computation.52 | convolution fusion | flops 6442450944 | bytes 17825792 | tf_op jit(solution)/shard_map/dot_general | solution.py:1244
  283.0 14.0 %multiply_convert_fusion.2 = (bf16[2048,768]{1,0:T(8,128)(2,1)S(1)}, f32[2048,768]{1,0:T(8,128)}) fusion(f32[2048,768]{1,0:T(8,128)} %fusion.15, bf16[2048,2048]{1,0:T(8,128)(2,1)} %get-tuple-element.62.normed_far, bf16[768,2048]{1,0:T(8,128)(2,1)} %bitcast.68), kind=kOutput, calls=%fused_computation.2 | convolution fusion | flops 6458179584 | bytes 27262976 | tf_op jit(solution)/shard_map/dot_general | solution.py:1244
  297.0 11.5 %convolution_convert_fusion = bf16[2048,768]{1,0:T(8,128)(2,1)} fusion(bf16[2048,2048]{1,0:T(8,128)(2,1)} %get-tuple-element.59, bf16[2048,768]{1,0:T(8,128)(2,1)S(1)} %get-tuple-element.75.hidden), kind=kOutput, calls=%fused_computation.7 | convolution fusion | flops 6444023808 | bytes 14680064 | tf_op jit(solution)/shard_map/dot_general | solution.py:1248
  308.6 18.4 %multiply_convert_fusion = (bf16[2048,768]{1,0:T(8,128)(2,1)}, bf16[2048,768]{1,0:T(8,128)(2,1)}) fusion(f32[2048,768]{1,0:T(8,128)} %fusion.15, f32[2048,768]{1,0:T(8,128)} %get-tuple-element.149, bf16[2048,2048]{1,0:T(8,128)(2,1)} %get-tuple-element.59, bf16[768,2048]{1,0:T(8,128)(2,1)} %all-gather.17.cloned.1.call-done.w_down), kind=kOutput, calls=%fused_computation | convolution fusion | flops 6477053952 | bytes 30408704 | tf_op jit(solution)/shard_map/dot_general | solution.py:1244
  326.9 93.6 %turn_step.1 = (f32[256,2048]{1,0:T(8,128)}, f32[8,2048]{1,0:T(8,128)}, bf16[2048,1536]{1,0:T(8,128)(2,1)}, bf16[2048,2048]{1,0:T(8,128)(2,1)}) custom-call(bf16[2048,768]{1,0:T(8,128)(2,1)} %get-tuple-element.135.left0, bf16[2048,768]{1,0:T(8,128)(2,1)} %get-tuple-element.134.left1, bf16[768,2048]{1,0:T(8,128)(2,1)} %bitcast.67, ...), custom_call_target="tpu_custom_call" | custom-call | tf_op jit(solution)/shard_map/turn_step/pallas_call | solution.py:1156
  421.8 8.8 %fusion.16.grad_mixed_far = f32[2048,320]{1,0:T(8,128)} fusion(bf16[2048,2048]{1,0:T(8,128)(2,1)} %get-tuple-element.68, bf16[320,2048]{1,0:T(8,128)(2,1)S(1)} %bitcast.80), kind=kOutput, calls=%fused_computation.53 | convolution fusion | flops 2684354560 | bytes 12320768 | tf_op jit(solution)/shard_map/dot_general | solution.py:1244
  430.6 72.8 %mixer_backward.1 = (bf16[2048,640]{1,0:T(8,128)(2,1)}, f32[320,320]{1,0:T(8,128)}, f32[320,320]{1,0:T(8,128)}, f32[8,320]{1,0:T(8,128)}, bf16[256,2048]{1,0:T(8,128)(2,1)}) custom-call(f32[2048,320]{1,0:T(8,128)} %fusion.16.grad_mixed_far, f32[2048,640]{1,0:T(8,128)} %fusion.14.branches_far, f32[2048,320]{1,0:T(8,128)} %get-tuple-element.69.states_far, ...), custom_call_target="tpu_custom_call" | custom-call | tf_op jit(solution)/shard_map/mixer_backward/pallas_call | solution.py:447
  503.4 6.9 %convolution_convert_fusion.2 = bf16[2048,320]{0,1:T(8,128)(2,1)S(1)} fusion(bf16[2048,2048]{1,0:T(8,128)(2,1)} %get-tuple-element.68, bf16[2048,320]{1,0:T(8,128)(2,1)} %get-tuple-element.60.left), kind=kOutput, calls=%fused_computation.9 | convolution fusion | flops 2685009920 | bytes 11010048 | tf_op jit(solution)/shard_map/dot_general | solution.py:1248
  510.3 8.3 %convolution_convert_fusion.1 = bf16[2048,640]{0,1:T(8,128)(2,1)S(1)} fusion(bf16[2048,2048]{1,0:T(8,128)(2,1)} %get-tuple-element.54, bf16[2048,640]{1,0:T(8,128)(2,1)S(1)} %copy-done.3), kind=kOutput, calls=%fused_computation.8 | convolution fusion | flops 5370019840 | bytes 13631488 | tf_op jit(solution)/shard_map/dot_general | solution.py:1248
  521.1 12.1 %reduce-scatter.6.cloned.1.call-done = bf16[512,1536]{1,0:T(8,128)(2,1)} async-done(((bf16[2048,1536]{1,0:T(8,128)(2,1)}), bf16[512,1536]{1,0:T(8,128)(2,1)}) %reduce-scatter.6.cloned.1.call-update) | async-done | bytes 1572880 | tf_op jit(solution)/shard_map/reduce_scatter | solution.py:1340
  534.6 70.3 %final_step.1 = (f32[256,2048]{1,0:T(8,128)}, f32[32,128]{1,0:T(8,128)}, f32[336,128]{1,0:T(8,128)}) custom-call(bf16[2048,640]{1,0:T(8,128)(2,1)} %get-tuple-element.79.left, bf16[640,2048]{1,0:T(8,128)(2,1)} %bitcast.61, bf16[256,2048]{1,0:T(8,128)(2,1)} %bitcast.59, f32[1,2048]{1,0:T(1,128)} %bitcast.86, f32[8,2048]{1,0:T(8,128)} %get-tuple-element.80.mlp_gains, ...), custom_call_target="tpu_custom_call" | custom-call | tf_op jit(solution)/shard_map/final_step/pallas_call | solution.py:1045
  609.9 29.4 %owners_step.3 = (bf16[8,64,1536]{2,1,0:T(8,128)(2,1)}, bf16[8,64,768]{2,1,0:T(8,128)(2,1)}) custom-call(bf16[8,64,1536]{2,1,0:T(8,128)(2,1)} %bitcast.75, bf16[8,64,768]{2,1,0:T(8,128)(2,1)} %bitcast.83), custom_call_target="tpu_custom_call" | custom-call | tf_op jit(solution)/shard_map/owners_step/pallas_call | solution.py:1083
  639.4 4.2 place_columns.6
  652.0 15.3 %owners_step.2 = (bf16[8,64,640]{2,1,0:T(8,128)(2,1)}, bf16[8,64,320]{2,1,0:T(8,128)(2,1)}) custom-call(bf16[8,64,640]{2,1,0:T(8,128)(2,1)} %bitcast.71, bf16[8,64,320]{2,1,0:T(8,128)(2,1)} %bitcast.76), custom_call_target="tpu_custom_call" | custom-call | tf_op jit(solution)/shard_map/owners_step/pallas_call | solution.py:1083
  667.3 2.6 place_columns.4
  674.2 3.1 copy.63
  (90 shorter events, 39.8 us)
Async XLA Ops:
  7.2 70.3 %copy-start = (bf16[2048,768]{1,0:T(8,128)(2,1)S(1)}, bf16[2048,768]{1,0:T(8,128)(2,1)}, u32[]{:S(2)}) copy-start(bf16[2048,768]{1,0:T(8,128)(2,1)} %param.26) | copy-start | bytes 9437188
  7.2 77.3 %all-gather.13.cloned.1.call-start = ((), (), s32[]{:S(2)}) async-start(), calls=%async_computation.8 | async-start | bytes 3276800 | tf_op jit(solution)/shard_map/all_gather | solution.py:1290
  9.4 117.0 %all-gather.15.cloned.1.call-start = ((), (), s32[]{:S(2)}) async-start(), calls=%async_computation.9 | async-start | bytes 1638400 | tf_op jit(solution)/shard_map/all_gather | solution.py:1290
  11.2 259.9 %all-gather.9.cloned.1.call-start = ((), (), s32[]{:S(2)}) async-start(), calls=%async_computation.3 | async-start | bytes 3932160 | tf_op jit(solution)/shard_map/all_gather | solution.py:1290
  74.1 9.5 %copy-start.10 = (f32[2560]{0:T(1024)S(1)}, f32[2560]{0:T(1024)}, u32[]{:S(2)}) copy-start(f32[2560]{0:T(1024)} %param.19) | copy-start | bytes 30724
  74.1 9.5 %copy-start.11 = (f32[2560]{0:T(1024)S(1)}, f32[2560]{0:T(1024)}, u32[]{:S(2)}) copy-start(f32[2560]{0:T(1024)} %param.22) | copy-start | bytes 30724
  74.1 9.6 %copy-start.7 = (f32[4,2560]{1,0:T(4,128)S(1)}, f32[4,2560]{1,0:T(4,128)}, u32[]{:S(2)}) copy-start(f32[4,2560]{1,0:T(4,128)} %param.18) | copy-start | bytes 122884
  74.1 9.6 %copy-start.8 = (f32[2,2560]{1,0:T(2,128)S(1)}, f32[2,2560]{1,0:T(2,128)}, u32[]{:S(2)}) copy-start(f32[2,2560]{1,0:T(2,128)} %param.21) | copy-start | bytes 61444
  76.8 206.1 %all-gather.11.cloned.1.call-start = ((), (), s32[]{:S(2)}) async-start(), calls=%async_computation.4 | async-start | bytes 3932160 | tf_op jit(solution)/shard_map/all_gather | solution.py:1290
  77.4 231.1 %all-gather.17.cloned.1.call-start = ((), (), s32[]{:S(2)}) async-start(), calls=%async_computation.10 | async-start | bytes 3932160 | tf_op jit(solution)/shard_map/all_gather | solution.py:1290
  81.1 339.5 %reduce-scatter.4.cloned.1.call-start = ((), (), s32[]{:S(2)}) async-start(), calls=%async_computation.5 | async-start | bytes 3932160 | tf_op jit(solution)/shard_map/reduce_scatter | solution.py:1340
  297.0 11.5 %copy-start.2 = (bf16[2048,768]{1,0:T(8,128)(2,1)}, bf16[2048,768]{1,0:T(8,128)(2,1)S(1)}, u32[]{:S(2)}) copy-start(bf16[2048,768]{1,0:T(8,128)(2,1)S(1)} %get-tuple-element.75.hidden) | copy-start | bytes 9437188
  308.5 224.7 %reduce-scatter.6.cloned.1.call-start = ((), (), s32[]{:S(2)}) async-start(), calls=%async_computation.6 | async-start | bytes 7864320 | tf_op jit(solution)/shard_map/reduce_scatter | solution.py:1340
  420.5 1.3 copy-start.4
  420.5 227.3 %reduce-scatter.8.cloned.1.call-start = ((), (), s32[]{:S(2)}) async-start(), calls=%async_computation.7 | async-start | bytes 4915200 | tf_op jit(solution)/shard_map/reduce_scatter | solution.py:1340
  503.4 6.9 %copy-start.3 = (bf16[2048,640]{1,0:T(8,128)(2,1)S(1)}, bf16[2048,640]{1,0:T(8,128)(2,1)}, u32[]{:S(2)}) copy-start(bf16[2048,640]{1,0:T(8,128)(2,1)} %get-tuple-element.79.left) | copy-start | bytes 7864324
  518.6 14.6 %copy-start.9 = (f32[8,320]{1,0:T(8,128)S(1)}, f32[8,320]{1,0:T(8,128)}, u32[]{:S(2)}) copy-start(f32[8,320]{1,0:T(8,128)} %get-tuple-element.83) | copy-start | bytes 30724
  518.6 14.6 %copy-start.5 = (f32[320,320]{1,0:T(8,128)S(1)}, f32[320,320]{1,0:T(8,128)}, u32[]{:S(2)}) copy-start(f32[320,320]{1,0:T(8,128)} %get-tuple-element.81) | copy-start | bytes 1228804
  518.7 14.6 %copy-start.6 = (f32[320,320]{1,0:T(8,128)S(1)}, f32[320,320]{1,0:T(8,128)}, u32[]{:S(2)}) copy-start(f32[320,320]{1,0:T(8,128)} %get-tuple-element.82) | copy-start | bytes 1228804
  651.1 26.2 %copy-start.1 = (bf16[2048,768]{1,0:T(8,128)(2,1)S(1)}, bf16[2048,768]{1,0:T(8,128)(2,1)}, u32[]{:S(2)}) copy-start(bf16[2048,768]{1,0:T(8,128)(2,1)} %param.26) | copy-start | bytes 9437188
Sparse Core Ops, SparseCore 0:
  10.2 58.8 all-gather.12
  71.2 31.4 all-gather.14
  104.9 66.6 all-gather.8
  173.5 62.0 all-gather.10
  237.6 62.1 all-gather.16
  308.6 58.3 reduce-scatter.3
  420.7 112.4 reduce-scatter.5
  535.5 79.6 reduce-scatter.7

commit v7 on v6

--- a/solution.py
+++ b/solution.py
@@ -31,9 +31,9 @@
     return x * half, slope
 
 
-def one_minus_exp(y):
+def one_minus_exp(y, power):
     series = 1.0 + y * (-1.0 / 2 + y * (1.0 / 6 + y * (-1.0 / 24 + y * (1.0 / 120 + y * (-1.0 / 720 + y * (1.0 / 5040))))))
-    return jnp.where(y < 0.35, y * series, 1.0 - jnp.exp(-y))
+    return jnp.where(y < 0.35, y * series, 1.0 - power)
 
 
 def sigmoid(x):
@@ -163,8 +163,9 @@
         conv_out[at, :] = conv_low
         recur_gate, input_gate, log_decay = gate_values(conv_low, wg[0], wg[1], vec)
         keep = m[:, 0:1]
-        put_tiles(decay_out, at, jnp.exp(log_decay) * keep)
-        scale = (1.0 - keep) + keep * jnp.sqrt(one_minus_exp(-2.0 * log_decay))
+        kept = jnp.exp(log_decay)
+        put_tiles(decay_out, at, kept * keep)
+        scale = (1.0 - keep) + keep * jnp.sqrt(one_minus_exp(-2.0 * log_decay, kept * kept))
         put_tiles(drive, at, scale * input_gate * conv_low.astype(F32))
         return none
 
@@ -228,9 +229,9 @@
 
 def mixer_backward_kernel(
     count, seg, grad_mixed_far, branches_far, states_far, decay_far, conv_far, mask_far, halo, cin, gate_blocks, vec_ref,
-    hidden, w_down, middle_far, grad_out, gw0_out, gw1_out, small_out, outputs,
+    hidden, w_down, middle_far, reduced0, reduced1, grad_out, gw0_out, gw1_out, small_out, outputs, owned0, owned1,
     tot, prod, ext, halo_send, halo_recv, summary, slots, uin, send_sem, recv_sem, halo_sems,
-    grad_mixed, branches, states, decay, conv_low_ref, mask, middle, wg, load, *buffers,
+    grad_mixed, branches, states, decay, conv_low_ref, mask, middle, wg, load, own0, own1, own2, own3, *buffers,
 ):
     place = Place()
     pairs = (
@@ -246,10 +247,13 @@
     for part in loads:
         part.start()
     me = lax.axis_index("t")
-    place.greet([{"t": lax.rem(me + step, count)} for step in range(1, count)])
+    place.greet([place.peer(*offset) for offset in BEYOND] + [{"t": lax.rem(me + step, count)} for step in range(1, count)])
     scatter = Scatter(place, pair_product([hidden], [w_down], outputs.shape[0]), *buffers)
+    owners = [Owners(place, reduced0, owned0, own0, own1), Owners(place, reduced1, owned1, own2, own3)]
     spread_blocks(gate_blocks, wg)
     scatter.run_first()
+    for part in owners:
+        part.begin()
     for part in loads:
         part.wait()
     rows = 8
@@ -309,10 +313,11 @@
         m = mask[at, :]
         keep = m[:, 0:1]
         recur_gate, input_gate, log_decay = gate_values(conv_low, wg[0], wg[1], vec)
-        root = jnp.sqrt(one_minus_exp(-2.0 * log_decay))
+        power = jnp.exp(2.0 * log_decay)
+        root = jnp.sqrt(one_minus_exp(-2.0 * log_decay, power))
         scale = (1.0 - keep) + keep * root
         driven_in = total * conv_vals
-        grad_log = total * before * get_tiles(decay, at, width) - driven_in * input_gate * keep * (jnp.exp(2.0 * log_decay) / root)
+        grad_log = total * before * get_tiles(decay, at, width) - driven_in * input_gate * keep * (power / root)
         grad0 = grad_log * log_decay * (1.0 - recur_gate)
         grad1 = driven_in * scale * input_gate * (1.0 - input_gate)
         low0 = grad0.astype(BF16)
@@ -388,6 +393,8 @@
 
     for_slices(0, outputs.shape[0], body)
     scatter.finish()
+    for part in owners:
+        part.finish()
 
 
 def whole(count):
@@ -438,7 +445,7 @@
     )(branches, *ids, gate_blocks, vec, cot, quarters)
 
 
-def mixer_backward(count, seg, grad_mixed, branches, states, decay, conv_low, mask, halo, cin, gate_blocks, vec, hidden, w_down, middle):
+def mixer_backward(count, seg, grad_mixed, branches, states, decay, conv_low, mask, halo, cin, gate_blocks, vec, hidden, w_down, middle, reduced):
     n, width = branches.shape[0], branches.shape[1] // 2
     tokens, depth = n // 8, w_down.shape[1]
     full = functools.partial(jax.ShapeDtypeStruct, (n, width))
@@ -451,9 +458,10 @@
             jax.ShapeDtypeStruct((n, 2 * width), BF16),
             jax.ShapeDtypeStruct((width, width), F32), jax.ShapeDtypeStruct((width, width), F32),
             jax.ShapeDtypeStruct((8, width), F32), jax.ShapeDtypeStruct((tokens, depth), BF16),
+            *[jax.ShapeDtypeStruct(part.shape, BF16) for part in reduced],
         ),
-        in_specs=[*[ANYWHERE] * 6, *whole(6), ANYWHERE],
-        out_specs=tuple(whole(5)),
+        in_specs=[*[ANYWHERE] * 6, *whole(6), *[ANYWHERE] * 3],
+        out_specs=(*whole(5), *[ANYWHERE] * 2),
         scratch_shapes=[
             pltpu.VMEM((tiles, n, LANES), F32),
             pltpu.VMEM((tiles, n, LANES), F32),
@@ -469,10 +477,11 @@
             *[pltpu.VMEM(part.shape, part.dtype) for part in (grad_mixed, branches, states, decay, conv_low, mask, middle)],
             pltpu.VMEM((2, width, width), BF16),
             pltpu.SemaphoreType.DMA((7,)),
+            *[pltpu.SemaphoreType.DMA((8,))] * 4,
             *Scatter.scratch(tokens, depth),
         ],
         compiler_params=mixer_params(2),
-    )(grad_mixed, branches, states, decay, conv_low, mask, halo, cin, gate_blocks, vec, hidden, w_down, middle)
+    )(grad_mixed, branches, states, decay, conv_low, mask, halo, cin, gate_blocks, vec, hidden, w_down, middle, *reduced)
 
 
 class Place:
@@ -584,14 +593,25 @@
         self.pass_second()
         self.pass_third()
 
+    def finish_core(self):
+        for part in (0, 1):
+            self.arrived(4 + part, self.place.chunk(0, 0, 1), part)
+
+    def finish_near(self):
+        self.arrived(8, self.place.chunk(0, 1, 1), 2)
+        self.arrived(9, self.place.chunk(1, 0, 1), 2)
+
+    def finish_far(self):
+        for part in (0, 1):
+            self.arrived(10 + part, self.place.chunk(1, 1, 1), part)
+
     def finish(self):
-        place = self.place
-        self.arrived(4, place.chunk(0, 0, 1), 0)
-        self.arrived(5, place.chunk(0, 0, 1), 1)
-        self.arrived(8, place.chunk(0, 1, 1), 2)
-        self.arrived(9, place.chunk(1, 0, 1), 2)
-        self.arrived(10, place.chunk(1, 1, 1), 0)
-        self.arrived(11, place.chunk(1, 1, 1), 1)
+        self.finish_core()
+        self.finish_near()
+        self.finish_far()
+        self.finish_sends()
+
+    def finish_sends(self):
         for moved in self.kept:
             moved.wait_send()
         for keep in self.local:
@@ -821,22 +841,22 @@
     gather.finish()
 
 
-def turn_kernel(left0, left1, right0, right1, middle, gain, cot, normed_far, grad_middle_out, gain_out, grads_out, gathered, *scratch):
-    buffers, (block, send, recv, normed, load) = scratch[:SCATTER_BUFFERS], scratch[SCATTER_BUFFERS:]
+def turn_kernel(
+    left0, left1, right0, right1, middle, gain, cot, w_out, normed_far,
+    grad_middle_out, gain_out, grads_out, mixed_out, gathered, *scratch,
+):
+    buffers, (block, send, recv, normed, chunk_ref, load) = scratch[:SCATTER_BUFFERS], scratch[SCATTER_BUFFERS:]
     loaded = pltpu.make_async_copy(normed_far, normed, load.at[0])
     loaded.start()
     tokens = cot.shape[0]
     place = Place()
     place.greet()
     scatter = Scatter(place, pair_product([left0, left1], [right0, right1], tokens), *buffers)
-    hidden = left0.shape[1]
-
     def weight_grads(start, stop):
         def step(n, none):
             at = pl.ds(pl.multiple_of(n * 256, 256), 256)
-            for k, part in enumerate((left0, left1)):
-                value = lax.dot_general(normed[:, at], part[...], (((0,), (0,)), ((), ())), preferred_element_type=F32)
-                grads_out[at, k * hidden : (k + 1) * hidden] = value.astype(BF16)
+            value = lax.dot_general(normed[:, at], left1[...], (((0,), (0,)), ((), ())), preferred_element_type=F32)
+            grads_out[at, :] = value.astype(BF16)
             return none
 
         lax.fori_loop(start, stop, step, 0)
@@ -870,9 +890,31 @@
     gather.pass_first()
     weight_grads(3 * steps // 4, steps)
     gather.pass_second()
+
+    def mixed_back(source, chunk):
+        at = pl.ds(pl.multiple_of(chunk * tokens, tokens), tokens)
+        if source is None:
+            fetch = pltpu.make_async_copy(gathered.at[at], chunk_ref, load.at[0])
+            fetch.start()
+            fetch.wait()
+            source = chunk_ref
+        value = lax.dot_general(source[...], w_out[...], (((1,), (1,)), ((), ())), preferred_element_type=F32)
+        mixed_out[at, :] = value
+
+    mixed_back(block, place.chunk(0, 0, 0))
+    mixed_back(None, place.chunk(0, 1, 0))
+    mixed_back(None, place.chunk(1, 0, 0))
+    gather.finish_core()
+    mixed_back(None, place.chunk(0, 0, 1))
     gather.pass_third()
+    mixed_back(None, place.chunk(1, 1, 0))
+    gather.finish_near()
+    mixed_back(None, place.chunk(0, 1, 1))
+    mixed_back(None, place.chunk(1, 0, 1))
+    gather.finish_far()
+    mixed_back(None, place.chunk(1, 1, 1))
     scatter.finish()
-    gather.finish()
+    gather.finish_sends()
 
 
 class Owners:
@@ -957,13 +999,14 @@
             copy.wait_send()
 
 
-def sum_everywhere(place, count, values, inbox, plane_box, send, recv):
+def sum_everywhere(place, count, values, inbox, plane_sum, plane_box, send, recv):
     me = lax.axis_index("t")
+    own = place.chunk(0, 0, 0)
     moved = []
 
-    def copy(number, target, peer):
+    def copy(number, source, target, peer):
         return pltpu.make_async_remote_copy(
-            src_ref=values.at[min(number, 3)],
+            src_ref=source,
             dst_ref=target,
             send_sem=send.at[number],
             recv_sem=recv.at[number],
@@ -971,18 +1014,23 @@
             device_id_type=MESH,
         )
 
-    for number, peer in enumerate((place.core, place.across, place.along)):
-        moved.append(copy(number, inbox.at[number], peer))
+    for number, offset in enumerate(OTHERS):
+        moved.append(copy(number, values, inbox.at[own], place.peer(*offset)))
         moved[-1].start()
-        copy(number, inbox.at[number], peer).wait_recv()
-        values[number + 1] = values[number] + inbox[number]
+    inbox[own] = values[...]
+    for number, offset in enumerate(OTHERS):
+        copy(number, values, inbox.at[place.chunk(*offset)], place.peer(*offset)).wait_recv()
+    total = inbox[0]
+    for n in range(1, 8):
+        total = total + inbox[n]
+    plane_sum[...] = total
     for step in range(1, count):
-        moved.append(copy(2 + step, plane_box.at[me], {"t": lax.rem(me + step, count)}))
+        moved.append(copy(6 + step, plane_sum, plane_box.at[me], {"t": lax.rem(me + step, count)}))
         moved[-1].start()
-    plane_box[me] = values[3]
+    plane_box[me] = total
     for step in range(1, count):
         other = lax.rem(me + count - step, count)
-        copy(2 + step, plane_box.at[other], {"t": other}).wait_recv()
+        copy(6 + step, plane_sum, plane_box.at[other], {"t": other}).wait_recv()
     total = plane_box[0]
     for z in range(1, count):
         total = total + plane_box[z]
@@ -992,19 +1040,22 @@
 
 
 def final_kernel(
-    count, with_gates, left, right, own_in, gain, mlp_gains, pieces, grad_middle, grad_out, gains_out, gates_out,
-    gain_sum, values, inbox, plane_box, sum_send, sum_recv, rows_recv, gates_all, gates_send, gates_recv,
-    *buffers,
+    count, with_gates, left, right, own_in, gain, mlp_gains, pieces, grad_middle, reduced,
+    grad_out, gains_out, gates_out, owned,
+    gain_sum, values, inbox, plane_sum, plane_box, sum_send, sum_recv, rows_recv, gates_all, gates_send, gates_recv,
+    own_send, own_recv, *buffers,
 ):
     tokens, width = own_in.shape
     place = Place()
     me = lax.axis_index("t")
     place.greet([place.peer(*offset) for offset in BEYOND] + [{"t": lax.rem(me + step, count)} for step in range(1, count)])
     scatter = Scatter(place, pair_product([left], [right], tokens), *buffers)
+    owners = Owners(place, reduced, owned, own_send, own_recv)
     gates = GateSums(place, count, pieces, rows_recv, gates_all, gates_send, gates_recv)
     scatter.run_first()
     if with_gates:
         gates.begin()
+    owners.begin()
     scatter.run_second()
     if with_gates:
         gates.pass_on()
@@ -1026,16 +1077,17 @@
     lines = width // LANES
     for base, row in ((0, jnp.sum(mlp_gains[...], axis=0, keepdims=True)), (lines, jnp.sum(gain_sum[...], axis=0, keepdims=True))):
         for n in range(lines):
-            values[0, base + n : base + n + 1, :] = row[:, n * LANES : (n + 1) * LANES]
-    gains_out[...] = sum_everywhere(place, count, values, inbox, plane_box, sum_send, sum_recv)
+            values[base + n : base + n + 1, :] = row[:, n * LANES : (n + 1) * LANES]
+    gains_out[...] = sum_everywhere(place, count, values, inbox, plane_sum, plane_box, sum_send, sum_recv)
     if with_gates:
         gates.finish(gates_out)
     else:
         gates_out[...] = jnp.zeros_like(gates_out)
+    owners.finish()
     scatter.finish()
 
 
-def final_step(planes, left, right, own_in, gain, mlp_gains, pieces, grad_middle):
+def final_step(planes, left, right, own_in, gain, mlp_gains, pieces, grad_middle, reduced):
     tokens, width = own_in.shape
     with_gates = pieces.shape[0] == planes
     block = pieces.shape[1:] if with_gates else (16, LANES)
@@ -1049,24 +1101,27 @@
             jax.ShapeDtypeStruct((tokens, width), F32),
             jax.ShapeDtypeStruct(sums, F32),
             jax.ShapeDtypeStruct(block, F32),
+            jax.ShapeDtypeStruct(reduced.shape, reduced.dtype),
         ),
-        in_specs=whole(7),
-        out_specs=tuple(whole(3)),
+        in_specs=[*whole(7), ANYWHERE],
+        out_specs=(*whole(3), ANYWHERE),
         scratch_shapes=[
             pltpu.VMEM((8, width), F32),
-            pltpu.VMEM((4, *sums), F32),
-            pltpu.VMEM((3, *sums), F32),
+            pltpu.VMEM(sums, F32),
+            pltpu.VMEM((8, *sums), F32),
+            pltpu.VMEM(sums, F32),
             pltpu.VMEM((planes, *sums), F32),
-            pltpu.SemaphoreType.DMA((planes + 2,)),
-            pltpu.SemaphoreType.DMA((planes + 2,)),
+            pltpu.SemaphoreType.DMA((planes + 6,)),
+            pltpu.SemaphoreType.DMA((planes + 6,)),
             pltpu.VMEM((slots, *block), BF16),
             pltpu.VMEM((slots, *block), BF16),
             pltpu.SemaphoreType.DMA((planes + 2,)),
             pltpu.SemaphoreType.DMA((planes + 2,)),
+            *OWNERS_SCRATCH,
             *Scatter.scratch(tokens, width),
         ],
         compiler_params=mixer_params(7),
-    )(left, right, own_in, gain[None], mlp_gains, pieces, grad_middle)
+    )(left, right, own_in, gain[None], mlp_gains, pieces, grad_middle, reduced)
 
 
 def owners_kernel(reduced0, reduced1, out0, out1, send0, recv0, send1, recv1):
@@ -1091,9 +1146,12 @@
     )(*reduced)
 
 
-def place_kernel(planes, hidden, pairs, sources, out):
-    piece = sources.shape[2] // (len(pairs) * (planes if hidden else 1))
-    for k in pairs:
+def place_kernel(planes, hidden, kinds, *refs):
+    given, out = refs[:-1], refs[-1]
+    each = kinds // len(given)
+    piece = given[0].shape[2] // (each * (planes if hidden else 1))
+    for kind in range(kinds):
+        sources, k = given[kind // each], kind % each
         if hidden:
             groups = [
                 ((t * 2 + i) * 4 * piece, [(i * 4 + r, (k * planes + t) * piece) for r in range(4)])
@@ -1104,24 +1162,24 @@
             groups = [(r * 2 * piece, [(i * 4 + r, k * piece) for i in range(2)]) for r in range(4)]
         for start, parts in groups:
             row = jnp.concatenate([sources[p, :, at : at + piece].astype(F32) for p, at in parts], axis=1)
-            if len(pairs) > 1:
-                out[:, k, start : start + row.shape[1]] = row
+            if kinds > 1:
+                out[:, kind, start : start + row.shape[1]] = row
             else:
                 out[:, start : start + row.shape[1]] = row
 
 
-def place_columns(planes, hidden, kinds, owned):
-    members, own_rows, columns = owned.shape
-    total = columns * members // kinds
+def place_columns(planes, hidden, kinds, *owned):
+    members, own_rows, columns = owned[0].shape
+    total = columns * len(owned) * members // kinds
     shape = (own_rows, kinds, total) if kinds > 1 else (own_rows, total)
     return pl.pallas_call(
-        functools.partial(place_kernel, planes, hidden, tuple(range(kinds))),
+        functools.partial(place_kernel, planes, hidden, kinds),
         name="place_columns",
         out_shape=jax.ShapeDtypeStruct(shape, F32),
-        in_specs=whole(1),
+        in_specs=whole(len(owned)),
         out_specs=pl.BlockSpec(memory_space=pltpu.VMEM),
         compiler_params=pltpu.CompilerParams(vmem_limit_bytes=60 * 1024 * 1024),
-    )(owned)
+    )(*owned)
 
 
 def first_gather(planes, normed, ids):
@@ -1151,7 +1209,7 @@
     )(mixed, w_out, own_in, gain[None])
 
 
-def turn_step(left0, left1, right0, right1, middle, gain, cot, normed):
+def turn_step(left0, left1, right0, right1, middle, gain, cot, w_out, normed):
     tokens, width = cot.shape
     return pl.pallas_call(
         turn_kernel,
@@ -1159,17 +1217,18 @@
         out_shape=(
             jax.ShapeDtypeStruct((tokens, width), F32),
             jax.ShapeDtypeStruct((8, width), F32),
-            jax.ShapeDtypeStruct((width, 2 * left0.shape[1]), BF16),
+            jax.ShapeDtypeStruct((width, left1.shape[1]), BF16),
+            jax.ShapeDtypeStruct((8 * tokens, w_out.shape[0]), F32),
             jax.ShapeDtypeStruct((8 * tokens, width), BF16),
         ),
-        in_specs=[*whole(7), ANYWHERE],
-        out_specs=(*whole(3), ANYWHERE),
+        in_specs=[*whole(8), ANYWHERE],
+        out_specs=(*whole(4), ANYWHERE),
         scratch_shapes=Scatter.scratch(tokens, width)
         + [pltpu.VMEM((tokens, width), BF16)]
         + GATHER_SCRATCH
-        + [pltpu.VMEM(normed.shape, BF16), pltpu.SemaphoreType.DMA((1,))],
+        + [pltpu.VMEM(normed.shape, BF16), pltpu.VMEM((tokens, width), BF16), pltpu.SemaphoreType.DMA((1,))],
         compiler_params=mixer_params(5),
-    )(left0, left1, right0, right1, middle, gain[None], cot, normed)
+    )(left0, left1, right0, right1, middle, gain[None], cot, w_out, normed)
 
 
 class Swap:
@@ -1268,6 +1327,7 @@
     r = lax.axis_index("g") * lax.axis_size("c") + lax.axis_index("c")
     member = 2 * r + i
     first = member * channels
+    own_rows = width // (planes * members)
 
     own_in = inputs.reshape(own_tokens, width)
     flat_in = own_in.astype(F32)
@@ -1345,21 +1405,26 @@
     grad_hidden = nt(cot, w_down, F32)
     grad_left = (grad_hidden * right * slope).astype(BF16)
     grad_right = (grad_hidden * act).astype(BF16)
-    grad_middle, grad_mlp_gain, grad_mlp_in, grad_mid = turn_step(
-        grad_left, grad_right, w_left, w_right, middle, mlp_gain, cot_own, normed_two
+    grad_left_w = tn(normed_two, grad_left, BF16)
+    grad_left_w, grad_left, grad_right = lax.optimization_barrier((grad_left_w, grad_left, grad_right))
+    grad_left_w = over_planes(grad_left_w)
+    grad_middle, grad_mlp_gain, grad_right_w, grad_mixed, grad_mid = turn_step(
+        grad_left, grad_right, w_left, w_right, middle, mlp_gain, cot_own, w_out, normed_two
     )
-    grad_mlp_in = over_planes(grad_mlp_in)
-    grad_down, grad_mid = lax.optimization_barrier((grad_down, grad_mid))
+    grad_right_w = over_planes(grad_right_w)
     grad_out = tn(grad_mid, mixed, BF16)
-    grad_mixed = nt(grad_mid, w_out, F32)
-    grad_branches, gw0, gw1, small, outputs = mixer_backward(
-        planes, seg, grad_mixed, branches, states, decay, conv_low, mask, halo, cin, gate_blocks, vec, hidden, w_down, middle
+
+    def by_owner(grad):
+        return grad.reshape(members, own_rows, -1)
+
+    grad_branches, gw0, gw1, small, outputs, owned_down, owned_left = mixer_backward(
+        planes, seg, grad_mixed, branches, states, decay, conv_low, mask, halo, cin, gate_blocks, vec, hidden, w_down, middle,
+        [by_owner(grad_down), by_owner(grad_left_w)],
     )
     grad_in = jnp.concatenate([tn(normed, grad_branches, BF16), grad_out], axis=1)
-    grad_mlp_in, grad_in, grad_branches = lax.optimization_barrier((grad_mlp_in, grad_in, grad_branches))
+    grad_right_w, grad_in, grad_branches = lax.optimization_barrier((grad_right_w, grad_in, grad_branches))
     grad_in = over_planes(grad_in)
     outputs = outputs.reshape(inputs.shape)
-    own_rows = width // (planes * members)
 
     column_block = lax.broadcasted_iota(jnp.int32, (block_width, channels), 1) // block_width
 
@@ -1373,25 +1438,21 @@
     if direct:
         pieces = gate_grads.reshape(gate_grads.shape[0], row_groups, -1).transpose(1, 0, 2)
         pieces = jnp.pad(pieces.astype(BF16), ((0, 0), (0, -pieces.shape[1] % 16), (0, LANES - part)))
-    grad_inputs, gains, gate_sums = final_step(
-        planes, grad_branches, in_w, own_in, mix_gain, grad_mlp_gain, pieces, grad_middle
+    grad_inputs, gains, gate_sums, owned_right = final_step(
+        planes, grad_branches, in_w, own_in, mix_gain, grad_mlp_gain, pieces, grad_middle, by_owner(grad_right_w)
     )
     grad_inputs = grad_inputs.reshape(inputs.shape)
     index = ((t * 2 + i) * row_groups + r) * own_rows
     gains = lax.dynamic_slice_in_dim(gains.reshape(2, width), index, own_rows, 1)
 
 
-    def exchanged(number, *grads):
-        return owners_step(number, [grad.reshape(members, own_rows, -1) for grad in grads])
-
-    owned_mlp_in, owned_down = exchanged(8, grad_mlp_in, grad_down)
     split = 2 * channels
-    owned_in, owned_out = exchanged(9, grad_in[:, :split], grad_in[:, split:])
-
-    def columns(owned, kinds, hidden):
+    owned_in, owned_out = owners_step(8, [by_owner(grad_in[:, :split]), by_owner(grad_in[:, split:])])
+
+    def columns(kinds, hidden, *owned):
         if direct:
-            return place_columns(planes, hidden, kinds, owned)
-        owned = owned.reshape(2, row_groups, own_rows, kinds, planes if hidden else 1, -1).astype(F32)
+            return place_columns(planes, hidden, kinds, *owned)
+        owned = jnp.concatenate(owned, axis=2).reshape(2, row_groups, own_rows, kinds, planes if hidden else 1, -1).astype(F32)
         order = (2, 3, 4, 0, 1, 5) if hidden else (2, 3, 1, 0, 4, 5)
         owned = owned.transpose(order).reshape(own_rows, kinds, -1)
         return owned if kinds > 1 else owned[:, 0]
@@ -1408,16 +1469,16 @@
         outputs,
         grad_inputs,
         gains[1],
-        columns(owned_in, 2, False),
+        columns(2, False, owned_in),
         small[0:4],
         small[4],
         grad_gate_weight,
         small[5:7],
         small[7],
-        columns(owned_out, 1, False),
+        columns(1, False, owned_out),
         gains[0],
-        columns(owned_mlp_in, 2, True),
-        columns(owned_down, 1, True),
+        columns(2, True, owned_left, owned_right),
+        columns(1, True, owned_down),
     )
 
 

time: 688 us -> 670 us (0.974)
  Pallas kernels: 513 us -> 492 us
    pallas_call x2 -> x1, Pallas kernels: 44.7 us -> 15.3 us  [owners_step(): pl.pallas_call(owners_kernel, name='owners_step', out_shape=tuple((jax.Sh...]
    dot_general x3 -> x4, matrix products: 26.7 us -> 39.4 us  [tn(): lax.dot_general(left, right, (((0,), (0,)), ((), ())), preferred_element_...]
    dot_general x5 -> x4, matrix products: 64.4 us -> 53.9 us  [nt(): lax.dot_general(left, right, (((1,), (1,)), ((), ())), preferred_element_...]
    pallas_call x1, Pallas kernels: 93.6 us -> 101 us  [turn_step(): pl.pallas_call(turn_kernel, name='turn_step', out_shape=(jax.ShapeDtypeSt...]
  transfers between devices with their start and end apart: 8 -> 9, of which waited for: 1 -> 1; matrix products, arithmetic and copies ran while one was open for 19% -> 16% of each run, Pallas kernels for 72% -> 71%
where the time goes in v7:
time: 670 us; the launch traced here: 666 us
  Pallas kernels  492 us (73%)
  matrix products  93.3 us (14%)
  local copies, waits for them, and re-layouts  43.2 us (6%)
  between operations  14.4 us (2%)
  waiting for transfers between devices  13.7 us (2%)
  other arithmetic  8.36 us (1%)
    pallas_call x1, Pallas kernels, turn_step(): pl.pallas_call(turn_kernel, name='turn_step', out_shape=(jax.ShapeDtypeSt...  101 us
    pallas_call x1, Pallas kernels, middle_step(): pl.pallas_call(middle_kernel, name='middle_step', out_shape=(jax.ShapeDty...  85.1 us
    pallas_call x1, Pallas kernels, final_step(): pl.pallas_call(functools.partial(final_kernel, planes, with_gates), name=...  73.9 us
    pallas_call x1, Pallas kernels, mixer_backward(): pl.pallas_call(functools.partial(mixer_backward_kernel, count, seg), name...  70.5 us
    pallas_call x1, Pallas kernels, mixer_forward(): pl.pallas_call(functools.partial(mixer_forward_kernel, count, seg, rows_h...  59.6 us
    dot_general x4, matrix products, nt(): lax.dot_general(left, right, (((1,), (1,)), ((), ())), preferred_element_...  53.9 us
    pallas_call x1, Pallas kernels, first_gather(): pl.pallas_call(functools.partial(first_gather_kernel, planes), name='firs...  45.6 us
    dot_general x4, matrix products, tn(): lax.dot_general(left, right, (((0,), (0,)), ((), ())), preferred_element_...  39.4 us
  transfers between devices with their start and end apart: 9, of which 1 were waited for; matrix products, arithmetic and copies ran while one was open for 16% of the time, Pallas kernels for 71%

profile of v7, /device:TPU:0, one launch (start us, length us, event | category | flops | bytes accessed | tf_op | source)
XLA Modules:
  0.0 666.3 jit_solution(14945263136173246142)
XLA Ops:
  14.1 2.5 multiply_convert_fusion.3.normed
  16.6 45.6 %first_gather.1 = (bf16[2048,2048]{1,0:T(8,128)(2,1)}, f32[8,8,128]{2,1,0:T(8,128)}, f32[8,8,128]{2,1,0:T(8,128)}, f32[8,8,128]{2,1,0:T(8,128)}) custom-call(bf16[256,2048]{1,0:T(8,128)(2,1)} %multiply_convert_fusion.3.normed, f32[8,128]{1,0:T(8,128)} %pad.8.ids), custom_call_target="tpu_custom_call" | custom-call | tf_op jit(solution)/shard_map/first_gather/pallas_call | solution.py:1188
  62.2 5.8 constant_dynamic-slice_fusion.2
  68.1 6.0 copy.52
  74.1 2.7 fusion.13
  84.7 30.4 %swap.1 = bf16[2,4,80,2048]{3,2,1,0:T(8,128)(2,1)} custom-call(bf16[4,2,80,2048]{3,2,1,0:T(8,128)(2,1)} %bitcast.73), custom_call_target="tpu_custom_call" | custom-call | tf_op jit(solution)/shard_map/swap/pallas_call | solution.py:1287
  115.2 11.4 %fusion.14.branches_far = f32[2048,640]{1,0:T(8,128)} fusion(bf16[2048,2048]{1,0:T(8,128)(2,1)} %get-tuple-element.57, bf16[640,2048]{1,0:T(8,128)(2,1)} %bitcast.61), kind=kOutput, calls=%fused_computation.52 | convolution fusion | flops 5368709120 | bytes 16252928 | tf_op jit(solution)/shard_map/dot_general | solution.py:1303
  126.6 59.6 %mixer_forward.1 = (bf16[2048,320]{1,0:T(8,128)(2,1)}, f32[3,2048,128]{2,1,0:T(8,128)}, f32[2048,320]{1,0:T(8,128)}, bf16[2048,320]{1,0:T(8,128)(2,1)}, f32[128,...) custom-call(f32[2048,640]{1,0:T(8,128)} %fusion.14.branches_far, ...), custom_call_target="tpu_custom_call" | custom-call | tf_op jit(solution)/shard_map/mixer_forward/pallas_call | solution.py:414
  186.2 85.1 %middle_step.1 = (f32[256,2048]{1,0:T(8,128)}, bf16[2048,2048]{1,0:T(8,128)(2,1)}) custom-call(bf16[2048,320]{1,0:T(8,128)(2,1)} %get-tuple-element.62.left, bf16[320,2048]{1,0:T(8,128)(2,1)} %bitcast.64, bf16[256,2048]{1,0:T(8,128)(2,1)} %bitcast.59, f32[1,2048]{1,0:T(1,128)} %bitcast.86), custom_call_target="tpu_custom_call" | custom-call | tf_op jit(solution)/shard_map/middle_step/pallas_call | solution.py:1201
  271.4 11.8 %fusion.15 = f32[2048,768]{1,0:T(8,128)} fusion(bf16[2048,2048]{1,0:T(8,128)(2,1)} %get-tuple-element.64.normed_far, bf16[768,2048]{1,0:T(8,128)(2,1)} %bitcast.69), kind=kOutput, calls=%fused_computation.53 | convolution fusion | flops 6442450944 | bytes 17825792 | tf_op jit(solution)/shard_map/dot_general | solution.py:1303
  283.2 13.6 %multiply_convert_fusion.2 = (bf16[2048,768]{1,0:T(8,128)(2,1)S(1)}, f32[2048,768]{1,0:T(8,128)}) fusion(f32[2048,768]{1,0:T(8,128)} %fusion.15, bf16[2048,2048]{1,0:T(8,128)(2,1)} %get-tuple-element.64.normed_far, bf16[768,2048]{1,0:T(8,128)(2,1)} %bitcast.71), kind=kOutput, calls=%fused_computation.2 | convolution fusion | flops 6458179584 | bytes 27262976 | tf_op jit(solution)/shard_map/dot_general | solution.py:1303
  296.8 11.6 %convolution_convert_fusion.1 = bf16[2048,768]{1,0:T(8,128)(2,1)} fusion(bf16[2048,2048]{1,0:T(8,128)(2,1)} %get-tuple-element.65, bf16[2048,768]{1,0:T(8,128)(2,1)S(1)} %get-tuple-element.78.hidden), kind=kOutput, calls=%fused_computation.8 | convolution fusion | flops 6444023808 | bytes 14680064 | tf_op jit(solution)/shard_map/dot_general | solution.py:1307
  308.4 17.0 %multiply_convert_fusion = (bf16[2048,768]{1,0:T(8,128)(2,1)}, bf16[2048,768]{1,0:T(8,128)(2,1)S(1)}) fusion(f32[2048,768]{1,0:T(8,128)} %fusion.15, f32[2048,768]{1,0:T(8,128)} %get-tuple-element.155, bf16[2048,2048]{1,0:T(8,128)(2,1)} %get-tuple-element.65, bf16[768,2048]{1,0:T(8,128)(2,1)} %all-gather.17.cloned.1.call-done.w_down), kind=kOutput, calls=%fused_computation | convolution fusion | flops 6477053952 | bytes 30408704 | tf_op jit(solution)/shard_map/dot_general | solution.py:1303
  325.4 11.5 %convolution_convert_fusion = bf16[2048,768]{1,0:T(8,128)(2,1)} fusion(bf16[2048,2048]{1,0:T(8,128)(2,1)} %get-tuple-element.64.normed_far, bf16[2048,768]{1,0:T(8,128)(2,1)S(1)} %get-tuple-element.68.left0), kind=kOutput, calls=%fused_computation.7 | convolution fusion | flops 6444023808 | bytes 14680064 | tf_op jit(solution)/shard_map/dot_general | solution.py:1307
  337.8 100.6 %turn_step.1 = (f32[256,2048]{1,0:T(8,128)}, f32[8,2048]{1,0:T(8,128)}, bf16[2048,768]{1,0:T(8,128)(2,1)}, f32[2048,320]{1,0:T(8,128)}, bf16[2048,2048]{1,0:T(8,128)(2,1)}) custom-call(bf16[2048,768]{1,0:T(8,128)(2,1)} %copy-done.3, bf16[2048,768]{1,0:T(8,128)(2,1)} %get-tuple-element.69.left1, bf16[768,2048]{1,0:T(8,128)(2,1)} %bitcast.70, ...), custom_call_target="tpu_custom_call" | custom-call | tf_op jit(solution)/shard_map/turn_step/pallas_call | solution.py:1214
  438.6 7.4 %convolution_convert_fusion.3 = bf16[2048,320]{0,1:T(8,128)(2,1)} fusion(bf16[2048,2048]{1,0:T(8,128)(2,1)} %get-tuple-element.84, bf16[2048,320]{1,0:T(8,128)(2,1)S(1)} %copy-done.4), kind=kOutput, calls=%fused_computation.10 | convolution fusion | flops 2685009920 | bytes 11010048 | tf_op jit(solution)/shard_map/dot_general | solution.py:1307
  446.0 12.3 %reduce-scatter.5.cloned.1.call-done = bf16[512,768]{1,0:T(8,128)(2,1)} async-done(((bf16[2048,768]{1,0:T(8,128)(2,1)}), bf16[512,768]{1,0:T(8,128)(2,1)}) %reduce-scatter.5.cloned.1.call-update) | async-done | bytes 786448 | tf_op jit(solution)/shard_map/reduce_scatter | solution.py:1400
  458.3 70.5 %mixer_backward.1 = (bf16[2048,640]{1,0:T(8,128)(2,1)}, f32[320,320]{1,0:T(8,128)}, f32[320,320]{1,0:T(8,128)}, f32[8,320]{1,0:T(8,128)}, bf16[256,2048]{1,0:T(8...) custom-call(f32[2048,320]{1,0:T(8,128)} %get-tuple-element.71.grad_mixed_far, ...), custom_call_target="tpu_custom_call" | custom-call | tf_op jit(solution)/shard_map/mixer_backward/pallas_call | solution.py:454
  528.9 9.0 %convolution_convert_fusion.2 = bf16[2048,640]{0,1:T(8,128)(2,1)S(1)} fusion(bf16[2048,2048]{1,0:T(8,128)(2,1)} %get-tuple-element.57, bf16[2048,640]{1,0:T(8,128)(2,1)} %get-tuple-element.85.left), kind=kOutput, calls=%fused_computation.9 | convolution fusion | flops 5370019840 | bytes 13631488 | tf_op jit(solution)/shard_map/dot_general | solution.py:1307
  542.8 73.9 %final_step.1 = (f32[256,2048]{1,0:T(8,128)}, f32[32,128]{1,0:T(8,128)}, f32[336,128]{1,0:T(8,128)}, bf16[8,64,768]{2,1,0:T(8,128)(2,1)}) custom-call(bf16[2048,640]{1,0:T(8,128)(2,1)} %get-tuple-element.85.left, bf16[640,2048]{1,0:T(8,128)(2,1)} %bitcast.62, bf16[256,2048]{1,0:T(8,128)(2,1)} %bitcast.60, f32[1,2048]{1,0:T(1,128)} %bitcast.88, ...), custom_call_target="tpu_custom_call" | custom-call | tf_op jit(solution)/shard_map/final_step/pallas_call | solution.py:1097
  624.1 4.1 place_columns.6
  634.3 15.3 %owners_step.1 = (bf16[8,64,640]{2,1,0:T(8,128)(2,1)}, bf16[8,64,320]{2,1,0:T(8,128)(2,1)}) custom-call(bf16[8,64,640]{2,1,0:T(8,128)(2,1)} %bitcast.74, bf16[8,64,320]{2,1,0:T(8,128)(2,1)} %bitcast.78), custom_call_target="tpu_custom_call" | custom-call | tf_op jit(solution)/shard_map/owners_step/pallas_call | solution.py:1138
  649.6 2.6 place_columns.4
  656.4 3.1 copy.59
  (92 shorter events, 38.2 us)
Async XLA Ops:
  7.2 70.3 %copy-start = (bf16[2048,768]{1,0:T(8,128)(2,1)S(1)}, bf16[2048,768]{1,0:T(8,128)(2,1)}, u32[]{:S(2)}) copy-start(bf16[2048,768]{1,0:T(8,128)(2,1)} %param.26) | copy-start | bytes 9437188
  7.2 77.5 %all-gather.13.cloned.1.call-start = ((), (), s32[]{:S(2)}) async-start(), calls=%async_computation.10 | async-start | bytes 3276800 | tf_op jit(solution)/shard_map/all_gather | solution.py:1350
  9.4 117.2 %all-gather.15.cloned.1.call-start = ((), (), s32[]{:S(2)}) async-start(), calls=%async_computation.11 | async-start | bytes 1638400 | tf_op jit(solution)/shard_map/all_gather | solution.py:1350
  11.2 260.2 %all-gather.9.cloned.1.call-start = ((), (), s32[]{:S(2)}) async-start(), calls=%async_computation.4 | async-start | bytes 3932160 | tf_op jit(solution)/shard_map/all_gather | solution.py:1350
  74.1 7.6 %copy-start.10 = (f32[2560]{0:T(1024)S(1)}, f32[2560]{0:T(1024)}, u32[]{:S(2)}) copy-start(f32[2560]{0:T(1024)} %param.22) | copy-start | bytes 30724
  74.1 7.7 %copy-start.11 = (f32[2560]{0:T(1024)S(1)}, f32[2560]{0:T(1024)}, u32[]{:S(2)}) copy-start(f32[2560]{0:T(1024)} %param.19) | copy-start | bytes 30724
  74.1 7.7 %copy-start.7 = (f32[4,2560]{1,0:T(4,128)S(1)}, f32[4,2560]{1,0:T(4,128)}, u32[]{:S(2)}) copy-start(f32[4,2560]{1,0:T(4,128)} %param.18) | copy-start | bytes 122884
  74.1 7.7 %copy-start.8 = (f32[2,2560]{1,0:T(2,128)S(1)}, f32[2,2560]{1,0:T(2,128)}, u32[]{:S(2)}) copy-start(f32[2,2560]{1,0:T(2,128)} %param.21) | copy-start | bytes 61444
  76.8 206.3 %all-gather.11.cloned.1.call-start = ((), (), s32[]{:S(2)}) async-start(), calls=%async_computation.5 | async-start | bytes 3932160 | tf_op jit(solution)/shard_map/all_gather | solution.py:1350
  77.4 231.0 %all-gather.17.cloned.1.call-start = ((), (), s32[]{:S(2)}) async-start(), calls=%async_computation.12 | async-start | bytes 3932160 | tf_op jit(solution)/shard_map/all_gather | solution.py:1350
  81.1 364.9 %reduce-scatter.7.cloned.1.call-start = ((), (), s32[]{:S(2)}) async-start(), calls=%async_computation.7 | async-start | bytes 3932160 | tf_op jit(solution)/shard_map/reduce_scatter | solution.py:1400
  296.8 11.6 %copy-start.2 = (bf16[2048,768]{1,0:T(8,128)(2,1)}, bf16[2048,768]{1,0:T(8,128)(2,1)S(1)}, u32[]{:S(2)}) copy-start(bf16[2048,768]{1,0:T(8,128)(2,1)S(1)} %get-tuple-element.78.hidden) | copy-start | bytes 9437188
  325.4 11.5 %copy-start.3 = (bf16[2048,768]{1,0:T(8,128)(2,1)}, bf16[2048,768]{1,0:T(8,128)(2,1)S(1)}, u32[]{:S(2)}) copy-start(bf16[2048,768]{1,0:T(8,128)(2,1)S(1)} %get-tuple-element.68.left0) | copy-start | bytes 9437188
  337.0 121.4 %reduce-scatter.5.cloned.1.call-start = ((), (), s32[]{:S(2)}) async-start(), calls=%async_computation.6 | async-start | bytes 3932160 | tf_op jit(solution)/shard_map/reduce_scatter | solution.py:1400
  337.7 202.6 %reduce-scatter.9.cloned.1.call-start = ((), (), s32[]{:S(2)}) async-start(), calls=%async_computation.8 | async-start | bytes 3932160 | tf_op jit(solution)/shard_map/reduce_scatter | solution.py:1400
  337.8 100.8 %copy-start.4 = (bf16[2048,320]{1,0:T(8,128)(2,1)S(1)}, bf16[2048,320]{1,0:T(8,128)(2,1)}, u32[]{:S(2)}) copy-start(bf16[2048,320]{1,0:T(8,128)(2,1)} %get-tuple-element.62.left) | copy-start | bytes 3932164
  438.4 191.8 %reduce-scatter.11.cloned.1.call-start = ((), (), s32[]{:S(2)}) async-start(), calls=%async_computation.9 | async-start | bytes 4915200 | tf_op jit(solution)/shard_map/reduce_scatter | solution.py:1400
  528.8 9.0 %copy-start.5 = (bf16[2048,320]{0,1:T(8,128)(2,1)S(1)}, bf16[2048,320]{0,1:T(8,128)(2,1)}, u32[]{:S(2)}) copy-start(bf16[2048,320]{0,1:T(8,128)(2,1)} %convolution_convert_fusion.3) | copy-start | bytes 3932164
  537.9 2.5 copy-start.9
  537.9 2.5 copy-start.6
  633.3 26.2 %copy-start.1 = (bf16[2048,768]{1,0:T(8,128)(2,1)S(1)}, bf16[2048,768]{1,0:T(8,128)(2,1)}, u32[]{:S(2)}) copy-start(bf16[2048,768]{1,0:T(8,128)(2,1)} %param.26) | copy-start | bytes 9437188
Sparse Core Ops, SparseCore 0:
  10.2 58.8 all-gather.12
  71.2 31.4 all-gather.14
  104.9 66.6 all-gather.8
  173.5 62.0 all-gather.10
  237.6 62.1 all-gather.16
  337.1 58.5 reduce-scatter.6
  398.0 60.2 reduce-scatter.4
  460.6 61.8 reduce-scatter.8
  540.4 79.4 reduce-scatter.10

commit v8 on v7

--- a/solution.py
+++ b/solution.py
@@ -229,9 +229,9 @@
 
 def mixer_backward_kernel(
     count, seg, grad_mixed_far, branches_far, states_far, decay_far, conv_far, mask_far, halo, cin, gate_blocks, vec_ref,
-    hidden, w_down, middle_far, reduced0, reduced1, grad_out, gw0_out, gw1_out, small_out, outputs, owned0, owned1,
+    hidden, w_down, middle_far, reduced, grad_out, gw0_out, gw1_out, small_out, pieces_out, outputs, owned,
     tot, prod, ext, halo_send, halo_recv, summary, slots, uin, send_sem, recv_sem, halo_sems,
-    grad_mixed, branches, states, decay, conv_low_ref, mask, middle, wg, load, own0, own1, own2, own3, *buffers,
+    grad_mixed, branches, states, decay, conv_low_ref, mask, middle, wg, load, own_send, own_recv, *buffers,
 ):
     place = Place()
     pairs = (
@@ -249,11 +249,10 @@
     me = lax.axis_index("t")
     place.greet([place.peer(*offset) for offset in BEYOND] + [{"t": lax.rem(me + step, count)} for step in range(1, count)])
     scatter = Scatter(place, pair_product([hidden], [w_down], outputs.shape[0]), *buffers)
-    owners = [Owners(place, reduced0, owned0, own0, own1), Owners(place, reduced1, owned1, own2, own3)]
+    owners = Owners(place, reduced, owned, own_send, own_recv)
     spread_blocks(gate_blocks, wg)
     scatter.run_first()
-    for part in owners:
-        part.begin()
+    owners.begin()
     for part in loads:
         part.wait()
     rows = 8
@@ -314,10 +313,12 @@
         keep = m[:, 0:1]
         recur_gate, input_gate, log_decay = gate_values(conv_low, wg[0], wg[1], vec)
         power = jnp.exp(2.0 * log_decay)
-        root = jnp.sqrt(one_minus_exp(-2.0 * log_decay, power))
+        gone = one_minus_exp(-2.0 * log_decay, power)
+        inverse = lax.rsqrt(gone)
+        root = gone * inverse
         scale = (1.0 - keep) + keep * root
         driven_in = total * conv_vals
-        grad_log = total * before * get_tiles(decay, at, width) - driven_in * input_gate * keep * (power / root)
+        grad_log = total * before * get_tiles(decay, at, width) - driven_in * input_gate * keep * (power * inverse)
         grad0 = grad_log * log_decay * (1.0 - recur_gate)
         grad1 = driven_in * scale * input_gate * (1.0 - input_gate)
         low0 = grad0.astype(BF16)
@@ -350,6 +351,19 @@
 
     lax.fori_loop(0, 2 * rows, gates, 0)
     small_out[7:8, :] = small_out[7:8, :] * vec[8:9]
+    size, part = gate_blocks.shape[1], width // 4
+
+    def padded(values):
+        short = [values, jnp.zeros((values.shape[0], LANES - part), F32)]
+        return jnp.concatenate(short, axis=1)
+
+    for r in range(4):
+        first = r * part // size * size
+        at = slice(r * part, (r + 1) * part)
+        for k, square in enumerate((gw0_out, gw1_out)):
+            pieces_out[r, k * size : (k + 1) * size, :] = padded(square[first : first + size, at]).astype(BF16)
+        rest = jnp.concatenate([padded(small_out[:, at]), jnp.zeros((8, LANES), F32)], axis=0)
+        pieces_out[r, 2 * size :, :] = rest.astype(BF16)
     for r in range(rows):
         halo_send[r * HALO : (r + 1) * HALO, :] = get_tiles(tot, pl.ds(r * seg, HALO), width)
     halo_copy = pltpu.make_async_remote_copy(
@@ -393,8 +407,7 @@
 
     for_slices(0, outputs.shape[0], body)
     scatter.finish()
-    for part in owners:
-        part.finish()
+    owners.finish()
 
 
 def whole(count):
@@ -457,11 +470,13 @@
         out_shape=(
             jax.ShapeDtypeStruct((n, 2 * width), BF16),
             jax.ShapeDtypeStruct((width, width), F32), jax.ShapeDtypeStruct((width, width), F32),
-            jax.ShapeDtypeStruct((8, width), F32), jax.ShapeDtypeStruct((tokens, depth), BF16),
-            *[jax.ShapeDtypeStruct(part.shape, BF16) for part in reduced],
+            jax.ShapeDtypeStruct((8, width), F32),
+            jax.ShapeDtypeStruct((4, 2 * gate_blocks.shape[1] + 16, LANES), BF16),
+            jax.ShapeDtypeStruct((tokens, depth), BF16),
+            jax.ShapeDtypeStruct(reduced.shape, BF16),
         ),
-        in_specs=[*[ANYWHERE] * 6, *whole(6), *[ANYWHERE] * 3],
-        out_specs=(*whole(5), *[ANYWHERE] * 2),
+        in_specs=[*[ANYWHERE] * 6, *whole(6), *[ANYWHERE] * 2],
+        out_specs=(*whole(6), ANYWHERE),
         scratch_shapes=[
             pltpu.VMEM((tiles, n, LANES), F32),
             pltpu.VMEM((tiles, n, LANES), F32),
@@ -477,11 +492,11 @@
             *[pltpu.VMEM(part.shape, part.dtype) for part in (grad_mixed, branches, states, decay, conv_low, mask, middle)],
             pltpu.VMEM((2, width, width), BF16),
             pltpu.SemaphoreType.DMA((7,)),
-            *[pltpu.SemaphoreType.DMA((8,))] * 4,
+            *[pltpu.SemaphoreType.DMA((8,))] * 2,
             *Scatter.scratch(tokens, depth),
         ],
         compiler_params=mixer_params(2),
-    )(grad_mixed, branches, states, decay, conv_low, mask, halo, cin, gate_blocks, vec, hidden, w_down, middle, *reduced)
+    )(grad_mixed, branches, states, decay, conv_low, mask, halo, cin, gate_blocks, vec, hidden, w_down, middle, reduced)
 
 
 class Place:
@@ -891,28 +906,40 @@
     weight_grads(3 * steps // 4, steps)
     gather.pass_second()
 
-    def mixed_back(source, chunk):
+    def fetch(slot, chunk):
         at = pl.ds(pl.multiple_of(chunk * tokens, tokens), tokens)
-        if source is None:
-            fetch = pltpu.make_async_copy(gathered.at[at], chunk_ref, load.at[0])
-            fetch.start()
-            fetch.wait()
-            source = chunk_ref
-        value = lax.dot_general(source[...], w_out[...], (((1,), (1,)), ((), ())), preferred_element_type=F32)
-        mixed_out[at, :] = value
-
-    mixed_back(block, place.chunk(0, 0, 0))
-    mixed_back(None, place.chunk(0, 1, 0))
-    mixed_back(None, place.chunk(1, 0, 0))
+        copy = pltpu.make_async_copy(gathered.at[at], chunk_ref.at[slot], load.at[slot])
+        copy.start()
+        return copy, slot, chunk
+
+    def mixed_back(fetched):
+        copy, slot, chunk = fetched
+        copy.wait()
+        mixed_of(chunk_ref[slot], chunk)
+
+    def mixed_of(values, chunk):
+        at = pl.ds(pl.multiple_of(chunk * tokens, tokens), tokens)
+        mixed_out[at, :] = lax.dot_general(values, w_out[...], (((1,), (1,)), ((), ())), preferred_element_type=F32)
+
+    ahead = fetch(0, place.chunk(0, 1, 0))
+    mixed_of(block[...], place.chunk(0, 0, 0))
+    after = fetch(1, place.chunk(1, 0, 0))
+    mixed_back(ahead)
     gather.finish_core()
-    mixed_back(None, place.chunk(0, 0, 1))
+    ahead = fetch(0, place.chunk(0, 0, 1))
+    mixed_back(after)
     gather.pass_third()
-    mixed_back(None, place.chunk(1, 1, 0))
+    after = fetch(1, place.chunk(1, 1, 0))
+    mixed_back(ahead)
     gather.finish_near()
-    mixed_back(None, place.chunk(0, 1, 1))
-    mixed_back(None, place.chunk(1, 0, 1))
+    ahead = fetch(0, place.chunk(0, 1, 1))
+    mixed_back(after)
+    after = fetch(1, place.chunk(1, 0, 1))
+    mixed_back(ahead)
     gather.finish_far()
-    mixed_back(None, place.chunk(1, 1, 1))
+    ahead = fetch(0, place.chunk(1, 1, 1))
+    mixed_back(after)
+    mixed_back(ahead)
     scatter.finish()
     gather.finish_sends()
 
@@ -1040,22 +1067,23 @@
 
 
 def final_kernel(
-    count, with_gates, left, right, own_in, gain, mlp_gains, pieces, grad_middle, reduced,
-    grad_out, gains_out, gates_out, owned,
+    count, with_gates, left, right, own_in, gain, mlp_gains, pieces, grad_middle, reduced0, reduced1,
+    grad_out, gains_out, gates_out, owned0, owned1,
     gain_sum, values, inbox, plane_sum, plane_box, sum_send, sum_recv, rows_recv, gates_all, gates_send, gates_recv,
-    own_send, own_recv, *buffers,
+    send0, recv0, send1, recv1, *buffers,
 ):
     tokens, width = own_in.shape
     place = Place()
     me = lax.axis_index("t")
     place.greet([place.peer(*offset) for offset in BEYOND] + [{"t": lax.rem(me + step, count)} for step in range(1, count)])
     scatter = Scatter(place, pair_product([left], [right], tokens), *buffers)
-    owners = Owners(place, reduced, owned, own_send, own_recv)
+    owners = [Owners(place, reduced0, owned0, send0, recv0), Owners(place, reduced1, owned1, send1, recv1)]
     gates = GateSums(place, count, pieces, rows_recv, gates_all, gates_send, gates_recv)
     scatter.run_first()
     if with_gates:
         gates.begin()
-    owners.begin()
+    for part in owners:
+        part.begin()
     scatter.run_second()
     if with_gates:
         gates.pass_on()
@@ -1083,16 +1111,15 @@
         gates.finish(gates_out)
     else:
         gates_out[...] = jnp.zeros_like(gates_out)
-    owners.finish()
+    for part in owners:
+        part.finish()
     scatter.finish()
 
 
-def final_step(planes, left, right, own_in, gain, mlp_gains, pieces, grad_middle, reduced):
+def final_step(planes, with_gates, left, right, own_in, gain, mlp_gains, pieces, grad_middle, reduced):
     tokens, width = own_in.shape
-    with_gates = pieces.shape[0] == planes
     block = pieces.shape[1:] if with_gates else (16, LANES)
     slots = planes if with_gates else 1
-    pieces = pieces if with_gates else jnp.zeros((1, *block), BF16)
     sums = (2 * width // LANES, LANES)
     return pl.pallas_call(
         functools.partial(final_kernel, planes, with_gates),
@@ -1101,10 +1128,10 @@
             jax.ShapeDtypeStruct((tokens, width), F32),
             jax.ShapeDtypeStruct(sums, F32),
             jax.ShapeDtypeStruct(block, F32),
-            jax.ShapeDtypeStruct(reduced.shape, reduced.dtype),
+            *[jax.ShapeDtypeStruct(part.shape, part.dtype) for part in reduced],
         ),
-        in_specs=[*whole(7), ANYWHERE],
-        out_specs=(*whole(3), ANYWHERE),
+        in_specs=[*whole(7), ANYWHERE, ANYWHERE],
+        out_specs=(*whole(3), ANYWHERE, ANYWHERE),
         scratch_shapes=[
             pltpu.VMEM((8, width), F32),
             pltpu.VMEM(sums, F32),
@@ -1118,66 +1145,68 @@
             pltpu.SemaphoreType.DMA((planes + 2,)),
             pltpu.SemaphoreType.DMA((planes + 2,)),
             *OWNERS_SCRATCH,
+            *OWNERS_SCRATCH,
             *Scatter.scratch(tokens, width),
         ],
         compiler_params=mixer_params(7),
-    )(left, right, own_in, gain[None], mlp_gains, pieces, grad_middle, reduced)
-
-
-def owners_kernel(reduced0, reduced1, out0, out1, send0, recv0, send1, recv1):
+    )(left, right, own_in, gain[None], mlp_gains, pieces, grad_middle, *reduced)
+
+
+def owners_kernel(reduced, out, send, recv):
     place = Place()
     place.greet([place.peer(*offset) for offset in BEYOND])
-    owners = [Owners(place, reduced0, out0, send0, recv0), Owners(place, reduced1, out1, send1, recv1)]
-    for part in owners:
-        part.begin()
-    for part in owners:
-        part.finish()
-
-
-def owners_step(number, reduced):
+    owners = Owners(place, reduced, out, send, recv)
+    owners.begin()
+    owners.finish()
+
+
+def owners_step(reduced):
     return pl.pallas_call(
         owners_kernel,
         name="owners_step",
-        out_shape=tuple(jax.ShapeDtypeStruct(part.shape, part.dtype) for part in reduced),
-        in_specs=[ANYWHERE] * 2,
-        out_specs=(ANYWHERE,) * 2,
-        scratch_shapes=[*OWNERS_SCRATCH, *OWNERS_SCRATCH],
-        compiler_params=mixer_params(number),
-    )(*reduced)
-
-
-def place_kernel(planes, hidden, kinds, *refs):
-    given, out = refs[:-1], refs[-1]
-    each = kinds // len(given)
+        out_shape=jax.ShapeDtypeStruct(reduced.shape, reduced.dtype),
+        in_specs=[ANYWHERE],
+        out_specs=ANYWHERE,
+        scratch_shapes=OWNERS_SCRATCH,
+        compiler_params=mixer_params(8),
+    )(reduced)
+
+
+def place_kernel(planes, hidden, outs, *refs):
+    given, results = refs[: -len(outs)], refs[-len(outs) :]
+    each = sum(outs) // len(given)
     piece = given[0].shape[2] // (each * (planes if hidden else 1))
-    for kind in range(kinds):
-        sources, k = given[kind // each], kind % each
-        if hidden:
-            groups = [
-                ((t * 2 + i) * 4 * piece, [(i * 4 + r, (k * planes + t) * piece) for r in range(4)])
-                for t in range(planes)
-                for i in range(2)
-            ]
-        else:
-            groups = [(r * 2 * piece, [(i * 4 + r, k * piece) for i in range(2)]) for r in range(4)]
-        for start, parts in groups:
-            row = jnp.concatenate([sources[p, :, at : at + piece].astype(F32) for p, at in parts], axis=1)
-            if kinds > 1:
-                out[:, kind, start : start + row.shape[1]] = row
+    kind = 0
+    for count, out in zip(outs, results):
+        for slot in range(count):
+            sources, k = given[kind // each], kind % each
+            kind += 1
+            if hidden:
+                groups = [
+                    ((t * 2 + i) * 4 * piece, [(i * 4 + r, (k * planes + t) * piece) for r in range(4)])
+                    for t in range(planes)
+                    for i in range(2)
+                ]
             else:
-                out[:, start : start + row.shape[1]] = row
-
-
-def place_columns(planes, hidden, kinds, *owned):
+                groups = [(r * 2 * piece, [(i * 4 + r, k * piece) for i in range(2)]) for r in range(4)]
+            for start, parts in groups:
+                row = jnp.concatenate([sources[p, :, at : at + piece].astype(F32) for p, at in parts], axis=1)
+                if count > 1:
+                    out[:, slot, start : start + row.shape[1]] = row
+                else:
+                    out[:, start : start + row.shape[1]] = row
+
+
+def place_columns(planes, hidden, outs, *owned):
     members, own_rows, columns = owned[0].shape
-    total = columns * len(owned) * members // kinds
-    shape = (own_rows, kinds, total) if kinds > 1 else (own_rows, total)
+    total = columns * len(owned) * members // sum(outs)
+    shapes = [(own_rows, count, total) if count > 1 else (own_rows, total) for count in outs]
     return pl.pallas_call(
-        functools.partial(place_kernel, planes, hidden, kinds),
+        functools.partial(place_kernel, planes, hidden, outs),
         name="place_columns",
-        out_shape=jax.ShapeDtypeStruct(shape, F32),
+        out_shape=tuple(jax.ShapeDtypeStruct(shape, F32) for shape in shapes),
         in_specs=whole(len(owned)),
-        out_specs=pl.BlockSpec(memory_space=pltpu.VMEM),
+        out_specs=tuple(whole(len(outs))),
         compiler_params=pltpu.CompilerParams(vmem_limit_bytes=60 * 1024 * 1024),
     )(*owned)
 
@@ -1226,7 +1255,7 @@
         scratch_shapes=Scatter.scratch(tokens, width)
         + [pltpu.VMEM((tokens, width), BF16)]
         + GATHER_SCRATCH
-        + [pltpu.VMEM(normed.shape, BF16), pltpu.VMEM((tokens, width), BF16), pltpu.SemaphoreType.DMA((1,))],
+        + [pltpu.VMEM(normed.shape, BF16), pltpu.VMEM((2, tokens, width), BF16), pltpu.SemaphoreType.DMA((2,))],
         compiler_params=mixer_params(5),
     )(left0, left1, right0, right1, middle, gain[None], cot, w_out, normed)
 
@@ -1417,49 +1446,48 @@
     def by_owner(grad):
         return grad.reshape(members, own_rows, -1)
 
-    grad_branches, gw0, gw1, small, outputs, owned_down, owned_left = mixer_backward(
+    grad_branches, gw0, gw1, small, pieces, outputs, owned_down = mixer_backward(
         planes, seg, grad_mixed, branches, states, decay, conv_low, mask, halo, cin, gate_blocks, vec, hidden, w_down, middle,
-        [by_owner(grad_down), by_owner(grad_left_w)],
+        by_owner(grad_down),
     )
     grad_in = jnp.concatenate([tn(normed, grad_branches, BF16), grad_out], axis=1)
     grad_right_w, grad_in, grad_branches = lax.optimization_barrier((grad_right_w, grad_in, grad_branches))
     grad_in = over_planes(grad_in)
     outputs = outputs.reshape(inputs.shape)
 
-    column_block = lax.broadcasted_iota(jnp.int32, (block_width, channels), 1) // block_width
-
-    def diagonal(gw):
-        return sum(
-            jnp.where(column_block == n, gw[n * block_width : (n + 1) * block_width], 0.0) for n in range(blocks)
-        )
-
-    gate_grads = jnp.concatenate([diagonal(gw0), diagonal(gw1), small], axis=0)
-    pieces = jnp.zeros((0, 8, LANES), F32)
-    if direct:
-        pieces = gate_grads.reshape(gate_grads.shape[0], row_groups, -1).transpose(1, 0, 2)
-        pieces = jnp.pad(pieces.astype(BF16), ((0, 0), (0, -pieces.shape[1] % 16), (0, LANES - part)))
-    grad_inputs, gains, gate_sums, owned_right = final_step(
-        planes, grad_branches, in_w, own_in, mix_gain, grad_mlp_gain, pieces, grad_middle, by_owner(grad_right_w)
+    grad_inputs, gains, gate_grads, owned_left, owned_right = final_step(
+        planes, direct, grad_branches, in_w, own_in, mix_gain, grad_mlp_gain, pieces, grad_middle,
+        [by_owner(grad_left_w), by_owner(grad_right_w)],
     )
     grad_inputs = grad_inputs.reshape(inputs.shape)
     index = ((t * 2 + i) * row_groups + r) * own_rows
     gains = lax.dynamic_slice_in_dim(gains.reshape(2, width), index, own_rows, 1)
 
 
-    split = 2 * channels
-    owned_in, owned_out = owners_step(8, [by_owner(grad_in[:, :split]), by_owner(grad_in[:, split:])])
-
-    def columns(kinds, hidden, *owned):
+    owned_in = owners_step(by_owner(grad_in))
+
+    def columns(hidden, outs, *owned):
         if direct:
-            return place_columns(planes, hidden, kinds, *owned)
-        owned = jnp.concatenate(owned, axis=2).reshape(2, row_groups, own_rows, kinds, planes if hidden else 1, -1).astype(F32)
+            return place_columns(planes, hidden, outs, *owned)
+        owned = jnp.concatenate(owned, axis=2)
+        owned = owned.reshape(2, row_groups, own_rows, sum(outs), planes if hidden else 1, -1).astype(F32)
         order = (2, 3, 4, 0, 1, 5) if hidden else (2, 3, 1, 0, 4, 5)
-        owned = owned.transpose(order).reshape(own_rows, kinds, -1)
-        return owned if kinds > 1 else owned[:, 0]
-
+        owned = owned.transpose(order).reshape(own_rows, sum(outs), -1)
+        return (owned[:, :2], owned[:, 2])
+
+    grad_in_weight, grad_out_weight = columns(False, (2, 1), owned_in)
+    grad_mlp_in, grad_down_weight = columns(True, (2, 1), owned_left, owned_right, owned_down)
     if direct:
-        gate_grads = gate_sums[:, :part]
+        gate_grads = gate_grads[:, :part]
     else:
+        column_block = lax.broadcasted_iota(jnp.int32, (block_width, channels), 1) // block_width
+
+        def diagonal(gw):
+            return sum(
+                jnp.where(column_block == n, gw[n * block_width : (n + 1) * block_width], 0.0) for n in range(blocks)
+            )
+
+        gate_grads = jnp.concatenate([diagonal(gw0), diagonal(gw1), small], axis=0)
         placed = jnp.zeros((gate_grads.shape[0], recur_width), F32)
         placed = lax.dynamic_update_slice_in_dim(placed, gate_grads, first, 1)
         gate_grads = lax.psum_scatter(placed, EVERY, scatter_dimension=1, tiled=True)
@@ -1469,16 +1497,16 @@
         outputs,
         grad_inputs,
         gains[1],
-        columns(2, False, owned_in),
+        grad_in_weight,
         small[0:4],
         small[4],
         grad_gate_weight,
         small[5:7],
         small[7],
-        columns(1, False, owned_out),
+        grad_out_weight,
         gains[0],
-        columns(2, True, owned_left, owned_right),
-        columns(1, True, owned_down),
+        grad_mlp_in,
+        grad_down_weight,
     )
 
 

time: 670 us -> 690 us (1.030)
  waiting for transfers between devices: 13.7 us -> 32.1 us
    reduce_scatter x4, waiting for transfers between devices: 12.3 us -> 30.7 us  [over_planes(): return lax.psum_scatter(grad, 't', scatter_dimension=0, tiled=True)]
    pallas_call x1, Pallas kernels: 73.9 us -> 82.6 us  [final_step(): pl.pallas_call(functools.partial(final_kernel, planes, with_gates), name=...]
    pallas_call x5 -> x3, Pallas kernels: 26.5 us -> 23 us  [the longest x1 15.2 us: owners_step(): pl.pallas_call(owners_kernel, name='owners_step', out_shape=jax.ShapeDtyp...]
    unnamed x30 -> x26, local copies, waits for them, and re-layouts: 15.2 us -> 15.8 us
  transfers between devices with their start and end apart: 9 -> 9, of which waited for: 1 -> 1; matrix products, arithmetic and copies ran while one was open for 16% -> 19% of each run, Pallas kernels for 71% -> 70%
where the time goes in v8:
time: 690 us; the launch traced here: 686 us
  Pallas kernels  496 us (72%)
  matrix products  95.1 us (14%)
  local copies, waits for them, and re-layouts  40.8 us (6%)
  waiting for transfers between devices  32.1 us (5%)
  between operations  14.6 us (2%)
  other arithmetic  7.17 us (1%)
    pallas_call x1, Pallas kernels, turn_step(): pl.pallas_call(turn_kernel, name='turn_step', out_shape=(jax.ShapeDtypeSt...  96.9 us
    pallas_call x1, Pallas kernels, middle_step(): pl.pallas_call(middle_kernel, name='middle_step', out_shape=(jax.ShapeDty...  85.2 us
    pallas_call x1, Pallas kernels, final_step(): pl.pallas_call(functools.partial(final_kernel, planes, with_gates), name=...  82.6 us
    pallas_call x1, Pallas kernels, mixer_backward(): pl.pallas_call(functools.partial(mixer_backward_kernel, count, seg), name...  72.2 us
    pallas_call x1, Pallas kernels, mixer_forward(): pl.pallas_call(functools.partial(mixer_forward_kernel, count, seg, rows_h...  59.6 us
    dot_general x4, matrix products, nt(): lax.dot_general(left, right, (((1,), (1,)), ((), ())), preferred_element_...  55 us
    pallas_call x1, Pallas kernels, first_gather(): pl.pallas_call(functools.partial(first_gather_kernel, planes), name='firs...  45.6 us
    dot_general x4, matrix products, tn(): lax.dot_general(left, right, (((0,), (0,)), ((), ())), preferred_element_...  40 us
  transfers between devices with their start and end apart: 9, of which 1 were waited for; matrix products, arithmetic and copies ran while one was open for 19% of the time, Pallas kernels for 70%

profile of v8, /device:TPU:0, one launch (start us, length us, event | category | flops | bytes accessed | tf_op | source)
XLA Modules:
  0.0 685.8 jit_solution(4673531619346665582)
XLA Ops:
  14.1 2.5 multiply_convert_fusion.3.normed
  16.6 45.6 %first_gather.1 = (bf16[2048,2048]{1,0:T(8,128)(2,1)}, f32[8,8,128]{2,1,0:T(8,128)}, f32[8,8,128]{2,1,0:T(8,128)}, f32[8,8,128]{2,1,0:T(8,128)}) custom-call(bf16[256,2048]{1,0:T(8,128)(2,1)} %multiply_convert_fusion.3.normed, f32[8,128]{1,0:T(8,128)} %pad.4.ids), custom_call_target="tpu_custom_call" | custom-call | tf_op jit(solution)/shard_map/first_gather/pallas_call | solution.py:1217
  62.2 5.8 constant_dynamic-slice_fusion.2
  68.1 6.0 copy.39
  74.1 2.7 fusion.2
  84.5 30.4 %swap.1 = bf16[2,4,80,2048]{3,2,1,0:T(8,128)(2,1)} custom-call(bf16[4,2,80,2048]{3,2,1,0:T(8,128)(2,1)} %bitcast.71), custom_call_target="tpu_custom_call" | custom-call | tf_op jit(solution)/shard_map/swap/pallas_call | solution.py:1316
  115.0 11.4 %fusion.3.branches_far = f32[2048,640]{1,0:T(8,128)} fusion(bf16[2048,2048]{1,0:T(8,128)(2,1)} %get-tuple-element.57, bf16[640,2048]{1,0:T(8,128)(2,1)} %bitcast.58), kind=kOutput, calls=%fused_computation.34 | convolution fusion | flops 5368709120 | bytes 16252928 | tf_op jit(solution)/shard_map/dot_general | solution.py:1332
  126.4 59.6 %mixer_forward.1 = (bf16[2048,320]{1,0:T(8,128)(2,1)}, f32[3,2048,128]{2,1,0:T(8,128)}, f32[2048,320]{1,0:T(8,128)}, bf16[2048,320]{1,0:T(8,128)(2,1)}, f32[128,...) custom-call(f32[2048,640]{1,0:T(8,128)} %fusion.3.branches_far, ...), custom_call_target="tpu_custom_call" | custom-call | tf_op jit(solution)/shard_map/mixer_forward/pallas_call | solution.py:427
  186.0 85.2 %middle_step.1 = (f32[256,2048]{1,0:T(8,128)}, bf16[2048,2048]{1,0:T(8,128)(2,1)}) custom-call(bf16[2048,320]{1,0:T(8,128)(2,1)} %get-tuple-element.62.left, bf16[320,2048]{1,0:T(8,128)(2,1)} %bitcast.61, bf16[256,2048]{1,0:T(8,128)(2,1)} %bitcast.56, f32[1,2048]{1,0:T(1,128)} %bitcast.80), custom_call_target="tpu_custom_call" | custom-call | tf_op jit(solution)/shard_map/middle_step/pallas_call | solution.py:1230
  271.2 11.8 %fusion.4 = f32[2048,768]{1,0:T(8,128)} fusion(bf16[2048,2048]{1,0:T(8,128)(2,1)} %get-tuple-element.64.normed_far, bf16[768,2048]{1,0:T(8,128)(2,1)} %bitcast.67), kind=kOutput, calls=%fused_computation.35 | convolution fusion | flops 6442450944 | bytes 17825792 | tf_op jit(solution)/shard_map/dot_general | solution.py:1332
  283.0 14.0 %multiply_convert_fusion.2 = (bf16[2048,768]{1,0:T(8,128)(2,1)S(1)}, f32[2048,768]{1,0:T(8,128)}) fusion(f32[2048,768]{1,0:T(8,128)} %fusion.4, bf16[2048,2048]{1,0:T(8,128)(2,1)} %get-tuple-element.64.normed_far, bf16[768,2048]{1,0:T(8,128)(2,1)} %bitcast.69), kind=kOutput, calls=%fused_computation.2 | convolution fusion | flops 6458179584 | bytes 27262976 | tf_op jit(solution)/shard_map/dot_general | solution.py:1332
  297.0 11.5 %convolution_convert_fusion.1 = bf16[2048,768]{1,0:T(8,128)(2,1)} fusion(bf16[2048,2048]{1,0:T(8,128)(2,1)} %get-tuple-element.65, bf16[2048,768]{1,0:T(8,128)(2,1)S(1)} %get-tuple-element.78.hidden), kind=kOutput, calls=%fused_computation.8 | convolution fusion | flops 6444023808 | bytes 14680064 | tf_op jit(solution)/shard_map/dot_general | solution.py:1336
  308.6 17.8 %multiply_convert_fusion = (bf16[2048,768]{1,0:T(8,128)(2,1)}, bf16[2048,768]{1,0:T(8,128)(2,1)S(1)}) fusion(f32[2048,768]{1,0:T(8,128)} %fusion.4, f32[2048,768]{1,0:T(8,128)} %get-tuple-element.140, bf16[2048,2048]{1,0:T(8,128)(2,1)} %get-tuple-element.65, bf16[768,2048]{1,0:T(8,128)(2,1)} %all-gather.17.cloned.1.call-done.w_down), kind=kOutput, calls=%fused_computation | convolution fusion | flops 6477053952 | bytes 30408704 | tf_op jit(solution)/shard_map/dot_general | solution.py:1332
  326.4 11.6 %convolution_convert_fusion = bf16[2048,768]{1,0:T(8,128)(2,1)} fusion(bf16[2048,2048]{1,0:T(8,128)(2,1)} %get-tuple-element.64.normed_far, bf16[2048,768]{1,0:T(8,128)(2,1)S(1)} %get-tuple-element.68.left0), kind=kOutput, calls=%fused_computation.7 | convolution fusion | flops 6444023808 | bytes 14680064 | tf_op jit(solution)/shard_map/dot_general | solution.py:1336
  338.0 96.9 %turn_step.1 = (f32[256,2048]{1,0:T(8,128)}, f32[8,2048]{1,0:T(8,128)}, bf16[2048,768]{1,0:T(8,128)(2,1)}, f32[2048,320]{1,0:T(8,128)}, bf16[2048,2048]{1,0:T(8,128)(2,1)}) custom-call(bf16[2048,768]{1,0:T(8,128)(2,1)} %copy-done.3, bf16[2048,768]{1,0:T(8,128)(2,1)} %get-tuple-element.69.left1, bf16[768,2048]{1,0:T(8,128)(2,1)} %bitcast.68, ...), custom_call_target="tpu_custom_call" | custom-call | tf_op jit(solution)/shard_map/turn_step/pallas_call | solution.py:1243
  436.3 7.9 %convolution_convert_fusion.3 = bf16[2048,320]{0,1:T(8,128)(2,1)} fusion(bf16[2048,2048]{1,0:T(8,128)(2,1)} %get-tuple-element.83, bf16[2048,320]{1,0:T(8,128)(2,1)S(1)} %copy-done.4), kind=kOutput, calls=%fused_computation.10 | convolution fusion | flops 2685009920 | bytes 11010048 | tf_op jit(solution)/shard_map/dot_general | solution.py:1336
  444.2 72.2 %mixer_backward.1 = (bf16[2048,640]{1,0:T(8,128)(2,1)}, f32[320,320]{1,0:T(8,128)}, f32[320,320]{1,0:T(8,128)}, f32[8,320]{1,0:T(8,128)}, bf16[4,336,128]{2,1,0:...) custom-call(f32[2048,320]{1,0:T(8,128)} %get-tuple-element.71.grad_mixed_far, ...), custom_call_target="tpu_custom_call" | custom-call | tf_op jit(solution)/shard_map/mixer_backward/pallas_call | solution.py:467
  516.5 9.0 %convolution_convert_fusion.2 = bf16[2048,640]{0,1:T(8,128)(2,1)S(1)} fusion(bf16[2048,2048]{1,0:T(8,128)(2,1)} %get-tuple-element.57, bf16[2048,640]{1,0:T(8,128)(2,1)} %get-tuple-element.84.left), kind=kOutput, calls=%fused_computation.9 | convolution fusion | flops 5370019840 | bytes 13631488 | tf_op jit(solution)/shard_map/dot_general | solution.py:1336
  528.0 30.7 %reduce-scatter.9.cloned.1.call-done = bf16[512,768]{1,0:T(8,128)(2,1)} async-done(((bf16[2048,768]{1,0:T(8,128)(2,1)}), bf16[512,768]{1,0:T(8,128)(2,1)}) %reduce-scatter.9.cloned.1.call-update) | async-done | bytes 786448 | tf_op jit(solution)/shard_map/reduce_scatter | solution.py:1429
  558.7 82.6 %final_step.1 = (f32[256,2048]{1,0:T(8,128)}, f32[32,128]{1,0:T(8,128)}, f32[336,128]{1,0:T(8,128)}, bf16[8,64,768]{2,1,0:T(8,128)(2,1)}, bf16[8,64,768]{2,1,0:T(8,128)(2,1)}) custom-call(bf16[2048,640]{1,0:T(8,128)(2,1)} %get-tuple-element.84.left, bf16[640,2048]{1,0:T(8,128)(2,1)} %bitcast.59, bf16[256,2048]{1,0:T(8,128)(2,1)} %bitcast.57, ...), custom_call_target="tpu_custom_call" | custom-call | tf_op jit(solution)/shard_map/final_step/pallas_call | solution.py:1124
  646.2 4.9 place_columns.3
  655.3 15.2 %owners_step.1.refs_0_ = bf16[8,64,960]{2,1,0:T(8,128)(2,1)} custom-call(bf16[8,64,960]{2,1,0:T(8,128)(2,1)} %bitcast.65), custom_call_target="tpu_custom_call" | custom-call | tf_op jit(solution)/shard_map/owners_step/pallas_call | solution.py:1164
  670.5 2.9 place_columns.2
  675.7 3.1 copy.46
  (75 shorter events, 29.7 us)
Async XLA Ops:
  7.2 70.3 %copy-start = (bf16[2048,768]{1,0:T(8,128)(2,1)S(1)}, bf16[2048,768]{1,0:T(8,128)(2,1)}, u32[]{:S(2)}) copy-start(bf16[2048,768]{1,0:T(8,128)(2,1)} %param.26) | copy-start | bytes 9437188
  7.2 77.3 %all-gather.13.cloned.1.call-start = ((), (), s32[]{:S(2)}) async-start(), calls=%async_computation.10 | async-start | bytes 3276800 | tf_op jit(solution)/shard_map/all_gather | solution.py:1379
  9.4 117.0 %all-gather.15.cloned.1.call-start = ((), (), s32[]{:S(2)}) async-start(), calls=%async_computation.11 | async-start | bytes 1638400 | tf_op jit(solution)/shard_map/all_gather | solution.py:1379
  11.2 260.0 %all-gather.9.cloned.1.call-start = ((), (), s32[]{:S(2)}) async-start(), calls=%async_computation.4 | async-start | bytes 3932160 | tf_op jit(solution)/shard_map/all_gather | solution.py:1379
  74.1 7.4 %copy-start.8 = (f32[2560]{0:T(1024)S(1)}, f32[2560]{0:T(1024)}, u32[]{:S(2)}) copy-start(f32[2560]{0:T(1024)} %param.19) | copy-start | bytes 30724
  74.1 7.4 %copy-start.9 = (f32[2560]{0:T(1024)S(1)}, f32[2560]{0:T(1024)}, u32[]{:S(2)}) copy-start(f32[2560]{0:T(1024)} %param.22) | copy-start | bytes 30724
  74.1 7.5 %copy-start.6 = (f32[4,2560]{1,0:T(4,128)S(1)}, f32[4,2560]{1,0:T(4,128)}, u32[]{:S(2)}) copy-start(f32[4,2560]{1,0:T(4,128)} %param.18) | copy-start | bytes 122884
  74.1 7.5 %copy-start.7 = (f32[2,2560]{1,0:T(2,128)S(1)}, f32[2,2560]{1,0:T(2,128)}, u32[]{:S(2)}) copy-start(f32[2,2560]{1,0:T(2,128)} %param.21) | copy-start | bytes 61444
  76.8 206.1 %all-gather.11.cloned.1.call-start = ((), (), s32[]{:S(2)}) async-start(), calls=%async_computation.5 | async-start | bytes 3932160 | tf_op jit(solution)/shard_map/all_gather | solution.py:1379
  77.4 231.1 %all-gather.17.cloned.1.call-start = ((), (), s32[]{:S(2)}) async-start(), calls=%async_computation.12 | async-start | bytes 3932160 | tf_op jit(solution)/shard_map/all_gather | solution.py:1379
  81.1 363.1 %reduce-scatter.5.cloned.1.call-start = ((), (), s32[]{:S(2)}) async-start(), calls=%async_computation.6 | async-start | bytes 3932160 | tf_op jit(solution)/shard_map/reduce_scatter | solution.py:1429
  297.0 11.5 %copy-start.2 = (bf16[2048,768]{1,0:T(8,128)(2,1)}, bf16[2048,768]{1,0:T(8,128)(2,1)S(1)}, u32[]{:S(2)}) copy-start(bf16[2048,768]{1,0:T(8,128)(2,1)S(1)} %get-tuple-element.78.hidden) | copy-start | bytes 9437188
  308.5 219.4 %reduce-scatter.7.cloned.1.call-start = ((), (), s32[]{:S(2)}) async-start(), calls=%async_computation.7 | async-start | bytes 3932160 | tf_op jit(solution)/shard_map/reduce_scatter | solution.py:1429
  326.4 11.6 %copy-start.3 = (bf16[2048,768]{1,0:T(8,128)(2,1)}, bf16[2048,768]{1,0:T(8,128)(2,1)S(1)}, u32[]{:S(2)}) copy-start(bf16[2048,768]{1,0:T(8,128)(2,1)S(1)} %get-tuple-element.68.left0) | copy-start | bytes 9437188
  434.9 1.4 copy-start.4
  434.9 123.8 %reduce-scatter.9.cloned.1.call-start = ((), (), s32[]{:S(2)}) async-start(), calls=%async_computation.8 | async-start | bytes 3932160 | tf_op jit(solution)/shard_map/reduce_scatter | solution.py:1429
  435.7 217.4 %reduce-scatter.11.cloned.1.call-start = ((), (), s32[]{:S(2)}) async-start(), calls=%async_computation.9 | async-start | bytes 4915200 | tf_op jit(solution)/shard_map/reduce_scatter | solution.py:1429
  516.5 9.0 %copy-start.5 = (bf16[2048,320]{0,1:T(8,128)(2,1)S(1)}, bf16[2048,320]{0,1:T(8,128)(2,1)}, u32[]{:S(2)}) copy-start(bf16[2048,320]{0,1:T(8,128)(2,1)} %convolution_convert_fusion.3) | copy-start | bytes 3932164
  651.7 27.1 %copy-start.1 = (bf16[2048,768]{1,0:T(8,128)(2,1)S(1)}, bf16[2048,768]{1,0:T(8,128)(2,1)}, u32[]{:S(2)}) copy-start(bf16[2048,768]{1,0:T(8,128)(2,1)} %param.26) | copy-start | bytes 9437188
Sparse Core Ops, SparseCore 0:
  10.2 58.8 all-gather.12
  71.2 31.4 all-gather.14
  104.9 66.6 all-gather.8
  173.5 62.0 all-gather.10
  237.6 62.1 all-gather.16
  308.6 58.3 reduce-scatter.4
  435.0 59.6 reduce-scatter.6
  497.0 61.6 reduce-scatter.8
  561.0 78.6 reduce-scatter.10

commit v9 on v8

--- a/solution.py
+++ b/solution.py
@@ -857,31 +857,27 @@
 
 
 def turn_kernel(
-    left0, left1, right0, right1, middle, gain, cot, w_out, normed_far,
-    grad_middle_out, gain_out, grads_out, mixed_out, gathered, *scratch,
+    left0, left1, right0, right1, middle, gain, cot, normed_far, grad_middle_out, gain_out, grads_out, block_out, *scratch
 ):
-    buffers, (block, send, recv, normed, chunk_ref, load) = scratch[:SCATTER_BUFFERS], scratch[SCATTER_BUFFERS:]
+    buffers, (normed, load) = scratch[:SCATTER_BUFFERS], scratch[SCATTER_BUFFERS:]
     loaded = pltpu.make_async_copy(normed_far, normed, load.at[0])
     loaded.start()
-    tokens = cot.shape[0]
+    tokens, hidden = cot.shape[0], left0.shape[1]
     place = Place()
     place.greet()
     scatter = Scatter(place, pair_product([left0, left1], [right0, right1], tokens), *buffers)
-    def weight_grads(start, stop):
-        def step(n, none):
-            at = pl.ds(pl.multiple_of(n * 256, 256), 256)
-            value = lax.dot_general(normed[:, at], left1[...], (((0,), (0,)), ((), ())), preferred_element_type=F32)
-            grads_out[at, :] = value.astype(BF16)
-            return none
-
-        lax.fori_loop(start, stop, step, 0)
-
-    steps = normed.shape[1] // 256
     scatter.run_first()
+    scatter.run_second()
     loaded.wait()
-    weight_grads(0, steps // 4)
-    scatter.run_second()
-    weight_grads(steps // 4, steps // 2)
+
+    def weight_grads(n, none):
+        at = pl.ds(pl.multiple_of(n * 256, 256), 256)
+        for k, part in enumerate((left0, left1)):
+            value = lax.dot_general(normed[:, at], part[...], (((0,), (0,)), ((), ())), preferred_element_type=F32)
+            grads_out[at, k * hidden : (k + 1) * hidden] = value.astype(BF16)
+        return none
+
+    lax.fori_loop(0, normed.shape[1] // 256, weight_grads, 0)
     gain_out[...] = jnp.zeros_like(gain_out)
 
     def body(at):
@@ -892,19 +888,23 @@
         inner = jnp.mean(values * weighted, axis=-1, keepdims=True)
         total = cot[at, :].astype(F32) + scale * weighted - values * (scale * scale * scale * inner)
         grad_middle_out[at, :] = total
-        block[at, :] = total.astype(BF16)
+        block_out[at, :] = total.astype(BF16)
         term = grad * values * scale
         gain_out[...] += term[0:8] + term[8:16]
 
-    gather = Gather(place, block, gathered, send, recv)
     for part in (0, 1):
         scatter.run_third(part)
         for_slices(part * tokens // 2, (part + 1) * tokens // 2, body)
-        gather.begin(part)
-    weight_grads(steps // 2, 3 * steps // 4)
-    gather.pass_first()
-    weight_grads(3 * steps // 4, steps)
-    gather.pass_second()
+    scatter.finish()
+
+
+def spread_kernel(block, w_out, mixed, mixed_out, out_grad, gathered, send, recv, chunk_ref, total, load):
+    tokens = block.shape[0]
+    place = Place()
+    place.greet()
+    gather = Gather(place, block, gathered, send, recv)
+    gather.begin_whole()
+    total[...] = jnp.zeros_like(total)
 
     def fetch(slot, chunk):
         at = pl.ds(pl.multiple_of(chunk * tokens, tokens), tokens)
@@ -912,35 +912,46 @@
         copy.start()
         return copy, slot, chunk
 
-    def mixed_back(fetched):
+    def use(fetched):
         copy, slot, chunk = fetched
         copy.wait()
-        mixed_of(chunk_ref[slot], chunk)
-
-    def mixed_of(values, chunk):
+        use_chunk(chunk_ref.at[slot], chunk)
+
+    def use_chunk(values, chunk):
         at = pl.ds(pl.multiple_of(chunk * tokens, tokens), tokens)
-        mixed_out[at, :] = lax.dot_general(values, w_out[...], (((1,), (1,)), ((), ())), preferred_element_type=F32)
-
-    ahead = fetch(0, place.chunk(0, 1, 0))
-    mixed_of(block[...], place.chunk(0, 0, 0))
-    after = fetch(1, place.chunk(1, 0, 0))
-    mixed_back(ahead)
+        mixed_out[at, :] = lax.dot_general(values[...], w_out[...], (((1,), (1,)), ((), ())), preferred_element_type=F32)
+        part = mixed[at, :]
+
+        def rows(n, none):
+            columns = pl.ds(pl.multiple_of(n * 256, 256), 256)
+            turned = (((0,), (0,)), ((), ()))
+            total[columns, :] += lax.dot_general(values[:, columns], part, turned, preferred_element_type=F32)
+            return none
+
+        lax.fori_loop(0, values.shape[1] // 256, rows, 0)
+
+    use_chunk(block, place.chunk(0, 0, 0))
+    gather.pass_first()
     gather.finish_core()
     ahead = fetch(0, place.chunk(0, 0, 1))
-    mixed_back(after)
-    gather.pass_third()
-    after = fetch(1, place.chunk(1, 1, 0))
-    mixed_back(ahead)
+    use(ahead)
+    gather.pass_second()
+    ahead = fetch(0, place.chunk(0, 1, 0))
+    after = fetch(1, place.chunk(1, 0, 0))
+    use(ahead)
     gather.finish_near()
     ahead = fetch(0, place.chunk(0, 1, 1))
-    mixed_back(after)
+    use(after)
+    gather.pass_third()
     after = fetch(1, place.chunk(1, 0, 1))
-    mixed_back(ahead)
+    use(ahead)
+    ahead = fetch(0, place.chunk(1, 1, 0))
+    use(after)
     gather.finish_far()
-    ahead = fetch(0, place.chunk(1, 1, 1))
-    mixed_back(after)
-    mixed_back(ahead)
-    scatter.finish()
+    after = fetch(1, place.chunk(1, 1, 1))
+    use(ahead)
+    use(after)
+    out_grad[...] = total[...].astype(BF16)
     gather.finish_sends()
 
 
@@ -1067,23 +1078,22 @@
 
 
 def final_kernel(
-    count, with_gates, left, right, own_in, gain, mlp_gains, pieces, grad_middle, reduced0, reduced1,
-    grad_out, gains_out, gates_out, owned0, owned1,
+    count, with_gates, left, right, own_in, gain, mlp_gains, pieces, grad_middle, reduced,
+    grad_out, gains_out, gates_out, owned,
     gain_sum, values, inbox, plane_sum, plane_box, sum_send, sum_recv, rows_recv, gates_all, gates_send, gates_recv,
-    send0, recv0, send1, recv1, *buffers,
+    own_send, own_recv, *buffers,
 ):
     tokens, width = own_in.shape
     place = Place()
     me = lax.axis_index("t")
     place.greet([place.peer(*offset) for offset in BEYOND] + [{"t": lax.rem(me + step, count)} for step in range(1, count)])
     scatter = Scatter(place, pair_product([left], [right], tokens), *buffers)
-    owners = [Owners(place, reduced0, owned0, send0, recv0), Owners(place, reduced1, owned1, send1, recv1)]
+    owners = Owners(place, reduced, owned, own_send, own_recv)
     gates = GateSums(place, count, pieces, rows_recv, gates_all, gates_send, gates_recv)
     scatter.run_first()
     if with_gates:
         gates.begin()
-    for part in owners:
-        part.begin()
+    owners.begin()
     scatter.run_second()
     if with_gates:
         gates.pass_on()
@@ -1111,8 +1121,7 @@
         gates.finish(gates_out)
     else:
         gates_out[...] = jnp.zeros_like(gates_out)
-    for part in owners:
-        part.finish()
+    owners.finish()
     scatter.finish()
 
 
@@ -1128,10 +1137,10 @@
             jax.ShapeDtypeStruct((tokens, width), F32),
             jax.ShapeDtypeStruct(sums, F32),
             jax.ShapeDtypeStruct(block, F32),
-            *[jax.ShapeDtypeStruct(part.shape, part.dtype) for part in reduced],
+            jax.ShapeDtypeStruct(reduced.shape, reduced.dtype),
         ),
-        in_specs=[*whole(7), ANYWHERE, ANYWHERE],
-        out_specs=(*whole(3), ANYWHERE, ANYWHERE),
+        in_specs=[*whole(7), ANYWHERE],
+        out_specs=(*whole(3), ANYWHERE),
         scratch_shapes=[
             pltpu.VMEM((8, width), F32),
             pltpu.VMEM(sums, F32),
@@ -1145,42 +1154,39 @@
             pltpu.SemaphoreType.DMA((planes + 2,)),
             pltpu.SemaphoreType.DMA((planes + 2,)),
             *OWNERS_SCRATCH,
-            *OWNERS_SCRATCH,
             *Scatter.scratch(tokens, width),
         ],
         compiler_params=mixer_params(7),
-    )(left, right, own_in, gain[None], mlp_gains, pieces, grad_middle, *reduced)
-
-
-def owners_kernel(reduced, out, send, recv):
+    )(left, right, own_in, gain[None], mlp_gains, pieces, grad_middle, reduced)
+
+
+def owners_kernel(reduced0, reduced1, out0, out1, send0, recv0, send1, recv1):
     place = Place()
     place.greet([place.peer(*offset) for offset in BEYOND])
-    owners = Owners(place, reduced, out, send, recv)
-    owners.begin()
-    owners.finish()
+    owners = [Owners(place, reduced0, out0, send0, recv0), Owners(place, reduced1, out1, send1, recv1)]
+    for part in owners:
+        part.begin()
+    for part in owners:
+        part.finish()
 
 
 def owners_step(reduced):
     return pl.pallas_call(
         owners_kernel,
         name="owners_step",
-        out_shape=jax.ShapeDtypeStruct(reduced.shape, reduced.dtype),
-        in_specs=[ANYWHERE],
-        out_specs=ANYWHERE,
-        scratch_shapes=OWNERS_SCRATCH,
+        out_shape=tuple(jax.ShapeDtypeStruct(part.shape, part.dtype) for part in reduced),
+        in_specs=[ANYWHERE] * 2,
+        out_specs=(ANYWHERE,) * 2,
+        scratch_shapes=[*OWNERS_SCRATCH, *OWNERS_SCRATCH],
         compiler_params=mixer_params(8),
-    )(reduced)
+    )(*reduced)
 
 
 def place_kernel(planes, hidden, outs, *refs):
     given, results = refs[: -len(outs)], refs[-len(outs) :]
-    each = sum(outs) // len(given)
-    piece = given[0].shape[2] // (each * (planes if hidden else 1))
-    kind = 0
-    for count, out in zip(outs, results):
-        for slot in range(count):
-            sources, k = given[kind // each], kind % each
-            kind += 1
+    for count, sources, out in zip(outs, given, results):
+        piece = sources.shape[2] // (count * (planes if hidden else 1))
+        for k in range(count):
             if hidden:
                 groups = [
                     ((t * 2 + i) * 4 * piece, [(i * 4 + r, (k * planes + t) * piece) for r in range(4)])
@@ -1192,14 +1198,14 @@
             for start, parts in groups:
                 row = jnp.concatenate([sources[p, :, at : at + piece].astype(F32) for p, at in parts], axis=1)
                 if count > 1:
-                    out[:, slot, start : start + row.shape[1]] = row
+                    out[:, k, start : start + row.shape[1]] = row
                 else:
                     out[:, start : start + row.shape[1]] = row
 
 
 def place_columns(planes, hidden, outs, *owned):
     members, own_rows, columns = owned[0].shape
-    total = columns * len(owned) * members // sum(outs)
+    total = columns * members // outs[0]
     shapes = [(own_rows, count, total) if count > 1 else (own_rows, total) for count in outs]
     return pl.pallas_call(
         functools.partial(place_kernel, planes, hidden, outs),
@@ -1238,7 +1244,7 @@
     )(mixed, w_out, own_in, gain[None])
 
 
-def turn_step(left0, left1, right0, right1, middle, gain, cot, w_out, normed):
+def turn_step(left0, left1, right0, right1, middle, gain, cot, normed):
     tokens, width = cot.shape
     return pl.pallas_call(
         turn_kernel,
@@ -1246,18 +1252,37 @@
         out_shape=(
             jax.ShapeDtypeStruct((tokens, width), F32),
             jax.ShapeDtypeStruct((8, width), F32),
-            jax.ShapeDtypeStruct((width, left1.shape[1]), BF16),
+            jax.ShapeDtypeStruct((width, 2 * left1.shape[1]), BF16),
+            jax.ShapeDtypeStruct((tokens, width), BF16),
+        ),
+        in_specs=[*whole(7), ANYWHERE],
+        out_specs=tuple(whole(4)),
+        scratch_shapes=Scatter.scratch(tokens, width)
+        + [pltpu.VMEM(normed.shape, BF16), pltpu.SemaphoreType.DMA((1,))],
+        compiler_params=mixer_params(5),
+    )(left0, left1, right0, right1, middle, gain[None], cot, normed)
+
+
+def spread_step(block, w_out, mixed):
+    tokens, width = block.shape
+    return pl.pallas_call(
+        spread_kernel,
+        name="turn_spread",
+        out_shape=(
             jax.ShapeDtypeStruct((8 * tokens, w_out.shape[0]), F32),
+            jax.ShapeDtypeStruct((width, w_out.shape[0]), BF16),
             jax.ShapeDtypeStruct((8 * tokens, width), BF16),
         ),
-        in_specs=[*whole(8), ANYWHERE],
-        out_specs=(*whole(4), ANYWHERE),
-        scratch_shapes=Scatter.scratch(tokens, width)
-        + [pltpu.VMEM((tokens, width), BF16)]
-        + GATHER_SCRATCH
-        + [pltpu.VMEM(normed.shape, BF16), pltpu.VMEM((2, tokens, width), BF16), pltpu.SemaphoreType.DMA((2,))],
-        compiler_params=mixer_params(5),
-    )(left0, left1, right0, right1, middle, gain[None], cot, w_out, normed)
+        in_specs=whole(3),
+        out_specs=(*whole(2), ANYWHERE),
+        scratch_shapes=GATHER_SCRATCH
+        + [
+            pltpu.VMEM((2, tokens, width), BF16),
+            pltpu.VMEM((width, w_out.shape[0]), F32),
+            pltpu.SemaphoreType.DMA((2,)),
+        ],
+        compiler_params=mixer_params(10),
+    )(block, w_out, mixed)
 
 
 class Swap:
@@ -1434,14 +1459,13 @@
     grad_hidden = nt(cot, w_down, F32)
     grad_left = (grad_hidden * right * slope).astype(BF16)
     grad_right = (grad_hidden * act).astype(BF16)
-    grad_left_w = tn(normed_two, grad_left, BF16)
-    grad_left_w, grad_left, grad_right = lax.optimization_barrier((grad_left_w, grad_left, grad_right))
-    grad_left_w = over_planes(grad_left_w)
-    grad_middle, grad_mlp_gain, grad_right_w, grad_mixed, grad_mid = turn_step(
-        grad_left, grad_right, w_left, w_right, middle, mlp_gain, cot_own, w_out, normed_two
+    grad_middle, grad_mlp_gain, grad_mlp_in, grad_mid_own = turn_step(
+        grad_left, grad_right, w_left, w_right, middle, mlp_gain, cot_own, normed_two
     )
-    grad_right_w = over_planes(grad_right_w)
-    grad_out = tn(grad_mid, mixed, BF16)
+    grad_down, grad_mid_own = lax.optimization_barrier((grad_down, grad_mid_own))
+    grad_mlp_in = over_planes(grad_mlp_in)
+    grad_mixed, grad_out, _ = spread_step(grad_mid_own, w_out, mixed)
+    grad_out = over_planes(grad_out)
 
     def by_owner(grad):
         return grad.reshape(members, own_rows, -1)
@@ -1450,21 +1474,21 @@
         planes, seg, grad_mixed, branches, states, decay, conv_low, mask, halo, cin, gate_blocks, vec, hidden, w_down, middle,
         by_owner(grad_down),
     )
-    grad_in = jnp.concatenate([tn(normed, grad_branches, BF16), grad_out], axis=1)
-    grad_right_w, grad_in, grad_branches = lax.optimization_barrier((grad_right_w, grad_in, grad_branches))
+    grad_in = tn(normed, grad_branches, BF16)
+    grad_in, grad_branches = lax.optimization_barrier((grad_in, grad_branches))
     grad_in = over_planes(grad_in)
     outputs = outputs.reshape(inputs.shape)
 
-    grad_inputs, gains, gate_grads, owned_left, owned_right = final_step(
+    grad_inputs, gains, gate_grads, owned_mlp_in = final_step(
         planes, direct, grad_branches, in_w, own_in, mix_gain, grad_mlp_gain, pieces, grad_middle,
-        [by_owner(grad_left_w), by_owner(grad_right_w)],
+        by_owner(grad_mlp_in),
     )
     grad_inputs = grad_inputs.reshape(inputs.shape)
     index = ((t * 2 + i) * row_groups + r) * own_rows
     gains = lax.dynamic_slice_in_dim(gains.reshape(2, width), index, own_rows, 1)
 
 
-    owned_in = owners_step(by_owner(grad_in))
+    owned_in, owned_out = owners_step([by_owner(grad_in), by_owner(grad_out)])
 
     def columns(hidden, outs, *owned):
         if direct:
@@ -1475,8 +1499,8 @@
         owned = owned.transpose(order).reshape(own_rows, sum(outs), -1)
         return (owned[:, :2], owned[:, 2])
 
-    grad_in_weight, grad_out_weight = columns(False, (2, 1), owned_in)
-    grad_mlp_in, grad_down_weight = columns(True, (2, 1), owned_left, owned_right, owned_down)
+    grad_in_weight, grad_out_weight = columns(False, (2, 1), owned_in, owned_out)
+    grad_mlp_in, grad_down_weight = columns(True, (2, 1), owned_mlp_in, owned_down)
     if direct:
         gate_grads = gate_grads[:, :part]
     else:

time: 690 us -> 788 us (1.14)
  waiting for transfers between devices: 32.1 us -> 147 us
  matrix products: 95.1 us -> 78.1 us
    reduce_scatter x4, waiting for transfers between devices: 30.7 us -> 146 us  [over_planes(): return lax.psum_scatter(grad, 't', scatter_dimension=0, tiled=True)]
    pallas_call x1 -> x2, Pallas kernels: 15.2 us -> 67.6 us  [the longest x1 52.2 us: spread_step(): pl.pallas_call(spread_kernel, name='turn_spread', out_shape=(jax.ShapeDty...]
    pallas_call x1, Pallas kernels: 96.9 us -> 57.9 us  [turn_step(): pl.pallas_call(turn_kernel, name='turn_step', out_shape=(jax.ShapeDtypeSt...]
    dot_general x4 -> x2, matrix products: 40 us -> 22.6 us  [tn(): lax.dot_general(left, right, (((0,), (0,)), ((), ())), preferred_element_...]
    unnamed x26 -> x20, local copies, waits for them, and re-layouts: 15.8 us -> 15.2 us
  transfers between devices with their start and end apart: 9 -> 9, of which waited for: 1 -> 2; matrix products, arithmetic and copies ran while one was open for 19% -> 14% of each run, Pallas kernels for 70% -> 46%
where the time goes in v9:
time: 788 us; the launch traced here: 784 us
  Pallas kernels  502 us (64%)
  waiting for transfers between devices  147 us (19%)
  matrix products  78.1 us (10%)
  local copies, waits for them, and re-layouts  37.9 us (5%)
  between operations  14.3 us (2%)
    reduce_scatter x4, waiting for transfers between devices, over_planes(): return lax.psum_scatter(grad, 't', scatter_dimension=0, tiled=True)  146 us
    pallas_call x1, Pallas kernels, middle_step(): pl.pallas_call(middle_kernel, name='middle_step', out_shape=(jax.ShapeDty...  85.1 us
    pallas_call x1, Pallas kernels, final_step(): pl.pallas_call(functools.partial(final_kernel, planes, with_gates), name=...  82.1 us
    pallas_call x1, Pallas kernels, mixer_backward(): pl.pallas_call(functools.partial(mixer_backward_kernel, count, seg), name...  65.4 us
    pallas_call x1, Pallas kernels, mixer_forward(): pl.pallas_call(functools.partial(mixer_forward_kernel, count, seg, rows_h...  59.7 us
    pallas_call x1, Pallas kernels, turn_step(): pl.pallas_call(turn_kernel, name='turn_step', out_shape=(jax.ShapeDtypeSt...  57.9 us
    dot_general x4, matrix products, nt(): lax.dot_general(left, right, (((1,), (1,)), ((), ())), preferred_element_...  55.5 us
    pallas_call x1, Pallas kernels, spread_step(): pl.pallas_call(spread_kernel, name='turn_spread', out_shape=(jax.ShapeDty...  52.2 us
  transfers between devices with their start and end apart: 9, of which 2 were waited for; matrix products, arithmetic and copies ran while one was open for 14% of the time, Pallas kernels for 46%

profile of v9, /device:TPU:0, one launch (start us, length us, event | category | flops | bytes accessed | tf_op | source)
XLA Modules:
  0.0 784.3 jit_solution(7820804068993227417)
XLA Ops:
  14.1 2.5 multiply_convert_fusion.3.normed
  16.6 45.6 %first_gather.1 = (bf16[2048,2048]{1,0:T(8,128)(2,1)}, f32[8,8,128]{2,1,0:T(8,128)}, f32[8,8,128]{2,1,0:T(8,128)}, f32[8,8,128]{2,1,0:T(8,128)}) custom-call(bf16[256,2048]{1,0:T(8,128)(2,1)} %multiply_convert_fusion.3.normed, f32[8,128]{1,0:T(8,128)} %pad.4.ids), custom_call_target="tpu_custom_call" | custom-call | tf_op jit(solution)/shard_map/first_gather/pallas_call | solution.py:1223
  62.2 5.8 constant_dynamic-slice_fusion.2
  68.1 6.1 copy.37
  74.1 2.7 fusion.2
  84.4 30.4 %swap.1 = bf16[2,4,80,2048]{3,2,1,0:T(8,128)(2,1)} custom-call(bf16[4,2,80,2048]{3,2,1,0:T(8,128)(2,1)} %bitcast.66), custom_call_target="tpu_custom_call" | custom-call | tf_op jit(solution)/shard_map/swap/pallas_call | solution.py:1341
  114.8 11.4 %fusion.3.branches_far = f32[2048,640]{1,0:T(8,128)} fusion(bf16[2048,2048]{1,0:T(8,128)(2,1)} %get-tuple-element.57, bf16[640,2048]{1,0:T(8,128)(2,1)} %bitcast.54), kind=kOutput, calls=%fused_computation.31 | convolution fusion | flops 5368709120 | bytes 16252928 | tf_op jit(solution)/shard_map/dot_general | solution.py:1357
  126.3 59.7 %mixer_forward.1 = (bf16[2048,320]{1,0:T(8,128)(2,1)}, f32[3,2048,128]{2,1,0:T(8,128)}, f32[2048,320]{1,0:T(8,128)}, bf16[2048,320]{1,0:T(8,128)(2,1)}, f32[128,...) custom-call(f32[2048,640]{1,0:T(8,128)} %fusion.3.branches_far, ...), custom_call_target="tpu_custom_call" | custom-call | tf_op jit(solution)/shard_map/mixer_forward/pallas_call | solution.py:427
  185.9 85.1 %middle_step.1 = (f32[256,2048]{1,0:T(8,128)}, bf16[2048,2048]{1,0:T(8,128)(2,1)}) custom-call(bf16[2048,320]{1,0:T(8,128)(2,1)} %get-tuple-element.63.left.mixed, bf16[320,2048]{1,0:T(8,128)(2,1)} %bitcast.57, bf16[256,2048]{1,0:T(8,128)(2,1)} %bitcast.52, f32[1,2048]{1,0:T(1,128)} %bitcast.76), custom_call_target="tpu_custom_call" | custom-call | tf_op jit(solution)/shard_map/middle_step/pallas_call | solution.py:1236
  271.1 11.8 %fusion.4 = f32[2048,768]{1,0:T(8,128)} fusion(bf16[2048,2048]{1,0:T(8,128)(2,1)} %get-tuple-element.65.normed_far, bf16[768,2048]{1,0:T(8,128)(2,1)} %bitcast.62), kind=kOutput, calls=%fused_computation.32 | convolution fusion | flops 6442450944 | bytes 17825792 | tf_op jit(solution)/shard_map/dot_general | solution.py:1357
  282.9 13.7 %multiply_convert_fusion.2 = (bf16[2048,768]{1,0:T(8,128)(2,1)S(1)}, f32[2048,768]{1,0:T(8,128)}) fusion(f32[2048,768]{1,0:T(8,128)} %fusion.4, bf16[2048,2048]{1,0:T(8,128)(2,1)} %get-tuple-element.65.normed_far, bf16[768,2048]{1,0:T(8,128)(2,1)} %bitcast.64), kind=kOutput, calls=%fused_computation.2 | convolution fusion | flops 6458179584 | bytes 27262976 | tf_op jit(solution)/shard_map/dot_general | solution.py:1357
  296.6 11.5 %convolution_convert_fusion = bf16[2048,768]{1,0:T(8,128)(2,1)} fusion(bf16[2048,2048]{1,0:T(8,128)(2,1)} %get-tuple-element.62, bf16[2048,768]{1,0:T(8,128)(2,1)S(1)} %get-tuple-element.79.hidden), kind=kOutput, calls=%fused_computation.6 | convolution fusion | flops 6444023808 | bytes 14680064 | tf_op jit(solution)/shard_map/dot_general | solution.py:1361
  308.2 18.6 %multiply_convert_fusion = (bf16[2048,768]{1,0:T(8,128)(2,1)}, bf16[2048,768]{1,0:T(8,128)(2,1)}) fusion(f32[2048,768]{1,0:T(8,128)} %fusion.4, f32[2048,768]{1,0:T(8,128)} %get-tuple-element.140, bf16[2048,2048]{1,0:T(8,128)(2,1)} %get-tuple-element.62, bf16[768,2048]{1,0:T(8,128)(2,1)} %all-gather.17.cloned.1.call-done.w_down), kind=kOutput, calls=%fused_computation | convolution fusion | flops 6477053952 | bytes 30408704 | tf_op jit(solution)/shard_map/dot_general | solution.py:1357
  326.8 57.9 %turn_step.1 = (f32[256,2048]{1,0:T(8,128)}, f32[8,2048]{1,0:T(8,128)}, bf16[2048,1536]{1,0:T(8,128)(2,1)}, bf16[256,2048]{1,0:T(8,128)(2,1)}) custom-call(bf16[2048,768]{1,0:T(8,128)(2,1)} %get-tuple-element.128.left0, bf16[2048,768]{1,0:T(8,128)(2,1)} %get-tuple-element.127.left1, bf16[768,2048]{1,0:T(8,128)(2,1)} %bitcast.63, bf16[768,2048]{1,0:T(8,128)(2,1)} %bitcast.65, ...), custom_call_target="tpu_custom_call" | custom-call | tf_op jit(solution)/shard_map/turn_step/pallas_call | solution.py:1249
  384.8 52.2 %turn_spread.1 = (f32[2048,320]{1,0:T(8,128)}, bf16[2048,320]{1,0:T(8,128)(2,1)}, bf16[2048,2048]{1,0:T(8,128)(2,1)}) custom-call(bf16[256,2048]{1,0:T(8,128)(2,1)} %get-tuple-element.71.block, bf16[320,2048]{1,0:T(8,128)(2,1)} %bitcast.58, bf16[2048,320]{1,0:T(8,128)(2,1)} %get-tuple-element.63.left.mixed), custom_call_target="tpu_custom_call" | custom-call | tf_op jit(solution)/shard_map/turn_spread/pallas_call | solution.py:1268
  437.1 65.4 %mixer_backward.1 = (bf16[2048,640]{1,0:T(8,128)(2,1)}, f32[320,320]{1,0:T(8,128)}, f32[320,320]{1,0:T(8,128)}, f32[8,320]{1,0:T(8,128)}, bf16[4,336,128]{2,1,0:...) custom-call(f32[2048,320]{1,0:T(8,128)} %get-tuple-element.72.grad_mixed_far, ...), custom_call_target="tpu_custom_call" | custom-call | tf_op jit(solution)/shard_map/mixer_backward/pallas_call | solution.py:467
  502.5 11.1 %convolution_convert_fusion.1 = bf16[2048,640]{1,0:T(8,128)(2,1)} fusion(bf16[2048,2048]{1,0:T(8,128)(2,1)} %get-tuple-element.57, bf16[2048,640]{1,0:T(8,128)(2,1)} %get-tuple-element.83.left), kind=kOutput, calls=%fused_computation.7 | convolution fusion | flops 5370019840 | bytes 13631488 | tf_op jit(solution)/shard_map/dot_general | solution.py:1361
  514.4 51.1 %reduce-scatter.9.cloned.1.call-done = bf16[512,640]{1,0:T(8,128)(2,1)} async-done(((bf16[2048,640]{1,0:T(8,128)(2,1)}), bf16[512,640]{1,0:T(8,128)(2,1)}) %reduce-scatter.9.cloned.1.call-update) | async-done | bytes 655376 | tf_op jit(solution)/shard_map/reduce_scatter | solution.py:1454
  565.5 15.4 %owners_step.1 = (bf16[8,64,640]{2,1,0:T(8,128)(2,1)}, bf16[8,64,320]{2,1,0:T(8,128)(2,1)}) custom-call(bf16[8,64,640]{2,1,0:T(8,128)(2,1)} %bitcast.74, bf16[8,64,320]{2,1,0:T(8,128)(2,1)} %bitcast.75), custom_call_target="tpu_custom_call" | custom-call | tf_op jit(solution)/shard_map/owners_step/pallas_call | solution.py:1174
  580.9 2.9 place_columns.2
  583.8 94.5 %reduce-scatter.7.cloned.1.call-done = bf16[512,1536]{1,0:T(8,128)(2,1)} async-done(((bf16[2048,1536]{1,0:T(8,128)(2,1)}), bf16[512,1536]{1,0:T(8,128)(2,1)}) %reduce-scatter.7.cloned.1.call-update) | async-done | bytes 1572880 | tf_op jit(solution)/shard_map/reduce_scatter | solution.py:1454
  678.3 82.1 %final_step.1 = (f32[256,2048]{1,0:T(8,128)}, f32[32,128]{1,0:T(8,128)}, f32[336,128]{1,0:T(8,128)}, bf16[8,64,1536]{2,1,0:T(8,128)(2,1)}) custom-call(bf16[2048,640]{1,0:T(8,128)(2,1)} %get-tuple-element.83.left, bf16[640,2048]{1,0:T(8,128)(2,1)} %bitcast.55, bf16[256,2048]{1,0:T(8,128)(2,1)} %bitcast.53, f32[1,2048]{1,0:T(1,128)} %bitcast.78, ...), custom_call_target="tpu_custom_call" | custom-call | tf_op jit(solution)/shard_map/final_step/pallas_call | solution.py:1133
  767.2 4.9 place_columns.3
  774.4 3.1 copy.44
  (66 shorter events, 24.3 us)
Async XLA Ops:
  7.2 70.3 %copy-start = (bf16[2048,768]{1,0:T(8,128)(2,1)S(1)}, bf16[2048,768]{1,0:T(8,128)(2,1)}, u32[]{:S(2)}) copy-start(bf16[2048,768]{1,0:T(8,128)(2,1)} %param.26) | copy-start | bytes 9437188
  7.2 77.2 %all-gather.13.cloned.1.call-start = ((), (), s32[]{:S(2)}) async-start(), calls=%async_computation.10 | async-start | bytes 3276800 | tf_op jit(solution)/shard_map/all_gather | solution.py:1404
  9.4 116.8 %all-gather.15.cloned.1.call-start = ((), (), s32[]{:S(2)}) async-start(), calls=%async_computation.11 | async-start | bytes 1638400 | tf_op jit(solution)/shard_map/all_gather | solution.py:1404
  11.2 259.9 %all-gather.9.cloned.1.call-start = ((), (), s32[]{:S(2)}) async-start(), calls=%async_computation.4 | async-start | bytes 3932160 | tf_op jit(solution)/shard_map/all_gather | solution.py:1404
  68.0 15.4 %copy-start.5 = (f32[2560]{0:T(1024)S(1)}, f32[2560]{0:T(1024)}, u32[]{:S(2)}) copy-start(f32[2560]{0:T(1024)} %param.19) | copy-start | bytes 30724
  68.0 15.4 %copy-start.6 = (f32[2560]{0:T(1024)S(1)}, f32[2560]{0:T(1024)}, u32[]{:S(2)}) copy-start(f32[2560]{0:T(1024)} %param.22) | copy-start | bytes 30724
  68.1 15.5 %copy-start.3 = (f32[4,2560]{1,0:T(4,128)S(1)}, f32[4,2560]{1,0:T(4,128)}, u32[]{:S(2)}) copy-start(f32[4,2560]{1,0:T(4,128)} %param.18) | copy-start | bytes 122884
  68.1 15.5 %copy-start.4 = (f32[2,2560]{1,0:T(2,128)S(1)}, f32[2,2560]{1,0:T(2,128)}, u32[]{:S(2)}) copy-start(f32[2,2560]{1,0:T(2,128)} %param.21) | copy-start | bytes 61444
  76.8 206.1 %all-gather.11.cloned.1.call-start = ((), (), s32[]{:S(2)}) async-start(), calls=%async_computation.5 | async-start | bytes 3932160 | tf_op jit(solution)/shard_map/all_gather | solution.py:1404
  77.4 230.7 %all-gather.17.cloned.1.call-start = ((), (), s32[]{:S(2)}) async-start(), calls=%async_computation.12 | async-start | bytes 3932160 | tf_op jit(solution)/shard_map/all_gather | solution.py:1404
  81.1 303.7 %reduce-scatter.5.cloned.1.call-start = ((), (), s32[]{:S(2)}) async-start(), calls=%async_computation.6 | async-start | bytes 3932160 | tf_op jit(solution)/shard_map/reduce_scatter | solution.py:1454
  296.6 11.5 %copy-start.2 = (bf16[2048,768]{1,0:T(8,128)(2,1)}, bf16[2048,768]{1,0:T(8,128)(2,1)S(1)}, u32[]{:S(2)}) copy-start(bf16[2048,768]{1,0:T(8,128)(2,1)S(1)} %get-tuple-element.79.hidden) | copy-start | bytes 9437188
  308.2 206.2 %reduce-scatter.11.cloned.1.call-start = ((), (), s32[]{:S(2)}) async-start(), calls=%async_computation.9 | async-start | bytes 1966080 | tf_op jit(solution)/shard_map/reduce_scatter | solution.py:1454
  437.0 128.5 %reduce-scatter.9.cloned.1.call-start = ((), (), s32[]{:S(2)}) async-start(), calls=%async_computation.8 | async-start | bytes 3276800 | tf_op jit(solution)/shard_map/reduce_scatter | solution.py:1454
  513.6 164.7 %reduce-scatter.7.cloned.1.call-start = ((), (), s32[]{:S(2)}) async-start(), calls=%async_computation.7 | async-start | bytes 7864320 | tf_op jit(solution)/shard_map/reduce_scatter | solution.py:1454
  678.3 99.2 %copy-start.1 = (bf16[2048,768]{1,0:T(8,128)(2,1)S(1)}, bf16[2048,768]{1,0:T(8,128)(2,1)}, u32[]{:S(2)}) copy-start(bf16[2048,768]{1,0:T(8,128)(2,1)} %param.26) | copy-start | bytes 9437188
Sparse Core Ops, SparseCore 0:
  10.2 58.8 all-gather.12
  71.2 31.4 all-gather.14
  104.9 66.6 all-gather.8
  173.5 62.0 all-gather.10
  237.6 62.1 all-gather.16
  308.3 58.3 reduce-scatter.4
  437.1 32.8 reduce-scatter.10
  513.7 51.7 reduce-scatter.8
  567.8 110.4 reduce-scatter.6

commit v10 on v9

--- a/solution.py
+++ b/solution.py
@@ -1465,7 +1465,6 @@
     grad_down, grad_mid_own = lax.optimization_barrier((grad_down, grad_mid_own))
     grad_mlp_in = over_planes(grad_mlp_in)
     grad_mixed, grad_out, _ = spread_step(grad_mid_own, w_out, mixed)
-    grad_out = over_planes(grad_out)
 
     def by_owner(grad):
         return grad.reshape(members, own_rows, -1)
@@ -1474,6 +1473,8 @@
         planes, seg, grad_mixed, branches, states, decay, conv_low, mask, halo, cin, gate_blocks, vec, hidden, w_down, middle,
         by_owner(grad_down),
     )
+    grad_mlp_in, grad_out, grad_branches = lax.optimization_barrier((grad_mlp_in, grad_out, grad_branches))
+    grad_out = over_planes(grad_out)
     grad_in = tn(normed, grad_branches, BF16)
     grad_in, grad_branches = lax.optimization_barrier((grad_in, grad_branches))
     grad_in = over_planes(grad_in)

time: 788 us -> 644 us (0.82)
  waiting for transfers between devices: 147 us -> 0.72 us
    reduce_scatter x4, waiting for transfers between devices: 146 us -> 0.04 us  [over_planes(): return lax.psum_scatter(grad, 't', scatter_dimension=0, tiled=True)]
  transfers between devices with their start and end apart: 9 -> 9, of which waited for: 2 -> 0; matrix products, arithmetic and copies ran while one was open for 14% -> 18% of each run, Pallas kernels for 46% -> 76%
where the time goes in v10:
time: 644 us; the launch traced here: 640 us
  Pallas kernels  503 us (78%)
  matrix products  78.4 us (12%)
  local copies, waits for them, and re-layouts  37.9 us (6%)
  between operations  14.3 us (2%)
    pallas_call x1, Pallas kernels, middle_step(): pl.pallas_call(middle_kernel, name='middle_step', out_shape=(jax.ShapeDty...  85.2 us
    pallas_call x1, Pallas kernels, final_step(): pl.pallas_call(functools.partial(final_kernel, planes, with_gates), name=...  82 us
    pallas_call x1, Pallas kernels, mixer_backward(): pl.pallas_call(functools.partial(mixer_backward_kernel, count, seg), name...  67.5 us
    pallas_call x1, Pallas kernels, mixer_forward(): pl.pallas_call(functools.partial(mixer_forward_kernel, count, seg, rows_h...  59.7 us
    pallas_call x1, Pallas kernels, turn_step(): pl.pallas_call(turn_kernel, name='turn_step', out_shape=(jax.ShapeDtypeSt...  57.9 us
    dot_general x4, matrix products, nt(): lax.dot_general(left, right, (((1,), (1,)), ((), ())), preferred_element_...  55.6 us
    pallas_call x1, Pallas kernels, spread_step(): pl.pallas_call(spread_kernel, name='turn_spread', out_shape=(jax.ShapeDty...  52 us
    pallas_call x1, Pallas kernels, first_gather(): pl.pallas_call(functools.partial(first_gather_kernel, planes), name='firs...  45.6 us
  transfers between devices with their start and end apart: 9, of which 0 were waited for; matrix products, arithmetic and copies ran while one was open for 18% of the time, Pallas kernels for 76%

profile of v10, /device:TPU:0, one launch (start us, length us, event | category | flops | bytes accessed | tf_op | source)
XLA Modules:
  0.0 640.1 jit_solution(14470717800098461226)
XLA Ops:
  14.1 2.5 multiply_convert_fusion.3.normed
  16.6 45.6 %first_gather.1 = (bf16[2048,2048]{1,0:T(8,128)(2,1)}, f32[8,8,128]{2,1,0:T(8,128)}, f32[8,8,128]{2,1,0:T(8,128)}, f32[8,8,128]{2,1,0:T(8,128)}) custom-call(bf16[256,2048]{1,0:T(8,128)(2,1)} %multiply_convert_fusion.3.normed, f32[8,128]{1,0:T(8,128)} %pad.4.ids), custom_call_target="tpu_custom_call" | custom-call | tf_op jit(solution)/shard_map/first_gather/pallas_call | solution.py:1223
  62.2 5.8 constant_dynamic-slice_fusion.2
  68.1 6.1 copy.37
  74.1 2.7 fusion.2
  78.9 2.2 copy.38
  84.4 30.4 %swap.1 = bf16[2,4,80,2048]{3,2,1,0:T(8,128)(2,1)} custom-call(bf16[4,2,80,2048]{3,2,1,0:T(8,128)(2,1)} %bitcast.66), custom_call_target="tpu_custom_call" | custom-call | tf_op jit(solution)/shard_map/swap/pallas_call | solution.py:1341
  114.9 11.4 %fusion.3.branches_far = f32[2048,640]{1,0:T(8,128)} fusion(bf16[2048,2048]{1,0:T(8,128)(2,1)} %get-tuple-element.60, bf16[640,2048]{1,0:T(8,128)(2,1)} %bitcast.54), kind=kOutput, calls=%fused_computation.31 | convolution fusion | flops 5368709120 | bytes 16252928 | tf_op jit(solution)/shard_map/dot_general | solution.py:1357
  126.3 59.7 %mixer_forward.1 = (bf16[2048,320]{1,0:T(8,128)(2,1)}, f32[3,2048,128]{2,1,0:T(8,128)}, f32[2048,320]{1,0:T(8,128)}, bf16[2048,320]{1,0:T(8,128)(2,1)}, f32[128,...) custom-call(f32[2048,640]{1,0:T(8,128)} %fusion.3.branches_far, ...), custom_call_target="tpu_custom_call" | custom-call | tf_op jit(solution)/shard_map/mixer_forward/pallas_call | solution.py:427
  186.0 85.2 %middle_step.1 = (f32[256,2048]{1,0:T(8,128)}, bf16[2048,2048]{1,0:T(8,128)(2,1)}) custom-call(bf16[2048,320]{1,0:T(8,128)(2,1)} %get-tuple-element.66.left.mixed, bf16[320,2048]{1,0:T(8,128)(2,1)} %bitcast.57, bf16[256,2048]{1,0:T(8,128)(2,1)} %bitcast.52, f32[1,2048]{1,0:T(1,128)} %bitcast.76), custom_call_target="tpu_custom_call" | custom-call | tf_op jit(solution)/shard_map/middle_step/pallas_call | solution.py:1236
  271.2 11.8 %fusion.4 = f32[2048,768]{1,0:T(8,128)} fusion(bf16[2048,2048]{1,0:T(8,128)(2,1)} %get-tuple-element.68.normed_far, bf16[768,2048]{1,0:T(8,128)(2,1)} %bitcast.62), kind=kOutput, calls=%fused_computation.32 | convolution fusion | flops 6442450944 | bytes 17825792 | tf_op jit(solution)/shard_map/dot_general | solution.py:1357
  283.0 13.7 %multiply_convert_fusion.2 = (bf16[2048,768]{1,0:T(8,128)(2,1)S(1)}, f32[2048,768]{1,0:T(8,128)}) fusion(f32[2048,768]{1,0:T(8,128)} %fusion.4, bf16[2048,2048]{1,0:T(8,128)(2,1)} %get-tuple-element.68.normed_far, bf16[768,2048]{1,0:T(8,128)(2,1)} %bitcast.64), kind=kOutput, calls=%fused_computation.2 | convolution fusion | flops 6458179584 | bytes 27262976 | tf_op jit(solution)/shard_map/dot_general | solution.py:1357
  296.7 11.5 %convolution_convert_fusion = bf16[2048,768]{1,0:T(8,128)(2,1)} fusion(bf16[2048,2048]{1,0:T(8,128)(2,1)} %get-tuple-element.65, bf16[2048,768]{1,0:T(8,128)(2,1)S(1)} %get-tuple-element.82.hidden), kind=kOutput, calls=%fused_computation.6 | convolution fusion | flops 6444023808 | bytes 14680064 | tf_op jit(solution)/shard_map/dot_general | solution.py:1361
  308.3 18.7 %multiply_convert_fusion = (bf16[2048,768]{1,0:T(8,128)(2,1)}, bf16[2048,768]{1,0:T(8,128)(2,1)}) fusion(f32[2048,768]{1,0:T(8,128)} %fusion.4, f32[2048,768]{1,0:T(8,128)} %get-tuple-element.146, bf16[2048,2048]{1,0:T(8,128)(2,1)} %get-tuple-element.65, bf16[768,2048]{1,0:T(8,128)(2,1)} %all-gather.17.cloned.1.call-done.w_down), kind=kOutput, calls=%fused_computation | convolution fusion | flops 6477053952 | bytes 30408704 | tf_op jit(solution)/shard_map/dot_general | solution.py:1357
  326.9 57.9 %turn_step.1 = (f32[256,2048]{1,0:T(8,128)}, f32[8,2048]{1,0:T(8,128)}, bf16[2048,1536]{1,0:T(8,128)(2,1)}, bf16[256,2048]{1,0:T(8,128)(2,1)}) custom-call(bf16[2048,768]{1,0:T(8,128)(2,1)} %get-tuple-element.134.left0, bf16[2048,768]{1,0:T(8,128)(2,1)} %get-tuple-element.133.left1, bf16[768,2048]{1,0:T(8,128)(2,1)} %bitcast.63, bf16[768,2048]{1,0:T(8,128)(2,1)} %bitcast.65, ...), custom_call_target="tpu_custom_call" | custom-call | tf_op jit(solution)/shard_map/turn_step/pallas_call | solution.py:1249
  385.0 52.0 %turn_spread.1 = (f32[2048,320]{1,0:T(8,128)}, bf16[2048,320]{1,0:T(8,128)(2,1)}, bf16[2048,2048]{1,0:T(8,128)(2,1)}) custom-call(bf16[256,2048]{1,0:T(8,128)(2,1)} %get-tuple-element.74.block, bf16[320,2048]{1,0:T(8,128)(2,1)} %bitcast.58, bf16[2048,320]{1,0:T(8,128)(2,1)} %get-tuple-element.66.left.mixed), custom_call_target="tpu_custom_call" | custom-call | tf_op jit(solution)/shard_map/turn_spread/pallas_call | solution.py:1268
  437.0 67.5 %mixer_backward.1 = (bf16[2048,640]{1,0:T(8,128)(2,1)}, f32[320,320]{1,0:T(8,128)}, f32[320,320]{1,0:T(8,128)}, f32[8,320]{1,0:T(8,128)}, bf16[4,336,128]{2,1,0:...) custom-call(f32[2048,320]{1,0:T(8,128)} %get-tuple-element.75.grad_mixed_far, ...), custom_call_target="tpu_custom_call" | custom-call | tf_op jit(solution)/shard_map/mixer_backward/pallas_call | solution.py:467
  504.6 11.3 %convolution_convert_fusion.1 = bf16[2048,640]{1,0:T(8,128)(2,1)} fusion(bf16[2048,2048]{1,0:T(8,128)(2,1)} %get-tuple-element.60, bf16[2048,640]{1,0:T(8,128)(2,1)} %get-tuple-element.89.left), kind=kOutput, calls=%fused_computation.7 | convolution fusion | flops 5370019840 | bytes 13631488 | tf_op jit(solution)/shard_map/dot_general | solution.py:1361
  515.9 82.0 %final_step.1 = (f32[256,2048]{1,0:T(8,128)}, f32[32,128]{1,0:T(8,128)}, f32[336,128]{1,0:T(8,128)}, bf16[8,64,1536]{2,1,0:T(8,128)(2,1)}) custom-call(bf16[2048,640]{1,0:T(8,128)(2,1)} %get-tuple-element.89.left, bf16[640,2048]{1,0:T(8,128)(2,1)} %bitcast.55, bf16[256,2048]{1,0:T(8,128)(2,1)} %bitcast.53, f32[1,2048]{1,0:T(1,128)} %bitcast.78, ...), custom_call_target="tpu_custom_call" | custom-call | tf_op jit(solution)/shard_map/final_step/pallas_call | solution.py:1133
  602.9 4.9 place_columns.3
  609.7 15.4 %owners_step.1 = (bf16[8,64,640]{2,1,0:T(8,128)(2,1)}, bf16[8,64,320]{2,1,0:T(8,128)(2,1)}) custom-call(bf16[8,64,640]{2,1,0:T(8,128)(2,1)} %bitcast.74, bf16[8,64,320]{2,1,0:T(8,128)(2,1)} %bitcast.75), custom_call_target="tpu_custom_call" | custom-call | tf_op jit(solution)/shard_map/owners_step/pallas_call | solution.py:1174
  625.0 2.9 place_columns.2
  627.9 2.3 copy.43
  630.2 3.1 copy.44
  (66 shorter events, 19.2 us)
Async XLA Ops:
  7.2 70.3 %copy-start = (bf16[2048,768]{1,0:T(8,128)(2,1)S(1)}, bf16[2048,768]{1,0:T(8,128)(2,1)}, u32[]{:S(2)}) copy-start(bf16[2048,768]{1,0:T(8,128)(2,1)} %param.26) | copy-start | bytes 9437188
  7.2 77.2 %all-gather.13.cloned.1.call-start = ((), (), s32[]{:S(2)}) async-start(), calls=%async_computation.10 | async-start | bytes 3276800 | tf_op jit(solution)/shard_map/all_gather | solution.py:1404
  9.4 116.9 %all-gather.15.cloned.1.call-start = ((), (), s32[]{:S(2)}) async-start(), calls=%async_computation.11 | async-start | bytes 1638400 | tf_op jit(solution)/shard_map/all_gather | solution.py:1404
  11.2 259.9 %all-gather.9.cloned.1.call-start = ((), (), s32[]{:S(2)}) async-start(), calls=%async_computation.4 | async-start | bytes 3932160 | tf_op jit(solution)/shard_map/all_gather | solution.py:1404
  68.0 15.5 %copy-start.5 = (f32[2560]{0:T(1024)S(1)}, f32[2560]{0:T(1024)}, u32[]{:S(2)}) copy-start(f32[2560]{0:T(1024)} %param.19) | copy-start | bytes 30724
  68.0 15.5 %copy-start.6 = (f32[2560]{0:T(1024)S(1)}, f32[2560]{0:T(1024)}, u32[]{:S(2)}) copy-start(f32[2560]{0:T(1024)} %param.22) | copy-start | bytes 30724
  68.1 15.6 %copy-start.3 = (f32[4,2560]{1,0:T(4,128)S(1)}, f32[4,2560]{1,0:T(4,128)}, u32[]{:S(2)}) copy-start(f32[4,2560]{1,0:T(4,128)} %param.18) | copy-start | bytes 122884
  68.1 15.6 %copy-start.4 = (f32[2,2560]{1,0:T(2,128)S(1)}, f32[2,2560]{1,0:T(2,128)}, u32[]{:S(2)}) copy-start(f32[2,2560]{1,0:T(2,128)} %param.21) | copy-start | bytes 61444
  76.8 206.1 %all-gather.11.cloned.1.call-start = ((), (), s32[]{:S(2)}) async-start(), calls=%async_computation.5 | async-start | bytes 3932160 | tf_op jit(solution)/shard_map/all_gather | solution.py:1404
  77.4 230.8 %all-gather.17.cloned.1.call-start = ((), (), s32[]{:S(2)}) async-start(), calls=%async_computation.12 | async-start | bytes 3932160 | tf_op jit(solution)/shard_map/all_gather | solution.py:1404
  81.1 303.9 %reduce-scatter.5.cloned.1.call-start = ((), (), s32[]{:S(2)}) async-start(), calls=%async_computation.6 | async-start | bytes 3932160 | tf_op jit(solution)/shard_map/reduce_scatter | solution.py:1454
  296.7 11.5 %copy-start.2 = (bf16[2048,768]{1,0:T(8,128)(2,1)}, bf16[2048,768]{1,0:T(8,128)(2,1)S(1)}, u32[]{:S(2)}) copy-start(bf16[2048,768]{1,0:T(8,128)(2,1)S(1)} %get-tuple-element.82.hidden) | copy-start | bytes 9437188
  308.2 196.3 %reduce-scatter.7.cloned.1.call-start = ((), (), s32[]{:S(2)}) async-start(), calls=%async_computation.7 | async-start | bytes 7864320 | tf_op jit(solution)/shard_map/reduce_scatter | solution.py:1454
  384.9 224.8 %reduce-scatter.11.cloned.1.call-start = ((), (), s32[]{:S(2)}) async-start(), calls=%async_computation.9 | async-start | bytes 1966080 | tf_op jit(solution)/shard_map/reduce_scatter | solution.py:1454
  504.6 105.1 %reduce-scatter.9.cloned.1.call-start = ((), (), s32[]{:S(2)}) async-start(), calls=%async_computation.8 | async-start | bytes 3276800 | tf_op jit(solution)/shard_map/reduce_scatter | solution.py:1454
  515.9 117.5 %copy-start.1 = (bf16[2048,768]{1,0:T(8,128)(2,1)S(1)}, bf16[2048,768]{1,0:T(8,128)(2,1)}, u32[]{:S(2)}) copy-start(bf16[2048,768]{1,0:T(8,128)(2,1)} %param.26) | copy-start | bytes 9437188
Sparse Core Ops, SparseCore 0:
  10.2 58.8 all-gather.12
  71.2 31.4 all-gather.14
  104.9 66.6 all-gather.8
  173.5 62.0 all-gather.10
  237.6 62.1 all-gather.16
  308.4 58.3 reduce-scatter.4
  385.0 109.7 reduce-scatter.6
  504.7 35.1 reduce-scatter.10
  542.2 57.5 reduce-scatter.8

commit v11 on v10

--- a/solution.py
+++ b/solution.py
@@ -1037,68 +1037,68 @@
             copy.wait_send()
 
 
-def sum_everywhere(place, count, values, inbox, plane_sum, plane_box, send, recv):
-    me = lax.axis_index("t")
-    own = place.chunk(0, 0, 0)
-    moved = []
-
-    def copy(number, source, target, peer):
+class SmallSum:
+    def __init__(self, place, count, values, inbox, plane_sum, plane_box, send, recv):
+        self.place, self.count, self.values, self.inbox = place, count, values, inbox
+        self.plane_sum, self.plane_box, self.send, self.recv = plane_sum, plane_box, send, recv
+        self.me = lax.axis_index("t")
+        self.moved = []
+
+    def copy(self, number, source, target, peer):
         return pltpu.make_async_remote_copy(
             src_ref=source,
             dst_ref=target,
-            send_sem=send.at[number],
-            recv_sem=recv.at[number],
+            send_sem=self.send.at[number],
+            recv_sem=self.recv.at[number],
             device_id=peer,
             device_id_type=MESH,
         )
 
-    for number, offset in enumerate(OTHERS):
-        moved.append(copy(number, values, inbox.at[own], place.peer(*offset)))
-        moved[-1].start()
-    inbox[own] = values[...]
-    for number, offset in enumerate(OTHERS):
-        copy(number, values, inbox.at[place.chunk(*offset)], place.peer(*offset)).wait_recv()
-    total = inbox[0]
-    for n in range(1, 8):
-        total = total + inbox[n]
-    plane_sum[...] = total
-    for step in range(1, count):
-        moved.append(copy(6 + step, plane_sum, plane_box.at[me], {"t": lax.rem(me + step, count)}))
-        moved[-1].start()
-    plane_box[me] = total
-    for step in range(1, count):
-        other = lax.rem(me + count - step, count)
-        copy(6 + step, plane_sum, plane_box.at[other], {"t": other}).wait_recv()
-    total = plane_box[0]
-    for z in range(1, count):
-        total = total + plane_box[z]
-    for sent in moved:
-        sent.wait_send()
-    return total
+    def begin(self):
+        own = self.place.chunk(0, 0, 0)
+        for number, offset in enumerate(OTHERS):
+            self.moved.append(self.copy(number, self.values, self.inbox.at[own], self.place.peer(*offset)))
+            self.moved[-1].start()
+        self.inbox[own] = self.values[...]
+
+    def pass_on(self):
+        for number, offset in enumerate(OTHERS):
+            slot = self.inbox.at[self.place.chunk(*offset)]
+            self.copy(number, self.values, slot, self.place.peer(*offset)).wait_recv()
+        total = self.inbox[0]
+        for n in range(1, 8):
+            total = total + self.inbox[n]
+        self.plane_sum[...] = total
+        self.plane_box[self.me] = total
+        for step in range(1, self.count):
+            to = {"t": lax.rem(self.me + step, self.count)}
+            self.moved.append(self.copy(6 + step, self.plane_sum, self.plane_box.at[self.me], to))
+            self.moved[-1].start()
+
+    def finish(self, out):
+        for step in range(1, self.count):
+            other = lax.rem(self.me + self.count - step, self.count)
+            self.copy(6 + step, self.plane_sum, self.plane_box.at[other], {"t": other}).wait_recv()
+        total = self.plane_box[0]
+        for z in range(1, self.count):
+            total = total + self.plane_box[z]
+        out[...] = total
+        for sent in self.moved:
+            sent.wait_send()
 
 
 def final_kernel(
-    count, with_gates, left, right, own_in, gain, mlp_gains, pieces, grad_middle, reduced,
-    grad_out, gains_out, gates_out, owned,
-    gain_sum, values, inbox, plane_sum, plane_box, sum_send, sum_recv, rows_recv, gates_all, gates_send, gates_recv,
-    own_send, own_recv, *buffers,
+    left, right, own_in, gain, mlp_gains, grad_middle, reduced, grad_out, values_out, owned,
+    gain_sum, own_send, own_recv, *buffers,
 ):
     tokens, width = own_in.shape
     place = Place()
-    me = lax.axis_index("t")
-    place.greet([place.peer(*offset) for offset in BEYOND] + [{"t": lax.rem(me + step, count)} for step in range(1, count)])
+    place.greet([place.peer(*offset) for offset in BEYOND])
     scatter = Scatter(place, pair_product([left], [right], tokens), *buffers)
     owners = Owners(place, reduced, owned, own_send, own_recv)
-    gates = GateSums(place, count, pieces, rows_recv, gates_all, gates_send, gates_recv)
     scatter.run_first()
-    if with_gates:
-        gates.begin()
     owners.begin()
     scatter.run_second()
-    if with_gates:
-        gates.pass_on()
-    scatter.run_third(0)
-    scatter.run_third(1)
     gain_sum[...] = jnp.zeros_like(gain_sum)
 
     def body(at):
@@ -1111,42 +1111,79 @@
         term = grad * x * scale
         gain_sum[...] += term[0:8] + term[8:16]
 
-    for_slices(0, tokens, body)
+    for part in (0, 1):
+        scatter.run_third(part)
+        for_slices(part * tokens // 2, (part + 1) * tokens // 2, body)
     lines = width // LANES
     for base, row in ((0, jnp.sum(mlp_gains[...], axis=0, keepdims=True)), (lines, jnp.sum(gain_sum[...], axis=0, keepdims=True))):
         for n in range(lines):
-            values[base + n : base + n + 1, :] = row[:, n * LANES : (n + 1) * LANES]
-    gains_out[...] = sum_everywhere(place, count, values, inbox, plane_sum, plane_box, sum_send, sum_recv)
+            values_out[base + n : base + n + 1, :] = row[:, n * LANES : (n + 1) * LANES]
+    owners.finish()
+    scatter.finish()
+
+
+def final_step(left, right, own_in, gain, mlp_gains, grad_middle, reduced):
+    tokens, width = own_in.shape
+    return pl.pallas_call(
+        final_kernel,
+        name="final_step",
+        out_shape=(
+            jax.ShapeDtypeStruct((tokens, width), F32),
+            jax.ShapeDtypeStruct((2 * width // LANES, LANES), F32),
+            jax.ShapeDtypeStruct(reduced.shape, reduced.dtype),
+        ),
+        in_specs=[*whole(6), ANYWHERE],
+        out_specs=(*whole(2), ANYWHERE),
+        scratch_shapes=[pltpu.VMEM((8, width), F32), *OWNERS_SCRATCH, *Scatter.scratch(tokens, width)],
+        compiler_params=mixer_params(7),
+    )(left, right, own_in, gain[None], mlp_gains, grad_middle, reduced)
+
+
+def owners_kernel(
+    count, with_gates, pieces, values, reduced0, reduced1, gates_out, gains_out, out0, out1,
+    inbox, plane_sum, plane_box, sum_send, sum_recv, rows_recv, gates_all, gates_send, gates_recv,
+    send0, recv0, send1, recv1,
+):
+    place = Place()
+    me = lax.axis_index("t")
+    place.greet([place.peer(*offset) for offset in BEYOND] + [{"t": lax.rem(me + step, count)} for step in range(1, count)])
+    owners = [Owners(place, reduced0, out0, send0, recv0), Owners(place, reduced1, out1, send1, recv1)]
+    gates = GateSums(place, count, pieces, rows_recv, gates_all, gates_send, gates_recv)
+    gains = SmallSum(place, count, values, inbox, plane_sum, plane_box, sum_send, sum_recv)
+    gains.begin()
+    if with_gates:
+        gates.begin()
+    for part in owners:
+        part.begin()
+    gains.pass_on()
+    if with_gates:
+        gates.pass_on()
+    gains.finish(gains_out)
     if with_gates:
         gates.finish(gates_out)
     else:
         gates_out[...] = jnp.zeros_like(gates_out)
-    owners.finish()
-    scatter.finish()
-
-
-def final_step(planes, with_gates, left, right, own_in, gain, mlp_gains, pieces, grad_middle, reduced):
-    tokens, width = own_in.shape
-    block = pieces.shape[1:] if with_gates else (16, LANES)
+    for part in owners:
+        part.finish()
+
+
+def owners_step(planes, with_gates, pieces, values, reduced):
+    block = pieces.shape[1:]
     slots = planes if with_gates else 1
-    sums = (2 * width // LANES, LANES)
     return pl.pallas_call(
-        functools.partial(final_kernel, planes, with_gates),
-        name="final_step",
+        functools.partial(owners_kernel, planes, with_gates),
+        name="owners_step",
         out_shape=(
-            jax.ShapeDtypeStruct((tokens, width), F32),
-            jax.ShapeDtypeStruct(sums, F32),
             jax.ShapeDtypeStruct(block, F32),
-            jax.ShapeDtypeStruct(reduced.shape, reduced.dtype),
+            jax.ShapeDtypeStruct(values.shape, F32),
+            *[jax.ShapeDtypeStruct(part.shape, part.dtype) for part in reduced],
         ),
-        in_specs=[*whole(7), ANYWHERE],
-        out_specs=(*whole(3), ANYWHERE),
+        in_specs=[*whole(2), ANYWHERE, ANYWHERE],
+        out_specs=(*whole(2), ANYWHERE, ANYWHERE),
         scratch_shapes=[
-            pltpu.VMEM((8, width), F32),
-            pltpu.VMEM(sums, F32),
-            pltpu.VMEM((8, *sums), F32),
-            pltpu.VMEM(sums, F32),
-            pltpu.VMEM((planes, *sums), F32),
+            pltpu.VMEM((8, *values.shape), F32),
+            pltpu.VMEM(values.shape, F32),
+            pltpu.VMEM((planes, *values.shape), F32),
             pltpu.SemaphoreType.DMA((planes + 6,)),
             pltpu.SemaphoreType.DMA((planes + 6,)),
             pltpu.VMEM((slots, *block), BF16),
@@ -1154,36 +1191,18 @@
             pltpu.SemaphoreType.DMA((planes + 2,)),
             pltpu.SemaphoreType.DMA((planes + 2,)),
             *OWNERS_SCRATCH,
-            *Scatter.scratch(tokens, width),
+            *OWNERS_SCRATCH,
         ],
-        compiler_params=mixer_params(7),
-    )(left, right, own_in, gain[None], mlp_gains, pieces, grad_middle, reduced)
-
-
-def owners_kernel(reduced0, reduced1, out0, out1, send0, recv0, send1, recv1):
-    place = Place()
-    place.greet([place.peer(*offset) for offset in BEYOND])
-    owners = [Owners(place, reduced0, out0, send0, recv0), Owners(place, reduced1, out1, send1, recv1)]
-    for part in owners:
-        part.begin()
-    for part in owners:
-        part.finish()
-
-
-def owners_step(reduced):
-    return pl.pallas_call(
-        owners_kernel,
-        name="owners_step",
-        out_shape=tuple(jax.ShapeDtypeStruct(part.shape, part.dtype) for part in reduced),
-        in_specs=[ANYWHERE] * 2,
-        out_specs=(ANYWHERE,) * 2,
-        scratch_shapes=[*OWNERS_SCRATCH, *OWNERS_SCRATCH],
         compiler_params=mixer_params(8),
-    )(*reduced)
-
-
-def place_kernel(planes, hidden, outs, *refs):
-    given, results = refs[: -len(outs)], refs[-len(outs) :]
+    )(pieces, values, *reduced)
+
+
+def place_kernel(planes, hidden, outs, through, *refs):
+    count = len(outs)
+    given, passed, results, copied = refs[:count], refs[count : count + through], refs[count + through : 2 * count + through], refs[2 * count + through :]
+    copies = [pltpu.make_async_copy(passed[n], copied[n], copied[-1].at[n]) for n in range(through)]
+    for copy in copies:
+        copy.start()
     for count, sources, out in zip(outs, given, results):
         piece = sources.shape[2] // (count * (planes if hidden else 1))
         for k in range(count):
@@ -1201,20 +1220,26 @@
                     out[:, k, start : start + row.shape[1]] = row
                 else:
                     out[:, start : start + row.shape[1]] = row
-
-
-def place_columns(planes, hidden, outs, *owned):
+    for copy in copies:
+        copy.wait()
+
+
+def place_columns(planes, hidden, outs, owned, through=()):
     members, own_rows, columns = owned[0].shape
     total = columns * members // outs[0]
     shapes = [(own_rows, count, total) if count > 1 else (own_rows, total) for count in outs]
     return pl.pallas_call(
-        functools.partial(place_kernel, planes, hidden, outs),
+        functools.partial(place_kernel, planes, hidden, outs, len(through)),
         name="place_columns",
-        out_shape=tuple(jax.ShapeDtypeStruct(shape, F32) for shape in shapes),
-        in_specs=whole(len(owned)),
-        out_specs=tuple(whole(len(outs))),
+        out_shape=(
+            *[jax.ShapeDtypeStruct(shape, F32) for shape in shapes],
+            *[jax.ShapeDtypeStruct(part.shape, part.dtype) for part in through],
+        ),
+        in_specs=[*whole(len(owned)), *[ANYWHERE] * len(through)],
+        out_specs=(*whole(len(outs)), *[ANYWHERE] * len(through)),
+        scratch_shapes=[pltpu.SemaphoreType.DMA((len(through),))] if through else [],
         compiler_params=pltpu.CompilerParams(vmem_limit_bytes=60 * 1024 * 1024),
-    )(*owned)
+    )(*owned, *through)
 
 
 def first_gather(planes, normed, ids):
@@ -1473,35 +1498,35 @@
         planes, seg, grad_mixed, branches, states, decay, conv_low, mask, halo, cin, gate_blocks, vec, hidden, w_down, middle,
         by_owner(grad_down),
     )
-    grad_mlp_in, grad_out, grad_branches = lax.optimization_barrier((grad_mlp_in, grad_out, grad_branches))
+    grad_mlp_in, grad_branches = lax.optimization_barrier((grad_mlp_in, grad_branches))
     grad_out = over_planes(grad_out)
     grad_in = tn(normed, grad_branches, BF16)
     grad_in, grad_branches = lax.optimization_barrier((grad_in, grad_branches))
     grad_in = over_planes(grad_in)
     outputs = outputs.reshape(inputs.shape)
 
-    grad_inputs, gains, gate_grads, owned_mlp_in = final_step(
-        planes, direct, grad_branches, in_w, own_in, mix_gain, grad_mlp_gain, pieces, grad_middle,
-        by_owner(grad_mlp_in),
+    grad_inputs, values, owned_mlp_in = final_step(
+        grad_branches, in_w, own_in, mix_gain, grad_mlp_gain, grad_middle, by_owner(grad_mlp_in)
     )
+    gate_grads, gains, owned_in, owned_out = owners_step(planes, direct, pieces, values, [by_owner(grad_in), by_owner(grad_out)])
     grad_inputs = grad_inputs.reshape(inputs.shape)
     index = ((t * 2 + i) * row_groups + r) * own_rows
     gains = lax.dynamic_slice_in_dim(gains.reshape(2, width), index, own_rows, 1)
 
 
-    owned_in, owned_out = owners_step([by_owner(grad_in), by_owner(grad_out)])
-
-    def columns(hidden, outs, *owned):
+    def columns(hidden, outs, owned, through=()):
         if direct:
-            return place_columns(planes, hidden, outs, *owned)
+            return place_columns(planes, hidden, outs, owned, through)
         owned = jnp.concatenate(owned, axis=2)
         owned = owned.reshape(2, row_groups, own_rows, sum(outs), planes if hidden else 1, -1).astype(F32)
         order = (2, 3, 4, 0, 1, 5) if hidden else (2, 3, 1, 0, 4, 5)
         owned = owned.transpose(order).reshape(own_rows, sum(outs), -1)
-        return (owned[:, :2], owned[:, 2])
-
-    grad_in_weight, grad_out_weight = columns(False, (2, 1), owned_in, owned_out)
-    grad_mlp_in, grad_down_weight = columns(True, (2, 1), owned_mlp_in, owned_down)
+        return (owned[:, :2], owned[:, 2], *through)
+
+    grad_in_weight, grad_out_weight = columns(False, (2, 1), [owned_in, owned_out])
+    grad_mlp_in, grad_down_weight, outputs, grad_inputs = columns(
+        True, (2, 1), [owned_mlp_in, owned_down], [outputs, grad_inputs]
+    )
     if direct:
         gate_grads = gate_grads[:, :part]
     else:

time: 644 us -> 727 us (1.13)
  Pallas kernels: 503 us -> 592 us
    pallas_call x4, Pallas kernels: 105 us -> 193 us  [the longest x2 103 us: place_columns(): pl.pallas_call(functools.partial(place_kernel, planes, hidden, outs, len(...]
    unnamed x20 -> x18, local copies, waits for them, and re-layouts: 15.2 us -> 9.81 us
  transfers between devices with their start and end apart: 9 -> 9, of which waited for: 0 -> 0; matrix products, arithmetic and copies ran while one was open for 18% -> 15% of each run, Pallas kernels for 76% -> 78%
where the time goes in v11:
time: 727 us; the launch traced here: 723 us
  Pallas kernels  592 us (81%)
  matrix products  78.2 us (11%)
  local copies, waits for them, and re-layouts  32.5 us (4%)
  between operations  14.4 us (2%)
    pallas_call x2, Pallas kernels, place_columns(): pl.pallas_call(functools.partial(place_kernel, planes, hidden, outs, len(...  103 us
    pallas_call x1, Pallas kernels, middle_step(): pl.pallas_call(middle_kernel, name='middle_step', out_shape=(jax.ShapeDty...  85.2 us
    pallas_call x1, Pallas kernels, mixer_backward(): pl.pallas_call(functools.partial(mixer_backward_kernel, count, seg), name...  67.8 us
    pallas_call x1, Pallas kernels, final_step(): pl.pallas_call(final_kernel, name='final_step', out_shape=(jax.ShapeDtype...  67.3 us
    pallas_call x1, Pallas kernels, mixer_forward(): pl.pallas_call(functools.partial(mixer_forward_kernel, count, seg, rows_h...  59.6 us
    pallas_call x1, Pallas kernels, turn_step(): pl.pallas_call(turn_kernel, name='turn_step', out_shape=(jax.ShapeDtypeSt...  57.9 us
    dot_general x4, matrix products, nt(): lax.dot_general(left, right, (((1,), (1,)), ((), ())), preferred_element_...  55.6 us
    pallas_call x1, Pallas kernels, spread_step(): pl.pallas_call(spread_kernel, name='turn_spread', out_shape=(jax.ShapeDty...  52 us
  transfers between devices with their start and end apart: 9, of which 0 were waited for; matrix products, arithmetic and copies ran while one was open for 15% of the time, Pallas kernels for 78%

profile of v11, /device:TPU:0, one launch (start us, length us, event | category | flops | bytes accessed | tf_op | source)
XLA Modules:
  0.0 722.9 jit_solution(13714857008319688768)
XLA Ops:
  7.2 2.1 dynamic-slice_bitcast_fusion
  9.5 1.7 dynamic-slice_bitcast_fusion.1
  14.1 2.5 multiply_convert_fusion.3.normed
  16.6 45.6 %first_gather.1 = (bf16[2048,2048]{1,0:T(8,128)(2,1)}, f32[8,8,128]{2,1,0:T(8,128)}, f32[8,8,128]{2,1,0:T(8,128)}, f32[8,8,128]{2,1,0:T(8,128)}) custom-call(bf16[256,2048]{1,0:T(8,128)(2,1)} %multiply_convert_fusion.3.normed, f32[8,128]{1,0:T(8,128)} %pad.4.ids), custom_call_target="tpu_custom_call" | custom-call | tf_op jit(solution)/shard_map/first_gather/pallas_call | solution.py:1248
  62.2 5.8 constant_dynamic-slice_fusion.2
  68.1 6.1 copy.37
  74.1 2.7 fusion.2
  78.9 2.2 copy.38
  84.4 30.4 %swap.1 = bf16[2,4,80,2048]{3,2,1,0:T(8,128)(2,1)} custom-call(bf16[4,2,80,2048]{3,2,1,0:T(8,128)(2,1)} %bitcast.66), custom_call_target="tpu_custom_call" | custom-call | tf_op jit(solution)/shard_map/swap/pallas_call | solution.py:1366
  114.9 11.4 %fusion.3.branches_far = f32[2048,640]{1,0:T(8,128)} fusion(bf16[2048,2048]{1,0:T(8,128)(2,1)} %get-tuple-element.62, bf16[640,2048]{1,0:T(8,128)(2,1)} %bitcast.54), kind=kOutput, calls=%fused_computation.31 | convolution fusion | flops 5368709120 | bytes 16252928 | tf_op jit(solution)/shard_map/dot_general | solution.py:1382
  126.3 59.6 %mixer_forward.1 = (bf16[2048,320]{1,0:T(8,128)(2,1)}, f32[3,2048,128]{2,1,0:T(8,128)}, f32[2048,320]{1,0:T(8,128)}, bf16[2048,320]{1,0:T(8,128)(2,1)}, f32[128,...) custom-call(f32[2048,640]{1,0:T(8,128)} %fusion.3.branches_far, ...), custom_call_target="tpu_custom_call" | custom-call | tf_op jit(solution)/shard_map/mixer_forward/pallas_call | solution.py:427
  186.0 85.2 %middle_step.1 = (f32[256,2048]{1,0:T(8,128)}, bf16[2048,2048]{1,0:T(8,128)(2,1)}) custom-call(bf16[2048,320]{1,0:T(8,128)(2,1)} %get-tuple-element.68.left.mixed, bf16[320,2048]{1,0:T(8,128)(2,1)} %bitcast.57, bf16[256,2048]{1,0:T(8,128)(2,1)} %bitcast.52, f32[1,2048]{1,0:T(1,128)} %bitcast.76), custom_call_target="tpu_custom_call" | custom-call | tf_op jit(solution)/shard_map/middle_step/pallas_call | solution.py:1261
  271.2 11.8 %fusion.4 = f32[2048,768]{1,0:T(8,128)} fusion(bf16[2048,2048]{1,0:T(8,128)(2,1)} %get-tuple-element.70.normed_far, bf16[768,2048]{1,0:T(8,128)(2,1)} %bitcast.62), kind=kOutput, calls=%fused_computation.32 | convolution fusion | flops 6442450944 | bytes 17825792 | tf_op jit(solution)/shard_map/dot_general | solution.py:1382
  283.0 13.7 %multiply_convert_fusion.2 = (bf16[2048,768]{1,0:T(8,128)(2,1)S(1)}, f32[2048,768]{1,0:T(8,128)}) fusion(f32[2048,768]{1,0:T(8,128)} %fusion.4, bf16[2048,2048]{1,0:T(8,128)(2,1)} %get-tuple-element.70.normed_far, bf16[768,2048]{1,0:T(8,128)(2,1)} %bitcast.64), kind=kOutput, calls=%fused_computation.2 | convolution fusion | flops 6458179584 | bytes 27262976 | tf_op jit(solution)/shard_map/dot_general | solution.py:1382
  296.7 11.5 %convolution_convert_fusion = bf16[2048,768]{1,0:T(8,128)(2,1)} fusion(bf16[2048,2048]{1,0:T(8,128)(2,1)} %get-tuple-element.67, bf16[2048,768]{1,0:T(8,128)(2,1)S(1)} %get-tuple-element.85.hidden), kind=kOutput, calls=%fused_computation.6 | convolution fusion | flops 6444023808 | bytes 14680064 | tf_op jit(solution)/shard_map/dot_general | solution.py:1386
  308.3 18.7 %multiply_convert_fusion = (bf16[2048,768]{1,0:T(8,128)(2,1)}, bf16[2048,768]{1,0:T(8,128)(2,1)}) fusion(f32[2048,768]{1,0:T(8,128)} %fusion.4, f32[2048,768]{1,0:T(8,128)} %get-tuple-element.150, bf16[2048,2048]{1,0:T(8,128)(2,1)} %get-tuple-element.67, bf16[768,2048]{1,0:T(8,128)(2,1)} %all-gather.17.cloned.1.call-done.w_down), kind=kOutput, calls=%fused_computation | convolution fusion | flops 6477053952 | bytes 30408704 | tf_op jit(solution)/shard_map/dot_general | solution.py:1382
  326.9 57.9 %turn_step.1 = (f32[256,2048]{1,0:T(8,128)}, f32[8,2048]{1,0:T(8,128)}, bf16[2048,1536]{1,0:T(8,128)(2,1)}, bf16[256,2048]{1,0:T(8,128)(2,1)}) custom-call(bf16[2048,768]{1,0:T(8,128)(2,1)} %get-tuple-element.138.left0, bf16[2048,768]{1,0:T(8,128)(2,1)} %get-tuple-element.137.left1, bf16[768,2048]{1,0:T(8,128)(2,1)} %bitcast.63, bf16[768,2048]{1,0:T(8,128)(2,1)} %bitcast.65, ...), custom_call_target="tpu_custom_call" | custom-call | tf_op jit(solution)/shard_map/turn_step/pallas_call | solution.py:1274
  385.0 52.0 %turn_spread.1 = (f32[2048,320]{1,0:T(8,128)}, bf16[2048,320]{1,0:T(8,128)(2,1)}, bf16[2048,2048]{1,0:T(8,128)(2,1)}) custom-call(bf16[256,2048]{1,0:T(8,128)(2,1)} %get-tuple-element.77.block, bf16[320,2048]{1,0:T(8,128)(2,1)} %bitcast.58, bf16[2048,320]{1,0:T(8,128)(2,1)} %get-tuple-element.68.left.mixed), custom_call_target="tpu_custom_call" | custom-call | tf_op jit(solution)/shard_map/turn_spread/pallas_call | solution.py:1293
  437.1 67.8 %mixer_backward.1 = (bf16[2048,640]{1,0:T(8,128)(2,1)}, f32[320,320]{1,0:T(8,128)}, f32[320,320]{1,0:T(8,128)}, f32[8,320]{1,0:T(8,128)}, bf16[4,336,128]{2,1,0:...) custom-call(f32[2048,320]{1,0:T(8,128)} %get-tuple-element.78.grad_mixed_far, ...), custom_call_target="tpu_custom_call" | custom-call | tf_op jit(solution)/shard_map/mixer_backward/pallas_call | solution.py:467
  504.9 11.1 %convolution_convert_fusion.1 = bf16[2048,640]{1,0:T(8,128)(2,1)} fusion(bf16[2048,2048]{1,0:T(8,128)(2,1)} %get-tuple-element.62, bf16[2048,640]{1,0:T(8,128)(2,1)} %get-tuple-element.89.left), kind=kOutput, calls=%fused_computation.7 | convolution fusion | flops 5370019840 | bytes 13631488 | tf_op jit(solution)/shard_map/dot_general | solution.py:1386
  516.1 67.3 %final_step.1 = (f32[256,2048]{1,0:T(8,128)}, f32[32,128]{1,0:T(8,128)}, bf16[8,64,1536]{2,1,0:T(8,128)(2,1)}) custom-call(bf16[2048,640]{1,0:T(8,128)(2,1)} %get-tuple-element.89.left, bf16[640,2048]{1,0:T(8,128)(2,1)} %bitcast.55, bf16[256,2048]{1,0:T(8,128)(2,1)} %bitcast.53, f32[1,2048]{1,0:T(1,128)} %bitcast.78, f32[8,2048]{1,0:T(8,128)} %get-tuple-element.90.mlp_gains, ...), custom_call_target="tpu_custom_call" | custom-call | tf_op jit(solution)/shard_map/final_step/pallas_call | solution.py:1127
  583.4 100.2 %place_columns.2 = (f32[64,2,6144]{2,1,0:T(2,128)}, f32[64,6144]{1,0:T(8,128)}, bf16[2,128,2048]{2,1,0:T(8,128)(2,1)}, f32[2,128,2048]{2,1,0:T(8,128)}) custom-call(bf16[8,64,1536]{2,1,0:T(8,128)(2,1)} %get-tuple-element.93.refs_0_, bf16[8,64,768]{2,1,0:T(8,128)(2,1)} %get-tuple-element.94.refs_1_, bf16[2,128,2048]{2,1,0:T(8,128)(2,1)} %bitcast.72, ...), custom_call_target="tpu_custom_call" | custom-call | tf_op jit(solution)/shard_map/place_columns/pallas_call | solution.py:1231
  683.6 22.8 %owners_step.1 = (f32[336,128]{1,0:T(8,128)}, f32[32,128]{1,0:T(8,128)}, bf16[8,64,640]{2,1,0:T(8,128)(2,1)}, bf16[8,64,320]{2,1,0:T(8,128)(2,1)}) custom-call(bf16[4,336,128]{2,1,0:T(8,128)(2,1)} %get-tuple-element.99.pieces, f32[32,128]{1,0:T(8,128)} %get-tuple-element.100.values, bf16[8,64,640]{2,1,0:T(8,128)(2,1)} %bitcast.74, bf16[8,64,320]{2,1,0:T(8,128)(2,1)} %bitcast.75), custom_call_target="tpu_custom_call" | custom-call | tf_op jit(solution)/shard_map/owners_step/pallas_call | solution.py:1173
  713.3 2.9 place_columns.3
  (64 shorter events, 15.4 us)
Async XLA Ops:
  7.2 70.3 %copy-start = (bf16[2048,768]{1,0:T(8,128)(2,1)S(1)}, bf16[2048,768]{1,0:T(8,128)(2,1)}, u32[]{:S(2)}) copy-start(bf16[2048,768]{1,0:T(8,128)(2,1)} %param.26) | copy-start | bytes 9437188
  7.2 77.2 %all-gather.13.cloned.1.call-start = ((), (), s32[]{:S(2)}) async-start(), calls=%async_computation.10 | async-start | bytes 3276800 | tf_op jit(solution)/shard_map/all_gather | solution.py:1429
  9.4 116.9 %all-gather.15.cloned.1.call-start = ((), (), s32[]{:S(2)}) async-start(), calls=%async_computation.11 | async-start | bytes 1638400 | tf_op jit(solution)/shard_map/all_gather | solution.py:1429
  11.2 259.9 %all-gather.9.cloned.1.call-start = ((), (), s32[]{:S(2)}) async-start(), calls=%async_computation.4 | async-start | bytes 3932160 | tf_op jit(solution)/shard_map/all_gather | solution.py:1429
  68.0 13.3 %copy-start.5 = (f32[2560]{0:T(1024)S(1)}, f32[2560]{0:T(1024)}, u32[]{:S(2)}) copy-start(f32[2560]{0:T(1024)} %param.19) | copy-start | bytes 30724
  68.0 13.3 %copy-start.6 = (f32[2560]{0:T(1024)S(1)}, f32[2560]{0:T(1024)}, u32[]{:S(2)}) copy-start(f32[2560]{0:T(1024)} %param.22) | copy-start | bytes 30724
  68.1 13.4 %copy-start.3 = (f32[4,2560]{1,0:T(4,128)S(1)}, f32[4,2560]{1,0:T(4,128)}, u32[]{:S(2)}) copy-start(f32[4,2560]{1,0:T(4,128)} %param.18) | copy-start | bytes 122884
  68.1 13.4 %copy-start.4 = (f32[2,2560]{1,0:T(2,128)S(1)}, f32[2,2560]{1,0:T(2,128)}, u32[]{:S(2)}) copy-start(f32[2,2560]{1,0:T(2,128)} %param.21) | copy-start | bytes 61444
  76.8 206.1 %all-gather.11.cloned.1.call-start = ((), (), s32[]{:S(2)}) async-start(), calls=%async_computation.5 | async-start | bytes 3932160 | tf_op jit(solution)/shard_map/all_gather | solution.py:1429
  77.4 230.8 %all-gather.17.cloned.1.call-start = ((), (), s32[]{:S(2)}) async-start(), calls=%async_computation.12 | async-start | bytes 3932160 | tf_op jit(solution)/shard_map/all_gather | solution.py:1429
  81.1 303.9 %reduce-scatter.7.cloned.1.call-start = ((), (), s32[]{:S(2)}) async-start(), calls=%async_computation.7 | async-start | bytes 3932160 | tf_op jit(solution)/shard_map/reduce_scatter | solution.py:1479
  296.7 11.5 %copy-start.2 = (bf16[2048,768]{1,0:T(8,128)(2,1)}, bf16[2048,768]{1,0:T(8,128)(2,1)S(1)}, u32[]{:S(2)}) copy-start(bf16[2048,768]{1,0:T(8,128)(2,1)S(1)} %get-tuple-element.85.hidden) | copy-start | bytes 9437188
  308.2 196.7 %reduce-scatter.5.cloned.1.call-start = ((), (), s32[]{:S(2)}) async-start(), calls=%async_computation.6 | async-start | bytes 7864320 | tf_op jit(solution)/shard_map/reduce_scatter | solution.py:1479
  384.9 298.7 %reduce-scatter.11.cloned.1.call-start = ((), (), s32[]{:S(2)}) async-start(), calls=%async_computation.9 | async-start | bytes 1966080 | tf_op jit(solution)/shard_map/reduce_scatter | solution.py:1479
  437.0 246.6 %reduce-scatter.9.cloned.1.call-start = ((), (), s32[]{:S(2)}) async-start(), calls=%async_computation.8 | async-start | bytes 3276800 | tf_op jit(solution)/shard_map/reduce_scatter | solution.py:1479
  516.1 200.1 %copy-start.1 = (bf16[2048,768]{1,0:T(8,128)(2,1)S(1)}, bf16[2048,768]{1,0:T(8,128)(2,1)}, u32[]{:S(2)}) copy-start(bf16[2048,768]{1,0:T(8,128)(2,1)} %param.26) | copy-start | bytes 9437188
Sparse Core Ops, SparseCore 0:
  10.2 58.8 all-gather.12
  71.2 31.4 all-gather.14
  104.9 66.6 all-gather.8
  173.5 62.0 all-gather.10
  237.6 62.1 all-gather.16
  308.4 58.3 reduce-scatter.6
  385.0 109.8 reduce-scatter.4
  497.2 35.7 reduce-scatter.10
  535.3 51.0 reduce-scatter.8

commit v12 on v11

--- a/solution.py
+++ b/solution.py
@@ -1200,9 +1200,8 @@
 def place_kernel(planes, hidden, outs, through, *refs):
     count = len(outs)
     given, passed, results, copied = refs[:count], refs[count : count + through], refs[count + through : 2 * count + through], refs[2 * count + through :]
-    copies = [pltpu.make_async_copy(passed[n], copied[n], copied[-1].at[n]) for n in range(through)]
-    for copy in copies:
-        copy.start()
+    for source, target in zip(passed, copied):
+        target[...] = source[...]
     for count, sources, out in zip(outs, given, results):
         piece = sources.shape[2] // (count * (planes if hidden else 1))
         for k in range(count):
@@ -1220,8 +1219,6 @@
                     out[:, k, start : start + row.shape[1]] = row
                 else:
                     out[:, start : start + row.shape[1]] = row
-    for copy in copies:
-        copy.wait()
 
 
 def place_columns(planes, hidden, outs, owned, through=()):
@@ -1235,11 +1232,47 @@
             *[jax.ShapeDtypeStruct(shape, F32) for shape in shapes],
             *[jax.ShapeDtypeStruct(part.shape, part.dtype) for part in through],
         ),
-        in_specs=[*whole(len(owned)), *[ANYWHERE] * len(through)],
-        out_specs=(*whole(len(outs)), *[ANYWHERE] * len(through)),
-        scratch_shapes=[pltpu.SemaphoreType.DMA((len(through),))] if through else [],
+        in_specs=whole(len(owned) + len(through)),
+        out_specs=tuple(whole(len(outs) + len(through))),
         compiler_params=pltpu.CompilerParams(vmem_limit_bytes=60 * 1024 * 1024),
     )(*owned, *through)
+
+
+def last_kernel(planes, own_in, own_out, gates, gains, in_out, out_out, gate_out, taps_out, bias_out, logit_out, decay_out, mlp_out, mix_out):
+    place_kernel(planes, False, (2, 1), 0, own_in, own_out, in_out, out_out)
+    size, part = gate_out.shape[0], gate_out.shape[2]
+    for k in range(2):
+        gate_out[:, k, :] = gates[k * size : (k + 1) * size, :part]
+    rest = gates[2 * size : 2 * size + 8, :part]
+    taps_out[...] = rest[0:4]
+    bias_out[...] = rest[4:5]
+    logit_out[...] = rest[5:7]
+    decay_out[...] = rest[7:8]
+    own_rows = mlp_out.shape[1]
+    per_line = LANES // own_rows
+    index = lax.axis_index("t") * 8 + Place().chunk(0, 0, 0)
+    for base, out in ((0, mlp_out), (gains.shape[0] // 2, mix_out)):
+        line = gains[pl.ds(base + index // per_line, 1), :]
+        value = line[:, :own_rows]
+        for n in range(1, per_line):
+            value = jnp.where(index % per_line == n, line[:, n * own_rows : (n + 1) * own_rows], value)
+        out[...] = value
+
+
+def last_step(planes, own_in, own_out, gates, gains, size, part):
+    members, own_rows, columns = own_out.shape
+    shapes = [
+        (own_rows, 2, columns * members), (own_rows, columns * members),
+        (size, 2, part), (4, part), (1, part), (2, part), (1, part), (1, own_rows), (1, own_rows),
+    ]
+    return pl.pallas_call(
+        functools.partial(last_kernel, planes),
+        name="place_last",
+        out_shape=tuple(jax.ShapeDtypeStruct(shape, F32) for shape in shapes),
+        in_specs=whole(4),
+        out_specs=tuple(whole(9)),
+        compiler_params=pltpu.CompilerParams(vmem_limit_bytes=60 * 1024 * 1024),
+    )(own_in, own_out, gates, gains)
 
 
 def first_gather(planes, normed, ids):
@@ -1510,10 +1543,6 @@
     )
     gate_grads, gains, owned_in, owned_out = owners_step(planes, direct, pieces, values, [by_owner(grad_in), by_owner(grad_out)])
     grad_inputs = grad_inputs.reshape(inputs.shape)
-    index = ((t * 2 + i) * row_groups + r) * own_rows
-    gains = lax.dynamic_slice_in_dim(gains.reshape(2, width), index, own_rows, 1)
-
-
     def columns(hidden, outs, owned, through=()):
         if direct:
             return place_columns(planes, hidden, outs, owned, through)
@@ -1523,13 +1552,18 @@
         owned = owned.transpose(order).reshape(own_rows, sum(outs), -1)
         return (owned[:, :2], owned[:, 2], *through)
 
-    grad_in_weight, grad_out_weight = columns(False, (2, 1), [owned_in, owned_out])
     grad_mlp_in, grad_down_weight, outputs, grad_inputs = columns(
         True, (2, 1), [owned_mlp_in, owned_down], [outputs, grad_inputs]
     )
     if direct:
-        gate_grads = gate_grads[:, :part]
+        grad_in_weight, grad_out_weight, grad_gate_weight, taps, bias, logit_bias, decay_grad, mlp_sum, mix_sum = last_step(
+            planes, owned_in, owned_out, gate_grads, gains, block_width, part
+        )
+        bias, decay_grad, mlp_sum, mix_sum = bias[0], decay_grad[0], mlp_sum[0], mix_sum[0]
     else:
+        grad_in_weight, grad_out_weight = columns(False, (2, 1), [owned_in, owned_out])
+        index = ((t * 2 + i) * row_groups + r) * own_rows
+        mlp_sum, mix_sum = lax.dynamic_slice_in_dim(gains.reshape(2, width), index, own_rows, 1)
         column_block = lax.broadcasted_iota(jnp.int32, (block_width, channels), 1) // block_width
 
         def diagonal(gw):
@@ -1541,20 +1575,21 @@
         placed = jnp.zeros((gate_grads.shape[0], recur_width), F32)
         placed = lax.dynamic_update_slice_in_dim(placed, gate_grads, first, 1)
         gate_grads = lax.psum_scatter(placed, EVERY, scatter_dimension=1, tiled=True)
-    grad_gate_weight = jnp.stack([gate_grads[:block_width], gate_grads[block_width : 2 * block_width]], axis=1)
-    small = gate_grads[2 * block_width : 2 * block_width + 8]
+        grad_gate_weight = jnp.stack([gate_grads[:block_width], gate_grads[block_width : 2 * block_width]], axis=1)
+        rest = gate_grads[2 * block_width :]
+        taps, bias, logit_bias, decay_grad = rest[0:4], rest[4], rest[5:7], rest[7]
     return (
         outputs,
         grad_inputs,
-        gains[1],
+        mix_sum,
         grad_in_weight,
-        small[0:4],
-        small[4],
+        taps,
+        bias,
         grad_gate_weight,
-        small[5:7],
-        small[7],
+        logit_bias,
+        decay_grad,
         grad_out_weight,
-        gains[0],
+        mlp_sum,
         grad_mlp_in,
         grad_down_weight,
     )

time: 727 us -> 627 us (0.86)
  Pallas kernels: 592 us -> 499 us
    pallas_call x2 -> x1, Pallas kernels: 103 us -> 6.93 us  [place_columns(): pl.pallas_call(functools.partial(place_kernel, planes, hidden, outs, len(...]
  transfers between devices with their start and end apart: 9 -> 9, of which waited for: 0 -> 0; matrix products, arithmetic and copies ran while one was open for 15% -> 17% of each run, Pallas kernels for 78% -> 76%
where the time goes in v12:
time: 627 us; the launch traced here: 623 us
  Pallas kernels  499 us (80%)
  matrix products  78.2 us (12%)
  local copies, waits for them, and re-layouts  25.6 us (4%)
  between operations  14.3 us (2%)
    pallas_call x1, Pallas kernels, middle_step(): pl.pallas_call(middle_kernel, name='middle_step', out_shape=(jax.ShapeDty...  85.1 us
    pallas_call x1, Pallas kernels, mixer_backward(): pl.pallas_call(functools.partial(mixer_backward_kernel, count, seg), name...  68 us
    pallas_call x1, Pallas kernels, final_step(): pl.pallas_call(final_kernel, name='final_step', out_shape=(jax.ShapeDtype...  67.3 us
    pallas_call x1, Pallas kernels, mixer_forward(): pl.pallas_call(functools.partial(mixer_forward_kernel, count, seg, rows_h...  59.6 us
    pallas_call x1, Pallas kernels, turn_step(): pl.pallas_call(turn_kernel, name='turn_step', out_shape=(jax.ShapeDtypeSt...  58 us
    dot_general x4, matrix products, nt(): lax.dot_general(left, right, (((1,), (1,)), ((), ())), preferred_element_...  55.6 us
    pallas_call x1, Pallas kernels, spread_step(): pl.pallas_call(spread_kernel, name='turn_spread', out_shape=(jax.ShapeDty...  52 us
    pallas_call x1, Pallas kernels, first_gather(): pl.pallas_call(functools.partial(first_gather_kernel, planes), name='firs...  45.6 us
  transfers between devices with their start and end apart: 9, of which 0 were waited for; matrix products, arithmetic and copies ran while one was open for 17% of the time, Pallas kernels for 76%

profile of v12, /device:TPU:0, one launch (start us, length us, event | category | flops | bytes accessed | tf_op | source)
XLA Modules:
  0.0 622.9 jit_solution(15652362530895165833)
XLA Ops:
  7.2 2.1 dynamic-slice_bitcast_fusion
  9.5 1.7 dynamic-slice_bitcast_fusion.1
  14.1 2.5 multiply_convert_fusion.3.normed
  16.6 45.6 %first_gather.1 = (bf16[2048,2048]{1,0:T(8,128)(2,1)}, f32[8,8,128]{2,1,0:T(8,128)}, f32[8,8,128]{2,1,0:T(8,128)}, f32[8,8,128]{2,1,0:T(8,128)}) custom-call(bf16[256,2048]{1,0:T(8,128)(2,1)} %multiply_convert_fusion.3.normed, f32[8,128]{1,0:T(8,128)} %pad.4.ids), custom_call_target="tpu_custom_call" | custom-call | tf_op jit(solution)/shard_map/first_gather/pallas_call | solution.py:1281
  62.2 5.8 constant_dynamic-slice_fusion.1
  68.1 6.1 copy.35
  74.1 2.7 fusion.2
  78.9 2.2 copy.36
  84.4 30.4 %swap.1 = bf16[2,4,80,2048]{3,2,1,0:T(8,128)(2,1)} custom-call(bf16[4,2,80,2048]{3,2,1,0:T(8,128)(2,1)} %bitcast.58), custom_call_target="tpu_custom_call" | custom-call | tf_op jit(solution)/shard_map/swap/pallas_call | solution.py:1399
  114.9 11.4 %fusion.3.branches_far = f32[2048,640]{1,0:T(8,128)} fusion(bf16[2048,2048]{1,0:T(8,128)(2,1)} %get-tuple-element.69, bf16[640,2048]{1,0:T(8,128)(2,1)} %bitcast.46), kind=kOutput, calls=%fused_computation.23 | convolution fusion | flops 5368709120 | bytes 16252928 | tf_op jit(solution)/shard_map/dot_general | solution.py:1415
  126.3 59.6 %mixer_forward.1 = (bf16[2048,320]{1,0:T(8,128)(2,1)}, f32[3,2048,128]{2,1,0:T(8,128)}, f32[2048,320]{1,0:T(8,128)}, bf16[2048,320]{1,0:T(8,128)(2,1)}, f32[128,...) custom-call(f32[2048,640]{1,0:T(8,128)} %fusion.3.branches_far, ...), custom_call_target="tpu_custom_call" | custom-call | tf_op jit(solution)/shard_map/mixer_forward/pallas_call | solution.py:427
  185.9 85.1 %middle_step.1 = (f32[256,2048]{1,0:T(8,128)}, bf16[2048,2048]{1,0:T(8,128)(2,1)}) custom-call(bf16[2048,320]{1,0:T(8,128)(2,1)} %get-tuple-element.75.left.mixed, bf16[320,2048]{1,0:T(8,128)(2,1)} %bitcast.49, bf16[256,2048]{1,0:T(8,128)(2,1)} %bitcast.44, f32[1,2048]{1,0:T(1,128)} %bitcast.68), custom_call_target="tpu_custom_call" | custom-call | tf_op jit(solution)/shard_map/middle_step/pallas_call | solution.py:1294
  271.1 11.8 %fusion.4 = f32[2048,768]{1,0:T(8,128)} fusion(bf16[2048,2048]{1,0:T(8,128)(2,1)} %get-tuple-element.77.normed_far, bf16[768,2048]{1,0:T(8,128)(2,1)} %bitcast.54), kind=kOutput, calls=%fused_computation.24 | convolution fusion | flops 6442450944 | bytes 17825792 | tf_op jit(solution)/shard_map/dot_general | solution.py:1415
  282.9 13.7 %multiply_convert_fusion.2 = (bf16[2048,768]{1,0:T(8,128)(2,1)S(1)}, f32[2048,768]{1,0:T(8,128)}) fusion(f32[2048,768]{1,0:T(8,128)} %fusion.4, bf16[2048,2048]{1,0:T(8,128)(2,1)} %get-tuple-element.77.normed_far, bf16[768,2048]{1,0:T(8,128)(2,1)} %bitcast.56), kind=kOutput, calls=%fused_computation.2 | convolution fusion | flops 6458179584 | bytes 27262976 | tf_op jit(solution)/shard_map/dot_general | solution.py:1415
  296.6 11.5 %convolution_convert_fusion = bf16[2048,768]{1,0:T(8,128)(2,1)} fusion(bf16[2048,2048]{1,0:T(8,128)(2,1)} %get-tuple-element.74, bf16[2048,768]{1,0:T(8,128)(2,1)S(1)} %get-tuple-element.92.hidden), kind=kOutput, calls=%fused_computation.6 | convolution fusion | flops 6444023808 | bytes 14680064 | tf_op jit(solution)/shard_map/dot_general | solution.py:1419
  308.2 18.7 %multiply_convert_fusion = (bf16[2048,768]{1,0:T(8,128)(2,1)}, bf16[2048,768]{1,0:T(8,128)(2,1)}) fusion(f32[2048,768]{1,0:T(8,128)} %fusion.4, f32[2048,768]{1,0:T(8,128)} %get-tuple-element.132, bf16[2048,2048]{1,0:T(8,128)(2,1)} %get-tuple-element.74, bf16[768,2048]{1,0:T(8,128)(2,1)} %all-gather.17.cloned.1.call-done.w_down), kind=kOutput, calls=%fused_computation | convolution fusion | flops 6477053952 | bytes 30408704 | tf_op jit(solution)/shard_map/dot_general | solution.py:1415
  326.9 58.0 %turn_step.1 = (f32[256,2048]{1,0:T(8,128)}, f32[8,2048]{1,0:T(8,128)}, bf16[2048,1536]{1,0:T(8,128)(2,1)}, bf16[256,2048]{1,0:T(8,128)(2,1)}) custom-call(bf16[2048,768]{1,0:T(8,128)(2,1)} %get-tuple-element.126.left0, bf16[2048,768]{1,0:T(8,128)(2,1)} %get-tuple-element.125.left1, bf16[768,2048]{1,0:T(8,128)(2,1)} %bitcast.55, bf16[768,2048]{1,0:T(8,128)(2,1)} %bitcast.57, ...), custom_call_target="tpu_custom_call" | custom-call | tf_op jit(solution)/shard_map/turn_step/pallas_call | solution.py:1307
  385.0 52.0 %turn_spread.1 = (f32[2048,320]{1,0:T(8,128)}, bf16[2048,320]{1,0:T(8,128)(2,1)}, bf16[2048,2048]{1,0:T(8,128)(2,1)}) custom-call(bf16[256,2048]{1,0:T(8,128)(2,1)} %get-tuple-element.84.block, bf16[320,2048]{1,0:T(8,128)(2,1)} %bitcast.50, bf16[2048,320]{1,0:T(8,128)(2,1)} %get-tuple-element.75.left.mixed), custom_call_target="tpu_custom_call" | custom-call | tf_op jit(solution)/shard_map/turn_spread/pallas_call | solution.py:1326
  437.1 68.0 %mixer_backward.1 = (bf16[2048,640]{1,0:T(8,128)(2,1)}, f32[320,320]{1,0:T(8,128)}, f32[320,320]{1,0:T(8,128)}, f32[8,320]{1,0:T(8,128)}, bf16[4,336,128]{2,1,0:...) custom-call(f32[2048,320]{1,0:T(8,128)} %get-tuple-element.85.grad_mixed_far, ...), custom_call_target="tpu_custom_call" | custom-call | tf_op jit(solution)/shard_map/mixer_backward/pallas_call | solution.py:467
  505.1 11.1 %convolution_convert_fusion.1 = bf16[2048,640]{1,0:T(8,128)(2,1)} fusion(bf16[2048,2048]{1,0:T(8,128)(2,1)} %get-tuple-element.69, bf16[2048,640]{1,0:T(8,128)(2,1)} %get-tuple-element.96.left), kind=kOutput, calls=%fused_computation.7 | convolution fusion | flops 5370019840 | bytes 13631488 | tf_op jit(solution)/shard_map/dot_general | solution.py:1419
  516.2 67.3 %final_step.1 = (f32[256,2048]{1,0:T(8,128)}, f32[32,128]{1,0:T(8,128)}, bf16[8,64,1536]{2,1,0:T(8,128)(2,1)}) custom-call(bf16[2048,640]{1,0:T(8,128)(2,1)} %get-tuple-element.96.left, bf16[640,2048]{1,0:T(8,128)(2,1)} %bitcast.47, bf16[256,2048]{1,0:T(8,128)(2,1)} %bitcast.45, f32[1,2048]{1,0:T(1,128)} %bitcast.70, f32[8,2048]{1,0:T(8,128)} %get-tuple-element.97.mlp_gains, ...), custom_call_target="tpu_custom_call" | custom-call | tf_op jit(solution)/shard_map/final_step/pallas_call | solution.py:1127
  583.6 6.9 %place_columns.1 = (f32[64,2,6144]{2,1,0:T(2,128)}, f32[64,6144]{1,0:T(8,128)}, bf16[2,128,2048]{2,1,0:T(8,128)(2,1)}, f32[2,128,2048]{2,1,0:T(8,128)}) custom-call(bf16[8,64,1536]{2,1,0:T(8,128)(2,1)} %get-tuple-element.100.refs_0_, bf16[8,64,768]{2,1,0:T(8,128)(2,1)} %get-tuple-element.101.refs_1_, bf16[2,128,2048]{2,1,0:T(8,128)(2,1)} %bitcast.64, ...), custom_call_target="tpu_custom_call" | custom-call | tf_op jit(solution)/shard_map/place_columns/pallas_call | solution.py:1228
  590.5 22.6 %owners_step.1 = (f32[336,128]{1,0:T(8,128)}, f32[32,128]{1,0:T(8,128)}, bf16[8,64,640]{2,1,0:T(8,128)(2,1)}, bf16[8,64,320]{2,1,0:T(8,128)(2,1)}) custom-call(bf16[4,336,128]{2,1,0:T(8,128)(2,1)} %get-tuple-element.106.pieces, f32[32,128]{1,0:T(8,128)} %get-tuple-element.107.values, bf16[8,64,640]{2,1,0:T(8,128)(2,1)} %bitcast.66, bf16[8,64,320]{2,1,0:T(8,128)(2,1)} %bitcast.67), custom_call_target="tpu_custom_call" | custom-call | tf_op jit(solution)/shard_map/owners_step/pallas_call | solution.py:1173
  613.1 3.0 place_last.1
  (55 shorter events, 8.5 us)
Async XLA Ops:
  7.2 70.3 %copy-start = (bf16[2048,768]{1,0:T(8,128)(2,1)S(1)}, bf16[2048,768]{1,0:T(8,128)(2,1)}, u32[]{:S(2)}) copy-start(bf16[2048,768]{1,0:T(8,128)(2,1)} %param.26) | copy-start | bytes 9437188
  7.2 77.2 %all-gather.13.cloned.1.call-start = ((), (), s32[]{:S(2)}) async-start(), calls=%async_computation.10 | async-start | bytes 3276800 | tf_op jit(solution)/shard_map/all_gather | solution.py:1462
  9.4 116.9 %all-gather.15.cloned.1.call-start = ((), (), s32[]{:S(2)}) async-start(), calls=%async_computation.11 | async-start | bytes 1638400 | tf_op jit(solution)/shard_map/all_gather | solution.py:1462
  11.2 259.9 %all-gather.9.cloned.1.call-start = ((), (), s32[]{:S(2)}) async-start(), calls=%async_computation.4 | async-start | bytes 3932160 | tf_op jit(solution)/shard_map/all_gather | solution.py:1462
  68.0 13.3 %copy-start.5 = (f32[2560]{0:T(1024)S(1)}, f32[2560]{0:T(1024)}, u32[]{:S(2)}) copy-start(f32[2560]{0:T(1024)} %param.19) | copy-start | bytes 30724
  68.1 13.3 %copy-start.6 = (f32[2560]{0:T(1024)S(1)}, f32[2560]{0:T(1024)}, u32[]{:S(2)}) copy-start(f32[2560]{0:T(1024)} %param.22) | copy-start | bytes 30724
  68.1 13.4 %copy-start.3 = (f32[4,2560]{1,0:T(4,128)S(1)}, f32[4,2560]{1,0:T(4,128)}, u32[]{:S(2)}) copy-start(f32[4,2560]{1,0:T(4,128)} %param.18) | copy-start | bytes 122884
  68.1 13.4 %copy-start.4 = (f32[2,2560]{1,0:T(2,128)S(1)}, f32[2,2560]{1,0:T(2,128)}, u32[]{:S(2)}) copy-start(f32[2,2560]{1,0:T(2,128)} %param.21) | copy-start | bytes 61444
  76.8 206.0 %all-gather.11.cloned.1.call-start = ((), (), s32[]{:S(2)}) async-start(), calls=%async_computation.5 | async-start | bytes 3932160 | tf_op jit(solution)/shard_map/all_gather | solution.py:1462
  77.4 230.7 %all-gather.17.cloned.1.call-start = ((), (), s32[]{:S(2)}) async-start(), calls=%async_computation.12 | async-start | bytes 3932160 | tf_op jit(solution)/shard_map/all_gather | solution.py:1462
  81.1 303.9 %reduce-scatter.7.cloned.1.call-start = ((), (), s32[]{:S(2)}) async-start(), calls=%async_computation.7 | async-start | bytes 3932160 | tf_op jit(solution)/shard_map/reduce_scatter | solution.py:1512
  296.6 11.5 %copy-start.2 = (bf16[2048,768]{1,0:T(8,128)(2,1)}, bf16[2048,768]{1,0:T(8,128)(2,1)S(1)}, u32[]{:S(2)}) copy-start(bf16[2048,768]{1,0:T(8,128)(2,1)S(1)} %get-tuple-element.92.hidden) | copy-start | bytes 9437188
  308.2 197.0 %reduce-scatter.5.cloned.1.call-start = ((), (), s32[]{:S(2)}) async-start(), calls=%async_computation.6 | async-start | bytes 7864320 | tf_op jit(solution)/shard_map/reduce_scatter | solution.py:1512
  384.9 205.6 %reduce-scatter.11.cloned.1.call-start = ((), (), s32[]{:S(2)}) async-start(), calls=%async_computation.9 | async-start | bytes 1966080 | tf_op jit(solution)/shard_map/reduce_scatter | solution.py:1512
  437.0 153.4 %reduce-scatter.9.cloned.1.call-start = ((), (), s32[]{:S(2)}) async-start(), calls=%async_computation.8 | async-start | bytes 3276800 | tf_op jit(solution)/shard_map/reduce_scatter | solution.py:1512
  516.2 99.9 %copy-start.1 = (bf16[2048,768]{1,0:T(8,128)(2,1)S(1)}, bf16[2048,768]{1,0:T(8,128)(2,1)}, u32[]{:S(2)}) copy-start(bf16[2048,768]{1,0:T(8,128)(2,1)} %param.26) | copy-start | bytes 9437188
Sparse Core Ops, SparseCore 0:
  10.2 58.8 all-gather.12
  71.2 31.4 all-gather.14
  104.9 66.6 all-gather.8
  173.5 62.0 all-gather.10
  237.6 62.1 all-gather.16
  308.3 58.3 reduce-scatter.6
  385.0 109.7 reduce-scatter.4
  497.2 35.8 reduce-scatter.10
  535.3 51.0 reduce-scatter.8

commit v13 on v12

--- a/solution.py
+++ b/solution.py
@@ -1507,6 +1507,7 @@
     right = nt(normed_two, w_right, F32)
     act, slope = gelu_parts(left)
     hidden = (act * right).astype(BF16)
+    hidden, act, slope = lax.optimization_barrier((hidden, act.astype(BF16), (right * slope).astype(BF16)))
 
     def over_planes(grad):
         return lax.psum_scatter(grad, "t", scatter_dimension=0, tiled=True)
@@ -1515,8 +1516,8 @@
     grad_down, hidden, w_down = lax.optimization_barrier((grad_down, hidden, w_down))
     grad_down = over_planes(grad_down)
     grad_hidden = nt(cot, w_down, F32)
-    grad_left = (grad_hidden * right * slope).astype(BF16)
-    grad_right = (grad_hidden * act).astype(BF16)
+    grad_left = (grad_hidden * slope.astype(F32)).astype(BF16)
+    grad_right = (grad_hidden * act.astype(F32)).astype(BF16)
     grad_middle, grad_mlp_gain, grad_mlp_in, grad_mid_own = turn_step(
         grad_left, grad_right, w_left, w_right, middle, mlp_gain, cot_own, normed_two
     )

time: 627 us -> 629 us (level)
  no operation moved by 1% of the time
where the time goes in v13:
time: 629 us; the launch traced here: 625 us
  Pallas kernels  501 us (80%)
  matrix products  76.1 us (12%)
  local copies, waits for them, and re-layouts  27.4 us (4%)
  between operations  14.3 us (2%)
    pallas_call x1, Pallas kernels, middle_step(): pl.pallas_call(middle_kernel, name='middle_step', out_shape=(jax.ShapeDty...  85.2 us
    pallas_call x1, Pallas kernels, mixer_backward(): pl.pallas_call(functools.partial(mixer_backward_kernel, count, seg), name...  71 us
    pallas_call x1, Pallas kernels, final_step(): pl.pallas_call(final_kernel, name='final_step', out_shape=(jax.ShapeDtype...  67.2 us
    pallas_call x1, Pallas kernels, mixer_forward(): pl.pallas_call(functools.partial(mixer_forward_kernel, count, seg, rows_h...  59.6 us
    pallas_call x1, Pallas kernels, turn_step(): pl.pallas_call(turn_kernel, name='turn_step', out_shape=(jax.ShapeDtypeSt...  58 us
    dot_general x4, matrix products, nt(): lax.dot_general(left, right, (((1,), (1,)), ((), ())), preferred_element_...  53.4 us
    pallas_call x1, Pallas kernels, spread_step(): pl.pallas_call(spread_kernel, name='turn_spread', out_shape=(jax.ShapeDty...  52 us
    pallas_call x1, Pallas kernels, first_gather(): pl.pallas_call(functools.partial(first_gather_kernel, planes), name='firs...  45.6 us
  transfers between devices with their start and end apart: 9, of which 0 were waited for; matrix products, arithmetic and copies ran while one was open for 17% of the time, Pallas kernels for 76%

profile of v13, /device:TPU:0, one launch (start us, length us, event | category | flops | bytes accessed | tf_op | source)
XLA Modules:
  0.0 625.3 jit_solution(13890453694506866817)
XLA Ops:
  7.3 2.1 dynamic-slice_bitcast_fusion
  14.1 2.5 multiply_convert_fusion.4.normed
  16.6 45.6 %first_gather.1 = (bf16[2048,2048]{1,0:T(8,128)(2,1)}, f32[8,8,128]{2,1,0:T(8,128)}, f32[8,8,128]{2,1,0:T(8,128)}, f32[8,8,128]{2,1,0:T(8,128)}) custom-call(bf16[256,2048]{1,0:T(8,128)(2,1)} %multiply_convert_fusion.4.normed, f32[8,128]{1,0:T(8,128)} %pad.4.ids), custom_call_target="tpu_custom_call" | custom-call | tf_op jit(solution)/shard_map/first_gather/pallas_call | solution.py:1281
  62.2 5.8 constant_dynamic-slice_fusion.1
  68.1 6.0 copy.35
  74.1 2.7 fusion.3
  78.8 2.2 copy.36
  84.3 30.4 %swap.1 = bf16[2,4,80,2048]{3,2,1,0:T(8,128)(2,1)} custom-call(bf16[4,2,80,2048]{3,2,1,0:T(8,128)(2,1)} %bitcast.58), custom_call_target="tpu_custom_call" | custom-call | tf_op jit(solution)/shard_map/swap/pallas_call | solution.py:1399
  114.8 11.4 %fusion.4.branches_far = f32[2048,640]{1,0:T(8,128)} fusion(bf16[2048,2048]{1,0:T(8,128)(2,1)} %get-tuple-element.72, bf16[640,2048]{1,0:T(8,128)(2,1)} %bitcast.46), kind=kOutput, calls=%fused_computation.25 | convolution fusion | flops 5368709120 | bytes 16252928 | tf_op jit(solution)/shard_map/dot_general | solution.py:1415
  126.2 59.6 %mixer_forward.1 = (bf16[2048,320]{1,0:T(8,128)(2,1)}, f32[3,2048,128]{2,1,0:T(8,128)}, f32[2048,320]{1,0:T(8,128)}, bf16[2048,320]{1,0:T(8,128)(2,1)}, f32[128,...) custom-call(f32[2048,640]{1,0:T(8,128)} %fusion.4.branches_far, ...), custom_call_target="tpu_custom_call" | custom-call | tf_op jit(solution)/shard_map/mixer_forward/pallas_call | solution.py:427
  185.8 85.2 %middle_step.1 = (f32[256,2048]{1,0:T(8,128)}, bf16[2048,2048]{1,0:T(8,128)(2,1)}) custom-call(bf16[2048,320]{1,0:T(8,128)(2,1)} %get-tuple-element.78.left.mixed, bf16[320,2048]{1,0:T(8,128)(2,1)} %bitcast.49, bf16[256,2048]{1,0:T(8,128)(2,1)} %bitcast.44, f32[1,2048]{1,0:T(1,128)} %bitcast.68), custom_call_target="tpu_custom_call" | custom-call | tf_op jit(solution)/shard_map/middle_step/pallas_call | solution.py:1294
  271.0 11.8 %fusion.5 = f32[2048,768]{1,0:T(8,128)} fusion(bf16[2048,2048]{1,0:T(8,128)(2,1)} %get-tuple-element.80.normed_far, bf16[768,2048]{1,0:T(8,128)(2,1)} %bitcast.54), kind=kOutput, calls=%fused_computation.26 | convolution fusion | flops 6442450944 | bytes 17825792 | tf_op jit(solution)/shard_map/dot_general | solution.py:1415
  282.8 16.0 %multiply_convert_fusion.2 = (bf16[2048,768]{1,0:T(8,128)(2,1)}, bf16[2048,768]{1,0:T(8,128)(2,1)S(1)}, bf16[2048,768]{1,0:T(8,128)(2,1)}) fusion(f32[2048,768]{1,0:T(8,128)} %fusion.5, bf16[2048,2048]{1,0:T(8,128)(2,1)} %get-tuple-element.80.normed_far, bf16[768,2048]{1,0:T(8,128)(2,1)} %bitcast.56), kind=kOutput, calls=%fused_computation.2 | convolution fusion | flops 6477053952 | bytes 27262976 | tf_op jit(solution)/shard_map/dot_general | solution.py:1415
  298.8 11.6 %convolution_convert_fusion = bf16[2048,768]{1,0:T(8,128)(2,1)} fusion(bf16[2048,2048]{1,0:T(8,128)(2,1)} %get-tuple-element.77, bf16[2048,768]{1,0:T(8,128)(2,1)S(1)} %get-tuple-element.98.hidden), kind=kOutput, calls=%fused_computation.7 | convolution fusion | flops 6444023808 | bytes 14680064 | tf_op jit(solution)/shard_map/dot_general | solution.py:1419
  310.5 1.8 copy-done.2
  312.3 14.2 %multiply_convert_fusion = (bf16[2048,768]{1,0:T(8,128)(2,1)}, bf16[2048,768]{1,0:T(8,128)(2,1)}) fusion(bf16[2048,768]{1,0:T(8,128)(2,1)} %get-tuple-element.85, bf16[2048,768]{1,0:T(8,128)(2,1)} %get-tuple-element.84, bf16[2048,2048]{1,0:T(8,128)(2,1)} %get-tuple-element.77, bf16[768,2048]{1,0:T(8,128)(2,1)S(1)} %copy-done.2), kind=kOutput, calls=%fused_computation | convolution fusion | flops 6451888128 | bytes 24117248 | tf_op jit(solution)/shard_map/dot_general | solution.py:1415
  326.5 58.0 %turn_step.1 = (f32[256,2048]{1,0:T(8,128)}, f32[8,2048]{1,0:T(8,128)}, bf16[2048,1536]{1,0:T(8,128)(2,1)}, bf16[256,2048]{1,0:T(8,128)(2,1)}) custom-call(bf16[2048,768]{1,0:T(8,128)(2,1)} %get-tuple-element.134.left0, bf16[2048,768]{1,0:T(8,128)(2,1)} %get-tuple-element.133.left1, bf16[768,2048]{1,0:T(8,128)(2,1)} %bitcast.55, bf16[768,2048]{1,0:T(8,128)(2,1)} %bitcast.57, ...), custom_call_target="tpu_custom_call" | custom-call | tf_op jit(solution)/shard_map/turn_step/pallas_call | solution.py:1307
  384.6 52.0 %turn_spread.1 = (f32[2048,320]{1,0:T(8,128)}, bf16[2048,320]{1,0:T(8,128)(2,1)}, bf16[2048,2048]{1,0:T(8,128)(2,1)}) custom-call(bf16[256,2048]{1,0:T(8,128)(2,1)} %get-tuple-element.90.block, bf16[320,2048]{1,0:T(8,128)(2,1)} %bitcast.50, bf16[2048,320]{1,0:T(8,128)(2,1)} %get-tuple-element.78.left.mixed), custom_call_target="tpu_custom_call" | custom-call | tf_op jit(solution)/shard_map/turn_spread/pallas_call | solution.py:1326
  436.9 71.0 %mixer_backward.1 = (bf16[2048,640]{1,0:T(8,128)(2,1)}, f32[320,320]{1,0:T(8,128)}, f32[320,320]{1,0:T(8,128)}, f32[8,320]{1,0:T(8,128)}, bf16[4,336,128]{2,1,0:...) custom-call(f32[2048,320]{1,0:T(8,128)} %get-tuple-element.91.grad_mixed_far, ...), custom_call_target="tpu_custom_call" | custom-call | tf_op jit(solution)/shard_map/mixer_backward/pallas_call | solution.py:467
  508.0 11.1 %convolution_convert_fusion.1 = bf16[2048,640]{1,0:T(8,128)(2,1)} fusion(bf16[2048,2048]{1,0:T(8,128)(2,1)} %get-tuple-element.72, bf16[2048,640]{1,0:T(8,128)(2,1)} %get-tuple-element.102.left), kind=kOutput, calls=%fused_computation.8 | convolution fusion | flops 5370019840 | bytes 13631488 | tf_op jit(solution)/shard_map/dot_general | solution.py:1419
  519.1 67.2 %final_step.1 = (f32[256,2048]{1,0:T(8,128)}, f32[32,128]{1,0:T(8,128)}, bf16[8,64,1536]{2,1,0:T(8,128)(2,1)}) custom-call(bf16[2048,640]{1,0:T(8,128)(2,1)} %get-tuple-element.102.left, bf16[640,2048]{1,0:T(8,128)(2,1)} %bitcast.47, bf16[256,2048]{1,0:T(8,128)(2,1)} %bitcast.45, f32[1,2048]{1,0:T(1,128)} %bitcast.70, ...), custom_call_target="tpu_custom_call" | custom-call | tf_op jit(solution)/shard_map/final_step/pallas_call | solution.py:1127
  586.3 7.1 %place_columns.1 = (f32[64,2,6144]{2,1,0:T(2,128)}, f32[64,6144]{1,0:T(8,128)}, bf16[2,128,2048]{2,1,0:T(8,128)(2,1)}, f32[2,128,2048]{2,1,0:T(8,128)}) custom-call(bf16[8,64,1536]{2,1,0:T(8,128)(2,1)} %get-tuple-element.106.refs_0_, bf16[8,64,768]{2,1,0:T(8,128)(2,1)} %get-tuple-element.107.refs_1_, bf16[2,128,2048]{2,1,0:T(8,128)(2,1)} %bitcast.64, ...), custom_call_target="tpu_custom_call" | custom-call | tf_op jit(solution)/shard_map/place_columns/pallas_call | solution.py:1228
  593.4 22.1 %owners_step.1 = (f32[336,128]{1,0:T(8,128)}, f32[32,128]{1,0:T(8,128)}, bf16[8,64,640]{2,1,0:T(8,128)(2,1)}, bf16[8,64,320]{2,1,0:T(8,128)(2,1)}) custom-call(bf16[4,336,128]{2,1,0:T(8,128)(2,1)} %get-tuple-element.112.pieces, f32[32,128]{1,0:T(8,128)} %get-tuple-element.113.values, bf16[8,64,640]{2,1,0:T(8,128)(2,1)} %bitcast.66, bf16[8,64,320]{2,1,0:T(8,128)(2,1)} %bitcast.67), custom_call_target="tpu_custom_call" | custom-call | tf_op jit(solution)/shard_map/owners_step/pallas_call | solution.py:1173
  615.5 3.0 place_last.1
  (59 shorter events, 10.4 us)
Async XLA Ops:
  7.2 70.3 %copy-start = (bf16[2048,768]{1,0:T(8,128)(2,1)S(1)}, bf16[2048,768]{1,0:T(8,128)(2,1)}, u32[]{:S(2)}) copy-start(bf16[2048,768]{1,0:T(8,128)(2,1)} %param.26) | copy-start | bytes 9437188
  7.2 6.9 %copy-start.5 = (f32[2048]{0:T(1024)S(1)}, f32[2048]{0:T(1024)}, u32[]{:S(2)}) copy-start(f32[2048]{0:T(1024)} %param.16) | copy-start | bytes 24580
  7.2 77.1 %all-gather.13.cloned.1.call-start = ((), (), s32[]{:S(2)}) async-start(), calls=%async_computation.10 | async-start | bytes 3276800 | tf_op jit(solution)/shard_map/all_gather | solution.py:1462
  9.4 116.8 %all-gather.15.cloned.1.call-start = ((), (), s32[]{:S(2)}) async-start(), calls=%async_computation.11 | async-start | bytes 1638400 | tf_op jit(solution)/shard_map/all_gather | solution.py:1462
  11.2 259.8 %all-gather.9.cloned.1.call-start = ((), (), s32[]{:S(2)}) async-start(), calls=%async_computation.4 | async-start | bytes 3932160 | tf_op jit(solution)/shard_map/all_gather | solution.py:1462
  76.8 4.5 copy-start.7
  76.8 4.5 copy-start.8
  76.8 4.6 copy-start.4
  76.8 4.6 copy-start.6
  76.8 206.0 %all-gather.11.cloned.1.call-start = ((), (), s32[]{:S(2)}) async-start(), calls=%async_computation.5 | async-start | bytes 3932160 | tf_op jit(solution)/shard_map/all_gather | solution.py:1462
  77.4 233.0 %all-gather.17.cloned.1.call-start = ((), (), s32[]{:S(2)}) async-start(), calls=%async_computation.12 | async-start | bytes 3932160 | tf_op jit(solution)/shard_map/all_gather | solution.py:1462
  81.1 303.6 %reduce-scatter.7.cloned.1.call-start = ((), (), s32[]{:S(2)}) async-start(), calls=%async_computation.7 | async-start | bytes 3932160 | tf_op jit(solution)/shard_map/reduce_scatter | solution.py:1513
  298.8 11.6 %copy-start.3 = (bf16[2048,768]{1,0:T(8,128)(2,1)}, bf16[2048,768]{1,0:T(8,128)(2,1)S(1)}, u32[]{:S(2)}) copy-start(bf16[2048,768]{1,0:T(8,128)(2,1)S(1)} %get-tuple-element.98.hidden) | copy-start | bytes 9437188
  310.4 1.9 copy-start.2
  310.4 197.6 %reduce-scatter.5.cloned.1.call-start = ((), (), s32[]{:S(2)}) async-start(), calls=%async_computation.6 | async-start | bytes 7864320 | tf_op jit(solution)/shard_map/reduce_scatter | solution.py:1513
  384.6 208.8 %reduce-scatter.11.cloned.1.call-start = ((), (), s32[]{:S(2)}) async-start(), calls=%async_computation.9 | async-start | bytes 1966080 | tf_op jit(solution)/shard_map/reduce_scatter | solution.py:1513
  436.7 156.7 %reduce-scatter.9.cloned.1.call-start = ((), (), s32[]{:S(2)}) async-start(), calls=%async_computation.8 | async-start | bytes 3276800 | tf_op jit(solution)/shard_map/reduce_scatter | solution.py:1513
  586.3 32.3 %copy-start.1 = (bf16[2048,768]{1,0:T(8,128)(2,1)S(1)}, bf16[2048,768]{1,0:T(8,128)(2,1)}, u32[]{:S(2)}) copy-start(bf16[2048,768]{1,0:T(8,128)(2,1)} %param.26) | copy-start | bytes 9437188
Sparse Core Ops, SparseCore 0:
  10.2 58.8 all-gather.12
  71.2 31.4 all-gather.14
  104.9 66.6 all-gather.8
  173.5 62.0 all-gather.10
  237.6 62.1 all-gather.16
  310.5 58.3 reduce-scatter.6
  384.7 109.7 reduce-scatter.4
  496.8 35.7 reduce-scatter.10
  534.9 51.0 reduce-scatter.8

commit v14 on v12

--- a/solution.py
+++ b/solution.py
@@ -1015,10 +1015,15 @@
             self.moved[-1].start()
         self.rows_recv[self.rank] = self.pieces[self.rank]
 
-    def pass_on(self):
+    def settle(self, out):
         for number, offset in enumerate(self.near):
             other = lax.rem(self.place.chunk(*offset), 4)
             self.copy(number, self.pieces.at[other], self.rows_recv.at[other], self.place.peer(*offset)).wait_recv()
+        out[...] = self.rows_recv[...]
+        for copy in self.moved:
+            copy.wait_send()
+
+    def pass_on(self):
         for step in range(1, self.count):
             to = lax.rem(self.me + step, self.count)
             self.moved.append(self.copy(2 + step, self.rows_recv.at[to], self.gates_all.at[self.me], {"t": to}))
@@ -1088,15 +1093,17 @@
 
 
 def final_kernel(
-    left, right, own_in, gain, mlp_gains, grad_middle, reduced, grad_out, values_out, owned,
-    gain_sum, own_send, own_recv, *buffers,
+    left, right, own_in, gain, mlp_gains, grad_middle, pieces, reduced, grad_out, values_out, rows_out, owned,
+    gain_sum, rows_recv, gates_send, gates_recv, own_send, own_recv, *buffers,
 ):
     tokens, width = own_in.shape
     place = Place()
     place.greet([place.peer(*offset) for offset in BEYOND])
     scatter = Scatter(place, pair_product([left], [right], tokens), *buffers)
     owners = Owners(place, reduced, owned, own_send, own_recv)
+    gates = GateSums(place, 0, pieces, rows_recv, None, gates_send, gates_recv)
     scatter.run_first()
+    gates.begin()
     owners.begin()
     scatter.run_second()
     gain_sum[...] = jnp.zeros_like(gain_sum)
@@ -1118,11 +1125,12 @@
     for base, row in ((0, jnp.sum(mlp_gains[...], axis=0, keepdims=True)), (lines, jnp.sum(gain_sum[...], axis=0, keepdims=True))):
         for n in range(lines):
             values_out[base + n : base + n + 1, :] = row[:, n * LANES : (n + 1) * LANES]
+    gates.settle(rows_out)
     owners.finish()
     scatter.finish()
 
 
-def final_step(left, right, own_in, gain, mlp_gains, grad_middle, reduced):
+def final_step(left, right, own_in, gain, mlp_gains, grad_middle, pieces, reduced):
     tokens, width = own_in.shape
     return pl.pallas_call(
         final_kernel,
@@ -1130,34 +1138,40 @@
         out_shape=(
             jax.ShapeDtypeStruct((tokens, width), F32),
             jax.ShapeDtypeStruct((2 * width // LANES, LANES), F32),
+            jax.ShapeDtypeStruct(pieces.shape, pieces.dtype),
             jax.ShapeDtypeStruct(reduced.shape, reduced.dtype),
         ),
-        in_specs=[*whole(6), ANYWHERE],
-        out_specs=(*whole(2), ANYWHERE),
-        scratch_shapes=[pltpu.VMEM((8, width), F32), *OWNERS_SCRATCH, *Scatter.scratch(tokens, width)],
+        in_specs=[*whole(7), ANYWHERE],
+        out_specs=(*whole(3), ANYWHERE),
+        scratch_shapes=[
+            pltpu.VMEM((8, width), F32),
+            pltpu.VMEM(pieces.shape, BF16),
+            pltpu.SemaphoreType.DMA((3,)),
+            pltpu.SemaphoreType.DMA((3,)),
+            *OWNERS_SCRATCH,
+            *Scatter.scratch(tokens, width),
+        ],
         compiler_params=mixer_params(7),
-    )(left, right, own_in, gain[None], mlp_gains, grad_middle, reduced)
+    )(left, right, own_in, gain[None], mlp_gains, grad_middle, pieces, reduced)
 
 
 def owners_kernel(
     count, with_gates, pieces, values, reduced0, reduced1, gates_out, gains_out, out0, out1,
-    inbox, plane_sum, plane_box, sum_send, sum_recv, rows_recv, gates_all, gates_send, gates_recv,
+    inbox, plane_sum, plane_box, sum_send, sum_recv, gates_all, gates_send, gates_recv,
     send0, recv0, send1, recv1,
 ):
     place = Place()
     me = lax.axis_index("t")
     place.greet([place.peer(*offset) for offset in BEYOND] + [{"t": lax.rem(me + step, count)} for step in range(1, count)])
     owners = [Owners(place, reduced0, out0, send0, recv0), Owners(place, reduced1, out1, send1, recv1)]
-    gates = GateSums(place, count, pieces, rows_recv, gates_all, gates_send, gates_recv)
+    gates = GateSums(place, count, None, pieces, gates_all, gates_send, gates_recv)
     gains = SmallSum(place, count, values, inbox, plane_sum, plane_box, sum_send, sum_recv)
     gains.begin()
     if with_gates:
-        gates.begin()
+        gates.pass_on()
     for part in owners:
         part.begin()
     gains.pass_on()
-    if with_gates:
-        gates.pass_on()
     gains.finish(gains_out)
     if with_gates:
         gates.finish(gates_out)
@@ -1186,7 +1200,6 @@
             pltpu.VMEM((planes, *values.shape), F32),
             pltpu.SemaphoreType.DMA((planes + 6,)),
             pltpu.SemaphoreType.DMA((planes + 6,)),
-            pltpu.VMEM((slots, *block), BF16),
             pltpu.VMEM((slots, *block), BF16),
             pltpu.SemaphoreType.DMA((planes + 2,)),
             pltpu.SemaphoreType.DMA((planes + 2,)),
@@ -1538,8 +1551,8 @@
     grad_in = over_planes(grad_in)
     outputs = outputs.reshape(inputs.shape)
 
-    grad_inputs, values, owned_mlp_in = final_step(
-        grad_branches, in_w, own_in, mix_gain, grad_mlp_gain, grad_middle, by_owner(grad_mlp_in)
+    grad_inputs, values, pieces, owned_mlp_in = final_step(
+        grad_branches, in_w, own_in, mix_gain, grad_mlp_gain, grad_middle, pieces, by_owner(grad_mlp_in)
     )
     gate_grads, gains, owned_in, owned_out = owners_step(planes, direct, pieces, values, [by_owner(grad_in), by_owner(grad_out)])
     grad_inputs = grad_inputs.reshape(inputs.shape)

time: 627 us -> 627 us (level)
  transfers between devices with their start and end apart: 9 -> 9, of which waited for: 0 -> 0; matrix products, arithmetic and copies ran while one was open for 17% -> 17% of each run, Pallas kernels for 76% -> 77%
where the time goes in v14:
time: 627 us; the launch traced here: 623 us
  Pallas kernels  499 us (80%)
  matrix products  78.2 us (12%)
  local copies, waits for them, and re-layouts  25.6 us (4%)
  between operations  14.3 us (2%)
    pallas_call x1, Pallas kernels, middle_step(): pl.pallas_call(middle_kernel, name='middle_step', out_shape=(jax.ShapeDty...  85.1 us
    pallas_call x1, Pallas kernels, final_step(): pl.pallas_call(final_kernel, name='final_step', out_shape=(jax.ShapeDtype...  71.1 us
    pallas_call x1, Pallas kernels, mixer_backward(): pl.pallas_call(functools.partial(mixer_backward_kernel, count, seg), name...  68 us
    pallas_call x1, Pallas kernels, mixer_forward(): pl.pallas_call(functools.partial(mixer_forward_kernel, count, seg, rows_h...  59.6 us
    pallas_call x1, Pallas kernels, turn_step(): pl.pallas_call(turn_kernel, name='turn_step', out_shape=(jax.ShapeDtypeSt...  58 us
    dot_general x4, matrix products, nt(): lax.dot_general(left, right, (((1,), (1,)), ((), ())), preferred_element_...  55.6 us
    pallas_call x1, Pallas kernels, spread_step(): pl.pallas_call(spread_kernel, name='turn_spread', out_shape=(jax.ShapeDty...  52 us
    pallas_call x1, Pallas kernels, first_gather(): pl.pallas_call(functools.partial(first_gather_kernel, planes), name='firs...  45.6 us
  transfers between devices with their start and end apart: 9, of which 0 were waited for; matrix products, arithmetic and copies ran while one was open for 17% of the time, Pallas kernels for 77%

profile of v14, /device:TPU:0, one launch (start us, length us, event | category | flops | bytes accessed | tf_op | source)
XLA Modules:
  0.0 623.0 jit_solution(8558951488533283771)
XLA Ops:
  7.2 2.1 dynamic-slice_bitcast_fusion
  9.5 1.7 dynamic-slice_bitcast_fusion.1
  14.1 2.5 multiply_convert_fusion.3.normed
  16.6 45.6 %first_gather.1 = (bf16[2048,2048]{1,0:T(8,128)(2,1)}, f32[8,8,128]{2,1,0:T(8,128)}, f32[8,8,128]{2,1,0:T(8,128)}, f32[8,8,128]{2,1,0:T(8,128)}) custom-call(bf16[256,2048]{1,0:T(8,128)(2,1)} %multiply_convert_fusion.3.normed, f32[8,128]{1,0:T(8,128)} %pad.4.ids), custom_call_target="tpu_custom_call" | custom-call | tf_op jit(solution)/shard_map/first_gather/pallas_call | solution.py:1294
  62.2 5.8 constant_dynamic-slice_fusion.1
  68.1 6.1 copy.35
  74.1 2.7 fusion.2
  78.9 2.2 copy.36
  84.4 30.4 %swap.1 = bf16[2,4,80,2048]{3,2,1,0:T(8,128)(2,1)} custom-call(bf16[4,2,80,2048]{3,2,1,0:T(8,128)(2,1)} %bitcast.58), custom_call_target="tpu_custom_call" | custom-call | tf_op jit(solution)/shard_map/swap/pallas_call | solution.py:1412
  114.9 11.4 %fusion.3.branches_far = f32[2048,640]{1,0:T(8,128)} fusion(bf16[2048,2048]{1,0:T(8,128)(2,1)} %get-tuple-element.70, bf16[640,2048]{1,0:T(8,128)(2,1)} %bitcast.46), kind=kOutput, calls=%fused_computation.23 | convolution fusion | flops 5368709120 | bytes 16252928 | tf_op jit(solution)/shard_map/dot_general | solution.py:1428
  126.3 59.6 %mixer_forward.1 = (bf16[2048,320]{1,0:T(8,128)(2,1)}, f32[3,2048,128]{2,1,0:T(8,128)}, f32[2048,320]{1,0:T(8,128)}, bf16[2048,320]{1,0:T(8,128)(2,1)}, f32[128,...) custom-call(f32[2048,640]{1,0:T(8,128)} %fusion.3.branches_far, ...), custom_call_target="tpu_custom_call" | custom-call | tf_op jit(solution)/shard_map/mixer_forward/pallas_call | solution.py:427
  185.9 85.1 %middle_step.1 = (f32[256,2048]{1,0:T(8,128)}, bf16[2048,2048]{1,0:T(8,128)(2,1)}) custom-call(bf16[2048,320]{1,0:T(8,128)(2,1)} %get-tuple-element.76.left.mixed, bf16[320,2048]{1,0:T(8,128)(2,1)} %bitcast.49, bf16[256,2048]{1,0:T(8,128)(2,1)} %bitcast.44, f32[1,2048]{1,0:T(1,128)} %bitcast.68), custom_call_target="tpu_custom_call" | custom-call | tf_op jit(solution)/shard_map/middle_step/pallas_call | solution.py:1307
  271.1 11.8 %fusion.4 = f32[2048,768]{1,0:T(8,128)} fusion(bf16[2048,2048]{1,0:T(8,128)(2,1)} %get-tuple-element.78.normed_far, bf16[768,2048]{1,0:T(8,128)(2,1)} %bitcast.54), kind=kOutput, calls=%fused_computation.24 | convolution fusion | flops 6442450944 | bytes 17825792 | tf_op jit(solution)/shard_map/dot_general | solution.py:1428
  282.9 13.7 %multiply_convert_fusion.2 = (bf16[2048,768]{1,0:T(8,128)(2,1)S(1)}, f32[2048,768]{1,0:T(8,128)}) fusion(f32[2048,768]{1,0:T(8,128)} %fusion.4, bf16[2048,2048]{1,0:T(8,128)(2,1)} %get-tuple-element.78.normed_far, bf16[768,2048]{1,0:T(8,128)(2,1)} %bitcast.56), kind=kOutput, calls=%fused_computation.2 | convolution fusion | flops 6458179584 | bytes 27262976 | tf_op jit(solution)/shard_map/dot_general | solution.py:1428
  296.6 11.5 %convolution_convert_fusion = bf16[2048,768]{1,0:T(8,128)(2,1)} fusion(bf16[2048,2048]{1,0:T(8,128)(2,1)} %get-tuple-element.75, bf16[2048,768]{1,0:T(8,128)(2,1)S(1)} %get-tuple-element.93.hidden), kind=kOutput, calls=%fused_computation.6 | convolution fusion | flops 6444023808 | bytes 14680064 | tf_op jit(solution)/shard_map/dot_general | solution.py:1432
  308.2 18.7 %multiply_convert_fusion = (bf16[2048,768]{1,0:T(8,128)(2,1)}, bf16[2048,768]{1,0:T(8,128)(2,1)}) fusion(f32[2048,768]{1,0:T(8,128)} %fusion.4, f32[2048,768]{1,0:T(8,128)} %get-tuple-element.134, bf16[2048,2048]{1,0:T(8,128)(2,1)} %get-tuple-element.75, bf16[768,2048]{1,0:T(8,128)(2,1)} %all-gather.17.cloned.1.call-done.w_down), kind=kOutput, calls=%fused_computation | convolution fusion | flops 6477053952 | bytes 30408704 | tf_op jit(solution)/shard_map/dot_general | solution.py:1428
  326.9 58.0 %turn_step.1 = (f32[256,2048]{1,0:T(8,128)}, f32[8,2048]{1,0:T(8,128)}, bf16[2048,1536]{1,0:T(8,128)(2,1)}, bf16[256,2048]{1,0:T(8,128)(2,1)}) custom-call(bf16[2048,768]{1,0:T(8,128)(2,1)} %get-tuple-element.128.left0, bf16[2048,768]{1,0:T(8,128)(2,1)} %get-tuple-element.127.left1, bf16[768,2048]{1,0:T(8,128)(2,1)} %bitcast.55, bf16[768,2048]{1,0:T(8,128)(2,1)} %bitcast.57, ...), custom_call_target="tpu_custom_call" | custom-call | tf_op jit(solution)/shard_map/turn_step/pallas_call | solution.py:1320
  385.0 52.0 %turn_spread.1 = (f32[2048,320]{1,0:T(8,128)}, bf16[2048,320]{1,0:T(8,128)(2,1)}, bf16[2048,2048]{1,0:T(8,128)(2,1)}) custom-call(bf16[256,2048]{1,0:T(8,128)(2,1)} %get-tuple-element.85.block, bf16[320,2048]{1,0:T(8,128)(2,1)} %bitcast.50, bf16[2048,320]{1,0:T(8,128)(2,1)} %get-tuple-element.76.left.mixed), custom_call_target="tpu_custom_call" | custom-call | tf_op jit(solution)/shard_map/turn_spread/pallas_call | solution.py:1339
  437.1 68.0 %mixer_backward.1 = (bf16[2048,640]{1,0:T(8,128)(2,1)}, f32[320,320]{1,0:T(8,128)}, f32[320,320]{1,0:T(8,128)}, f32[8,320]{1,0:T(8,128)}, bf16[4,336,128]{2,1,0:...) custom-call(f32[2048,320]{1,0:T(8,128)} %get-tuple-element.86.grad_mixed_far, ...), custom_call_target="tpu_custom_call" | custom-call | tf_op jit(solution)/shard_map/mixer_backward/pallas_call | solution.py:467
  505.1 11.1 %convolution_convert_fusion.1 = bf16[2048,640]{1,0:T(8,128)(2,1)} fusion(bf16[2048,2048]{1,0:T(8,128)(2,1)} %get-tuple-element.70, bf16[2048,640]{1,0:T(8,128)(2,1)} %get-tuple-element.97.left), kind=kOutput, calls=%fused_computation.7 | convolution fusion | flops 5370019840 | bytes 13631488 | tf_op jit(solution)/shard_map/dot_general | solution.py:1432
  516.2 71.1 %final_step.1 = (f32[256,2048]{1,0:T(8,128)}, f32[32,128]{1,0:T(8,128)}, bf16[4,336,128]{2,1,0:T(8,128)(2,1)}, bf16[8,64,1536]{2,1,0:T(8,128)(2,1)}) custom-call(bf16[2048,640]{1,0:T(8,128)(2,1)} %get-tuple-element.97.left, bf16[640,2048]{1,0:T(8,128)(2,1)} %bitcast.47, bf16[256,2048]{1,0:T(8,128)(2,1)} %bitcast.45, f32[1,2048]{1,0:T(1,128)} %bitcast.70, ...), custom_call_target="tpu_custom_call" | custom-call | tf_op jit(solution)/shard_map/final_step/pallas_call | solution.py:1135
  587.4 6.9 %place_columns.1 = (f32[64,2,6144]{2,1,0:T(2,128)}, f32[64,6144]{1,0:T(8,128)}, bf16[2,128,2048]{2,1,0:T(8,128)(2,1)}, f32[2,128,2048]{2,1,0:T(8,128)}) custom-call(bf16[8,64,1536]{2,1,0:T(8,128)(2,1)} %get-tuple-element.102.refs_0_, bf16[8,64,768]{2,1,0:T(8,128)(2,1)} %get-tuple-element.103.refs_1_, bf16[2,128,2048]{2,1,0:T(8,128)(2,1)} %bitcast.64, ...), custom_call_target="tpu_custom_call" | custom-call | tf_op jit(solution)/shard_map/place_columns/pallas_call | solution.py:1241
  594.3 18.8 %owners_step.1 = (f32[336,128]{1,0:T(8,128)}, f32[32,128]{1,0:T(8,128)}, bf16[8,64,640]{2,1,0:T(8,128)(2,1)}, bf16[8,64,320]{2,1,0:T(8,128)(2,1)}) custom-call(bf16[4,336,128]{2,1,0:T(8,128)(2,1)} %get-tuple-element.108.pieces, f32[32,128]{1,0:T(8,128)} %get-tuple-element.109.values, bf16[8,64,640]{2,1,0:T(8,128)(2,1)} %bitcast.66, bf16[8,64,320]{2,1,0:T(8,128)(2,1)} %bitcast.67), custom_call_target="tpu_custom_call" | custom-call | tf_op jit(solution)/shard_map/owners_step/pallas_call | solution.py:1187
  613.2 3.0 place_last.1
  (55 shorter events, 8.5 us)
Async XLA Ops:
  7.2 70.3 %copy-start = (bf16[2048,768]{1,0:T(8,128)(2,1)S(1)}, bf16[2048,768]{1,0:T(8,128)(2,1)}, u32[]{:S(2)}) copy-start(bf16[2048,768]{1,0:T(8,128)(2,1)} %param.26) | copy-start | bytes 9437188
  7.2 77.2 %all-gather.13.cloned.1.call-start = ((), (), s32[]{:S(2)}) async-start(), calls=%async_computation.10 | async-start | bytes 3276800 | tf_op jit(solution)/shard_map/all_gather | solution.py:1475
  9.4 116.9 %all-gather.15.cloned.1.call-start = ((), (), s32[]{:S(2)}) async-start(), calls=%async_computation.11 | async-start | bytes 1638400 | tf_op jit(solution)/shard_map/all_gather | solution.py:1475
  11.2 259.9 %all-gather.9.cloned.1.call-start = ((), (), s32[]{:S(2)}) async-start(), calls=%async_computation.4 | async-start | bytes 3932160 | tf_op jit(solution)/shard_map/all_gather | solution.py:1475
  68.0 13.3 %copy-start.5 = (f32[2560]{0:T(1024)S(1)}, f32[2560]{0:T(1024)}, u32[]{:S(2)}) copy-start(f32[2560]{0:T(1024)} %param.19) | copy-start | bytes 30724
  68.1 13.3 %copy-start.6 = (f32[2560]{0:T(1024)S(1)}, f32[2560]{0:T(1024)}, u32[]{:S(2)}) copy-start(f32[2560]{0:T(1024)} %param.22) | copy-start | bytes 30724
  68.1 13.4 %copy-start.3 = (f32[4,2560]{1,0:T(4,128)S(1)}, f32[4,2560]{1,0:T(4,128)}, u32[]{:S(2)}) copy-start(f32[4,2560]{1,0:T(4,128)} %param.18) | copy-start | bytes 122884
  68.1 13.4 %copy-start.4 = (f32[2,2560]{1,0:T(2,128)S(1)}, f32[2,2560]{1,0:T(2,128)}, u32[]{:S(2)}) copy-start(f32[2,2560]{1,0:T(2,128)} %param.21) | copy-start | bytes 61444
  76.8 206.0 %all-gather.11.cloned.1.call-start = ((), (), s32[]{:S(2)}) async-start(), calls=%async_computation.5 | async-start | bytes 3932160 | tf_op jit(solution)/shard_map/all_gather | solution.py:1475
  77.4 230.7 %all-gather.17.cloned.1.call-start = ((), (), s32[]{:S(2)}) async-start(), calls=%async_computation.12 | async-start | bytes 3932160 | tf_op jit(solution)/shard_map/all_gather | solution.py:1475
  81.1 303.9 %reduce-scatter.7.cloned.1.call-start = ((), (), s32[]{:S(2)}) async-start(), calls=%async_computation.7 | async-start | bytes 3932160 | tf_op jit(solution)/shard_map/reduce_scatter | solution.py:1525
  296.6 11.5 %copy-start.2 = (bf16[2048,768]{1,0:T(8,128)(2,1)}, bf16[2048,768]{1,0:T(8,128)(2,1)S(1)}, u32[]{:S(2)}) copy-start(bf16[2048,768]{1,0:T(8,128)(2,1)S(1)} %get-tuple-element.93.hidden) | copy-start | bytes 9437188
  308.2 197.0 %reduce-scatter.5.cloned.1.call-start = ((), (), s32[]{:S(2)}) async-start(), calls=%async_computation.6 | async-start | bytes 7864320 | tf_op jit(solution)/shard_map/reduce_scatter | solution.py:1525
  384.9 209.4 %reduce-scatter.11.cloned.1.call-start = ((), (), s32[]{:S(2)}) async-start(), calls=%async_computation.9 | async-start | bytes 1966080 | tf_op jit(solution)/shard_map/reduce_scatter | solution.py:1525
  437.0 157.3 %reduce-scatter.9.cloned.1.call-start = ((), (), s32[]{:S(2)}) async-start(), calls=%async_computation.8 | async-start | bytes 3276800 | tf_op jit(solution)/shard_map/reduce_scatter | solution.py:1525
  516.2 100.0 %copy-start.1 = (bf16[2048,768]{1,0:T(8,128)(2,1)S(1)}, bf16[2048,768]{1,0:T(8,128)(2,1)}, u32[]{:S(2)}) copy-start(bf16[2048,768]{1,0:T(8,128)(2,1)} %param.26) | copy-start | bytes 9437188
Sparse Core Ops, SparseCore 0:
  10.2 58.8 all-gather.12
  71.2 31.4 all-gather.14
  104.9 66.6 all-gather.8
  173.5 62.0 all-gather.10
  237.6 62.1 all-gather.16
  308.3 58.3 reduce-scatter.6
  385.0 109.7 reduce-scatter.4
  497.2 35.8 reduce-scatter.10
  535.3 51.0 reduce-scatter.8
